TPU v7x, 32 devices: a whole 2x2x4 slice. The times are simulated.
32 devices in a mesh: groups: 2 (over x), row: 8 (over z, y), col: 2 (over core).
Axes of the slice: x: 2, y: 2, z: 4, core: 2. Of those that a mesh axis runs over, the one named last changes fastest.
Arguments:
- a_vals: bfloat16 [64, 20, 64, 64], P(('groups', 'row'), 'col'), parts along dimension 0, may hold values from -0.75 to 0.75
- b_vals: bfloat16 [64, 20, 64, 64], P(('groups', 'row'), 'col'), parts along dimension 0, may hold values from -2 to 2
- cols: int32 [64, 20], P(('groups', 'row'), 'col'), parts along dimension 0, may hold values from 0 to 31, as said below
Outputs:
- c_vals: bfloat16 [64, 20, 64, 64], P(('groups', 'row'), 'col'), parts along dimension 0
There are 2 independent parts, one for each index of `groups`. A program takes and returns all parts, laid end to end along the dimension named above; each array names one. Nothing has to cross between parts.
Inputs may be any that keep to these rules, and one draw needn't show every extreme that they name: `cols`: within a block row all 20 columns differ; slots 0 to 9 hold columns below 16, the other slots columns from 16 on. For each group of 4 consecutive block rows (starting at a multiple of 4) and each half, exactly one group of 4 consecutive block columns (starting at a multiple of 4) in that half is named by every row of the group in every one of its columns, so that 4 * 4 slots of the group fall into it; no group of 4 block columns can receive more.
All inputs are finite; a program needn't handle non-finite values.
Results may differ from a plain program's by a relative error of at most 0.001.
Values may be sent and summed in bfloat16 or wider, within the bound.
No kernel may reach another device: no remote copies, remote signals or barrier semaphores. Data moves between devices by JAX's collectives and lax.ppermute only.
A program may use at most 128 MiB of HBM per device.

v0:
```python
import jax
import jax.numpy as jnp
from jax import lax
from jax.sharding import PartitionSpec as P


def multiply_rows(a_rows, a_cols, b_whole, b_cols, own_cols):
    inner = b_whole[a_cols]
    inner_cols = b_cols[a_cols]
    match = (inner_cols[:, :, :, None] == own_cols[:, None, None, :]).astype(jnp.bfloat16)
    picked = jnp.einsum(
        "rmno,rmnbc->rmobc", match, inner, preferred_element_type=jnp.float32
    ).astype(jnp.bfloat16)
    return jnp.einsum(
        "rmab,rmobc->roac", a_rows, picked, preferred_element_type=jnp.float32
    ).astype(jnp.bfloat16)


def local(a_vals, b_vals, cols):
    a_rows, b_rows, col_rows = (
        lax.all_to_all(a_vals, "col", split_axis=0, concat_axis=1, tiled=True),
        lax.all_to_all(b_vals, "col", split_axis=0, concat_axis=1, tiled=True),
        lax.all_to_all(cols, "col", split_axis=0, concat_axis=1, tiled=True),
    )
    b_whole, b_cols = (
        lax.all_gather(b_rows, ("row", "col"), axis=0, tiled=True),
        lax.all_gather(col_rows, ("row", "col"), axis=0, tiled=True),
    )
    blocks = multiply_rows(a_rows, col_rows, b_whole, b_cols, col_rows)
    return lax.all_to_all(blocks, "col", split_axis=1, concat_axis=0, tiled=True)


def solution(mesh):
    return jax.shard_map(
        local,
        mesh=mesh,
        in_specs=(
            P(("groups", "row"), "col", None, None),
            P(("groups", "row"), "col", None, None),
            P(("groups", "row"), "col"),
        ),
        out_specs=P(("groups", "row"), "col", None, None),
        check_vma=False,
    )
```

profile of v0, /device:TPU:0, one launch (start us, length us, event | category | flops | bytes accessed | tf_op | source)
XLA Modules:
  0.0 157.9 jit_solution(13741643612122663519)
XLA Ops:
  6.5 0.0 all-gather.3.cloned.1.call-start
  6.5 1.6 reshape.61
  8.1 4.0 %all_to_all.76 = bf16[2,2,40960]{2,1,0:T(2,128)(2,1)S(1)} all-to-all(bf16[2,2,40960]{2,1,0:T(2,128)(2,1)S(1)} %reshape.61), channel_id=1, replica_groups=mesh['groups'=2,'row'=8,'col'=2] {'col'}, dimensions={0} | all-to-all | bytes 655360 | tf_op jit(solution)/shard_map/all_to_all | solution.py:22
  12.1 0.4 reshape.62
  12.5 0.9 copy.31
  13.4 0.0 all-gather.3.cloned.1.call-update
  13.4 3.2 %all-to-all-start = ((s32[2,2,10]{2,1,0:T(2,128)}), s32[2,2,10]{2,1,0:T(2,128)S(1)}, u32[]{:S(2)}, u32[]{:S(2)}) async-start(s32[2,2,10]{2,1,0:T(2,128)} %bitcast.50), calls=%async_computation | async-start | bytes 4096 | tf_op jit(solution)/shard_map/all_to_all | solution.py:23
  16.7 2.3 %reshape.59 = bf16[2,2,40960]{2,1,0:T(2,128)(2,1)} reshape(bf16[4,10,64,64]{3,2,1,0:T(8,128)(2,1)} %param.3) | data formatting | bytes 655360
  19.0 0.0 all-to-all-done
  19.0 3.5 %all-to-all-start.2 = ((bf16[2,2,40960]{2,1,0:T(2,128)(2,1)}), bf16[2,2,40960]{2,1,0:T(2,128)(2,1)S(1)}, u32[]{:S(2)}, u32[]{:S(2)}) async-start(bf16[2,2,40960]{2,1,0:T(2,128)(2,1)} %reshape.59), calls=%async_computation.2 | async-start | bytes 655360 | tf_op jit(solution)/shard_map/all_to_all | solution.py:21
  22.5 0.1 all_to_all.59
  22.5 0.1 reshape.52
  22.6 0.1 all_to_all.58
  22.7 0.1 reshape.36
  22.8 23.3 %all-gather = s32[16,2,20]{2,1,0:T(2,128)S(1)} all-gather(s32[1,2,20]{2,1,0:T(2,128)S(1)} %reshape.52), channel_id=1, replica_groups=mesh['groups'=2,'row'=8,'col'=2] {'row','col'}, dimensions={0}, use_global_device_ids=true | all-gather | bytes 2720 | tf_op jit(solution)/shard_map/all_gather | solution.py:27
  46.1 0.6 gather_fusion
  46.7 0.0 all-to-all-done.2
  46.7 0.4 reshape.60
  47.2 57.1 %all-gather.3.cloned.1.call-done = bf16[32,20,64,64]{3,2,1,0:T(8,128)(2,1)} async-done(((bf16[2,20,64,64]{3,2,1,0:T(8,128)(2,1)}), bf16[32,20,64,64]{3,2,1,0:T(8,128)(2,1)}) %all-gather.3.cloned.1.call-update) | async-done | bytes 5242896 | tf_op jit(solution)/shard_map/all_gather | solution.py:26
  104.3 10.8 %gather_fusion.1 = bf16[40,20,64,64]{3,2,1,0:T(8,128)(2,1)} fusion(bf16[32,20,64,64]{3,2,1,0:T(8,128)(2,1)} %all-gather.3.cloned.1.call-done, s32[1024]{0:T(1024)S(1)} %pad_clamp_fusion), kind=kCustom, calls=%fused_computation.1 | custom fusion | bytes 13107360 | tf_op jit(solution)/shard_map/gather | solution.py:8
  115.0 19.3 %fusion.2 = bf16[2,20,20,64,64]{4,2,3,1,0:T(8,128)(2,1)} fusion(bf16[2,20,20,64,64]{4,3,2,1,0:T(8,128)(2,1)} %bitcast.41, s32[2,20]{1,0:T(2,128)S(1)} %all_to_all.58, s32[2,20,20]{2,1,0:T(8,128)S(1)} %reshape.58), kind=kOutput, calls=%fused_computation.4 | convolution fusion | flops 134364800 | bytes 13110560 | tf_op jit(solution)/shard_map/rmno,rmnbc->rmobc/dot_general | solution.py:11
  134.3 10.7 %fusion.13 = bf16[2,20,64,64]{2,3,1,0:T(8,128)(2,1)S(1)} fusion(bf16[2,20,64,64,1]{3,2,1,4,0:T(8,128)(2,1)S(1)} %bitcast.48, bf16[2,20,20,64,64]{4,2,3,1,0:T(8,128)(2,1)} %fusion.2), kind=kOutput, calls=%fused_computation.9 | convolution fusion | flops 419594240 | bytes 7208960 | tf_op jit(solution)/shard_map/rmab,rmobc->roac/dot_general | solution.py:14
  145.0 0.1 copy.54
  145.0 0.5 reshape.63
  145.5 4.0 %all_to_all.77 = bf16[2,2,40960]{2,1,0:T(2,128)(2,1)S(1)} all-to-all(bf16[2,2,40960]{2,1,0:T(2,128)(2,1)S(1)} %reshape.63), channel_id=1, replica_groups=mesh['groups'=2,'row'=8,'col'=2] {'col'}, dimensions={0} | all-to-all | bytes 655360 | tf_op jit(solution)/shard_map/all_to_all | solution.py:30
  149.5 0.4 reshape.64
  150.0 1.1 copy.36
  (5 shorter events, 0.1 us)
Async XLA Ops:
  6.5 97.7 %all-gather.3.cloned.1.call-start = ((), (), s32[]{:S(2)}) async-start(), calls=%async_computation.4 | async-start | bytes 11141120 | tf_op jit(solution)/shard_map/all_gather | solution.py:26
  13.4 5.5 %all-to-all-start = ((s32[2,2,10]{2,1,0:T(2,128)}), s32[2,2,10]{2,1,0:T(2,128)S(1)}, u32[]{:S(2)}, u32[]{:S(2)}) async-start(s32[2,2,10]{2,1,0:T(2,128)} %bitcast.50), calls=%async_computation | async-start | bytes 4096 | tf_op jit(solution)/shard_map/all_to_all | solution.py:23
  19.0 27.7 %all-to-all-start.2 = ((bf16[2,2,40960]{2,1,0:T(2,128)(2,1)}), bf16[2,2,40960]{2,1,0:T(2,128)(2,1)S(1)}, u32[]{:S(2)}, u32[]{:S(2)}) async-start(bf16[2,2,40960]{2,1,0:T(2,128)(2,1)} %reshape.59), calls=%async_computation.2 | async-start | bytes 655360 | tf_op jit(solution)/shard_map/all_to_all | solution.py:21
Sparse Core Ops, SparseCore 0:
  13.6 90.6 all-gather.2
where the time goes:
time: 158 us
  waiting for transfers between devices  57.1 us (36%)
  blocking collectives  31.3 us (20%)
  matrix products  30 us (19%)
  local copies, waits for them, and re-layouts  19.3 us (12%)
  between operations  13.5 us (9%)
  starting transfers between devices  6.69 us (4%)
    all_gather x1, waiting for transfers between devices, local(): lax.all_gather(b_rows, ('row', 'col'), axis=0, tiled=True)  57.1 us
    all_gather x1, blocking collectives, local(): lax.all_gather(col_rows, ('row', 'col'), axis=0, tiled=True)  23.3 us
    dot_general x1, matrix products, multiply_rows(): jnp.einsum('rmno,rmnbc->rmobc', match, inner, preferred_element_type=jnp....  19.3 us
    gather x1, local copies, waits for them, and re-layouts, multiply_rows(): inner = b_whole[a_cols]  10.8 us
    dot_general x1, matrix products, multiply_rows(): jnp.einsum('rmab,rmobc->roac', a_rows, picked, preferred_element_type=jnp...  10.7 us
    unnamed x7, local copies, waits for them, and re-layouts  5.69 us
    all_to_all x1, blocking collectives, local(): lax.all_to_all(b_vals, 'col', split_axis=0, concat_axis=1, tiled=True)  4 us
    all_to_all x1, blocking collectives, local(): lax.all_to_all(blocks, 'col', split_axis=1, concat_axis=0, tiled=True)  4 us
  transfers between devices with their start and end apart: 3, of which 1 were waited for; matrix products, arithmetic and copies ran while one was open for 2% of the time, Pallas kernels for 0%

commit v1 on v0

v1 whole, which is shorter than its diff:
```python
import functools

import jax
import jax.numpy as jnp
from jax import lax
from jax.experimental import pallas as pl
from jax.experimental.pallas import tpu as pltpu
from jax.sharding import PartitionSpec as P

VMEM = pltpu.VMEM
LIMIT = 48 * 1024 * 1024


def pack_kernel(b_ref, o_ref):
    pairs, slots = o_ref.shape[:2]
    for p in range(pairs):
        for n in range(slots):
            o_ref[p, n] = jnp.concatenate([b_ref[2 * p, n], b_ref[2 * p + 1, n]], axis=-1)


def pack(b_vals):
    rows, slots, bs, _ = b_vals.shape
    return pl.pallas_call(
        pack_kernel,
        out_shape=jax.ShapeDtypeStruct((rows // 2, slots, bs, 2 * bs), b_vals.dtype),
        in_specs=[pl.BlockSpec(memory_space=VMEM)],
        out_specs=pl.BlockSpec(memory_space=VMEM),
        compiler_params=pltpu.CompilerParams(vmem_limit_bytes=LIMIT),
    )(b_vals)


def dense_kernel(where_ref, own_ref, other_ref, o_ref, blocks):
    rows, slots = own_ref.shape[:2]
    blocks[:, :slots] = own_ref[...]
    blocks[:, slots : 2 * slots] = other_ref[...]
    blocks[:, 2 * slots] = jnp.zeros_like(blocks[:, 2 * slots])
    bs = own_ref.shape[-1]
    for i in range(rows):
        def body(q, carry):
            left = blocks[i, where_ref[i, 2 * q]]
            right = blocks[i, where_ref[i, 2 * q + 1]]
            o_ref[q, i * bs : (i + 1) * bs, :] = jnp.concatenate([left, right], axis=-1)
            return carry

        lax.fori_loop(0, o_ref.shape[0], body, 0)


def dense_rows(where, own, other):
    rows, slots, bs, _ = own.shape
    return pl.pallas_call(
        dense_kernel,
        out_shape=jax.ShapeDtypeStruct((where.shape[1] // 2, rows * bs, 2 * bs), own.dtype),
        grid_spec=pltpu.PrefetchScalarGridSpec(
            num_scalar_prefetch=1,
            grid=(),
            in_specs=[pl.BlockSpec(memory_space=VMEM)] * 2,
            out_specs=pl.BlockSpec(memory_space=VMEM),
            scratch_shapes=[VMEM((rows, 2 * slots + 1, bs, bs), own.dtype)],
        ),
        compiler_params=pltpu.CompilerParams(vmem_limit_bytes=LIMIT),
    )(where, own, other)


def product_kernel(where_ref, place_ref, a_ref, g_ref, o_ref, blocks, total, sems):
    sources, pairs, slots, bs, _ = g_ref.shape
    groups = total.shape[0]
    copies = [
        pltpu.make_async_copy(g_ref.at[s], blocks.at[s, :, pl.ds(0, slots)], sems.at[s])
        for s in range(sources)
    ]
    for copy in copies:
        copy.start()
    blocks[:, :, slots] = jnp.zeros_like(blocks[:, :, slots])
    low = lax.broadcasted_iota(jnp.int32, (bs, 2 * bs), 1) < bs

    def turn(x):
        return jnp.concatenate([x[:, bs:], x[:, :bs]], axis=-1)

    for s, copy in enumerate(copies):
        copy.wait()
        a = jnp.concatenate([a_ref[s * pairs + p] for p in range(pairs)], axis=-1)
        for g in range(groups):
            panel = []
            for p in range(pairs):
                for h in range(2):
                    j = (s * pairs + p) * 2 + h
                    tiles = []
                    for q in (2 * g, 2 * g + 1):
                        left = blocks[s, p, where_ref[j, 2 * q]]
                        right = blocks[s, p, where_ref[j, 2 * q + 1]]
                        if h == 0:
                            right = turn(right)
                        else:
                            left = turn(left)
                        tiles.append(jnp.where(low, left, right))
                    panel.append(jnp.concatenate(tiles, axis=-1))
            part = jnp.dot(a, jnp.concatenate(panel, axis=0), preferred_element_type=jnp.float32)
            for t in range(2):
                piece = part[:, t * 2 * bs : (t + 1) * 2 * bs]
                if s == 0:
                    total[g, t] = piece
                else:
                    total[g, t] += piece
    for i in range(o_ref.shape[0]):
        for k in range(slots):
            l = place_ref[i, k]
            tile = total[l // 4, (l // 2) % 2, i * bs : (i + 1) * bs, :]
            tile = jnp.where(l % 2 == 0, tile, pltpu.roll(tile, bs, 1))
            o_ref[i, k] = tile[:, :bs].astype(o_ref.dtype)


def product(where, place, a, gathered):
    sources, pairs, slots, bs, _ = gathered.shape
    rows = a.shape[1] // bs
    groups = where.shape[1] // 4
    return pl.pallas_call(
        product_kernel,
        out_shape=jax.ShapeDtypeStruct((rows, slots, bs, bs), gathered.dtype),
        grid_spec=pltpu.PrefetchScalarGridSpec(
            num_scalar_prefetch=2,
            grid=(),
            in_specs=[pl.BlockSpec(memory_space=VMEM), pl.BlockSpec(memory_space=pl.ANY)],
            out_specs=pl.BlockSpec(memory_space=VMEM),
            scratch_shapes=[
                VMEM((sources, pairs, slots + 1, bs, 2 * bs), gathered.dtype),
                VMEM((groups, 2, rows * bs, 2 * bs), jnp.float32),
                pltpu.SemaphoreType.DMA((sources,)),
            ],
        ),
        compiler_params=pltpu.CompilerParams(vmem_limit_bytes=LIMIT),
    )(where, place, a, gathered)


def slot_of(cols, first, count):
    slots = cols.shape[1]
    hit = cols[:, :, None] == first + jnp.arange(count, dtype=jnp.int32)[None, None, :]
    slot = jnp.arange(slots, dtype=jnp.int32)[None, :, None]
    return slots - jnp.sum(jnp.where(hit, slots - slot, 0), axis=1)


def local(sources, a_vals, b_vals, cols):
    rows, slots, bs, _ = a_vals.shape
    half = sources * rows // 2
    me = lax.axis_index("col")
    gathered = lax.all_gather(pack(b_vals), "row", axis=0)
    all_cols = lax.all_gather(cols, ("row", "col"), axis=0).reshape(sources, 2, rows, slots)
    swap = [(0, 1), (1, 0)]
    a_other = lax.ppermute(a_vals, "col", swap)
    my_half = lax.dynamic_index_in_dim(all_cols, me, 1, keepdims=False).reshape(sources * rows, slots)
    chip = lax.dynamic_index_in_dim(all_cols, lax.axis_index("row"), 0, keepdims=False)
    other = lax.dynamic_index_in_dim(chip, 1 - me, 0, keepdims=False)
    a_where = slot_of(jnp.concatenate([cols, other], axis=1), 0, 2 * half)
    a = dense_rows(a_where, a_vals, a_other)
    b_where = slot_of(my_half, me * half, half)
    return product(b_where, cols - me * half, a, gathered)


def solution(mesh):
    return jax.shard_map(
        functools.partial(local, mesh.shape["row"]),
        mesh=mesh,
        in_specs=(
            P(("groups", "row"), "col", None, None),
            P(("groups", "row"), "col", None, None),
            P(("groups", "row"), "col"),
        ),
        out_specs=P(("groups", "row"), "col", None, None),
        check_vma=False,
    )
```

time: 158 us -> 81.2 us (0.51)
  waiting for transfers between devices: 57.1 us -> 26.4 us
  matrix products: 30 us -> 0 us
  local copies, waits for them, and re-layouts: 19.3 us -> 4.17 us
  Pallas kernels: 0 us -> 11.5 us
  blocking collectives: 31.3 us -> 23.2 us
  starting transfers between devices: 6.69 us -> 0.52 us
  other arithmetic: 0.01 us -> 1.66 us
    all_gather x1, waiting for transfers between devices: 57.1 us -> 26.3 us  [local(): gathered = lax.all_gather(pack(b_vals), 'row', axis=0)]
    dot_general x2 -> x0, matrix products: 30 us -> none  [the longest x1 19.3 us: multiply_rows(): jnp.einsum('rmno,rmnbc->rmobc', match, inner, preferred_element_type=jnp....]
    pallas_call x0 -> x3, Pallas kernels: none -> 11.5 us  [the longest x1 5.44 us: dense_rows(): pl.pallas_call(dense_kernel, out_shape=jax.ShapeDtypeStruct((where.shape[...]
    gather x3 -> x0, local copies, waits for them, and re-layouts: 11.3 us -> none  [the longest x1 10.8 us: multiply_rows(): inner = b_whole[a_cols]]
    all_to_all x2 -> x0, blocking collectives: 7.99 us -> none  [the longest x1 4 us: local(): lax.all_to_all(b_vals, 'col', split_axis=0, concat_axis=1, tiled=True)]
    all_to_all x2 -> x0, starting transfers between devices: 6.69 us -> none  [the longest x1 3.45 us: local(): lax.all_to_all(a_vals, 'col', split_axis=0, concat_axis=1, tiled=True)]
    all_to_all x6 -> x0, local copies, waits for them, and re-layouts: 2.18 us -> none  [the longest x1 1.09 us: local(): lax.all_to_all(blocks, 'col', split_axis=1, concat_axis=0, tiled=True)]
    unnamed x7 -> x6, local copies, waits for them, and re-layouts: 5.69 us -> 3.91 us
  transfers between devices with their start and end apart: 3 -> 2, of which waited for: 1 -> 1; matrix products, arithmetic and copies ran while one was open for 2% -> 2% of each run, Pallas kernels for 0% -> 7%
where the time goes in v1:
time: 81.2 us; the launch traced here: 80.9 us
  waiting for transfers between devices  26.4 us (33%)
  blocking collectives  23.2 us (29%)
  between operations  13.4 us (17%)
  Pallas kernels  11.5 us (14%)
  local copies, waits for them, and re-layouts  4.17 us (5%)
  other arithmetic  1.66 us (2%)
    all_gather x1, waiting for transfers between devices, local(): gathered = lax.all_gather(pack(b_vals), 'row', axis=0)  26.3 us
    all_gather x1, blocking collectives, local(): lax.all_gather(cols, ('row', 'col'), axis=0)  23.2 us
    pallas_call x1, Pallas kernels, dense_rows(): pl.pallas_call(dense_kernel, out_shape=jax.ShapeDtypeStruct((where.shape[...  5.44 us
    pallas_call x1, Pallas kernels, product(): pl.pallas_call(product_kernel, out_shape=jax.ShapeDtypeStruct((rows, slot...  5.22 us
    unnamed x6, local copies, waits for them, and re-layouts  3.91 us
  transfers between devices with their start and end apart: 2, of which 1 were waited for; matrix products, arithmetic and copies ran while one was open for 2% of the time, Pallas kernels for 7%

profile of v1, /device:TPU:0, one launch (start us, length us, event | category | flops | bytes accessed | tf_op | source)
XLA Modules:
  0.0 80.9 jit_solution(5226311418312588327)
XLA Ops:
  6.5 0.0 all-gather.5.cloned.1.call-start
  6.5 0.0 copy-start.1
  6.5 1.1 %copy-done.1 = bf16[4,10,64,64]{3,2,1,0:T(8,128)(2,1)S(1)} copy-done((bf16[4,10,64,64]{3,2,1,0:T(8,128)(2,1)S(1)}, bf16[4,10,64,64]{3,2,1,0:T(8,128)(2,1)}, u32[]{:S(2)}) %copy-start.1) | copy-done | bytes 327704
  7.6 0.9 %shard_map.38 = bf16[2,10,64,128]{3,2,1,0:T(8,128)(2,1)} custom-call(bf16[4,10,64,64]{3,2,1,0:T(8,128)(2,1)S(1)} %copy-done.1), custom_call_target="tpu_custom_call" | custom-call | tf_op jit(solution)/shard_map/pallas_call | solution.py:23
  8.5 0.0 all-gather.5.cloned.1.call-update
  8.5 0.5 collective-permute-start
  9.0 23.2 %all-gather.2 = s32[16,4,10]{2,1,0:T(4,128)S(1)} all-gather(s32[1,4,10]{2,1,0:T(4,128)} %bitcast.10), channel_id=2, replica_groups=mesh['groups'=2,'row'=8,'col'=2] {'row','col'}, dimensions={0}, use_global_device_ids=true | all-gather | bytes 2720 | tf_op jit(solution)/shard_map/all_gather | solution.py:146
  32.3 0.8 pad_add_fusion
  33.0 0.1 copy.12
  33.1 0.1 copy.9
  33.2 0.1 select_reduce_fusion.1
  33.4 0.7 broadcast_subtract_fusion.2.place_ref
  34.0 0.1 select_reduce_fusion
  34.1 0.1 copy.11
  34.2 0.0 collective-permute-done.other_ref
  34.2 0.0 copy-start.2
  34.2 1.1 %copy-done.2 = bf16[4,10,64,64]{3,2,1,0:T(8,128)(2,1)S(1)} copy-done((bf16[4,10,64,64]{3,2,1,0:T(8,128)(2,1)S(1)}, bf16[4,10,64,64]{3,2,1,0:T(8,128)(2,1)}, u32[]{:S(2)}) %copy-start.2) | copy-done | bytes 327704
  35.3 5.4 %shard_map.37.a_ref = bf16[16,256,128]{2,1,0:T(8,128)(2,1)S(1)} custom-call(s32[4,32]{1,0:T(4,128)S(1)} %broadcast_subtract_fusion.1.where_ref, bf16[4,10,64,64]{3,2,1,0:T(8,128)(2,1)S(1)} %copy-done.2, bf16[4,10,64,64]{3,2,1,0:T(8,128)(2,1)S(1)} %collective-permute-done.other_ref), custom_call_target="tpu_custom_call" | custom-call | tf_op jit(solution)/shard_map/pallas_call | solution.py:50
  40.8 26.3 %all-gather.5.cloned.1.call-done = bf16[16,10,64,128]{3,2,1,0:T(8,128)(2,1)} async-done(((bf16[2,10,64,128]{3,2,1,0:T(8,128)(2,1)}), bf16[16,10,64,128]{3,2,1,0:T(8,128)(2,1)}) %all-gather.5.cloned.1.call-update) | async-done | bytes 2621456 | tf_op jit(solution)/shard_map/all_gather | solution.py:145
  67.1 0.0 copy-start
  67.1 1.7 %copy-done = bf16[16,10,64,128]{3,2,1,0:T(8,128)(2,1)S(1)} copy-done((bf16[16,10,64,128]{3,2,1,0:T(8,128)(2,1)S(1)}, bf16[16,10,64,128]{3,2,1,0:T(8,128)(2,1)}, u32[]{:S(2)}) %copy-start) | copy-done | bytes 2621464
  68.8 5.2 %shard_map.39 = bf16[4,10,64,64]{3,2,1,0:T(8,128)(2,1)} custom-call(s32[32,16]{1,0:T(8,128)S(1)} %broadcast_subtract_fusion.where_ref, s32[4,10]{1,0:T(4,128)S(1)} %broadcast_subtract_fusion.2.place_ref, bf16[16,256,128]{2,1,0:T(8,128)(2,1)S(1)} %shard_map.37.a_ref, bf16[8,2,10,64,128]{4,3,2,1,0:T(8,128)(2,1)S(1)} %bitcast.6), custom_call_target="tpu_custom_call" | custom-call | tf_op jit(solution)/shard_map/pallas_call | solution.py:116
  (7 shorter events, 0.0 us)
Async XLA Ops:
  6.5 60.6 %all-gather.5.cloned.1.call-start = ((), (), s32[]{:S(2)}) async-start(), calls=%async_computation | async-start | bytes 2949120 | tf_op jit(solution)/shard_map/all_gather | solution.py:145
  6.5 1.1 %copy-start.1 = (bf16[4,10,64,64]{3,2,1,0:T(8,128)(2,1)S(1)}, bf16[4,10,64,64]{3,2,1,0:T(8,128)(2,1)}, u32[]{:S(2)}) copy-start(bf16[4,10,64,64]{3,2,1,0:T(8,128)(2,1)} %b_ref.1) | copy-start | bytes 983044
  8.5 25.7 %collective-permute-start = (bf16[4,10,64,64]{3,2,1,0:T(8,128)(2,1)}, bf16[4,10,64,64]{3,2,1,0:T(8,128)(2,1)S(1)}, u32[]{:S(2)}, u32[]{:S(2)}) collective-permute-start(bf16[4,10,64,64]{3,2,1,0:T(8,128)(2,1)} %own_ref.1), channel_id=1, source_target_pairs={{0,1},{1,0},{2,3},{3,2},{4,5},{5,4},{6,7},{7,6},{8,9},{9,8},{10,11... | collective-permute-start | bytes 983048 | tf_op jit(solution)/shard_map/ppermute | solution.py:148
  34.2 1.1 %copy-start.2 = (bf16[4,10,64,64]{3,2,1,0:T(8,128)(2,1)S(1)}, bf16[4,10,64,64]{3,2,1,0:T(8,128)(2,1)}, u32[]{:S(2)}) copy-start(bf16[4,10,64,64]{3,2,1,0:T(8,128)(2,1)} %own_ref.1) | copy-start | bytes 983044
  67.1 1.7 %copy-start = (bf16[16,10,64,128]{3,2,1,0:T(8,128)(2,1)S(1)}, bf16[16,10,64,128]{3,2,1,0:T(8,128)(2,1)}, u32[]{:S(2)}) copy-start(bf16[16,10,64,128]{3,2,1,0:T(8,128)(2,1)} %all-gather.5.cloned.1.call-done) | copy-start | bytes 7864324
Sparse Core Ops, SparseCore 0:
  9.5 57.5 all-gather.4

commit v2 on v0

v2 whole, which is shorter than its diff:
```python
import functools

import jax
import jax.numpy as jnp
import numpy as np
from jax import lax
from jax.experimental import pallas as pl
from jax.experimental.pallas import tpu as pltpu
from jax.sharding import PartitionSpec as P

VMEM = pltpu.VMEM
SMEM = pltpu.SMEM
LIMIT = 48 * 1024 * 1024
FOOT = 16


def params():
    return pltpu.CompilerParams(vmem_limit_bytes=LIMIT)


def cost(flops, size):
    return pl.CostEstimate(flops=flops, bytes_accessed=size, transcendentals=0)


def pack_kernel(half, cols_ref, b_ref, *o_refs):
    _, slots, bs, _ = b_ref.shape
    row = lax.broadcasted_iota(jnp.int32, (FOOT, 2 * bs), 0)
    lane = lax.broadcasted_iota(jnp.int32, (FOOT, 2 * bs), 1)
    for p, o_ref in enumerate(o_refs):
        for n in range(slots):
            o_ref[n * bs : (n + 1) * bs, :] = jnp.concatenate([b_ref[2 * p, n], b_ref[2 * p + 1, n]], axis=-1)
        foot = jnp.full((FOOT, 2 * bs), slots, jnp.int32)
        for h in range(2):
            for n in range(slots):
                here = (row == h) & (lane == lax.rem(cols_ref[2 * p + h, n], half))
                foot = jnp.where(here, n, foot)
        o_ref[slots * bs :, :] = foot.astype(jnp.float32).astype(o_ref.dtype)


def pack(half, cols, b_vals):
    rows, slots, bs, _ = b_vals.shape
    shape = jax.ShapeDtypeStruct((slots * bs + FOOT, 2 * bs), b_vals.dtype)
    return pl.pallas_call(
        functools.partial(pack_kernel, half),
        out_shape=[shape] * (rows // 2),
        grid_spec=pltpu.PrefetchScalarGridSpec(
            num_scalar_prefetch=1,
            grid=(),
            in_specs=[pl.BlockSpec(memory_space=VMEM)],
            out_specs=[pl.BlockSpec(memory_space=VMEM)] * (rows // 2),
        ),
        compiler_params=params(),
        cost_estimate=cost(0, 2 * b_vals.size * 2),
    )(cols, b_vals)


def dense_kernel(cols_ref, others_ref, own_ref, other_ref, o_ref, blocks, where):
    rows, slots, bs, _ = own_ref.shape
    count = o_ref.shape[0]
    blocks[:, :slots] = own_ref[...]
    blocks[:, slots : 2 * slots] = other_ref[...]
    blocks[:, 2 * slots] = jnp.zeros_like(blocks[:, 2 * slots])
    for i in range(rows):
        def clear(j, carry):
            where[i, j] = 2 * slots
            return carry

        lax.fori_loop(0, 2 * count, clear, 0, unroll=8)
        for m in range(slots):
            where[i, cols_ref[i, m]] = m
            where[i, others_ref[i, m]] = slots + m

    def body(q, carry):
        for i in range(rows):
            left = blocks[i, where[i, 2 * q]]
            right = blocks[i, where[i, 2 * q + 1]]
            o_ref[q, i * bs : (i + 1) * bs, :] = jnp.concatenate([left, right], axis=-1)
        return carry

    lax.fori_loop(0, count, body, 0, unroll=4)


def dense_rows(count, cols, others, own, other):
    rows, slots, bs, _ = own.shape
    return pl.pallas_call(
        dense_kernel,
        out_shape=jax.ShapeDtypeStruct((count // 2, rows * bs, 2 * bs), own.dtype),
        grid_spec=pltpu.PrefetchScalarGridSpec(
            num_scalar_prefetch=2,
            grid=(),
            in_specs=[pl.BlockSpec(memory_space=VMEM)] * 2,
            out_specs=pl.BlockSpec(memory_space=VMEM),
            scratch_shapes=[VMEM((rows, 2 * slots + 1, bs, bs), own.dtype), SMEM((rows, count), jnp.int32)],
        ),
        compiler_params=params(),
        cost_estimate=cost(0, 4 * own.size * 2),
    )(cols, others, own, other)


def add_products(done, ids_ref, a_ref, parts, total, first, feet, where, sem):
    groups, bs = total.shape[0], total.shape[3] // 2
    slots = (parts[0][0].shape[0] - FOOT) // bs
    pairs = len(parts[0])
    for s, source in enumerate(parts):
        for p, part in enumerate(source):
            feet[s * pairs + p] = part[slots * bs :, :].astype(jnp.float32).astype(jnp.int32)
    copy = pltpu.make_async_copy(feet, where, sem)
    copy.start()
    copy.wait()
    low = lax.broadcasted_iota(jnp.int32, (bs, 2 * bs), 1) < bs

    def block(part, slot):
        at = pl.multiple_of(jnp.minimum(slot, slots - 1) * bs, bs)
        return jnp.where(slot < slots, part[pl.ds(at, bs), :], jnp.zeros((bs, 2 * bs), part.dtype))

    def turn(x):
        return jnp.concatenate([x[:, bs:], x[:, :bs]], axis=-1)

    for s, source in enumerate(parts):
        a = jnp.concatenate([a_ref[ids_ref[done + s] * pairs + p] for p in range(pairs)], axis=-1)

        def body(g, carry, s=s, source=source, a=a):
            panel = []
            for p, part in enumerate(source):
                for h in range(2):
                    tiles = []
                    for q in (2 * g, 2 * g + 1):
                        left = block(part, where[s * pairs + p, h, 2 * q])
                        right = block(part, where[s * pairs + p, h, 2 * q + 1])
                        if h == 0:
                            right = turn(right)
                        else:
                            left = turn(left)
                        tiles.append(jnp.where(low, left, right))
                    panel.append(jnp.concatenate(tiles, axis=-1))
            sums = jnp.dot(a, jnp.concatenate(panel, axis=0), preferred_element_type=jnp.float32)
            for t in range(2):
                piece = sums[:, t * 2 * bs : (t + 1) * 2 * bs]
                if s == 0 and first:
                    total[g, t] = piece
                else:
                    total[g, t] += piece
            return carry

        lax.fori_loop(0, groups, body, 0, unroll=min(groups, 4))


def first_kernel(done, pairs, ids_ref, a_ref, *refs):
    *parts, total, feet, where, sem = refs
    parts = [parts[k : k + pairs] for k in range(0, len(parts), pairs)]
    add_products(done, ids_ref, a_ref, parts, total, True, feet, where, sem)


def middle_kernel(done, pairs, ids_ref, a_ref, before, *refs):
    *parts, total, feet, where, sem = refs
    parts = [parts[k : k + pairs] for k in range(0, len(parts), pairs)]
    add_products(done, ids_ref, a_ref, parts, total, False, feet, where, sem)


def last_kernel(done, pairs, ids_ref, place_ref, a_ref, total, *refs):
    *parts, o_ref, feet, where, sem = refs
    parts = [parts[k : k + pairs] for k in range(0, len(parts), pairs)]
    add_products(done, ids_ref, a_ref, parts, total, False, feet, where, sem)
    rows, slots, bs, _ = o_ref.shape
    half = total.shape[0] * 4
    for i in range(rows):
        for k in range(slots):
            l = lax.rem(place_ref[i, k], half)
            tile = total[l // 4, (l // 2) % 2, i * bs : (i + 1) * bs, :]
            tile = jnp.where(l % 2 == 0, tile, pltpu.roll(tile, bs, 1))
            o_ref[i, k] = tile[:, :bs].astype(o_ref.dtype)


def product(kernel, done, ids, a, total, parts, out, place=None):
    pairs = len(parts[0])
    flat = [part for source in parts for part in source]
    scalars = [ids] if place is None else [ids, place]
    arrays = [a] if total is None else [a, total]
    aliases = {} if total is None or place is not None else {len(scalars) + 1: 0}
    lanes = flat[0].shape[1]
    return pl.pallas_call(
        functools.partial(kernel, done, pairs),
        out_shape=out,
        grid_spec=pltpu.PrefetchScalarGridSpec(
            num_scalar_prefetch=len(scalars),
            grid=(),
            in_specs=[pl.BlockSpec(memory_space=VMEM)] * (len(arrays) + len(flat)),
            out_specs=pl.BlockSpec(memory_space=VMEM),
            scratch_shapes=[
                VMEM((len(flat), FOOT, lanes), jnp.int32),
                SMEM((len(flat), FOOT, lanes), jnp.int32),
                pltpu.SemaphoreType.DMA,
            ],
        ),
        input_output_aliases=aliases,
        compiler_params=params(),
        cost_estimate=cost(2 * a.shape[1] * 256 * 1024 * len(parts), 2 * len(flat) * flat[0].size),
    )(*scalars, *arrays, *flat)


def local(order, a_vals, b_vals, cols):
    sources = len(order)
    rows, slots, bs, _ = a_vals.shape
    half = sources * rows // 2
    pairs = rows // 2
    spots = {r: k for k, r in enumerate(order)}
    hops = {1: sources // 2, -1: (sources - 1) // 2}
    trips = [(way, step) for step in range(1, hops[1] + 1) for way in (1, -1) if step <= hops[way]]
    def ring(way):
        return [
            (order[r] * 2 + c, order[(r + (way if c == 0 else -way)) % sources] * 2 + c)
            for r in range(sources)
            for c in range(2)
        ]

    names = np.asarray(
        [
            [[r] + [order[(spots[r] - (w if c == 0 else -w) * t) % sources] for w, t in trips] for c in range(2)]
            for r in range(sources)
        ],
        np.int32,
    )
    ids = jnp.asarray(names)[lax.axis_index("row"), lax.axis_index("col")]

    own = pack(half, cols, b_vals)
    swap = [(0, 1), (1, 0)]
    others = lax.ppermute(cols, "col", swap)
    a_other = lax.ppermute(a_vals, "col", swap)
    rounds = [[own]]
    held = {1: list(own), -1: list(own)}
    for step in range(1, hops[1] + 1):
        ways = [way for way in (1, -1) if step <= hops[way]]
        for p in range(pairs):
            for way in ways:
                held[way][p] = lax.ppermute(held[way][p], ("row", "col"), ring(way))
        rounds.append([list(held[way]) for way in ways])
    a = dense_rows(2 * half, cols, others, a_vals, a_other)
    total_shape = jax.ShapeDtypeStruct((half // 4, 2, rows * bs, 2 * bs), jnp.float32)
    total, done = None, 0
    for step, parts in enumerate(rounds):
        if step == 0:
            total = product(first_kernel, done, ids, a, None, parts, total_shape)
        elif step < len(rounds) - 1:
            total = product(middle_kernel, done, ids, a, total, parts, total_shape)
        else:
            out = jax.ShapeDtypeStruct(a_vals.shape, a_vals.dtype)
            return product(last_kernel, done, ids, a, total, parts, out, cols)
        done += len(parts)


def ring_order(mesh):
    count = mesh.shape["row"]
    coords = [getattr(d, "coords", None) for d in mesh.devices[0, :, 0]]
    loop = [*range(0, count, 2), *range(count - 1 - count % 2, 0, -2)]
    if None not in coords:
        steps = [
            sum(abs(x - y) for x, y in zip(coords[loop[k - 1]], coords[loop[k]]))
            for k in range(count)
        ]
        if max(steps) <= 1:
            return loop
    return list(range(count))


def solution(mesh):
    return jax.shard_map(
        functools.partial(local, ring_order(mesh)),
        mesh=mesh,
        in_specs=(
            P(("groups", "row"), "col", None, None),
            P(("groups", "row"), "col", None, None),
            P(("groups", "row"), "col"),
        ),
        out_specs=P(("groups", "row"), "col", None, None),
        check_vma=False,
    )
```

time: 158 us -> 45.5 us (0.29)
  waiting for transfers between devices: 57.1 us -> 10.8 us
  blocking collectives: 31.3 us -> 0 us
  matrix products: 30 us -> 0 us
  local copies, waits for them, and re-layouts: 19.3 us -> 2.46 us
  Pallas kernels: 0 us -> 14.5 us
  between operations: 13.5 us -> 0.1 us
  starting transfers between devices: 6.69 us -> 17.4 us
    all_gather x1 -> x0, waiting for transfers between devices: 57.1 us -> none  [local(): lax.all_gather(b_rows, ('row', 'col'), axis=0, tiled=True)]
    dot_general x2 -> x0, matrix products: 30 us -> none  [the longest x1 19.3 us: multiply_rows(): jnp.einsum('rmno,rmnbc->rmobc', match, inner, preferred_element_type=jnp....]
    all_gather x1 -> x0, blocking collectives: 23.3 us -> none  [local(): lax.all_gather(col_rows, ('row', 'col'), axis=0, tiled=True)]
    ppermute x0 -> x16, starting transfers between devices: none -> 17.4 us  [the longest x14 17.2 us: local(): held[way][p] = lax.ppermute(held[way][p], ('row', 'col'), ring(way))]
    pallas_call x0 -> x7, Pallas kernels: none -> 14.5 us  [the longest x5 12 us: product(): pl.pallas_call(functools.partial(kernel, done, pairs), out_shape=out, gri...]
    gather x3 -> x0, local copies, waits for them, and re-layouts: 11.3 us -> none  [the longest x1 10.8 us: multiply_rows(): inner = b_whole[a_cols]]
    ppermute x0 -> x16, waiting for transfers between devices: none -> 10.8 us  [the longest x14 9.69 us: local(): held[way][p] = lax.ppermute(held[way][p], ('row', 'col'), ring(way))]
    all_to_all x2 -> x0, blocking collectives: 7.99 us -> none  [the longest x1 4 us: local(): lax.all_to_all(b_vals, 'col', split_axis=0, concat_axis=1, tiled=True)]
  transfers between devices with their start and end apart: 3 -> 16, of which waited for: 1 -> 7; matrix products, arithmetic and copies ran while one was open for 2% -> 2% of each run, Pallas kernels for 0% -> 23%
where the time goes in v2:
time: 45.5 us; the launch traced here: 45.3 us
  starting transfers between devices  17.4 us (38%)
  Pallas kernels  14.5 us (32%)
  waiting for transfers between devices  10.8 us (24%)
  local copies, waits for them, and re-layouts  2.46 us (5%)
    ppermute x14, starting transfers between devices, local(): held[way][p] = lax.ppermute(held[way][p], ('row', 'col'), ring(way))  17.2 us
    pallas_call x5, Pallas kernels, product(): pl.pallas_call(functools.partial(kernel, done, pairs), out_shape=out, gri...  12 us
    ppermute x14, waiting for transfers between devices, local(): held[way][p] = lax.ppermute(held[way][p], ('row', 'col'), ring(way))  9.69 us
    pallas_call x1, Pallas kernels, dense_rows(): pl.pallas_call(dense_kernel, out_shape=jax.ShapeDtypeStruct((count // 2,...  1.83 us
    unnamed x8, local copies, waits for them, and re-layouts  1.78 us
    ppermute x1, waiting for transfers between devices, local(): others = lax.ppermute(cols, 'col', swap)  1.15 us
  transfers between devices with their start and end apart: 16, of which 7 were waited for; matrix products, arithmetic and copies ran while one was open for 2% of the time, Pallas kernels for 23%

profile of v2, /device:TPU:0, one launch (start us, length us, event | category | flops | bytes accessed | tf_op | source)
XLA Modules:
  0.0 45.3 jit_solution(14683610929728961889)
XLA Ops:
  0.0 0.0 copy-start.1
  0.0 1.1 %copy-done.1 = bf16[4,10,64,64]{3,2,1,0:T(8,128)(2,1)S(1)} copy-done((bf16[4,10,64,64]{3,2,1,0:T(8,128)(2,1)S(1)}, bf16[4,10,64,64]{3,2,1,0:T(8,128)(2,1)}, u32[]{:S(2)}) %copy-start.1) | copy-done | bytes 327704
  1.1 0.0 copy-start.2
  1.1 0.7 %copy-done.2 = s32[4,10]{1,0:T(4,128)S(1)} copy-done((s32[4,10]{1,0:T(4,128)S(1)}, s32[4,10]{1,0:T(4,128)}, u32[]{:S(2)}) %copy-start.2) | copy-done | bytes 184
  1.8 0.0 copy-start
  1.8 0.7 %shard_map.47 = (bf16[656,128]{1,0:T(8,128)(2,1)S(1)}, bf16[656,128]{1,0:T(8,128)(2,1)S(1)}) custom-call(s32[4,10]{1,0:T(4,128)S(1)} %copy-done.2, bf16[4,10,64,64]{3,2,1,0:T(8,128)(2,1)S(1)} %copy-done.1), custom_call_target="tpu_custom_call" | custom-call | bytes 655360 | tf_op jit(solution)/shard_map/pallas_call | solution.py:43
  2.5 3.1 %collective-permute-start.2 = (bf16[656,128]{1,0:T(8,128)(2,1)S(1)}, bf16[656,128]{1,0:T(8,128)(2,1)S(1)}, u32[]{:S(2)}, u32[]{:S(2)}) collective-permute-start(bf16[656,128]{1,0:T(8,128)(2,1)S(1)} %get-tuple-element.7.refs_0_), channel_id=1, source_target_pairs={{0,4},{1,3},{4,8},{5,1},{8,12},{9,5},{12,14},{13,9},{14,10},{15,13... | collective-permute-start | bytes 503816 | tf_op jit(solution)/shard_map/ppermute | solution.py:235
  5.6 1.6 %collective-permute-start.3 = (bf16[656,128]{1,0:T(8,128)(2,1)S(1)}, bf16[656,128]{1,0:T(8,128)(2,1)S(1)}, u32[]{:S(2)}, u32[]{:S(2)}) collective-permute-start(bf16[656,128]{1,0:T(8,128)(2,1)S(1)} %get-tuple-element.8.refs_1_), channel_id=1, source_target_pairs={{0,4},{1,3},{4,8},{5,1},{8,12},{9,5},{12,14},{13,9},{14,10},{15,13... | collective-permute-start | bytes 503816 | tf_op jit(solution)/shard_map/ppermute | solution.py:235
  7.2 0.4 collective-permute-start.4
  7.6 0.0 collective-permute-start.5
  7.6 2.3 %collective-permute-done.2.refs_0_ = bf16[656,128]{1,0:T(8,128)(2,1)S(1)} collective-permute-done((bf16[656,128]{1,0:T(8,128)(2,1)S(1)}, bf16[656,128]{1,0:T(8,128)(2,1)S(1)}, u32[]{:S(2)}, u32[]{:S(2)}) %collective-permute-start.2) | collective-permute-done | bytes 167968 | tf_op jit(solution)/shard_map/ppermute | solution.py:235
  10.0 2.5 %collective-permute-start.6 = (bf16[656,128]{1,0:T(8,128)(2,1)S(1)}, bf16[656,128]{1,0:T(8,128)(2,1)S(1)}, u32[]{:S(2)}, u32[]{:S(2)}) collective-permute-start(bf16[656,128]{1,0:T(8,128)(2,1)S(1)} %collective-permute-done.2.refs_0_), channel_id=1, source_target_pairs={{0,4},{1,3},{4,8},{5,1},{8,12},{9,5},{12,14},{13,9},{14,10},{15,13... | collective-permute-start | bytes 503816 | tf_op jit(solution)/shard_map/ppermute | solution.py:235
  12.5 1.1 %collective-permute-done.3.refs_1_ = bf16[656,128]{1,0:T(8,128)(2,1)S(1)} collective-permute-done((bf16[656,128]{1,0:T(8,128)(2,1)S(1)}, bf16[656,128]{1,0:T(8,128)(2,1)S(1)}, u32[]{:S(2)}, u32[]{:S(2)}) %collective-permute-start.3) | collective-permute-done | bytes 167968 | tf_op jit(solution)/shard_map/ppermute | solution.py:235
  13.6 2.5 %collective-permute-start.7 = (bf16[656,128]{1,0:T(8,128)(2,1)S(1)}, bf16[656,128]{1,0:T(8,128)(2,1)S(1)}, u32[]{:S(2)}, u32[]{:S(2)}) collective-permute-start(bf16[656,128]{1,0:T(8,128)(2,1)S(1)} %collective-permute-done.3.refs_1_), channel_id=1, source_target_pairs={{0,4},{1,3},{4,8},{5,1},{8,12},{9,5},{12,14},{13,9},{14,10},{15,13... | collective-permute-start | bytes 503816 | tf_op jit(solution)/shard_map/ppermute | solution.py:235
  16.1 0.0 collective-permute-start
  16.1 1.2 %collective-permute-done.others_ref = s32[4,10]{1,0:T(4,128)S(1)} collective-permute-done((s32[4,10]{1,0:T(4,128)S(1)}, s32[4,10]{1,0:T(4,128)S(1)}, u32[]{:S(2)}, u32[]{:S(2)}) %collective-permute-start) | collective-permute-done | bytes 192 | tf_op jit(solution)/shard_map/ppermute | solution.py:227
  17.2 0.0 copy-done
  17.2 0.2 collective-permute-start.1
  17.4 0.0 collective-permute-done.4.refs_2_
  17.4 0.0 collective-permute-start.8
  17.4 0.5 %collective-permute-done.5.refs_3_ = bf16[656,128]{1,0:T(8,128)(2,1)S(1)} collective-permute-done((bf16[656,128]{1,0:T(8,128)(2,1)S(1)}, bf16[656,128]{1,0:T(8,128)(2,1)S(1)}, u32[]{:S(2)}, u32[]{:S(2)}) %collective-permute-start.5) | collective-permute-done | bytes 167968 | tf_op jit(solution)/shard_map/ppermute | solution.py:235
  17.9 0.3 collective-permute-start.9
  18.1 0.0 collective-permute-done.6.refs_0_
  18.1 1.8 %collective-permute-start.10 = (bf16[656,128]{1,0:T(8,128)(2,1)S(1)}, bf16[656,128]{1,0:T(8,128)(2,1)S(1)}, u32[]{:S(2)}, u32[]{:S(2)}) collective-permute-start(bf16[656,128]{1,0:T(8,128)(2,1)S(1)} %collective-permute-done.6.refs_0_), channel_id=1, source_target_pairs={{0,4},{1,3},{4,8},{5,1},{8,12},{9,5},{12,14},{13,9},{14,10},{15,13... | collective-permute-start | bytes 503816 | tf_op jit(solution)/shard_map/ppermute | solution.py:235
  19.9 0.0 collective-permute-done.7.refs_1_
  19.9 1.6 %collective-permute-start.11 = (bf16[656,128]{1,0:T(8,128)(2,1)S(1)}, bf16[656,128]{1,0:T(8,128)(2,1)S(1)}, u32[]{:S(2)}, u32[]{:S(2)}) collective-permute-start(bf16[656,128]{1,0:T(8,128)(2,1)S(1)} %collective-permute-done.7.refs_1_), channel_id=1, source_target_pairs={{0,4},{1,3},{4,8},{5,1},{8,12},{9,5},{12,14},{13,9},{14,10},{15,13... | collective-permute-start | bytes 503816 | tf_op jit(solution)/shard_map/ppermute | solution.py:235
  21.5 0.0 copy-start.3
  21.5 1.5 %collective-permute-done.8.refs_2_ = bf16[656,128]{1,0:T(8,128)(2,1)S(1)} collective-permute-done((bf16[656,128]{1,0:T(8,128)(2,1)S(1)}, bf16[656,128]{1,0:T(8,128)(2,1)S(1)}, u32[]{:S(2)}, u32[]{:S(2)}) %collective-permute-start.8) | collective-permute-done | bytes 167968 | tf_op jit(solution)/shard_map/ppermute | solution.py:235
  23.0 0.0 collective-permute-start.12
  23.1 3.6 %collective-permute-done.9.refs_3_ = bf16[656,128]{1,0:T(8,128)(2,1)S(1)} collective-permute-done((bf16[656,128]{1,0:T(8,128)(2,1)S(1)}, bf16[656,128]{1,0:T(8,128)(2,1)S(1)}, u32[]{:S(2)}, u32[]{:S(2)}) %collective-permute-start.9) | collective-permute-done | bytes 167968 | tf_op jit(solution)/shard_map/ppermute | solution.py:235
  26.6 0.0 collective-permute-start.13
  26.6 0.0 collective-permute-done.10.refs_0_
  26.7 2.0 %collective-permute-start.14 = (bf16[656,128]{1,0:T(8,128)(2,1)S(1)}, bf16[656,128]{1,0:T(8,128)(2,1)S(1)}, u32[]{:S(2)}, u32[]{:S(2)}) collective-permute-start(bf16[656,128]{1,0:T(8,128)(2,1)S(1)} %collective-permute-done.10.refs_0_), channel_id=1, source_target_pairs={{0,4},{1,3},{4,8},{5,1},{8,12},{9,5},{12,14},{13,9},{14,10},{15,13... | collective-permute-start | bytes 503816 | tf_op jit(solution)/shard_map/ppermute | solution.py:235
  28.7 0.6 %collective-permute-done.11.refs_1_ = bf16[656,128]{1,0:T(8,128)(2,1)S(1)} collective-permute-done((bf16[656,128]{1,0:T(8,128)(2,1)S(1)}, bf16[656,128]{1,0:T(8,128)(2,1)S(1)}, u32[]{:S(2)}, u32[]{:S(2)}) %collective-permute-start.11) | collective-permute-done | bytes 167968 | tf_op jit(solution)/shard_map/ppermute | solution.py:235
  29.3 1.4 %collective-permute-start.15 = (bf16[656,128]{1,0:T(8,128)(2,1)S(1)}, bf16[656,128]{1,0:T(8,128)(2,1)S(1)}, u32[]{:S(2)}, u32[]{:S(2)}) collective-permute-start(bf16[656,128]{1,0:T(8,128)(2,1)S(1)} %collective-permute-done.11.refs_1_), channel_id=1, source_target_pairs={{0,4},{1,3},{4,8},{5,1},{8,12},{9,5},{12,14},{13,9},{14,10},{15,13... | collective-permute-start | bytes 503816 | tf_op jit(solution)/shard_map/ppermute | solution.py:235
  30.7 0.7 %dynamic-slice_bitcast_fusion.ids_ref = s32[8]{0:T(128)S(1)} fusion(s32[8,2,8]{2,1,0:T(2,128)} %constant.16.clone, s32[]{:T(128)S(6)} %select_n.6, s32[]{:T(128)S(6)} %select_n.7), kind=kLoop, calls=%fused_computation | loop fusion | bytes 72 | tf_op jit(solution)/shard_map/squeeze | solution.py:223
  31.4 0.0 collective-permute-done.1.other_ref
  31.4 0.0 copy-done.3
  31.4 1.8 %shard_map.46.a_ref = bf16[16,256,128]{2,1,0:T(8,128)(2,1)S(1)} custom-call(s32[4,10]{1,0:T(4,128)S(1)} %copy-done.3, s32[4,10]{1,0:T(4,128)S(1)} %collective-permute-done.others_ref, bf16[4,10,64,64]{3,2,1,0:T(8,128)(2,1)S(1)} %copy-done, bf16[4,10,64,64]{3,2,1,0:T(8,128)(2,1)S(1)} %collective-permute-done.1.other_ref), custom_call_target="tpu_custom_call" | custom-call | bytes 1310720 | tf_op jit(solution)/shard_map/pallas_call | solution.py:85
  33.2 1.8 %shard_map.48.before = f32[4,2,256,128]{3,2,1,0:T(8,128)S(1)} custom-call(s32[8]{0:T(128)S(1)} %dynamic-slice_bitcast_fusion.ids_ref, bf16[16,256,128]{2,1,0:T(8,128)(2,1)S(1)} %shard_map.46.a_ref, bf16[656,128]{1,0:T(8,128)(2,1)S(1)} %get-tuple-element.7.refs_0_, bf16[656,128]{1,0:T(8,128)(2,1)S(1)} %get-tuple-element.8.refs_1_), custom_call_target="tpu_custom_call" | custom-call | flops 134217728 | bytes 335872 | tf_op jit(solution)/shard_map/pallas_call | solution.py:181
  35.0 2.3 %shard_map.49.before = f32[4,2,256,128]{3,2,1,0:T(8,128)S(1)} custom-call(s32[8]{0:T(128)S(1)} %dynamic-slice_bitcast_fusion.ids_ref, bf16[16,256,128]{2,1,0:T(8,128)(2,1)S(1)} %shard_map.46.a_ref, f32[4,2,256,128]{3,2,1,0:T(8,128)S(1)} %shard_map.48.before, bf16[656,128]{1,0:T(8,128)(2,1)S(1)} %collective-permute-done.2.refs_0_, ...), custom_call_target="tpu_custom_call", output_to_operand_aliasing={{}: (2, {})} | custom-call | flops 268435456 | bytes 671744 | tf_op jit(solution)/shard_map/pallas_call | solution.py:181
  37.4 2.3 %shard_map.50.before = f32[4,2,256,128]{3,2,1,0:T(8,128)S(1)} custom-call(s32[8]{0:T(128)S(1)} %dynamic-slice_bitcast_fusion.ids_ref, bf16[16,256,128]{2,1,0:T(8,128)(2,1)S(1)} %shard_map.46.a_ref, f32[4,2,256,128]{3,2,1,0:T(8,128)S(1)} %shard_map.49.before, bf16[656,128]{1,0:T(8,128)(2,1)S(1)} %collective-permute-done.6.refs_0_, ...), custom_call_target="tpu_custom_call", output_to_operand_aliasing={{}: (2, {})} | custom-call | flops 268435456 | bytes 671744 | tf_op jit(solution)/shard_map/pallas_call | solution.py:181
  39.7 0.0 collective-permute-done.12.refs_2_
  39.7 0.0 collective-permute-done.13.refs_3_
  39.7 2.3 %shard_map.51.total = f32[4,2,256,128]{3,2,1,0:T(8,128)S(1)} custom-call(s32[8]{0:T(128)S(1)} %dynamic-slice_bitcast_fusion.ids_ref, bf16[16,256,128]{2,1,0:T(8,128)(2,1)S(1)} %shard_map.46.a_ref, f32[4,2,256,128]{3,2,1,0:T(8,128)S(1)} %shard_map.50.before, bf16[656,128]{1,0:T(8,128)(2,1)S(1)} %collective-permute-done.10.refs_0_, ...), custom_call_target="tpu_custom_call", output_to_operand_aliasing={{}: (2, {})} | custom-call | flops 268435456 | bytes 671744 | tf_op jit(solution)/shard_map/pallas_call | solution.py:181
  42.0 0.0 collective-permute-done.14.refs_0_
  42.0 0.0 collective-permute-done.15.refs_1_
  42.0 3.2 %shard_map.52 = bf16[4,10,64,64]{3,2,1,0:T(8,128)(2,1)} custom-call(s32[8]{0:T(128)S(1)} %dynamic-slice_bitcast_fusion.ids_ref, s32[4,10]{1,0:T(4,128)S(1)} %copy-done.3, bf16[16,256,128]{2,1,0:T(8,128)(2,1)S(1)} %shard_map.46.a_ref, f32[4,2,256,128]{3,2,1,0:T(8,128)S(1)} %shard_map.51.total, bf16[656,128]{1,0:T(8,128)(2,1)S(1)} %collective-permute-done.14.refs_0_, ...), custom_call_target="tpu_custom_call" | custom-call | flops 134217728 | bytes 335872 | tf_op jit(solution)/shard_map/pallas_call | solution.py:181
Async XLA Ops:
  0.0 1.1 %copy-start.1 = (bf16[4,10,64,64]{3,2,1,0:T(8,128)(2,1)S(1)}, bf16[4,10,64,64]{3,2,1,0:T(8,128)(2,1)}, u32[]{:S(2)}) copy-start(bf16[4,10,64,64]{3,2,1,0:T(8,128)(2,1)} %b_ref.1) | copy-start | bytes 983044
  1.1 0.7 %copy-start.2 = (s32[4,10]{1,0:T(4,128)S(1)}, s32[4,10]{1,0:T(4,128)}, u32[]{:S(2)}) copy-start(s32[4,10]{1,0:T(4,128)} %place_ref.1) | copy-start | bytes 484
  1.8 15.4 %copy-start = (bf16[4,10,64,64]{3,2,1,0:T(8,128)(2,1)S(1)}, bf16[4,10,64,64]{3,2,1,0:T(8,128)(2,1)}, u32[]{:S(2)}) copy-start(bf16[4,10,64,64]{3,2,1,0:T(8,128)(2,1)} %own_ref.1) | copy-start | bytes 983044
  2.5 7.5 %collective-permute-start.2 = (bf16[656,128]{1,0:T(8,128)(2,1)S(1)}, bf16[656,128]{1,0:T(8,128)(2,1)S(1)}, u32[]{:S(2)}, u32[]{:S(2)}) collective-permute-start(bf16[656,128]{1,0:T(8,128)(2,1)S(1)} %get-tuple-element.7.refs_0_), channel_id=1, source_target_pairs={{0,4},{1,3},{4,8},{5,1},{8,12},{9,5},{12,14},{13,9},{14,10},{15,13... | collective-permute-start | bytes 503816 | tf_op jit(solution)/shard_map/ppermute | solution.py:235
  5.6 8.0 %collective-permute-start.3 = (bf16[656,128]{1,0:T(8,128)(2,1)S(1)}, bf16[656,128]{1,0:T(8,128)(2,1)S(1)}, u32[]{:S(2)}, u32[]{:S(2)}) collective-permute-start(bf16[656,128]{1,0:T(8,128)(2,1)S(1)} %get-tuple-element.8.refs_1_), channel_id=1, source_target_pairs={{0,4},{1,3},{4,8},{5,1},{8,12},{9,5},{12,14},{13,9},{14,10},{15,13... | collective-permute-start | bytes 503816 | tf_op jit(solution)/shard_map/ppermute | solution.py:235
  7.2 10.2 %collective-permute-start.4 = (bf16[656,128]{1,0:T(8,128)(2,1)S(1)}, bf16[656,128]{1,0:T(8,128)(2,1)S(1)}, u32[]{:S(2)}, u32[]{:S(2)}) collective-permute-start(bf16[656,128]{1,0:T(8,128)(2,1)S(1)} %get-tuple-element.7.refs_0_), channel_id=1, source_target_pairs={{0,2},{1,5},{4,0},{5,9},{8,4},{9,13},{12,8},{13,15},{14,12},{15,11... | collective-permute-start | bytes 503816 | tf_op jit(solution)/shard_map/ppermute | solution.py:235
  7.6 10.3 %collective-permute-start.5 = (bf16[656,128]{1,0:T(8,128)(2,1)S(1)}, bf16[656,128]{1,0:T(8,128)(2,1)S(1)}, u32[]{:S(2)}, u32[]{:S(2)}) collective-permute-start(bf16[656,128]{1,0:T(8,128)(2,1)S(1)} %get-tuple-element.8.refs_1_), channel_id=1, source_target_pairs={{0,2},{1,5},{4,0},{5,9},{8,4},{9,13},{12,8},{13,15},{14,12},{15,11... | collective-permute-start | bytes 503816 | tf_op jit(solution)/shard_map/ppermute | solution.py:235
  10.0 8.2 %collective-permute-start.6 = (bf16[656,128]{1,0:T(8,128)(2,1)S(1)}, bf16[656,128]{1,0:T(8,128)(2,1)S(1)}, u32[]{:S(2)}, u32[]{:S(2)}) collective-permute-start(bf16[656,128]{1,0:T(8,128)(2,1)S(1)} %collective-permute-done.2.refs_0_), channel_id=1, source_target_pairs={{0,4},{1,3},{4,8},{5,1},{8,12},{9,5},{12,14},{13,9},{14,10},{15,13... | collective-permute-start | bytes 503816 | tf_op jit(solution)/shard_map/ppermute | solution.py:235
  13.6 6.3 %collective-permute-start.7 = (bf16[656,128]{1,0:T(8,128)(2,1)S(1)}, bf16[656,128]{1,0:T(8,128)(2,1)S(1)}, u32[]{:S(2)}, u32[]{:S(2)}) collective-permute-start(bf16[656,128]{1,0:T(8,128)(2,1)S(1)} %collective-permute-done.3.refs_1_), channel_id=1, source_target_pairs={{0,4},{1,3},{4,8},{5,1},{8,12},{9,5},{12,14},{13,9},{14,10},{15,13... | collective-permute-start | bytes 503816 | tf_op jit(solution)/shard_map/ppermute | solution.py:235
  16.1 1.2 %collective-permute-start = (s32[4,10]{1,0:T(4,128)S(1)}, s32[4,10]{1,0:T(4,128)S(1)}, u32[]{:S(2)}, u32[]{:S(2)}) collective-permute-start(s32[4,10]{1,0:T(4,128)S(1)} %copy-done.2), channel_id=1, source_target_pairs={{0,1},{1,0},{2,3},{3,2},{4,5},{5,4},{6,7},{7,6},{8,9},{9,8},{10,11... | collective-permute-start | bytes 488 | tf_op jit(solution)/shard_map/ppermute | solution.py:227
  17.2 14.2 %collective-permute-start.1 = (bf16[4,10,64,64]{3,2,1,0:T(8,128)(2,1)S(1)}, bf16[4,10,64,64]{3,2,1,0:T(8,128)(2,1)S(1)}, u32[]{:S(2)}, u32[]{:S(2)}) collective-permute-start(bf16[4,10,64,64]{3,2,1,0:T(8,128)(2,1)S(1)} %copy-done), channel_id=1, source_target_pairs={{0,1},{1,0},{2,3},{3,2},{4,5},{5,4},{6,7},{7,6},{8,9},{9,8},{10,11... | collective-permute-start | bytes 983048 | tf_op jit(solution)/shard_map/ppermute | solution.py:228
  17.4 5.6 %collective-permute-start.8 = (bf16[656,128]{1,0:T(8,128)(2,1)S(1)}, bf16[656,128]{1,0:T(8,128)(2,1)S(1)}, u32[]{:S(2)}, u32[]{:S(2)}) collective-permute-start(bf16[656,128]{1,0:T(8,128)(2,1)S(1)} %collective-permute-done.4.refs_2_), channel_id=1, source_target_pairs={{0,2},{1,5},{4,0},{5,9},{8,4},{9,13},{12,8},{13,15},{14,12},{15,11... | collective-permute-start | bytes 503816 | tf_op jit(solution)/shard_map/ppermute | solution.py:235
  17.9 8.8 %collective-permute-start.9 = (bf16[656,128]{1,0:T(8,128)(2,1)S(1)}, bf16[656,128]{1,0:T(8,128)(2,1)S(1)}, u32[]{:S(2)}, u32[]{:S(2)}) collective-permute-start(bf16[656,128]{1,0:T(8,128)(2,1)S(1)} %collective-permute-done.5.refs_3_), channel_id=1, source_target_pairs={{0,2},{1,5},{4,0},{5,9},{8,4},{9,13},{12,8},{13,15},{14,12},{15,11... | collective-permute-start | bytes 503816 | tf_op jit(solution)/shard_map/ppermute | solution.py:235
  18.1 8.5 %collective-permute-start.10 = (bf16[656,128]{1,0:T(8,128)(2,1)S(1)}, bf16[656,128]{1,0:T(8,128)(2,1)S(1)}, u32[]{:S(2)}, u32[]{:S(2)}) collective-permute-start(bf16[656,128]{1,0:T(8,128)(2,1)S(1)} %collective-permute-done.6.refs_0_), channel_id=1, source_target_pairs={{0,4},{1,3},{4,8},{5,1},{8,12},{9,5},{12,14},{13,9},{14,10},{15,13... | collective-permute-start | bytes 503816 | tf_op jit(solution)/shard_map/ppermute | solution.py:235
  19.9 9.4 %collective-permute-start.11 = (bf16[656,128]{1,0:T(8,128)(2,1)S(1)}, bf16[656,128]{1,0:T(8,128)(2,1)S(1)}, u32[]{:S(2)}, u32[]{:S(2)}) collective-permute-start(bf16[656,128]{1,0:T(8,128)(2,1)S(1)} %collective-permute-done.7.refs_1_), channel_id=1, source_target_pairs={{0,4},{1,3},{4,8},{5,1},{8,12},{9,5},{12,14},{13,9},{14,10},{15,13... | collective-permute-start | bytes 503816 | tf_op jit(solution)/shard_map/ppermute | solution.py:235
  21.5 9.9 %copy-start.3 = (s32[4,10]{1,0:T(4,128)S(1)}, s32[4,10]{1,0:T(4,128)}, u32[]{:S(2)}) copy-start(s32[4,10]{1,0:T(4,128)} %place_ref.1) | copy-start | bytes 484
  23.0 16.6 %collective-permute-start.12 = (bf16[656,128]{1,0:T(8,128)(2,1)S(1)}, bf16[656,128]{1,0:T(8,128)(2,1)S(1)}, u32[]{:S(2)}, u32[]{:S(2)}) collective-permute-start(bf16[656,128]{1,0:T(8,128)(2,1)S(1)} %collective-permute-done.8.refs_2_), channel_id=1, source_target_pairs={{0,2},{1,5},{4,0},{5,9},{8,4},{9,13},{12,8},{13,15},{14,12},{15,11... | collective-permute-start | bytes 503816 | tf_op jit(solution)/shard_map/ppermute | solution.py:235
  26.6 13.1 %collective-permute-start.13 = (bf16[656,128]{1,0:T(8,128)(2,1)S(1)}, bf16[656,128]{1,0:T(8,128)(2,1)S(1)}, u32[]{:S(2)}, u32[]{:S(2)}) collective-permute-start(bf16[656,128]{1,0:T(8,128)(2,1)S(1)} %collective-permute-done.9.refs_3_), channel_id=1, source_target_pairs={{0,2},{1,5},{4,0},{5,9},{8,4},{9,13},{12,8},{13,15},{14,12},{15,11... | collective-permute-start | bytes 503816 | tf_op jit(solution)/shard_map/ppermute | solution.py:235
  26.7 15.4 %collective-permute-start.14 = (bf16[656,128]{1,0:T(8,128)(2,1)S(1)}, bf16[656,128]{1,0:T(8,128)(2,1)S(1)}, u32[]{:S(2)}, u32[]{:S(2)}) collective-permute-start(bf16[656,128]{1,0:T(8,128)(2,1)S(1)} %collective-permute-done.10.refs_0_), channel_id=1, source_target_pairs={{0,4},{1,3},{4,8},{5,1},{8,12},{9,5},{12,14},{13,9},{14,10},{15,13... | collective-permute-start | bytes 503816 | tf_op jit(solution)/shard_map/ppermute | solution.py:235
  29.3 12.8 %collective-permute-start.15 = (bf16[656,128]{1,0:T(8,128)(2,1)S(1)}, bf16[656,128]{1,0:T(8,128)(2,1)S(1)}, u32[]{:S(2)}, u32[]{:S(2)}) collective-permute-start(bf16[656,128]{1,0:T(8,128)(2,1)S(1)} %collective-permute-done.11.refs_1_), channel_id=1, source_target_pairs={{0,4},{1,3},{4,8},{5,1},{8,12},{9,5},{12,14},{13,9},{14,10},{15,13... | collective-permute-start | bytes 503816 | tf_op jit(solution)/shard_map/ppermute | solution.py:235

commit v3 on v2

v3 whole, which is shorter than its diff:
```python
import functools
import math

import jax
import jax.numpy as jnp
import numpy as np
from jax import lax
from jax.experimental import pallas as pl
from jax.experimental.pallas import tpu as pltpu
from jax.sharding import PartitionSpec as P

VMEM = pltpu.VMEM
SMEM = pltpu.SMEM
LIMIT = 48 * 1024 * 1024
WHOLE = 63 * 1024 * 1024
BUSY = 50
FOOT = 16


def params(limit=LIMIT):
    return pltpu.CompilerParams(vmem_limit_bytes=limit)


def cost(flops, size):
    return pl.CostEstimate(flops=flops, bytes_accessed=size, transcendentals=0)


def pack_kernel(half, cols_hbm, b_hbm, *refs):
    *o_refs, cols_ref, b_ref, sem, sems = refs
    rows, slots, bs, _ = b_ref.shape
    copies = [pltpu.make_async_copy(b_hbm.at[r], b_ref.at[r], sems.at[r]) for r in range(rows)]
    fetch = pltpu.make_async_copy(cols_hbm, cols_ref, sem)
    fetch.start()
    for copy in copies:
        copy.start()
    row = lax.broadcasted_iota(jnp.int32, (FOOT, 2 * bs), 0)
    lane = lax.broadcasted_iota(jnp.int32, (FOOT, 2 * bs), 1)
    fetch.wait()
    for p, o_ref in enumerate(o_refs):
        foot = jnp.full((FOOT, 2 * bs), slots, jnp.int32)
        for h in range(2):
            for n in range(slots):
                here = (row == h) & (lane == lax.rem(cols_ref[2 * p + h, n], half))
                foot = jnp.where(here, n, foot)
        o_ref[slots * bs :, :] = foot.astype(jnp.float32).astype(o_ref.dtype)
        copies[2 * p].wait()
        copies[2 * p + 1].wait()
        for n in range(slots):
            o_ref[n * bs : (n + 1) * bs, :] = jnp.concatenate([b_ref[2 * p, n], b_ref[2 * p + 1, n]], axis=-1)


def pack(half, cols, b_vals):
    rows, slots, bs, _ = b_vals.shape
    shape = jax.ShapeDtypeStruct((slots * bs + FOOT, 2 * bs), b_vals.dtype)
    return pl.pallas_call(
        functools.partial(pack_kernel, half),
        out_shape=[shape] * (rows // 2),
        in_specs=[pl.BlockSpec(memory_space=pl.ANY)] * 2,
        out_specs=[pl.BlockSpec(memory_space=VMEM)] * (rows // 2),
        scratch_shapes=[
            SMEM(cols.shape, cols.dtype),
            VMEM(b_vals.shape, b_vals.dtype),
            pltpu.SemaphoreType.DMA,
            pltpu.SemaphoreType.DMA((rows,)),
        ],
        compiler_params=params(WHOLE),
        cost_estimate=cost(0, 2 * b_vals.size * 2),
    )(cols, b_vals)


def dense_kernel(ids_ref, cols_ref, others_ref, own_ref, other_ref, o_ref, blocks, where):
    rows, slots, bs, _ = own_ref.shape
    sources, pairs = o_ref.shape[:2]
    blocks[:, :slots] = own_ref[...]
    blocks[:, slots : 2 * slots] = other_ref[...]
    blocks[:, 2 * slots] = jnp.zeros_like(blocks[:, 2 * slots])
    for i in range(rows):
        def clear(j, carry):
            where[i, j] = 2 * slots
            return carry

        lax.fori_loop(0, 2 * sources * pairs, clear, 0, unroll=8)
        for m in range(slots):
            where[i, cols_ref[i, m]] = m
            where[i, others_ref[i, m]] = slots + m

    def body(s, carry):
        for p in range(pairs):
            j = (ids_ref[s] * pairs + p) * 2
            for i in range(rows):
                left = blocks[i, where[i, j]]
                right = blocks[i, where[i, j + 1]]
                o_ref[s, p, i * bs : (i + 1) * bs, :] = jnp.concatenate([left, right], axis=-1)
        return carry

    lax.fori_loop(0, sources, body, 0, unroll=2)


def dense_rows(ids, cols, others, own, other):
    rows, slots, bs, _ = own.shape
    sources = ids.shape[0]
    return pl.pallas_call(
        dense_kernel,
        out_shape=jax.ShapeDtypeStruct((sources, rows // 2, rows * bs, 2 * bs), own.dtype),
        grid_spec=pltpu.PrefetchScalarGridSpec(
            num_scalar_prefetch=3,
            grid=(),
            in_specs=[pl.BlockSpec(memory_space=VMEM)] * 2,
            out_specs=pl.BlockSpec(memory_space=VMEM),
            scratch_shapes=[
                VMEM((rows, 2 * slots + 1, bs, bs), own.dtype),
                SMEM((rows, sources * rows), jnp.int32),
            ],
        ),
        compiler_params=params(),
        cost_estimate=cost(0, BUSY * 8 * own.size),
    )(ids, cols, others, own, other)


def fetch_feet(parts, feet, where, sem):
    for k, part in enumerate(parts):
        feet[k] = part[part.shape[0] - FOOT :, :].astype(jnp.float32).astype(jnp.int32)
    copy = pltpu.make_async_copy(feet, where, sem)
    copy.start()
    return copy


def add_products(done, a_ref, parts, total, first, where):
    groups, bs = total.shape[0], total.shape[3] // 2
    slots = (parts[0].shape[0] - FOOT) // bs
    pairs = a_ref.shape[1]
    low = lax.broadcasted_iota(jnp.int32, (bs, 2 * bs), 1) < bs

    def block(part, slot):
        at = pl.multiple_of(jnp.minimum(slot, slots - 1) * bs, bs)
        return jnp.where(slot < slots, part[pl.ds(at, bs), :], jnp.zeros((bs, 2 * bs), part.dtype))

    def turn(x):
        return jnp.concatenate([x[:, bs:], x[:, :bs]], axis=-1)

    for s in range(len(parts) // pairs):
        source = parts[s * pairs : (s + 1) * pairs]
        a = jnp.concatenate([a_ref[done + s, p] for p in range(pairs)], axis=-1)

        def body(g, carry, s=s, source=source, a=a):
            panel = []
            for p, part in enumerate(source):
                for h in range(2):
                    tiles = []
                    for q in (2 * g, 2 * g + 1):
                        left = block(part, where[s * pairs + p, h, 2 * q])
                        right = block(part, where[s * pairs + p, h, 2 * q + 1])
                        if h == 0:
                            right = turn(right)
                        else:
                            left = turn(left)
                        tiles.append(jnp.where(low, left, right))
                    panel.append(jnp.concatenate(tiles, axis=-1))
            sums = jnp.dot(a, jnp.concatenate(panel, axis=0), preferred_element_type=jnp.float32)
            for t in range(2):
                piece = sums[:, t * 2 * bs : (t + 1) * 2 * bs]
                if s == 0 and first:
                    total[g, t] = piece
                else:
                    total[g, t] += piece
            return carry

        lax.fori_loop(0, groups, body, 0, unroll=min(groups, 4))


def first_kernel(done, a_ref, *refs):
    *parts, total, feet, where, sem = refs
    fetch_feet(parts, feet, where, sem).wait()
    add_products(done, a_ref, parts, total, True, where)


def middle_kernel(done, a_ref, before, *refs):
    *parts, total, feet, where, sem = refs
    fetch_feet(parts, feet, where, sem).wait()
    add_products(done, a_ref, parts, total, False, where)


def last_kernel(done, a_ref, total, cols_hbm, *refs):
    *parts, o_hbm, feet, where, sem, cols_ref, o_ref, cols_sem, sems = refs
    fetch = pltpu.make_async_copy(cols_hbm, cols_ref, cols_sem)
    fetch.start()
    fetch_feet(parts, feet, where, sem).wait()
    add_products(done, a_ref, parts, total, False, where)
    fetch.wait()
    rows, slots, bs, _ = o_ref.shape
    half = total.shape[0] * 4
    copies = [pltpu.make_async_copy(o_ref.at[i], o_hbm.at[i], sems.at[i]) for i in range(rows)]
    for i in range(rows):
        for k in range(slots):
            l = lax.rem(cols_ref[i, k], half)
            tile = total[l // 4, (l // 2) % 2, i * bs : (i + 1) * bs, :]
            tile = jnp.where(l % 2 == 0, tile, pltpu.roll(tile, bs, 1))
            o_ref[i, k] = tile[:, :bs].astype(o_ref.dtype)
        copies[i].start()
    for copy in copies:
        copy.wait()


def product(kernel, done, a, total, parts, out, cols=None):
    parts = [part for source in parts for part in source]
    hbm, vmem = pl.BlockSpec(memory_space=pl.ANY), pl.BlockSpec(memory_space=VMEM)
    lanes = parts[0].shape[1]
    scratch = [
        VMEM((len(parts), FOOT, lanes), jnp.int32),
        SMEM((len(parts), FOOT, lanes), jnp.int32),
        pltpu.SemaphoreType.DMA,
    ]
    arrays, specs = [a], [vmem]
    if total is not None:
        arrays, specs = arrays + [total], specs + [vmem]
    if cols is not None:
        arrays, specs = arrays + [cols], specs + [hbm]
        scratch += [
            SMEM(cols.shape, cols.dtype),
            VMEM(out.shape, out.dtype),
            pltpu.SemaphoreType.DMA,
            pltpu.SemaphoreType.DMA(out.shape[:1]),
        ]
    return pl.pallas_call(
        functools.partial(kernel, done),
        out_shape=out,
        in_specs=specs + [vmem] * len(parts),
        out_specs=vmem if cols is None else hbm,
        scratch_shapes=scratch,
        input_output_aliases={1: 0} if total is not None and cols is None else {},
        compiler_params=params(),
        cost_estimate=cost(BUSY * len(parts) * a.shape[2] * math.prod(out.shape) // 2, 0),
    )(*arrays, *parts)


def local(order, a_vals, b_vals, cols):
    sources = len(order)
    rows, slots, bs, _ = a_vals.shape
    half = sources * rows // 2
    pairs = rows // 2
    spots = {r: k for k, r in enumerate(order)}
    hops = {1: sources // 2, -1: (sources - 1) // 2}
    trips = [(way, step) for step in range(1, hops[1] + 1) for way in (1, -1) if step <= hops[way]]
    def ring(way):
        return [
            (order[r] * 2 + c, order[(r + (way if c == 0 else -way)) % sources] * 2 + c)
            for r in range(sources)
            for c in range(2)
        ]

    names = np.asarray(
        [
            [[r] + [order[(spots[r] - (w if c == 0 else -w) * t) % sources] for w, t in trips] for c in range(2)]
            for r in range(sources)
        ],
        np.int32,
    )
    ids = jnp.asarray(names)[lax.axis_index("row"), lax.axis_index("col")]

    own = pack(half, cols, b_vals)
    swap = [(0, 1), (1, 0)]
    *own, a_later, cols_later = lax.optimization_barrier((*own, a_vals, cols))
    others = lax.ppermute(cols_later, "col", swap)
    a_other = lax.ppermute(a_later, "col", swap)
    rounds = [[own]]
    held = {1: list(own), -1: list(own)}
    for step in range(1, hops[1] + 1):
        ways = [way for way in (1, -1) if step <= hops[way]]
        for p in range(pairs):
            for way in ways:
                held[way][p] = lax.ppermute(held[way][p], ("row", "col"), ring(way))
        rounds.append([list(held[way]) for way in ways])
    a = dense_rows(ids, cols, others, a_vals, a_other)
    total_shape = jax.ShapeDtypeStruct((half // 4, 2, rows * bs, 2 * bs), jnp.float32)
    total, done = None, 0
    for step, parts in enumerate(rounds):
        if step == 0:
            total = product(first_kernel, done, a, None, parts, total_shape)
        elif step < len(rounds) - 1:
            total = product(middle_kernel, done, a, total, parts, total_shape)
        else:
            out = jax.ShapeDtypeStruct(a_vals.shape, a_vals.dtype)
            return product(last_kernel, done, a, total, parts, out, cols)
        done += len(parts)


def ring_order(mesh):
    count = mesh.shape["row"]
    coords = [getattr(d, "coords", None) for d in mesh.devices[0, :, 0]]
    loop = [*range(0, count, 2), *range(count - 1 - count % 2, 0, -2)]
    if None not in coords:
        steps = [
            sum(abs(x - y) for x, y in zip(coords[loop[k - 1]], coords[loop[k]]))
            for k in range(count)
        ]
        if max(steps) <= 1:
            return loop
    return list(range(count))


def solution(mesh):
    return jax.shard_map(
        functools.partial(local, ring_order(mesh)),
        mesh=mesh,
        in_specs=(
            P(("groups", "row"), "col", None, None),
            P(("groups", "row"), "col", None, None),
            P(("groups", "row"), "col"),
        ),
        out_specs=P(("groups", "row"), "col", None, None),
        check_vma=False,
    )
```

time: 45.5 us -> 42.8 us (0.941)
  local copies, waits for them, and re-layouts: 2.46 us -> 0.84 us
  Pallas kernels: 14.5 us -> 13.2 us
  waiting for transfers between devices: 10.8 us -> 11.5 us
    pallas_call x6, Pallas kernels: 13.8 us -> 11.1 us  [the longest x5 9.28 us: product(): pl.pallas_call(functools.partial(kernel, done), out_shape=out, in_specs=s...]
    ppermute x14, waiting for transfers between devices: 9.69 us -> 11.4 us  [local(): held[way][p] = lax.ppermute(held[way][p], ('row', 'col'), ring(way))]
    unnamed x8, local copies, waits for them, and re-layouts: 1.78 us -> 0.16 us
    pallas_call x1, Pallas kernels: 0.72 us -> 2.03 us  [pack(): pl.pallas_call(functools.partial(pack_kernel, half), out_shape=[shape] *...]
    ppermute x2, waiting for transfers between devices: 1.16 us -> 0.01 us  [the longest x1 0.01 us: local(): others = lax.ppermute(cols_later, 'col', swap)]
    ppermute x14, starting transfers between devices: 17.2 us -> 16 us  [local(): held[way][p] = lax.ppermute(held[way][p], ('row', 'col'), ring(way))]
    ppermute x2, starting transfers between devices: 0.18 us -> 0.97 us  [the longest x1 0.52 us: local(): a_other = lax.ppermute(a_later, 'col', swap)]
  transfers between devices with their start and end apart: 16 -> 16, of which waited for: 7 -> 7; matrix products, arithmetic and copies ran while one was open for 2% -> 2% of each run, Pallas kernels for 23% -> 20%
where the time goes in v3:
time: 42.8 us; the launch traced here: 42.6 us
  starting transfers between devices  17 us (40%)
  Pallas kernels  13.2 us (31%)
  waiting for transfers between devices  11.5 us (27%)
  local copies, waits for them, and re-layouts  0.84 us (2%)
    ppermute x14, starting transfers between devices, local(): held[way][p] = lax.ppermute(held[way][p], ('row', 'col'), ring(way))  16 us
    ppermute x14, waiting for transfers between devices, local(): held[way][p] = lax.ppermute(held[way][p], ('row', 'col'), ring(way))  11.4 us
    pallas_call x5, Pallas kernels, product(): pl.pallas_call(functools.partial(kernel, done), out_shape=out, in_specs=s...  9.28 us
    pallas_call x1, Pallas kernels, pack(): pl.pallas_call(functools.partial(pack_kernel, half), out_shape=[shape] *...  2.03 us
    pallas_call x1, Pallas kernels, dense_rows(): pl.pallas_call(dense_kernel, out_shape=jax.ShapeDtypeStruct((sources, row...  1.84 us
  transfers between devices with their start and end apart: 16, of which 7 were waited for; matrix products, arithmetic and copies ran while one was open for 2% of the time, Pallas kernels for 20%

profile of v3, /device:TPU:0, one launch (start us, length us, event | category | flops | bytes accessed | tf_op | source)
XLA Modules:
  0.0 42.6 jit_solution(12591639445720787456)
XLA Ops:
  0.0 0.0 copy-start
  0.0 2.0 %shard_map.46 = (bf16[656,128]{1,0:T(8,128)(2,1)}, bf16[656,128]{1,0:T(8,128)(2,1)}) custom-call(s32[4,10]{1,0:T(4,128)} %cols_hbm.3, bf16[4,10,64,64]{3,2,1,0:T(8,128)(2,1)} %b_hbm.1), custom_call_target="tpu_custom_call" | custom-call | bytes 655360 | tf_op jit(solution)/shard_map/pallas_call | solution.py:55
  2.0 0.0 copy-start.1
  2.1 0.0 copy-done
  2.1 0.5 %collective-permute-start.1 = (bf16[4,10,64,64]{3,2,1,0:T(8,128)(2,1)S(1)}, bf16[4,10,64,64]{3,2,1,0:T(8,128)(2,1)S(1)}, u32[]{:S(2)}, u32[]{:S(2)}) collective-permute-start(bf16[4,10,64,64]{3,2,1,0:T(8,128)(2,1)S(1)} %copy-done), channel_id=1, source_target_pairs={{0,1},{1,0},{2,3},{3,2},{4,5},{5,4},{6,7},{7,6},{8,9},{9,8},{10,11... | collective-permute-start | bytes 983048 | tf_op jit(solution)/shard_map/ppermute | solution.py:264
  2.6 0.1 copy-done.1
  2.7 0.5 %collective-permute-start = (s32[4,10]{1,0:T(4,128)S(1)}, s32[4,10]{1,0:T(4,128)S(1)}, u32[]{:S(2)}, u32[]{:S(2)}) collective-permute-start(s32[4,10]{1,0:T(4,128)S(1)} %copy-done.1), channel_id=1, source_target_pairs={{0,1},{1,0},{2,3},{3,2},{4,5},{5,4},{6,7},{7,6},{8,9},{9,8},{10,11... | collective-permute-start | bytes 488 | tf_op jit(solution)/shard_map/ppermute | solution.py:263
  3.2 2.6 %collective-permute-start.2 = (bf16[656,128]{1,0:T(8,128)(2,1)}, bf16[656,128]{1,0:T(8,128)(2,1)S(1)}, u32[]{:S(2)}, u32[]{:S(2)}) collective-permute-start(bf16[656,128]{1,0:T(8,128)(2,1)} %get-tuple-element.15.refs_0_), channel_id=1, source_target_pairs={{0,4},{1,3},{4,8},{5,1},{8,12},{9,5},{12,14},{13,9},{14,10},{15,13... | collective-permute-start | bytes 503816 | tf_op jit(solution)/shard_map/ppermute | solution.py:271
  5.8 1.6 %collective-permute-start.3 = (bf16[656,128]{1,0:T(8,128)(2,1)}, bf16[656,128]{1,0:T(8,128)(2,1)S(1)}, u32[]{:S(2)}, u32[]{:S(2)}) collective-permute-start(bf16[656,128]{1,0:T(8,128)(2,1)} %get-tuple-element.16.refs_1_), channel_id=1, source_target_pairs={{0,4},{1,3},{4,8},{5,1},{8,12},{9,5},{12,14},{13,9},{14,10},{15,13... | collective-permute-start | bytes 503816 | tf_op jit(solution)/shard_map/ppermute | solution.py:271
  7.3 0.4 %collective-permute-start.4 = (bf16[656,128]{1,0:T(8,128)(2,1)}, bf16[656,128]{1,0:T(8,128)(2,1)S(1)}, u32[]{:S(2)}, u32[]{:S(2)}) collective-permute-start(bf16[656,128]{1,0:T(8,128)(2,1)} %get-tuple-element.15.refs_0_), channel_id=1, source_target_pairs={{0,2},{1,5},{4,0},{5,9},{8,4},{9,13},{12,8},{13,15},{14,12},{15,11... | collective-permute-start | bytes 503816 | tf_op jit(solution)/shard_map/ppermute | solution.py:271
  7.8 0.0 collective-permute-done.others_ref
  7.8 0.0 collective-permute-start.5
  7.8 0.7 %dynamic-slice_bitcast_fusion.ids_ref = s32[8]{0:T(128)S(1)} fusion(s32[8,2,8]{2,1,0:T(2,128)} %constant.16.clone, s32[]{:T(128)S(6)} %select_n.6, s32[]{:T(128)S(6)} %select_n.7), kind=kLoop, calls=%fused_computation | loop fusion | bytes 72 | tf_op jit(solution)/shard_map/squeeze | solution.py:258
  8.5 0.0 copy-start.2
  8.5 0.0 copy-start.3
  8.5 1.3 %collective-permute-done.2.refs_0_ = bf16[656,128]{1,0:T(8,128)(2,1)S(1)} collective-permute-done((bf16[656,128]{1,0:T(8,128)(2,1)}, bf16[656,128]{1,0:T(8,128)(2,1)S(1)}, u32[]{:S(2)}, u32[]{:S(2)}) %collective-permute-start.2) | collective-permute-done | bytes 167968 | tf_op jit(solution)/shard_map/ppermute | solution.py:271
  9.8 2.5 %collective-permute-start.6 = (bf16[656,128]{1,0:T(8,128)(2,1)S(1)}, bf16[656,128]{1,0:T(8,128)(2,1)S(1)}, u32[]{:S(2)}, u32[]{:S(2)}) collective-permute-start(bf16[656,128]{1,0:T(8,128)(2,1)S(1)} %collective-permute-done.2.refs_0_), channel_id=1, source_target_pairs={{0,4},{1,3},{4,8},{5,1},{8,12},{9,5},{12,14},{13,9},{14,10},{15,13... | collective-permute-start | bytes 503816 | tf_op jit(solution)/shard_map/ppermute | solution.py:271
  12.3 1.1 %collective-permute-done.3.refs_1_ = bf16[656,128]{1,0:T(8,128)(2,1)S(1)} collective-permute-done((bf16[656,128]{1,0:T(8,128)(2,1)}, bf16[656,128]{1,0:T(8,128)(2,1)S(1)}, u32[]{:S(2)}, u32[]{:S(2)}) %collective-permute-start.3) | collective-permute-done | bytes 167968 | tf_op jit(solution)/shard_map/ppermute | solution.py:271
  13.4 2.5 %collective-permute-start.7 = (bf16[656,128]{1,0:T(8,128)(2,1)S(1)}, bf16[656,128]{1,0:T(8,128)(2,1)S(1)}, u32[]{:S(2)}, u32[]{:S(2)}) collective-permute-start(bf16[656,128]{1,0:T(8,128)(2,1)S(1)} %collective-permute-done.3.refs_1_), channel_id=1, source_target_pairs={{0,4},{1,3},{4,8},{5,1},{8,12},{9,5},{12,14},{13,9},{14,10},{15,13... | collective-permute-start | bytes 503816 | tf_op jit(solution)/shard_map/ppermute | solution.py:271
  15.9 0.0 collective-permute-done.4.refs_2_
  15.9 0.0 collective-permute-start.8
  15.9 1.7 %collective-permute-done.5.refs_3_ = bf16[656,128]{1,0:T(8,128)(2,1)S(1)} collective-permute-done((bf16[656,128]{1,0:T(8,128)(2,1)}, bf16[656,128]{1,0:T(8,128)(2,1)S(1)}, u32[]{:S(2)}, u32[]{:S(2)}) %collective-permute-start.5) | collective-permute-done | bytes 167968 | tf_op jit(solution)/shard_map/ppermute | solution.py:271
  17.6 1.2 %collective-permute-start.9 = (bf16[656,128]{1,0:T(8,128)(2,1)S(1)}, bf16[656,128]{1,0:T(8,128)(2,1)S(1)}, u32[]{:S(2)}, u32[]{:S(2)}) collective-permute-start(bf16[656,128]{1,0:T(8,128)(2,1)S(1)} %collective-permute-done.5.refs_3_), channel_id=1, source_target_pairs={{0,2},{1,5},{4,0},{5,9},{8,4},{9,13},{12,8},{13,15},{14,12},{15,11... | collective-permute-start | bytes 503816 | tf_op jit(solution)/shard_map/ppermute | solution.py:271
  18.8 0.0 collective-permute-done.1.other_ref
  18.8 1.8 %shard_map.47.a_ref = bf16[8,2,256,128]{3,2,1,0:T(8,128)(2,1)S(1)} custom-call(s32[8]{0:T(128)S(1)} %dynamic-slice_bitcast_fusion.ids_ref, s32[4,10]{1,0:T(4,128)S(1)} %copy-done.1, s32[4,10]{1,0:T(4,128)S(1)} %collective-permute-done.others_ref, bf16[4,10,64,64]{3,2,1,0:T(8,128)(2,1)S(1)} %copy-done, ...), custom_call_target="tpu_custom_call" | custom-call | bytes 65536000 | tf_op jit(solution)/shard_map/pallas_call | solution.py:102
  20.7 0.0 copy-done.2
  20.7 0.0 copy-done.3
  20.7 1.3 %shard_map.48.before = f32[4,2,256,128]{3,2,1,0:T(8,128)S(1)} custom-call(bf16[8,2,256,128]{3,2,1,0:T(8,128)(2,1)S(1)} %shard_map.47.a_ref, bf16[656,128]{1,0:T(8,128)(2,1)S(1)} %copy-done.2, bf16[656,128]{1,0:T(8,128)(2,1)S(1)} %copy-done.3), custom_call_target="tpu_custom_call" | custom-call | flops 3355443200 | tf_op jit(solution)/shard_map/pallas_call | solution.py:224
  22.0 1.8 %shard_map.49.before = f32[4,2,256,128]{3,2,1,0:T(8,128)S(1)} custom-call(bf16[8,2,256,128]{3,2,1,0:T(8,128)(2,1)S(1)} %shard_map.47.a_ref, f32[4,2,256,128]{3,2,1,0:T(8,128)S(1)} %shard_map.48.before, bf16[656,128]{1,0:T(8,128)(2,1)S(1)} %collective-permute-done.2.refs_0_, ...), custom_call_target="tpu_custom_call", output_to_operand_aliasing={{}: (1, {})} | custom-call | flops 6710886400 | tf_op jit(solution)/shard_map/pallas_call | solution.py:224
  23.8 0.0 collective-permute-done.6.refs_0_
  23.8 0.9 %collective-permute-start.10 = (bf16[656,128]{1,0:T(8,128)(2,1)S(1)}, bf16[656,128]{1,0:T(8,128)(2,1)S(1)}, u32[]{:S(2)}, u32[]{:S(2)}) collective-permute-start(bf16[656,128]{1,0:T(8,128)(2,1)S(1)} %collective-permute-done.6.refs_0_), channel_id=1, source_target_pairs={{0,4},{1,3},{4,8},{5,1},{8,12},{9,5},{12,14},{13,9},{14,10},{15,13... | collective-permute-start | bytes 503816 | tf_op jit(solution)/shard_map/ppermute | solution.py:271
  24.7 0.0 collective-permute-done.7.refs_1_
  24.7 1.4 %collective-permute-start.11 = (bf16[656,128]{1,0:T(8,128)(2,1)S(1)}, bf16[656,128]{1,0:T(8,128)(2,1)S(1)}, u32[]{:S(2)}, u32[]{:S(2)}) collective-permute-start(bf16[656,128]{1,0:T(8,128)(2,1)S(1)} %collective-permute-done.7.refs_1_), channel_id=1, source_target_pairs={{0,4},{1,3},{4,8},{5,1},{8,12},{9,5},{12,14},{13,9},{14,10},{15,13... | collective-permute-start | bytes 503816 | tf_op jit(solution)/shard_map/ppermute | solution.py:271
  26.0 0.0 collective-permute-done.8.refs_2_
  26.0 0.7 %collective-permute-start.12 = (bf16[656,128]{1,0:T(8,128)(2,1)S(1)}, bf16[656,128]{1,0:T(8,128)(2,1)S(1)}, u32[]{:S(2)}, u32[]{:S(2)}) collective-permute-start(bf16[656,128]{1,0:T(8,128)(2,1)S(1)} %collective-permute-done.8.refs_2_), channel_id=1, source_target_pairs={{0,2},{1,5},{4,0},{5,9},{8,4},{9,13},{12,8},{13,15},{14,12},{15,11... | collective-permute-start | bytes 503816 | tf_op jit(solution)/shard_map/ppermute | solution.py:271
  26.7 0.0 collective-permute-done.9.refs_3_
  26.7 1.2 %collective-permute-start.13 = (bf16[656,128]{1,0:T(8,128)(2,1)S(1)}, bf16[656,128]{1,0:T(8,128)(2,1)S(1)}, u32[]{:S(2)}, u32[]{:S(2)}) collective-permute-start(bf16[656,128]{1,0:T(8,128)(2,1)S(1)} %collective-permute-done.9.refs_3_), channel_id=1, source_target_pairs={{0,2},{1,5},{4,0},{5,9},{8,4},{9,13},{12,8},{13,15},{14,12},{15,11... | collective-permute-start | bytes 503816 | tf_op jit(solution)/shard_map/ppermute | solution.py:271
  27.9 1.8 %shard_map.50.before = f32[4,2,256,128]{3,2,1,0:T(8,128)S(1)} custom-call(bf16[8,2,256,128]{3,2,1,0:T(8,128)(2,1)S(1)} %shard_map.47.a_ref, f32[4,2,256,128]{3,2,1,0:T(8,128)S(1)} %shard_map.49.before, bf16[656,128]{1,0:T(8,128)(2,1)S(1)} %collective-permute-done.6.refs_0_, ...), custom_call_target="tpu_custom_call", output_to_operand_aliasing={{}: (1, {})} | custom-call | flops 6710886400 | tf_op jit(solution)/shard_map/pallas_call | solution.py:224
  29.7 1.3 %collective-permute-done.10.refs_0_ = bf16[656,128]{1,0:T(8,128)(2,1)S(1)} collective-permute-done((bf16[656,128]{1,0:T(8,128)(2,1)S(1)}, bf16[656,128]{1,0:T(8,128)(2,1)S(1)}, u32[]{:S(2)}, u32[]{:S(2)}) %collective-permute-start.10) | collective-permute-done | bytes 167968 | tf_op jit(solution)/shard_map/ppermute | solution.py:271
  31.0 0.8 %collective-permute-start.14 = (bf16[656,128]{1,0:T(8,128)(2,1)S(1)}, bf16[656,128]{1,0:T(8,128)(2,1)S(1)}, u32[]{:S(2)}, u32[]{:S(2)}) collective-permute-start(bf16[656,128]{1,0:T(8,128)(2,1)S(1)} %collective-permute-done.10.refs_0_), channel_id=1, source_target_pairs={{0,4},{1,3},{4,8},{5,1},{8,12},{9,5},{12,14},{13,9},{14,10},{15,13... | collective-permute-start | bytes 503816 | tf_op jit(solution)/shard_map/ppermute | solution.py:271
  31.8 2.8 %collective-permute-done.11.refs_1_ = bf16[656,128]{1,0:T(8,128)(2,1)S(1)} collective-permute-done((bf16[656,128]{1,0:T(8,128)(2,1)S(1)}, bf16[656,128]{1,0:T(8,128)(2,1)S(1)}, u32[]{:S(2)}, u32[]{:S(2)}) %collective-permute-start.11) | collective-permute-done | bytes 167968 | tf_op jit(solution)/shard_map/ppermute | solution.py:271
  34.5 0.3 collective-permute-start.15
  34.8 0.0 collective-permute-done.12.refs_2_
  34.8 1.8 %collective-permute-done.13.refs_3_ = bf16[656,128]{1,0:T(8,128)(2,1)S(1)} collective-permute-done((bf16[656,128]{1,0:T(8,128)(2,1)S(1)}, bf16[656,128]{1,0:T(8,128)(2,1)S(1)}, u32[]{:S(2)}, u32[]{:S(2)}) %collective-permute-start.13) | collective-permute-done | bytes 167968 | tf_op jit(solution)/shard_map/ppermute | solution.py:271
  36.7 1.8 %shard_map.51.total = f32[4,2,256,128]{3,2,1,0:T(8,128)S(1)} custom-call(bf16[8,2,256,128]{3,2,1,0:T(8,128)(2,1)S(1)} %shard_map.47.a_ref, f32[4,2,256,128]{3,2,1,0:T(8,128)S(1)} %shard_map.50.before, bf16[656,128]{1,0:T(8,128)(2,1)S(1)} %collective-permute-done.10.refs_0_, ...), custom_call_target="tpu_custom_call", output_to_operand_aliasing={{}: (1, {})} | custom-call | flops 6710886400 | tf_op jit(solution)/shard_map/pallas_call | solution.py:224
  38.4 0.0 collective-permute-done.14.refs_0_
  38.5 1.4 %collective-permute-done.15.refs_1_ = bf16[656,128]{1,0:T(8,128)(2,1)S(1)} collective-permute-done((bf16[656,128]{1,0:T(8,128)(2,1)S(1)}, bf16[656,128]{1,0:T(8,128)(2,1)S(1)}, u32[]{:S(2)}, u32[]{:S(2)}) %collective-permute-start.15) | collective-permute-done | bytes 167968 | tf_op jit(solution)/shard_map/ppermute | solution.py:271
  39.9 2.7 %shard_map.52 = bf16[4,10,64,64]{3,2,1,0:T(8,128)(2,1)} custom-call(bf16[8,2,256,128]{3,2,1,0:T(8,128)(2,1)S(1)} %shard_map.47.a_ref, f32[4,2,256,128]{3,2,1,0:T(8,128)S(1)} %shard_map.51.total, s32[4,10]{1,0:T(4,128)S(1)} %copy-done.1, bf16[656,128]{1,0:T(8,128)(2,1)S(1)} %collective-permute-done.14.refs_0_, ...), custom_call_target="tpu_custom_call" | custom-call | flops 2097152000 | tf_op jit(solution)/shard_map/pallas_call | solution.py:224
Async XLA Ops:
  0.0 2.1 %copy-start = (bf16[4,10,64,64]{3,2,1,0:T(8,128)(2,1)S(1)}, bf16[4,10,64,64]{3,2,1,0:T(8,128)(2,1)}, u32[]{:S(2)}) copy-start(bf16[4,10,64,64]{3,2,1,0:T(8,128)(2,1)} %own_ref.1) | copy-start | bytes 983044
  2.0 0.7 %copy-start.1 = (s32[4,10]{1,0:T(4,128)S(1)}, s32[4,10]{1,0:T(4,128)}, u32[]{:S(2)}) copy-start(s32[4,10]{1,0:T(4,128)} %cols_hbm.3) | copy-start | bytes 484
  2.1 16.8 %collective-permute-start.1 = (bf16[4,10,64,64]{3,2,1,0:T(8,128)(2,1)S(1)}, bf16[4,10,64,64]{3,2,1,0:T(8,128)(2,1)S(1)}, u32[]{:S(2)}, u32[]{:S(2)}) collective-permute-start(bf16[4,10,64,64]{3,2,1,0:T(8,128)(2,1)S(1)} %copy-done), channel_id=1, source_target_pairs={{0,1},{1,0},{2,3},{3,2},{4,5},{5,4},{6,7},{7,6},{8,9},{9,8},{10,11... | collective-permute-start | bytes 983048 | tf_op jit(solution)/shard_map/ppermute | solution.py:264
  2.7 5.1 %collective-permute-start = (s32[4,10]{1,0:T(4,128)S(1)}, s32[4,10]{1,0:T(4,128)S(1)}, u32[]{:S(2)}, u32[]{:S(2)}) collective-permute-start(s32[4,10]{1,0:T(4,128)S(1)} %copy-done.1), channel_id=1, source_target_pairs={{0,1},{1,0},{2,3},{3,2},{4,5},{5,4},{6,7},{7,6},{8,9},{9,8},{10,11... | collective-permute-start | bytes 488 | tf_op jit(solution)/shard_map/ppermute | solution.py:263
  3.2 6.6 %collective-permute-start.2 = (bf16[656,128]{1,0:T(8,128)(2,1)}, bf16[656,128]{1,0:T(8,128)(2,1)S(1)}, u32[]{:S(2)}, u32[]{:S(2)}) collective-permute-start(bf16[656,128]{1,0:T(8,128)(2,1)} %get-tuple-element.15.refs_0_), channel_id=1, source_target_pairs={{0,4},{1,3},{4,8},{5,1},{8,12},{9,5},{12,14},{13,9},{14,10},{15,13... | collective-permute-start | bytes 503816 | tf_op jit(solution)/shard_map/ppermute | solution.py:271
  5.8 7.7 %collective-permute-start.3 = (bf16[656,128]{1,0:T(8,128)(2,1)}, bf16[656,128]{1,0:T(8,128)(2,1)S(1)}, u32[]{:S(2)}, u32[]{:S(2)}) collective-permute-start(bf16[656,128]{1,0:T(8,128)(2,1)} %get-tuple-element.16.refs_1_), channel_id=1, source_target_pairs={{0,4},{1,3},{4,8},{5,1},{8,12},{9,5},{12,14},{13,9},{14,10},{15,13... | collective-permute-start | bytes 503816 | tf_op jit(solution)/shard_map/ppermute | solution.py:271
  7.3 8.6 %collective-permute-start.4 = (bf16[656,128]{1,0:T(8,128)(2,1)}, bf16[656,128]{1,0:T(8,128)(2,1)S(1)}, u32[]{:S(2)}, u32[]{:S(2)}) collective-permute-start(bf16[656,128]{1,0:T(8,128)(2,1)} %get-tuple-element.15.refs_0_), channel_id=1, source_target_pairs={{0,2},{1,5},{4,0},{5,9},{8,4},{9,13},{12,8},{13,15},{14,12},{15,11... | collective-permute-start | bytes 503816 | tf_op jit(solution)/shard_map/ppermute | solution.py:271
  7.8 9.8 %collective-permute-start.5 = (bf16[656,128]{1,0:T(8,128)(2,1)}, bf16[656,128]{1,0:T(8,128)(2,1)S(1)}, u32[]{:S(2)}, u32[]{:S(2)}) collective-permute-start(bf16[656,128]{1,0:T(8,128)(2,1)} %get-tuple-element.16.refs_1_), channel_id=1, source_target_pairs={{0,2},{1,5},{4,0},{5,9},{8,4},{9,13},{12,8},{13,15},{14,12},{15,11... | collective-permute-start | bytes 503816 | tf_op jit(solution)/shard_map/ppermute | solution.py:271
  8.5 12.2 %copy-start.2 = (bf16[656,128]{1,0:T(8,128)(2,1)S(1)}, bf16[656,128]{1,0:T(8,128)(2,1)}, u32[]{:S(2)}) copy-start(bf16[656,128]{1,0:T(8,128)(2,1)} %get-tuple-element.15.refs_0_) | copy-start | bytes 503812
  8.5 12.2 %copy-start.3 = (bf16[656,128]{1,0:T(8,128)(2,1)S(1)}, bf16[656,128]{1,0:T(8,128)(2,1)}, u32[]{:S(2)}) copy-start(bf16[656,128]{1,0:T(8,128)(2,1)} %get-tuple-element.16.refs_1_) | copy-start | bytes 503812
  9.8 13.9 %collective-permute-start.6 = (bf16[656,128]{1,0:T(8,128)(2,1)S(1)}, bf16[656,128]{1,0:T(8,128)(2,1)S(1)}, u32[]{:S(2)}, u32[]{:S(2)}) collective-permute-start(bf16[656,128]{1,0:T(8,128)(2,1)S(1)} %collective-permute-done.2.refs_0_), channel_id=1, source_target_pairs={{0,4},{1,3},{4,8},{5,1},{8,12},{9,5},{12,14},{13,9},{14,10},{15,13... | collective-permute-start | bytes 503816 | tf_op jit(solution)/shard_map/ppermute | solution.py:271
  13.4 11.3 %collective-permute-start.7 = (bf16[656,128]{1,0:T(8,128)(2,1)S(1)}, bf16[656,128]{1,0:T(8,128)(2,1)S(1)}, u32[]{:S(2)}, u32[]{:S(2)}) collective-permute-start(bf16[656,128]{1,0:T(8,128)(2,1)S(1)} %collective-permute-done.3.refs_1_), channel_id=1, source_target_pairs={{0,4},{1,3},{4,8},{5,1},{8,12},{9,5},{12,14},{13,9},{14,10},{15,13... | collective-permute-start | bytes 503816 | tf_op jit(solution)/shard_map/ppermute | solution.py:271
  15.9 10.1 %collective-permute-start.8 = (bf16[656,128]{1,0:T(8,128)(2,1)S(1)}, bf16[656,128]{1,0:T(8,128)(2,1)S(1)}, u32[]{:S(2)}, u32[]{:S(2)}) collective-permute-start(bf16[656,128]{1,0:T(8,128)(2,1)S(1)} %collective-permute-done.4.refs_2_), channel_id=1, source_target_pairs={{0,2},{1,5},{4,0},{5,9},{8,4},{9,13},{12,8},{13,15},{14,12},{15,11... | collective-permute-start | bytes 503816 | tf_op jit(solution)/shard_map/ppermute | solution.py:271
  17.6 9.1 %collective-permute-start.9 = (bf16[656,128]{1,0:T(8,128)(2,1)S(1)}, bf16[656,128]{1,0:T(8,128)(2,1)S(1)}, u32[]{:S(2)}, u32[]{:S(2)}) collective-permute-start(bf16[656,128]{1,0:T(8,128)(2,1)S(1)} %collective-permute-done.5.refs_3_), channel_id=1, source_target_pairs={{0,2},{1,5},{4,0},{5,9},{8,4},{9,13},{12,8},{13,15},{14,12},{15,11... | collective-permute-start | bytes 503816 | tf_op jit(solution)/shard_map/ppermute | solution.py:271
  23.8 7.2 %collective-permute-start.10 = (bf16[656,128]{1,0:T(8,128)(2,1)S(1)}, bf16[656,128]{1,0:T(8,128)(2,1)S(1)}, u32[]{:S(2)}, u32[]{:S(2)}) collective-permute-start(bf16[656,128]{1,0:T(8,128)(2,1)S(1)} %collective-permute-done.6.refs_0_), channel_id=1, source_target_pairs={{0,4},{1,3},{4,8},{5,1},{8,12},{9,5},{12,14},{13,9},{14,10},{15,13... | collective-permute-start | bytes 503816 | tf_op jit(solution)/shard_map/ppermute | solution.py:271
  24.7 9.9 %collective-permute-start.11 = (bf16[656,128]{1,0:T(8,128)(2,1)S(1)}, bf16[656,128]{1,0:T(8,128)(2,1)S(1)}, u32[]{:S(2)}, u32[]{:S(2)}) collective-permute-start(bf16[656,128]{1,0:T(8,128)(2,1)S(1)} %collective-permute-done.7.refs_1_), channel_id=1, source_target_pairs={{0,4},{1,3},{4,8},{5,1},{8,12},{9,5},{12,14},{13,9},{14,10},{15,13... | collective-permute-start | bytes 503816 | tf_op jit(solution)/shard_map/ppermute | solution.py:271
  26.0 8.8 %collective-permute-start.12 = (bf16[656,128]{1,0:T(8,128)(2,1)S(1)}, bf16[656,128]{1,0:T(8,128)(2,1)S(1)}, u32[]{:S(2)}, u32[]{:S(2)}) collective-permute-start(bf16[656,128]{1,0:T(8,128)(2,1)S(1)} %collective-permute-done.8.refs_2_), channel_id=1, source_target_pairs={{0,2},{1,5},{4,0},{5,9},{8,4},{9,13},{12,8},{13,15},{14,12},{15,11... | collective-permute-start | bytes 503816 | tf_op jit(solution)/shard_map/ppermute | solution.py:271
  26.7 10.0 %collective-permute-start.13 = (bf16[656,128]{1,0:T(8,128)(2,1)S(1)}, bf16[656,128]{1,0:T(8,128)(2,1)S(1)}, u32[]{:S(2)}, u32[]{:S(2)}) collective-permute-start(bf16[656,128]{1,0:T(8,128)(2,1)S(1)} %collective-permute-done.9.refs_3_), channel_id=1, source_target_pairs={{0,2},{1,5},{4,0},{5,9},{8,4},{9,13},{12,8},{13,15},{14,12},{15,11... | collective-permute-start | bytes 503816 | tf_op jit(solution)/shard_map/ppermute | solution.py:271
  31.0 7.5 %collective-permute-start.14 = (bf16[656,128]{1,0:T(8,128)(2,1)S(1)}, bf16[656,128]{1,0:T(8,128)(2,1)S(1)}, u32[]{:S(2)}, u32[]{:S(2)}) collective-permute-start(bf16[656,128]{1,0:T(8,128)(2,1)S(1)} %collective-permute-done.10.refs_0_), channel_id=1, source_target_pairs={{0,4},{1,3},{4,8},{5,1},{8,12},{9,5},{12,14},{13,9},{14,10},{15,13... | collective-permute-start | bytes 503816 | tf_op jit(solution)/shard_map/ppermute | solution.py:271
  34.5 5.4 %collective-permute-start.15 = (bf16[656,128]{1,0:T(8,128)(2,1)S(1)}, bf16[656,128]{1,0:T(8,128)(2,1)S(1)}, u32[]{:S(2)}, u32[]{:S(2)}) collective-permute-start(bf16[656,128]{1,0:T(8,128)(2,1)S(1)} %collective-permute-done.11.refs_1_), channel_id=1, source_target_pairs={{0,4},{1,3},{4,8},{5,1},{8,12},{9,5},{12,14},{13,9},{14,10},{15,13... | collective-permute-start | bytes 503816 | tf_op jit(solution)/shard_map/ppermute | solution.py:271

commit v4 on v3

--- a/solution.py
+++ b/solution.py
@@ -13,7 +13,7 @@
 SMEM = pltpu.SMEM
 LIMIT = 48 * 1024 * 1024
 WHOLE = 63 * 1024 * 1024
-BUSY = 50
+BUSY = 100
 FOOT = 16
 
 
@@ -259,29 +259,28 @@
 
     own = pack(half, cols, b_vals)
     swap = [(0, 1), (1, 0)]
-    *own, a_later, cols_later = lax.optimization_barrier((*own, a_vals, cols))
-    others = lax.ppermute(cols_later, "col", swap)
-    a_other = lax.ppermute(a_later, "col", swap)
+    a_other, others = (lax.ppermute(x, "col", swap) for x in (a_vals, cols))
+    a = dense_rows(ids, cols, others, a_vals, a_other)
+    held = {way: list(own) for way in hops}
     rounds = [[own]]
-    held = {1: list(own), -1: list(own)}
     for step in range(1, hops[1] + 1):
-        ways = [way for way in (1, -1) if step <= hops[way]]
+        ways = [way for way in hops if step <= hops[way]]
         for p in range(pairs):
             for way in ways:
-                held[way][p] = lax.ppermute(held[way][p], ("row", "col"), ring(way))
+                part = held[way][p]
+                if step == 2:
+                    part, _ = lax.optimization_barrier((part, a))
+                held[way][p] = lax.ppermute(part, ("row", "col"), ring(way))
         rounds.append([list(held[way]) for way in ways])
-    a = dense_rows(ids, cols, others, a_vals, a_other)
+    rounds[:2] = [rounds[0] + rounds[1]]
     total_shape = jax.ShapeDtypeStruct((half // 4, 2, rows * bs, 2 * bs), jnp.float32)
-    total, done = None, 0
-    for step, parts in enumerate(rounds):
-        if step == 0:
-            total = product(first_kernel, done, a, None, parts, total_shape)
-        elif step < len(rounds) - 1:
-            total = product(middle_kernel, done, a, total, parts, total_shape)
-        else:
-            out = jax.ShapeDtypeStruct(a_vals.shape, a_vals.dtype)
-            return product(last_kernel, done, a, total, parts, out, cols)
-        done += len(parts)
+    total = product(first_kernel, 0, a, None, rounds[0], total_shape)
+    used = len(rounds[0])
+    for parts in rounds[1:-1]:
+        total = product(middle_kernel, used, a, total, parts, total_shape)
+        used += len(parts)
+    out = jax.ShapeDtypeStruct(a_vals.shape, a_vals.dtype)
+    return product(last_kernel, used, a, total, rounds[-1], out, cols)
 
 
 def ring_order(mesh):

time: 42.8 us -> 38.5 us (0.90)
  waiting for transfers between devices: 11.5 us -> 7.14 us
    ppermute x16, waiting for transfers between devices: 11.5 us -> 7.14 us  [the longest x14 5.99 us: local(): held[way][p] = lax.ppermute(part, ('row', 'col'), ring(way))]
    pallas_call x1, Pallas kernels: 1.84 us -> 2.92 us  [dense_rows(): pl.pallas_call(dense_kernel, out_shape=jax.ShapeDtypeStruct((sources, row...]
    pallas_call x5 -> x4, Pallas kernels: 9.28 us -> 8.5 us  [product(): pl.pallas_call(functools.partial(kernel, done), out_shape=out, in_specs=s...]
  transfers between devices with their start and end apart: 16 -> 16, of which waited for: 7 -> 5; matrix products, arithmetic and copies ran while one was open for 2% -> 2% of each run, Pallas kernels for 20% -> 28%
where the time goes in v4:
time: 38.5 us; the launch traced here: 38.4 us
  starting transfers between devices  17 us (44%)
  Pallas kernels  13.4 us (35%)
  waiting for transfers between devices  7.14 us (19%)
  local copies, waits for them, and re-layouts  0.7 us (2%)
    ppermute x14, starting transfers between devices, local(): held[way][p] = lax.ppermute(part, ('row', 'col'), ring(way))  16.6 us
    pallas_call x4, Pallas kernels, product(): pl.pallas_call(functools.partial(kernel, done), out_shape=out, in_specs=s...  8.5 us
    ppermute x14, waiting for transfers between devices, local(): held[way][p] = lax.ppermute(part, ('row', 'col'), ring(way))  5.99 us
    pallas_call x1, Pallas kernels, dense_rows(): pl.pallas_call(dense_kernel, out_shape=jax.ShapeDtypeStruct((sources, row...  2.92 us
    pallas_call x1, Pallas kernels, pack(): pl.pallas_call(functools.partial(pack_kernel, half), out_shape=[shape] *...  1.96 us
    ppermute x2, waiting for transfers between devices, local(): a_other, others = (lax.ppermute(x, 'col', swap) for x in (a_vals, cols))  1.16 us
  transfers between devices with their start and end apart: 16, of which 5 were waited for; matrix products, arithmetic and copies ran while one was open for 2% of the time, Pallas kernels for 28%

profile of v4, /device:TPU:0, one launch (start us, length us, event | category | flops | bytes accessed | tf_op | source)
XLA Modules:
  0.0 38.4 jit_solution(2972714307755268909)
XLA Ops:
  0.0 0.0 copy-start
  0.0 0.5 %collective-permute-start.1 = (bf16[4,10,64,64]{3,2,1,0:T(8,128)(2,1)}, bf16[4,10,64,64]{3,2,1,0:T(8,128)(2,1)}, u32[]{:S(2)}, u32[]{:S(2)}) collective-permute-start(bf16[4,10,64,64]{3,2,1,0:T(8,128)(2,1)} %own_ref.1), channel_id=1, source_target_pairs={{0,1},{1,0},{2,3},{3,2},{4,5},{5,4},{6,7},{7,6},{8,9},{9,8},{10,11... | collective-permute-start | bytes 983048 | tf_op jit(solution)/shard_map/ppermute | solution.py:262
  0.5 2.0 %shard_map.47 = (bf16[656,128]{1,0:T(8,128)(2,1)}, bf16[656,128]{1,0:T(8,128)(2,1)}) custom-call(s32[4,10]{1,0:T(4,128)} %cols_hbm.3, bf16[4,10,64,64]{3,2,1,0:T(8,128)(2,1)} %b_hbm.1), custom_call_target="tpu_custom_call" | custom-call | bytes 655360 | tf_op jit(solution)/shard_map/pallas_call | solution.py:55
  2.4 0.0 copy-start.1
  2.4 2.7 %collective-permute-start.2 = (bf16[656,128]{1,0:T(8,128)(2,1)}, bf16[656,128]{1,0:T(8,128)(2,1)S(1)}, u32[]{:S(2)}, u32[]{:S(2)}) collective-permute-start(bf16[656,128]{1,0:T(8,128)(2,1)} %get-tuple-element.11.refs_0_), channel_id=1, source_target_pairs={{0,4},{1,3},{4,8},{5,1},{8,12},{9,5},{12,14},{13,9},{14,10},{15,13... | collective-permute-start | bytes 503816 | tf_op jit(solution)/shard_map/ppermute | solution.py:273
  5.1 1.6 %collective-permute-start.3 = (bf16[656,128]{1,0:T(8,128)(2,1)}, bf16[656,128]{1,0:T(8,128)(2,1)S(1)}, u32[]{:S(2)}, u32[]{:S(2)}) collective-permute-start(bf16[656,128]{1,0:T(8,128)(2,1)} %get-tuple-element.12.refs_1_), channel_id=1, source_target_pairs={{0,4},{1,3},{4,8},{5,1},{8,12},{9,5},{12,14},{13,9},{14,10},{15,13... | collective-permute-start | bytes 503816 | tf_op jit(solution)/shard_map/ppermute | solution.py:273
  6.7 0.4 %collective-permute-start.4 = (bf16[656,128]{1,0:T(8,128)(2,1)}, bf16[656,128]{1,0:T(8,128)(2,1)S(1)}, u32[]{:S(2)}, u32[]{:S(2)}) collective-permute-start(bf16[656,128]{1,0:T(8,128)(2,1)} %get-tuple-element.11.refs_0_), channel_id=1, source_target_pairs={{0,2},{1,5},{4,0},{5,9},{8,4},{9,13},{12,8},{13,15},{14,12},{15,11... | collective-permute-start | bytes 503816 | tf_op jit(solution)/shard_map/ppermute | solution.py:273
  7.2 0.0 copy-done.1
  7.2 0.0 collective-permute-start
  7.2 1.2 %collective-permute-done.others_ref = s32[4,10]{1,0:T(4,128)S(1)} collective-permute-done((s32[4,10]{1,0:T(4,128)S(1)}, s32[4,10]{1,0:T(4,128)S(1)}, u32[]{:S(2)}, u32[]{:S(2)}) %collective-permute-start) | collective-permute-done | bytes 192 | tf_op jit(solution)/shard_map/ppermute | solution.py:262
  8.3 0.8 %collective-permute-start.5 = (bf16[656,128]{1,0:T(8,128)(2,1)}, bf16[656,128]{1,0:T(8,128)(2,1)S(1)}, u32[]{:S(2)}, u32[]{:S(2)}) collective-permute-start(bf16[656,128]{1,0:T(8,128)(2,1)} %get-tuple-element.12.refs_1_), channel_id=1, source_target_pairs={{0,2},{1,5},{4,0},{5,9},{8,4},{9,13},{12,8},{13,15},{14,12},{15,11... | collective-permute-start | bytes 503816 | tf_op jit(solution)/shard_map/ppermute | solution.py:273
  9.1 0.7 %dynamic-slice_bitcast_fusion.ids_ref = s32[8]{0:T(128)S(1)} fusion(s32[8,2,8]{2,1,0:T(2,128)} %constant.16.clone, s32[]{:T(128)S(6)} %select_n.6, s32[]{:T(128)S(6)} %select_n.7), kind=kLoop, calls=%fused_computation | loop fusion | bytes 72 | tf_op jit(solution)/shard_map/squeeze | solution.py:258
  9.8 0.0 copy-start.2
  9.8 0.0 copy-start.3
  9.8 0.0 collective-permute-done.1.other_ref
  9.8 0.0 copy-done
  9.8 2.9 %shard_map.46.a_ref = bf16[8,2,256,128]{3,2,1,0:T(8,128)(2,1)S(1)} custom-call(s32[8]{0:T(128)S(1)} %dynamic-slice_bitcast_fusion.ids_ref, s32[4,10]{1,0:T(4,128)S(1)} %copy-done.1, s32[4,10]{1,0:T(4,128)S(1)} %collective-permute-done.others_ref, bf16[4,10,64,64]{3,2,1,0:T(8,128)(2,1)S(1)} %copy-done, bf16[4,10,64,64]{3,2,1,0:T(8,128)(2,1)} %collective-permute-done.1.other_ref), custom_call_target="tpu_custom_call" | custom-call | bytes 131072000 | tf_op jit(solution)/shard_map/pallas_call | solution.py:102
  12.7 0.0 collective-permute-done.2.refs_2_
  12.7 1.3 %collective-permute-start.6 = (bf16[656,128]{1,0:T(8,128)(2,1)S(1)}, bf16[656,128]{1,0:T(8,128)(2,1)S(1)}, u32[]{:S(2)}, u32[]{:S(2)}) collective-permute-start(bf16[656,128]{1,0:T(8,128)(2,1)S(1)} %collective-permute-done.2.refs_2_), channel_id=1, source_target_pairs={{0,4},{1,3},{4,8},{5,1},{8,12},{9,5},{12,14},{13,9},{14,10},{15,13... | collective-permute-start | bytes 503816 | tf_op jit(solution)/shard_map/ppermute | solution.py:273
  14.0 0.0 collective-permute-done.3.refs_3_
  14.0 1.6 %collective-permute-start.7 = (bf16[656,128]{1,0:T(8,128)(2,1)S(1)}, bf16[656,128]{1,0:T(8,128)(2,1)S(1)}, u32[]{:S(2)}, u32[]{:S(2)}) collective-permute-start(bf16[656,128]{1,0:T(8,128)(2,1)S(1)} %collective-permute-done.3.refs_3_), channel_id=1, source_target_pairs={{0,4},{1,3},{4,8},{5,1},{8,12},{9,5},{12,14},{13,9},{14,10},{15,13... | collective-permute-start | bytes 503816 | tf_op jit(solution)/shard_map/ppermute | solution.py:273
  15.6 0.0 collective-permute-done.4.refs_4_
  15.6 0.4 %collective-permute-start.8 = (bf16[656,128]{1,0:T(8,128)(2,1)S(1)}, bf16[656,128]{1,0:T(8,128)(2,1)S(1)}, u32[]{:S(2)}, u32[]{:S(2)}) collective-permute-start(bf16[656,128]{1,0:T(8,128)(2,1)S(1)} %collective-permute-done.4.refs_4_), channel_id=1, source_target_pairs={{0,2},{1,5},{4,0},{5,9},{8,4},{9,13},{12,8},{13,15},{14,12},{15,11... | collective-permute-start | bytes 503816 | tf_op jit(solution)/shard_map/ppermute | solution.py:273
  16.1 0.0 collective-permute-done.5.refs_5_
  16.1 0.8 %collective-permute-start.9 = (bf16[656,128]{1,0:T(8,128)(2,1)S(1)}, bf16[656,128]{1,0:T(8,128)(2,1)S(1)}, u32[]{:S(2)}, u32[]{:S(2)}) collective-permute-start(bf16[656,128]{1,0:T(8,128)(2,1)S(1)} %collective-permute-done.5.refs_5_), channel_id=1, source_target_pairs={{0,2},{1,5},{4,0},{5,9},{8,4},{9,13},{12,8},{13,15},{14,12},{15,11... | collective-permute-start | bytes 503816 | tf_op jit(solution)/shard_map/ppermute | solution.py:273
  16.9 0.0 copy-done.2
  16.9 0.0 copy-done.3
  16.9 2.3 %shard_map.48.before = f32[4,2,256,128]{3,2,1,0:T(8,128)S(1)} custom-call(bf16[8,2,256,128]{3,2,1,0:T(8,128)(2,1)S(1)} %shard_map.46.a_ref, bf16[656,128]{1,0:T(8,128)(2,1)S(1)} %copy-done.2, bf16[656,128]{1,0:T(8,128)(2,1)S(1)} %copy-done.3, bf16[656,128]{1,0:T(8,128)(2,1)S(1)} %collective-permute-done.2.refs_2_, ...), custom_call_target="tpu_custom_call" | custom-call | flops 20132659200 | tf_op jit(solution)/shard_map/pallas_call | solution.py:224
  19.2 0.3 collective-permute-done.6.refs_0_
  19.5 1.4 %collective-permute-start.10 = (bf16[656,128]{1,0:T(8,128)(2,1)S(1)}, bf16[656,128]{1,0:T(8,128)(2,1)S(1)}, u32[]{:S(2)}, u32[]{:S(2)}) collective-permute-start(bf16[656,128]{1,0:T(8,128)(2,1)S(1)} %collective-permute-done.6.refs_0_), channel_id=1, source_target_pairs={{0,4},{1,3},{4,8},{5,1},{8,12},{9,5},{12,14},{13,9},{14,10},{15,13... | collective-permute-start | bytes 503816 | tf_op jit(solution)/shard_map/ppermute | solution.py:273
  20.9 2.2 %collective-permute-done.7.refs_1_ = bf16[656,128]{1,0:T(8,128)(2,1)S(1)} collective-permute-done((bf16[656,128]{1,0:T(8,128)(2,1)S(1)}, bf16[656,128]{1,0:T(8,128)(2,1)S(1)}, u32[]{:S(2)}, u32[]{:S(2)}) %collective-permute-start.7) | collective-permute-done | bytes 167968 | tf_op jit(solution)/shard_map/ppermute | solution.py:273
  23.1 1.4 %collective-permute-start.11 = (bf16[656,128]{1,0:T(8,128)(2,1)S(1)}, bf16[656,128]{1,0:T(8,128)(2,1)S(1)}, u32[]{:S(2)}, u32[]{:S(2)}) collective-permute-start(bf16[656,128]{1,0:T(8,128)(2,1)S(1)} %collective-permute-done.7.refs_1_), channel_id=1, source_target_pairs={{0,4},{1,3},{4,8},{5,1},{8,12},{9,5},{12,14},{13,9},{14,10},{15,13... | collective-permute-start | bytes 503816 | tf_op jit(solution)/shard_map/ppermute | solution.py:273
  24.5 0.0 collective-permute-done.8.refs_2_
  24.5 0.6 %collective-permute-start.12 = (bf16[656,128]{1,0:T(8,128)(2,1)S(1)}, bf16[656,128]{1,0:T(8,128)(2,1)S(1)}, u32[]{:S(2)}, u32[]{:S(2)}) collective-permute-start(bf16[656,128]{1,0:T(8,128)(2,1)S(1)} %collective-permute-done.8.refs_2_), channel_id=1, source_target_pairs={{0,2},{1,5},{4,0},{5,9},{8,4},{9,13},{12,8},{13,15},{14,12},{15,11... | collective-permute-start | bytes 503816 | tf_op jit(solution)/shard_map/ppermute | solution.py:273
  25.1 0.0 collective-permute-done.9.refs_3_
  25.1 1.6 %collective-permute-start.13 = (bf16[656,128]{1,0:T(8,128)(2,1)S(1)}, bf16[656,128]{1,0:T(8,128)(2,1)S(1)}, u32[]{:S(2)}, u32[]{:S(2)}) collective-permute-start(bf16[656,128]{1,0:T(8,128)(2,1)S(1)} %collective-permute-done.9.refs_3_), channel_id=1, source_target_pairs={{0,2},{1,5},{4,0},{5,9},{8,4},{9,13},{12,8},{13,15},{14,12},{15,11... | collective-permute-start | bytes 503816 | tf_op jit(solution)/shard_map/ppermute | solution.py:273
  26.7 1.8 %shard_map.49.before = f32[4,2,256,128]{3,2,1,0:T(8,128)S(1)} custom-call(bf16[8,2,256,128]{3,2,1,0:T(8,128)(2,1)S(1)} %shard_map.46.a_ref, f32[4,2,256,128]{3,2,1,0:T(8,128)S(1)} %shard_map.48.before, bf16[656,128]{1,0:T(8,128)(2,1)S(1)} %collective-permute-done.6.refs_0_, ...), custom_call_target="tpu_custom_call", output_to_operand_aliasing={{}: (1, {})} | custom-call | flops 13421772800 | tf_op jit(solution)/shard_map/pallas_call | solution.py:224
  28.5 0.0 collective-permute-done.10.refs_0_
  28.5 0.5 %collective-permute-start.14 = (bf16[656,128]{1,0:T(8,128)(2,1)S(1)}, bf16[656,128]{1,0:T(8,128)(2,1)S(1)}, u32[]{:S(2)}, u32[]{:S(2)}) collective-permute-start(bf16[656,128]{1,0:T(8,128)(2,1)S(1)} %collective-permute-done.10.refs_0_), channel_id=1, source_target_pairs={{0,4},{1,3},{4,8},{5,1},{8,12},{9,5},{12,14},{13,9},{14,10},{15,13... | collective-permute-start | bytes 503816 | tf_op jit(solution)/shard_map/ppermute | solution.py:273
  29.0 1.3 %collective-permute-done.11.refs_1_ = bf16[656,128]{1,0:T(8,128)(2,1)S(1)} collective-permute-done((bf16[656,128]{1,0:T(8,128)(2,1)S(1)}, bf16[656,128]{1,0:T(8,128)(2,1)S(1)}, u32[]{:S(2)}, u32[]{:S(2)}) %collective-permute-start.11) | collective-permute-done | bytes 167968 | tf_op jit(solution)/shard_map/ppermute | solution.py:273
  30.3 1.4 %collective-permute-start.15 = (bf16[656,128]{1,0:T(8,128)(2,1)S(1)}, bf16[656,128]{1,0:T(8,128)(2,1)S(1)}, u32[]{:S(2)}, u32[]{:S(2)}) collective-permute-start(bf16[656,128]{1,0:T(8,128)(2,1)S(1)} %collective-permute-done.11.refs_1_), channel_id=1, source_target_pairs={{0,4},{1,3},{4,8},{5,1},{8,12},{9,5},{12,14},{13,9},{14,10},{15,13... | collective-permute-start | bytes 503816 | tf_op jit(solution)/shard_map/ppermute | solution.py:273
  31.7 0.0 collective-permute-done.12.refs_2_
  31.7 2.2 %collective-permute-done.13.refs_3_ = bf16[656,128]{1,0:T(8,128)(2,1)S(1)} collective-permute-done((bf16[656,128]{1,0:T(8,128)(2,1)S(1)}, bf16[656,128]{1,0:T(8,128)(2,1)S(1)}, u32[]{:S(2)}, u32[]{:S(2)}) %collective-permute-start.13) | collective-permute-done | bytes 167968 | tf_op jit(solution)/shard_map/ppermute | solution.py:273
  33.9 1.8 %shard_map.50.total = f32[4,2,256,128]{3,2,1,0:T(8,128)S(1)} custom-call(bf16[8,2,256,128]{3,2,1,0:T(8,128)(2,1)S(1)} %shard_map.46.a_ref, f32[4,2,256,128]{3,2,1,0:T(8,128)S(1)} %shard_map.49.before, bf16[656,128]{1,0:T(8,128)(2,1)S(1)} %collective-permute-done.10.refs_0_, ...), custom_call_target="tpu_custom_call", output_to_operand_aliasing={{}: (1, {})} | custom-call | flops 13421772800 | tf_op jit(solution)/shard_map/pallas_call | solution.py:224
  35.7 0.0 collective-permute-done.14.refs_0_
  35.7 0.0 collective-permute-done.15.refs_1_
  35.7 2.7 %shard_map.51 = bf16[4,10,64,64]{3,2,1,0:T(8,128)(2,1)} custom-call(bf16[8,2,256,128]{3,2,1,0:T(8,128)(2,1)S(1)} %shard_map.46.a_ref, f32[4,2,256,128]{3,2,1,0:T(8,128)S(1)} %shard_map.50.total, s32[4,10]{1,0:T(4,128)S(1)} %copy-done.1, bf16[656,128]{1,0:T(8,128)(2,1)S(1)} %collective-permute-done.14.refs_0_, ...), custom_call_target="tpu_custom_call" | custom-call | flops 4194304000 | tf_op jit(solution)/shard_map/pallas_call | solution.py:224
Async XLA Ops:
  0.0 9.8 %copy-start = (bf16[4,10,64,64]{3,2,1,0:T(8,128)(2,1)S(1)}, bf16[4,10,64,64]{3,2,1,0:T(8,128)(2,1)}, u32[]{:S(2)}) copy-start(bf16[4,10,64,64]{3,2,1,0:T(8,128)(2,1)} %own_ref.1) | copy-start | bytes 983044
  0.0 9.8 %collective-permute-start.1 = (bf16[4,10,64,64]{3,2,1,0:T(8,128)(2,1)}, bf16[4,10,64,64]{3,2,1,0:T(8,128)(2,1)}, u32[]{:S(2)}, u32[]{:S(2)}) collective-permute-start(bf16[4,10,64,64]{3,2,1,0:T(8,128)(2,1)} %own_ref.1), channel_id=1, source_target_pairs={{0,1},{1,0},{2,3},{3,2},{4,5},{5,4},{6,7},{7,6},{8,9},{9,8},{10,11... | collective-permute-start | bytes 983048 | tf_op jit(solution)/shard_map/ppermute | solution.py:262
  2.4 4.7 %copy-start.1 = (s32[4,10]{1,0:T(4,128)S(1)}, s32[4,10]{1,0:T(4,128)}, u32[]{:S(2)}) copy-start(s32[4,10]{1,0:T(4,128)} %cols_hbm.3) | copy-start | bytes 484
  2.4 10.3 %collective-permute-start.2 = (bf16[656,128]{1,0:T(8,128)(2,1)}, bf16[656,128]{1,0:T(8,128)(2,1)S(1)}, u32[]{:S(2)}, u32[]{:S(2)}) collective-permute-start(bf16[656,128]{1,0:T(8,128)(2,1)} %get-tuple-element.11.refs_0_), channel_id=1, source_target_pairs={{0,4},{1,3},{4,8},{5,1},{8,12},{9,5},{12,14},{13,9},{14,10},{15,13... | collective-permute-start | bytes 503816 | tf_op jit(solution)/shard_map/ppermute | solution.py:273
  5.1 8.9 %collective-permute-start.3 = (bf16[656,128]{1,0:T(8,128)(2,1)}, bf16[656,128]{1,0:T(8,128)(2,1)S(1)}, u32[]{:S(2)}, u32[]{:S(2)}) collective-permute-start(bf16[656,128]{1,0:T(8,128)(2,1)} %get-tuple-element.12.refs_1_), channel_id=1, source_target_pairs={{0,4},{1,3},{4,8},{5,1},{8,12},{9,5},{12,14},{13,9},{14,10},{15,13... | collective-permute-start | bytes 503816 | tf_op jit(solution)/shard_map/ppermute | solution.py:273
  6.7 8.9 %collective-permute-start.4 = (bf16[656,128]{1,0:T(8,128)(2,1)}, bf16[656,128]{1,0:T(8,128)(2,1)S(1)}, u32[]{:S(2)}, u32[]{:S(2)}) collective-permute-start(bf16[656,128]{1,0:T(8,128)(2,1)} %get-tuple-element.11.refs_0_), channel_id=1, source_target_pairs={{0,2},{1,5},{4,0},{5,9},{8,4},{9,13},{12,8},{13,15},{14,12},{15,11... | collective-permute-start | bytes 503816 | tf_op jit(solution)/shard_map/ppermute | solution.py:273
  7.2 1.2 %collective-permute-start = (s32[4,10]{1,0:T(4,128)S(1)}, s32[4,10]{1,0:T(4,128)S(1)}, u32[]{:S(2)}, u32[]{:S(2)}) collective-permute-start(s32[4,10]{1,0:T(4,128)S(1)} %copy-done.1), channel_id=1, source_target_pairs={{0,1},{1,0},{2,3},{3,2},{4,5},{5,4},{6,7},{7,6},{8,9},{9,8},{10,11... | collective-permute-start | bytes 488 | tf_op jit(solution)/shard_map/ppermute | solution.py:262
  8.3 7.8 %collective-permute-start.5 = (bf16[656,128]{1,0:T(8,128)(2,1)}, bf16[656,128]{1,0:T(8,128)(2,1)S(1)}, u32[]{:S(2)}, u32[]{:S(2)}) collective-permute-start(bf16[656,128]{1,0:T(8,128)(2,1)} %get-tuple-element.12.refs_1_), channel_id=1, source_target_pairs={{0,2},{1,5},{4,0},{5,9},{8,4},{9,13},{12,8},{13,15},{14,12},{15,11... | collective-permute-start | bytes 503816 | tf_op jit(solution)/shard_map/ppermute | solution.py:273
  9.8 7.1 %copy-start.2 = (bf16[656,128]{1,0:T(8,128)(2,1)S(1)}, bf16[656,128]{1,0:T(8,128)(2,1)}, u32[]{:S(2)}) copy-start(bf16[656,128]{1,0:T(8,128)(2,1)} %get-tuple-element.11.refs_0_) | copy-start | bytes 503812
  9.8 7.1 %copy-start.3 = (bf16[656,128]{1,0:T(8,128)(2,1)S(1)}, bf16[656,128]{1,0:T(8,128)(2,1)}, u32[]{:S(2)}) copy-start(bf16[656,128]{1,0:T(8,128)(2,1)} %get-tuple-element.12.refs_1_) | copy-start | bytes 503812
  12.7 6.7 %collective-permute-start.6 = (bf16[656,128]{1,0:T(8,128)(2,1)S(1)}, bf16[656,128]{1,0:T(8,128)(2,1)S(1)}, u32[]{:S(2)}, u32[]{:S(2)}) collective-permute-start(bf16[656,128]{1,0:T(8,128)(2,1)S(1)} %collective-permute-done.2.refs_2_), channel_id=1, source_target_pairs={{0,4},{1,3},{4,8},{5,1},{8,12},{9,5},{12,14},{13,9},{14,10},{15,13... | collective-permute-start | bytes 503816 | tf_op jit(solution)/shard_map/ppermute | solution.py:273
  14.0 9.0 %collective-permute-start.7 = (bf16[656,128]{1,0:T(8,128)(2,1)S(1)}, bf16[656,128]{1,0:T(8,128)(2,1)S(1)}, u32[]{:S(2)}, u32[]{:S(2)}) collective-permute-start(bf16[656,128]{1,0:T(8,128)(2,1)S(1)} %collective-permute-done.3.refs_3_), channel_id=1, source_target_pairs={{0,4},{1,3},{4,8},{5,1},{8,12},{9,5},{12,14},{13,9},{14,10},{15,13... | collective-permute-start | bytes 503816 | tf_op jit(solution)/shard_map/ppermute | solution.py:273
  15.6 8.9 %collective-permute-start.8 = (bf16[656,128]{1,0:T(8,128)(2,1)S(1)}, bf16[656,128]{1,0:T(8,128)(2,1)S(1)}, u32[]{:S(2)}, u32[]{:S(2)}) collective-permute-start(bf16[656,128]{1,0:T(8,128)(2,1)S(1)} %collective-permute-done.4.refs_4_), channel_id=1, source_target_pairs={{0,2},{1,5},{4,0},{5,9},{8,4},{9,13},{12,8},{13,15},{14,12},{15,11... | collective-permute-start | bytes 503816 | tf_op jit(solution)/shard_map/ppermute | solution.py:273
  16.1 9.0 %collective-permute-start.9 = (bf16[656,128]{1,0:T(8,128)(2,1)S(1)}, bf16[656,128]{1,0:T(8,128)(2,1)S(1)}, u32[]{:S(2)}, u32[]{:S(2)}) collective-permute-start(bf16[656,128]{1,0:T(8,128)(2,1)S(1)} %collective-permute-done.5.refs_5_), channel_id=1, source_target_pairs={{0,2},{1,5},{4,0},{5,9},{8,4},{9,13},{12,8},{13,15},{14,12},{15,11... | collective-permute-start | bytes 503816 | tf_op jit(solution)/shard_map/ppermute | solution.py:273
  19.5 9.0 %collective-permute-start.10 = (bf16[656,128]{1,0:T(8,128)(2,1)S(1)}, bf16[656,128]{1,0:T(8,128)(2,1)S(1)}, u32[]{:S(2)}, u32[]{:S(2)}) collective-permute-start(bf16[656,128]{1,0:T(8,128)(2,1)S(1)} %collective-permute-done.6.refs_0_), channel_id=1, source_target_pairs={{0,4},{1,3},{4,8},{5,1},{8,12},{9,5},{12,14},{13,9},{14,10},{15,13... | collective-permute-start | bytes 503816 | tf_op jit(solution)/shard_map/ppermute | solution.py:273
  23.1 7.2 %collective-permute-start.11 = (bf16[656,128]{1,0:T(8,128)(2,1)S(1)}, bf16[656,128]{1,0:T(8,128)(2,1)S(1)}, u32[]{:S(2)}, u32[]{:S(2)}) collective-permute-start(bf16[656,128]{1,0:T(8,128)(2,1)S(1)} %collective-permute-done.7.refs_1_), channel_id=1, source_target_pairs={{0,4},{1,3},{4,8},{5,1},{8,12},{9,5},{12,14},{13,9},{14,10},{15,13... | collective-permute-start | bytes 503816 | tf_op jit(solution)/shard_map/ppermute | solution.py:273
  24.5 7.2 %collective-permute-start.12 = (bf16[656,128]{1,0:T(8,128)(2,1)S(1)}, bf16[656,128]{1,0:T(8,128)(2,1)S(1)}, u32[]{:S(2)}, u32[]{:S(2)}) collective-permute-start(bf16[656,128]{1,0:T(8,128)(2,1)S(1)} %collective-permute-done.8.refs_2_), channel_id=1, source_target_pairs={{0,2},{1,5},{4,0},{5,9},{8,4},{9,13},{12,8},{13,15},{14,12},{15,11... | collective-permute-start | bytes 503816 | tf_op jit(solution)/shard_map/ppermute | solution.py:273
  25.1 8.8 %collective-permute-start.13 = (bf16[656,128]{1,0:T(8,128)(2,1)S(1)}, bf16[656,128]{1,0:T(8,128)(2,1)S(1)}, u32[]{:S(2)}, u32[]{:S(2)}) collective-permute-start(bf16[656,128]{1,0:T(8,128)(2,1)S(1)} %collective-permute-done.9.refs_3_), channel_id=1, source_target_pairs={{0,2},{1,5},{4,0},{5,9},{8,4},{9,13},{12,8},{13,15},{14,12},{15,11... | collective-permute-start | bytes 503816 | tf_op jit(solution)/shard_map/ppermute | solution.py:273
  28.5 7.2 %collective-permute-start.14 = (bf16[656,128]{1,0:T(8,128)(2,1)S(1)}, bf16[656,128]{1,0:T(8,128)(2,1)S(1)}, u32[]{:S(2)}, u32[]{:S(2)}) collective-permute-start(bf16[656,128]{1,0:T(8,128)(2,1)S(1)} %collective-permute-done.10.refs_0_), channel_id=1, source_target_pairs={{0,4},{1,3},{4,8},{5,1},{8,12},{9,5},{12,14},{13,9},{14,10},{15,13... | collective-permute-start | bytes 503816 | tf_op jit(solution)/shard_map/ppermute | solution.py:273
  30.3 5.4 %collective-permute-start.15 = (bf16[656,128]{1,0:T(8,128)(2,1)S(1)}, bf16[656,128]{1,0:T(8,128)(2,1)S(1)}, u32[]{:S(2)}, u32[]{:S(2)}) collective-permute-start(bf16[656,128]{1,0:T(8,128)(2,1)S(1)} %collective-permute-done.11.refs_1_), channel_id=1, source_target_pairs={{0,4},{1,3},{4,8},{5,1},{8,12},{9,5},{12,14},{13,9},{14,10},{15,13... | collective-permute-start | bytes 503816 | tf_op jit(solution)/shard_map/ppermute | solution.py:273

commit v5 on v4

v5 whole, which is shorter than its diff:
```python
import functools
import math

import jax
import jax.numpy as jnp
import numpy as np
from jax import lax
from jax.experimental import pallas as pl
from jax.experimental.pallas import tpu as pltpu
from jax.sharding import PartitionSpec as P

VMEM = pltpu.VMEM
SMEM = pltpu.SMEM
LIMIT = 48 * 1024 * 1024
WHOLE = 63 * 1024 * 1024
BUSY = 5
FOOT = 16


def params(limit=LIMIT):
    return pltpu.CompilerParams(vmem_limit_bytes=limit)


def cost(flops, size):
    return pl.CostEstimate(flops=flops, bytes_accessed=size, transcendentals=0)


def pack_kernel(half, cols_hbm, b_hbm, o_ref, cols_ref, b_ref, sem, sems):
    rows, slots, bs, _ = b_ref.shape
    copies = [pltpu.make_async_copy(b_hbm.at[r], b_ref.at[r], sems.at[r]) for r in range(rows)]
    fetch = pltpu.make_async_copy(cols_hbm, cols_ref, sem)
    fetch.start()
    for copy in copies:
        copy.start()
    row = lax.broadcasted_iota(jnp.int32, (FOOT, 2 * bs), 0)
    lane = lax.broadcasted_iota(jnp.int32, (FOOT, 2 * bs), 1)
    fetch.wait()
    foot = jnp.full((FOOT, 2 * bs), slots, jnp.int32)
    for r in range(rows):
        for n in range(slots):
            here = (row == r) & (lane == lax.rem(cols_ref[r, n], half))
            foot = jnp.where(here, n, foot)
    o_ref[rows // 2 * slots * bs :, :] = foot.astype(jnp.float32).astype(o_ref.dtype)
    for p in range(rows // 2):
        copies[2 * p].wait()
        copies[2 * p + 1].wait()
        for n in range(slots):
            at = (p * slots + n) * bs
            o_ref[at : at + bs, :] = jnp.concatenate([b_ref[2 * p, n], b_ref[2 * p + 1, n]], axis=-1)


def pack(half, cols, b_vals):
    rows, slots, bs, _ = b_vals.shape
    return pl.pallas_call(
        functools.partial(pack_kernel, half),
        out_shape=jax.ShapeDtypeStruct((rows // 2 * slots * bs + FOOT, 2 * bs), b_vals.dtype),
        in_specs=[pl.BlockSpec(memory_space=pl.ANY)] * 2,
        out_specs=pl.BlockSpec(memory_space=VMEM),
        scratch_shapes=[
            SMEM(cols.shape, cols.dtype),
            VMEM(b_vals.shape, b_vals.dtype),
            pltpu.SemaphoreType.DMA,
            pltpu.SemaphoreType.DMA((rows,)),
        ],
        compiler_params=params(WHOLE),
        cost_estimate=cost(0, 2 * b_vals.size * 2),
    )(cols, b_vals)


def dense_kernel(cols_ref, others_ref, own_ref, other_ref, o_ref, blocks, where):
    rows, slots, bs, _ = own_ref.shape
    sources, pairs = o_ref.shape[:2]
    blocks[:, :slots] = own_ref[...]
    blocks[:, slots : 2 * slots] = other_ref[...]
    blocks[:, 2 * slots] = jnp.zeros_like(blocks[:, 2 * slots])
    for i in range(rows):
        def clear(j, carry):
            where[i, j] = 2 * slots
            return carry

        lax.fori_loop(0, 2 * sources * pairs, clear, 0, unroll=8)
        for m in range(slots):
            where[i, cols_ref[i, m]] = m
            where[i, others_ref[i, m]] = slots + m

    def body(s, carry):
        for p in range(pairs):
            j = (s * pairs + p) * 2
            for i in range(rows):
                left = blocks[i, where[i, j]]
                right = blocks[i, where[i, j + 1]]
                o_ref[s, p, i * bs : (i + 1) * bs, :] = jnp.concatenate([left, right], axis=-1)
        return carry

    lax.fori_loop(0, sources, body, 0, unroll=2)


def dense_rows(sources, cols, others, own, other):
    rows, slots, bs, _ = own.shape
    return pl.pallas_call(
        dense_kernel,
        out_shape=jax.ShapeDtypeStruct((sources, rows // 2, rows * bs, 2 * bs), own.dtype),
        grid_spec=pltpu.PrefetchScalarGridSpec(
            num_scalar_prefetch=2,
            grid=(),
            in_specs=[pl.BlockSpec(memory_space=VMEM)] * 2,
            out_specs=pl.BlockSpec(memory_space=VMEM),
            scratch_shapes=[
                VMEM((rows, 2 * slots + 1, bs, bs), own.dtype),
                SMEM((rows, sources * rows), jnp.int32),
            ],
        ),
        compiler_params=params(),
        cost_estimate=cost(0, BUSY * 8 * own.size),
    )(cols, others, own, other)


def look_up(table, k):
    value = jnp.int32(table[0])
    for n, entry in enumerate(table[1:], 1):
        value = jnp.where(k == n, entry, value)
    return value


def arrived_from(order, way, steps):
    spots = [order.index(r) for r in range(len(order))]
    ahead = jnp.where(lax.axis_index("col") == 0, way, -way) * steps
    return look_up(order, lax.rem(look_up(spots, lax.axis_index("row")) - ahead + len(order), len(order)))


def add_products(a, part, total, first, feet, where, sem):
    groups, bs = total.shape[0], total.shape[3] // 2
    pairs = a.shape[0]
    slots = (part.shape[0] - FOOT) // bs // pairs
    feet[...] = part[pairs * slots * bs :, :].astype(jnp.float32).astype(jnp.int32)
    copy = pltpu.make_async_copy(feet, where, sem)
    copy.start()
    copy.wait()
    low = lax.broadcasted_iota(jnp.int32, (bs, 2 * bs), 1) < bs
    panels = jnp.concatenate([a[p] for p in range(pairs)], axis=-1)

    def block(p, slot):
        at = pl.multiple_of((p * slots + jnp.minimum(slot, slots - 1)) * bs, bs)
        return jnp.where(slot < slots, part[pl.ds(at, bs), :], jnp.zeros((bs, 2 * bs), part.dtype))

    def turn(x):
        return jnp.concatenate([x[:, bs:], x[:, :bs]], axis=-1)

    def body(g, carry):
        panel = []
        for p in range(pairs):
            for h in range(2):
                tiles = []
                for q in (2 * g, 2 * g + 1):
                    left = block(p, where[2 * p + h, 2 * q])
                    right = block(p, where[2 * p + h, 2 * q + 1])
                    if h == 0:
                        right = turn(right)
                    else:
                        left = turn(left)
                    tiles.append(jnp.where(low, left, right))
                panel.append(jnp.concatenate(tiles, axis=-1))
        sums = jnp.dot(panels, jnp.concatenate(panel, axis=0), preferred_element_type=jnp.float32)
        for t in range(2):
            piece = sums[:, t * 2 * bs : (t + 1) * 2 * bs]
            if first:
                total[g, t] = piece
            else:
                total[g, t] += piece
        return carry

    lax.fori_loop(0, groups, body, 0, unroll=min(groups, 4))


def first_kernel(source, a_ref, part, total, *scratch):
    add_products(a_ref.at[source()], part, total, True, *scratch)


def middle_kernel(source, a_ref, before, part, total, *scratch):
    add_products(a_ref.at[source()], part, total, False, *scratch)


def last_kernel(source, a_ref, total, cols_hbm, part, o_hbm, feet, where, sem, cols_ref, o_ref, cols_sem, sems):
    fetch = pltpu.make_async_copy(cols_hbm, cols_ref, cols_sem)
    fetch.start()
    add_products(a_ref.at[source()], part, total, False, feet, where, sem)
    fetch.wait()
    rows, slots, bs, _ = o_ref.shape
    half = total.shape[0] * 4
    copies = [pltpu.make_async_copy(o_ref.at[i], o_hbm.at[i], sems.at[i]) for i in range(rows)]
    for i in range(rows):
        for k in range(slots):
            l = lax.rem(cols_ref[i, k], half)
            tile = total[l // 4, (l // 2) % 2, i * bs : (i + 1) * bs, :]
            tile = jnp.where(l % 2 == 0, tile, pltpu.roll(tile, bs, 1))
            o_ref[i, k] = tile[:, :bs].astype(o_ref.dtype)
        copies[i].start()
    for copy in copies:
        copy.wait()


def product(kernel, source, a, total, part, out, cols=None):
    hbm, vmem = pl.BlockSpec(memory_space=pl.ANY), pl.BlockSpec(memory_space=VMEM)
    scratch = [
        VMEM((FOOT, part.shape[1]), jnp.int32),
        SMEM((FOOT, part.shape[1]), jnp.int32),
        pltpu.SemaphoreType.DMA,
    ]
    arrays, specs = [a], [vmem]
    if total is not None:
        arrays, specs = arrays + [total], specs + [vmem]
    if cols is not None:
        arrays, specs = arrays + [cols], specs + [hbm]
        scratch += [
            SMEM(cols.shape, cols.dtype),
            VMEM(out.shape, out.dtype),
            pltpu.SemaphoreType.DMA,
            pltpu.SemaphoreType.DMA(out.shape[:1]),
        ]
    return pl.pallas_call(
        functools.partial(kernel, source),
        out_shape=out,
        in_specs=specs + [vmem],
        out_specs=vmem if cols is None else hbm,
        scratch_shapes=scratch,
        input_output_aliases={1: 0} if total is not None and cols is None else {},
        compiler_params=params(),
        cost_estimate=cost(BUSY * 2 * a.shape[2] * math.prod(out.shape), 0),
    )(*arrays, part)


def local(order, a_vals, b_vals, cols):
    sources = len(order)
    rows, slots, bs, _ = a_vals.shape
    half = sources * rows // 2
    hops = {1: sources // 2, -1: (sources - 1) // 2}

    def ring(way):
        return [
            (order[r] * 2 + c, order[(r + (way if c == 0 else -way)) % sources] * 2 + c)
            for r in range(sources)
            for c in range(2)
        ]

    own = pack(half, cols, b_vals)
    _, *mine = lax.optimization_barrier((own, a_vals, cols))
    swap = [(0, 1), (1, 0)]
    a_other, others = (lax.ppermute(x, "col", swap) for x in mine)
    a = dense_rows(sources, cols, others, a_vals, a_other)
    total_shape = jax.ShapeDtypeStruct((half // 4, 2, rows * bs, 2 * bs), jnp.float32)
    waiting = [(0, 1, own)]
    total = None

    def add():
        step, way, part = waiting.pop(0)
        kernel = first_kernel if total is None else middle_kernel
        return product(kernel, functools.partial(arrived_from, order, way, step), a, total, part, total_shape)

    held = {1: own, -1: own}
    for step in range(1, hops[1] + 1):
        for way in hops:
            if step > hops[way]:
                continue
            part = held[way]
            if step > 1:
                waiting.append((step - 1, way, part))
                if total is None:
                    part, a = lax.optimization_barrier((part, a))
                else:
                    part, total = lax.optimization_barrier((part, total))
            held[way] = lax.ppermute(part, ("row", "col"), ring(way))
            if step > 1:
                total = add()
    waiting += [(step - 1, -1, held[-1])] if hops[-1] < hops[1] else []
    waiting += [(hops[-1], -1, held[-1])] if hops[-1] == hops[1] else []
    while waiting:
        total = add()
    out = jax.ShapeDtypeStruct(a_vals.shape, a_vals.dtype)
    source = functools.partial(arrived_from, order, 1, hops[1])
    return product(last_kernel, source, a, total, held[1], out, cols)


def ring_order(mesh):
    count = mesh.shape["row"]
    coords = [getattr(d, "coords", None) for d in mesh.devices[0, :, 0]]
    loop = [*range(0, count, 2), *range(count - 1 - count % 2, 0, -2)]
    if None not in coords:
        steps = [
            sum(abs(x - y) for x, y in zip(coords[loop[k - 1]], coords[loop[k]]))
            for k in range(count)
        ]
        if max(steps) <= 1:
            return loop
    return list(range(count))


def solution(mesh):
    return jax.shard_map(
        functools.partial(local, ring_order(mesh)),
        mesh=mesh,
        in_specs=(
            P(("groups", "row"), "col", None, None),
            P(("groups", "row"), "col", None, None),
            P(("groups", "row"), "col"),
        ),
        out_specs=P(("groups", "row"), "col", None, None),
        check_vma=False,
    )
```

time: 38.5 us -> 43 us (1.12)
  waiting for transfers between devices: 7.14 us -> 15.8 us
  starting transfers between devices: 17 us -> 12.5 us
  Pallas kernels: 13.4 us -> 14.4 us
  local copies, waits for them, and re-layouts: 0.7 us -> 0.01 us
    ppermute x16 -> x9, waiting for transfers between devices: 7.14 us -> 15.8 us  [the longest x7 15 us: local(): held[way] = lax.ppermute(part, ('row', 'col'), ring(way))]
    ppermute x16 -> x9, starting transfers between devices: 17 us -> 12.5 us  [the longest x7 11.8 us: local(): held[way] = lax.ppermute(part, ('row', 'col'), ring(way))]
    pallas_call x5 -> x9, Pallas kernels: 10.5 us -> 12.6 us  [the longest x8 10.5 us: product(): pl.pallas_call(functools.partial(kernel, source), out_shape=out, in_specs...]
    pallas_call x1, Pallas kernels: 2.92 us -> 1.82 us  [dense_rows(): pl.pallas_call(dense_kernel, out_shape=jax.ShapeDtypeStruct((sources, row...]
    squeeze x1 -> x0, local copies, waits for them, and re-layouts: 0.68 us -> none  [local(): ids = jnp.asarray(names)[lax.axis_index('row'), lax.axis_index('col')]]
  transfers between devices with their start and end apart: 16 -> 9, of which waited for: 5 -> 5; matrix products, arithmetic and copies ran while one was open for 2% -> 0% of each run, Pallas kernels for 28% -> 23%
where the time goes in v5:
time: 43 us; the launch traced here: 42.9 us
  waiting for transfers between devices  15.8 us (37%)
  Pallas kernels  14.4 us (33%)
  starting transfers between devices  12.5 us (29%)
    ppermute x7, waiting for transfers between devices, local(): held[way] = lax.ppermute(part, ('row', 'col'), ring(way))  15 us
    ppermute x7, starting transfers between devices, local(): held[way] = lax.ppermute(part, ('row', 'col'), ring(way))  11.8 us
    pallas_call x8, Pallas kernels, product(): pl.pallas_call(functools.partial(kernel, source), out_shape=out, in_specs...  10.5 us
    pallas_call x1, Pallas kernels, pack(): pl.pallas_call(functools.partial(pack_kernel, half), out_shape=jax.ShapeD...  2.09 us
    pallas_call x1, Pallas kernels, dense_rows(): pl.pallas_call(dense_kernel, out_shape=jax.ShapeDtypeStruct((sources, row...  1.82 us
  transfers between devices with their start and end apart: 9, of which 5 were waited for; matrix products, arithmetic and copies ran while one was open for 0% of the time, Pallas kernels for 23%

profile of v5, /device:TPU:0, one launch (start us, length us, event | category | flops | bytes accessed | tf_op | source)
XLA Modules:
  0.0 42.9 jit_solution(16832342879461376746)
XLA Ops:
  0.0 0.0 copy-start.2
  0.0 0.0 copy-start
  0.0 2.1 %shard_map.37.part = bf16[1296,128]{1,0:T(8,128)(2,1)} custom-call(s32[4,10]{1,0:T(4,128)} %cols_hbm.3, bf16[4,10,64,64]{3,2,1,0:T(8,128)(2,1)} %b_hbm.1), custom_call_target="tpu_custom_call" | custom-call | bytes 655360 | tf_op jit(solution)/shard_map/pallas_call | solution.py:54
  2.1 0.0 copy-start.1
  2.1 3.1 %collective-permute-start = (bf16[1296,128]{1,0:T(8,128)(2,1)}, bf16[1296,128]{1,0:T(8,128)(2,1)S(1)}, u32[]{:S(2)}, u32[]{:S(2)}) collective-permute-start(bf16[1296,128]{1,0:T(8,128)(2,1)} %shard_map.37.part), channel_id=1, source_target_pairs={{0,4},{1,3},{4,8},{5,1},{8,12},{9,5},{12,14},{13,9},{14,10},{15,13... | collective-permute-start | bytes 995336 | tf_op jit(solution)/shard_map/ppermute | solution.py:271
  5.2 0.0 copy-done
  5.2 0.0 collective-permute-start.2
  5.2 1.1 %collective-permute-start.4 = (bf16[1296,128]{1,0:T(8,128)(2,1)}, bf16[1296,128]{1,0:T(8,128)(2,1)S(1)}, u32[]{:S(2)}, u32[]{:S(2)}) collective-permute-start(bf16[1296,128]{1,0:T(8,128)(2,1)} %shard_map.37.part), channel_id=1, source_target_pairs={{0,2},{1,5},{4,0},{5,9},{8,4},{9,13},{12,8},{13,15},{14,12},{15,11... | collective-permute-start | bytes 995336 | tf_op jit(solution)/shard_map/ppermute | solution.py:271
  6.3 0.0 copy-done.2
  6.3 0.7 %collective-permute-start.1 = (s32[4,10]{1,0:T(4,128)S(1)}, s32[4,10]{1,0:T(4,128)S(1)}, u32[]{:S(2)}, u32[]{:S(2)}) collective-permute-start(s32[4,10]{1,0:T(4,128)S(1)} %copy-done.2), channel_id=1, source_target_pairs={{0,1},{1,0},{2,3},{3,2},{4,5},{5,4},{6,7},{7,6},{8,9},{9,8},{10,11... | collective-permute-start | bytes 488 | tf_op jit(solution)/shard_map/ppermute | solution.py:248
  7.0 0.8 %collective-permute-done.1.others_ref = s32[4,10]{1,0:T(4,128)S(1)} collective-permute-done((s32[4,10]{1,0:T(4,128)S(1)}, s32[4,10]{1,0:T(4,128)S(1)}, u32[]{:S(2)}, u32[]{:S(2)}) %collective-permute-start.1) | collective-permute-done | bytes 192 | tf_op jit(solution)/shard_map/ppermute | solution.py:248
  7.8 0.0 collective-permute-done.2.other_ref
  7.8 1.8 %shard_map.38.a_ref = bf16[8,2,256,128]{3,2,1,0:T(8,128)(2,1)S(1)} custom-call(s32[4,10]{1,0:T(4,128)S(1)} %copy-done.2, s32[4,10]{1,0:T(4,128)S(1)} %collective-permute-done.1.others_ref, bf16[4,10,64,64]{3,2,1,0:T(8,128)(2,1)S(1)} %copy-done, bf16[4,10,64,64]{3,2,1,0:T(8,128)(2,1)S(1)} %collective-permute-done.2.other_ref), custom_call_target="tpu_custom_call" | custom-call | bytes 6553600 | tf_op jit(solution)/shard_map/pallas_call | solution.py:100
  9.7 2.9 %collective-permute-done.part = bf16[1296,128]{1,0:T(8,128)(2,1)S(1)} collective-permute-done((bf16[1296,128]{1,0:T(8,128)(2,1)}, bf16[1296,128]{1,0:T(8,128)(2,1)S(1)}, u32[]{:S(2)}, u32[]{:S(2)}) %collective-permute-start) | collective-permute-done | bytes 331808 | tf_op jit(solution)/shard_map/ppermute | solution.py:271
  12.6 2.4 %collective-permute-start.3 = (bf16[1296,128]{1,0:T(8,128)(2,1)S(1)}, bf16[1296,128]{1,0:T(8,128)(2,1)S(1)}, u32[]{:S(2)}, u32[]{:S(2)}) collective-permute-start(bf16[1296,128]{1,0:T(8,128)(2,1)S(1)} %collective-permute-done.part), channel_id=1, source_target_pairs={{0,4},{1,3},{4,8},{5,1},{8,12},{9,5},{12,14},{13,9},{14,10},{15,13... | collective-permute-start | bytes 995336 | tf_op jit(solution)/shard_map/ppermute | solution.py:271
  14.9 0.0 copy-done.1
  14.9 1.1 %shard_map.39.before = f32[4,2,256,128]{3,2,1,0:T(8,128)S(1)} custom-call(bf16[8,2,256,128]{3,2,1,0:T(8,128)(2,1)S(1)} %shard_map.38.a_ref, bf16[1296,128]{1,0:T(8,128)(2,1)S(1)} %copy-done.1), custom_call_target="tpu_custom_call" | custom-call | flops 671088640 | tf_op jit(solution)/shard_map/pallas_call | solution.py:220
  16.1 0.0 collective-permute-done.4.part
  16.1 1.0 %collective-permute-start.6 = (bf16[1296,128]{1,0:T(8,128)(2,1)S(1)}, bf16[1296,128]{1,0:T(8,128)(2,1)S(1)}, u32[]{:S(2)}, u32[]{:S(2)}) collective-permute-start(bf16[1296,128]{1,0:T(8,128)(2,1)S(1)} %collective-permute-done.4.part), channel_id=1, source_target_pairs={{0,2},{1,5},{4,0},{5,9},{8,4},{9,13},{12,8},{13,15},{14,12},{15,11... | collective-permute-start | bytes 995336 | tf_op jit(solution)/shard_map/ppermute | solution.py:271
  17.1 1.1 %shard_map.40.before = f32[4,2,256,128]{3,2,1,0:T(8,128)S(1)} custom-call(bf16[8,2,256,128]{3,2,1,0:T(8,128)(2,1)S(1)} %shard_map.38.a_ref, f32[4,2,256,128]{3,2,1,0:T(8,128)S(1)} %shard_map.39.before, bf16[1296,128]{1,0:T(8,128)(2,1)S(1)} %collective-permute-done.part), custom_call_target="tpu_custom_call", output_to_operand_aliasing={{}: (1, {})} | custom-call | flops 671088640 | tf_op jit(solution)/shard_map/pallas_call | solution.py:220
  18.2 5.7 %collective-permute-done.3.part = bf16[1296,128]{1,0:T(8,128)(2,1)S(1)} collective-permute-done((bf16[1296,128]{1,0:T(8,128)(2,1)S(1)}, bf16[1296,128]{1,0:T(8,128)(2,1)S(1)}, u32[]{:S(2)}, u32[]{:S(2)}) %collective-permute-start.3) | collective-permute-done | bytes 331808 | tf_op jit(solution)/shard_map/ppermute | solution.py:271
  23.9 1.7 %collective-permute-start.5 = (bf16[1296,128]{1,0:T(8,128)(2,1)S(1)}, bf16[1296,128]{1,0:T(8,128)(2,1)S(1)}, u32[]{:S(2)}, u32[]{:S(2)}) collective-permute-start(bf16[1296,128]{1,0:T(8,128)(2,1)S(1)} %collective-permute-done.3.part), channel_id=1, source_target_pairs={{0,4},{1,3},{4,8},{5,1},{8,12},{9,5},{12,14},{13,9},{14,10},{15,13... | collective-permute-start | bytes 995336 | tf_op jit(solution)/shard_map/ppermute | solution.py:271
  25.6 1.1 %shard_map.41.before = f32[4,2,256,128]{3,2,1,0:T(8,128)S(1)} custom-call(bf16[8,2,256,128]{3,2,1,0:T(8,128)(2,1)S(1)} %shard_map.38.a_ref, f32[4,2,256,128]{3,2,1,0:T(8,128)S(1)} %shard_map.40.before, bf16[1296,128]{1,0:T(8,128)(2,1)S(1)} %collective-permute-done.4.part), custom_call_target="tpu_custom_call", output_to_operand_aliasing={{}: (1, {})} | custom-call | flops 671088640 | tf_op jit(solution)/shard_map/pallas_call | solution.py:220
  26.8 0.0 collective-permute-done.6.part
  26.8 0.4 %collective-permute-start.7 = (bf16[1296,128]{1,0:T(8,128)(2,1)S(1)}, bf16[1296,128]{1,0:T(8,128)(2,1)S(1)}, u32[]{:S(2)}, u32[]{:S(2)}) collective-permute-start(bf16[1296,128]{1,0:T(8,128)(2,1)S(1)} %collective-permute-done.6.part), channel_id=1, source_target_pairs={{0,2},{1,5},{4,0},{5,9},{8,4},{9,13},{12,8},{13,15},{14,12},{15,11... | collective-permute-start | bytes 995336 | tf_op jit(solution)/shard_map/ppermute | solution.py:271
  27.2 1.1 %shard_map.42.before = f32[4,2,256,128]{3,2,1,0:T(8,128)S(1)} custom-call(bf16[8,2,256,128]{3,2,1,0:T(8,128)(2,1)S(1)} %shard_map.38.a_ref, f32[4,2,256,128]{3,2,1,0:T(8,128)S(1)} %shard_map.41.before, bf16[1296,128]{1,0:T(8,128)(2,1)S(1)} %collective-permute-done.3.part), custom_call_target="tpu_custom_call", output_to_operand_aliasing={{}: (1, {})} | custom-call | flops 671088640 | tf_op jit(solution)/shard_map/pallas_call | solution.py:220
  28.4 4.9 %collective-permute-done.5.part = bf16[1296,128]{1,0:T(8,128)(2,1)S(1)} collective-permute-done((bf16[1296,128]{1,0:T(8,128)(2,1)S(1)}, bf16[1296,128]{1,0:T(8,128)(2,1)S(1)}, u32[]{:S(2)}, u32[]{:S(2)}) %collective-permute-start.5) | collective-permute-done | bytes 331808 | tf_op jit(solution)/shard_map/ppermute | solution.py:271
  33.2 2.2 %collective-permute-start.8 = (bf16[1296,128]{1,0:T(8,128)(2,1)S(1)}, bf16[1296,128]{1,0:T(8,128)(2,1)S(1)}, u32[]{:S(2)}, u32[]{:S(2)}) collective-permute-start(bf16[1296,128]{1,0:T(8,128)(2,1)S(1)} %collective-permute-done.5.part), channel_id=1, source_target_pairs={{0,4},{1,3},{4,8},{5,1},{8,12},{9,5},{12,14},{13,9},{14,10},{15,13... | collective-permute-start | bytes 995336 | tf_op jit(solution)/shard_map/ppermute | solution.py:271
  35.4 1.1 %shard_map.43.before = f32[4,2,256,128]{3,2,1,0:T(8,128)S(1)} custom-call(bf16[8,2,256,128]{3,2,1,0:T(8,128)(2,1)S(1)} %shard_map.38.a_ref, f32[4,2,256,128]{3,2,1,0:T(8,128)S(1)} %shard_map.42.before, bf16[1296,128]{1,0:T(8,128)(2,1)S(1)} %collective-permute-done.6.part), custom_call_target="tpu_custom_call", output_to_operand_aliasing={{}: (1, {})} | custom-call | flops 671088640 | tf_op jit(solution)/shard_map/pallas_call | solution.py:220
  36.6 1.1 %shard_map.44.before = f32[4,2,256,128]{3,2,1,0:T(8,128)S(1)} custom-call(bf16[8,2,256,128]{3,2,1,0:T(8,128)(2,1)S(1)} %shard_map.38.a_ref, f32[4,2,256,128]{3,2,1,0:T(8,128)S(1)} %shard_map.43.before, bf16[1296,128]{1,0:T(8,128)(2,1)S(1)} %collective-permute-done.5.part), custom_call_target="tpu_custom_call", output_to_operand_aliasing={{}: (1, {})} | custom-call | flops 671088640 | tf_op jit(solution)/shard_map/pallas_call | solution.py:220
  37.7 0.0 collective-permute-done.7.part
  37.7 1.1 %shard_map.45.total = f32[4,2,256,128]{3,2,1,0:T(8,128)S(1)} custom-call(bf16[8,2,256,128]{3,2,1,0:T(8,128)(2,1)S(1)} %shard_map.38.a_ref, f32[4,2,256,128]{3,2,1,0:T(8,128)S(1)} %shard_map.44.before, bf16[1296,128]{1,0:T(8,128)(2,1)S(1)} %collective-permute-done.7.part), custom_call_target="tpu_custom_call", output_to_operand_aliasing={{}: (1, {})} | custom-call | flops 671088640 | tf_op jit(solution)/shard_map/pallas_call | solution.py:220
  38.9 1.5 %collective-permute-done.8.part = bf16[1296,128]{1,0:T(8,128)(2,1)S(1)} collective-permute-done((bf16[1296,128]{1,0:T(8,128)(2,1)S(1)}, bf16[1296,128]{1,0:T(8,128)(2,1)S(1)}, u32[]{:S(2)}, u32[]{:S(2)}) %collective-permute-start.8) | collective-permute-done | bytes 331808 | tf_op jit(solution)/shard_map/ppermute | solution.py:271
  40.4 2.5 %shard_map.46 = bf16[4,10,64,64]{3,2,1,0:T(8,128)(2,1)} custom-call(bf16[8,2,256,128]{3,2,1,0:T(8,128)(2,1)S(1)} %shard_map.38.a_ref, f32[4,2,256,128]{3,2,1,0:T(8,128)S(1)} %shard_map.45.total, s32[4,10]{1,0:T(4,128)S(1)} %copy-done.2, bf16[1296,128]{1,0:T(8,128)(2,1)S(1)} %collective-permute-done.8.part), custom_call_target="tpu_custom_call" | custom-call | flops 419430400 | tf_op jit(solution)/shard_map/pallas_call | solution.py:220
Async XLA Ops:
  0.0 6.3 %copy-start.2 = (s32[4,10]{1,0:T(4,128)S(1)}, s32[4,10]{1,0:T(4,128)}, u32[]{:S(2)}) copy-start(s32[4,10]{1,0:T(4,128)} %cols_hbm.3) | copy-start | bytes 484
  0.0 5.2 %copy-start = (bf16[4,10,64,64]{3,2,1,0:T(8,128)(2,1)S(1)}, bf16[4,10,64,64]{3,2,1,0:T(8,128)(2,1)}, u32[]{:S(2)}) copy-start(bf16[4,10,64,64]{3,2,1,0:T(8,128)(2,1)} %own_ref.1) | copy-start | bytes 983044
  2.1 12.8 %copy-start.1 = (bf16[1296,128]{1,0:T(8,128)(2,1)S(1)}, bf16[1296,128]{1,0:T(8,128)(2,1)}, u32[]{:S(2)}) copy-start(bf16[1296,128]{1,0:T(8,128)(2,1)} %shard_map.37.part) | copy-start | bytes 995332
  2.1 10.4 %collective-permute-start = (bf16[1296,128]{1,0:T(8,128)(2,1)}, bf16[1296,128]{1,0:T(8,128)(2,1)S(1)}, u32[]{:S(2)}, u32[]{:S(2)}) collective-permute-start(bf16[1296,128]{1,0:T(8,128)(2,1)} %shard_map.37.part), channel_id=1, source_target_pairs={{0,4},{1,3},{4,8},{5,1},{8,12},{9,5},{12,14},{13,9},{14,10},{15,13... | collective-permute-start | bytes 995336 | tf_op jit(solution)/shard_map/ppermute | solution.py:271
  5.2 2.6 %collective-permute-start.2 = (bf16[4,10,64,64]{3,2,1,0:T(8,128)(2,1)S(1)}, bf16[4,10,64,64]{3,2,1,0:T(8,128)(2,1)S(1)}, u32[]{:S(2)}, u32[]{:S(2)}) collective-permute-start(bf16[4,10,64,64]{3,2,1,0:T(8,128)(2,1)S(1)} %copy-done), channel_id=1, source_target_pairs={{0,1},{1,0},{2,3},{3,2},{4,5},{5,4},{6,7},{7,6},{8,9},{9,8},{10,11... | collective-permute-start | bytes 983048 | tf_op jit(solution)/shard_map/ppermute | solution.py:248
  5.2 10.9 %collective-permute-start.4 = (bf16[1296,128]{1,0:T(8,128)(2,1)}, bf16[1296,128]{1,0:T(8,128)(2,1)S(1)}, u32[]{:S(2)}, u32[]{:S(2)}) collective-permute-start(bf16[1296,128]{1,0:T(8,128)(2,1)} %shard_map.37.part), channel_id=1, source_target_pairs={{0,2},{1,5},{4,0},{5,9},{8,4},{9,13},{12,8},{13,15},{14,12},{15,11... | collective-permute-start | bytes 995336 | tf_op jit(solution)/shard_map/ppermute | solution.py:271
  6.3 1.6 %collective-permute-start.1 = (s32[4,10]{1,0:T(4,128)S(1)}, s32[4,10]{1,0:T(4,128)S(1)}, u32[]{:S(2)}, u32[]{:S(2)}) collective-permute-start(s32[4,10]{1,0:T(4,128)S(1)} %copy-done.2), channel_id=1, source_target_pairs={{0,1},{1,0},{2,3},{3,2},{4,5},{5,4},{6,7},{7,6},{8,9},{9,8},{10,11... | collective-permute-start | bytes 488 | tf_op jit(solution)/shard_map/ppermute | solution.py:248
  12.6 11.4 %collective-permute-start.3 = (bf16[1296,128]{1,0:T(8,128)(2,1)S(1)}, bf16[1296,128]{1,0:T(8,128)(2,1)S(1)}, u32[]{:S(2)}, u32[]{:S(2)}) collective-permute-start(bf16[1296,128]{1,0:T(8,128)(2,1)S(1)} %collective-permute-done.part), channel_id=1, source_target_pairs={{0,4},{1,3},{4,8},{5,1},{8,12},{9,5},{12,14},{13,9},{14,10},{15,13... | collective-permute-start | bytes 995336 | tf_op jit(solution)/shard_map/ppermute | solution.py:271
  16.1 10.7 %collective-permute-start.6 = (bf16[1296,128]{1,0:T(8,128)(2,1)S(1)}, bf16[1296,128]{1,0:T(8,128)(2,1)S(1)}, u32[]{:S(2)}, u32[]{:S(2)}) collective-permute-start(bf16[1296,128]{1,0:T(8,128)(2,1)S(1)} %collective-permute-done.4.part), channel_id=1, source_target_pairs={{0,2},{1,5},{4,0},{5,9},{8,4},{9,13},{12,8},{13,15},{14,12},{15,11... | collective-permute-start | bytes 995336 | tf_op jit(solution)/shard_map/ppermute | solution.py:271
  23.9 9.3 %collective-permute-start.5 = (bf16[1296,128]{1,0:T(8,128)(2,1)S(1)}, bf16[1296,128]{1,0:T(8,128)(2,1)S(1)}, u32[]{:S(2)}, u32[]{:S(2)}) collective-permute-start(bf16[1296,128]{1,0:T(8,128)(2,1)S(1)} %collective-permute-done.3.part), channel_id=1, source_target_pairs={{0,4},{1,3},{4,8},{5,1},{8,12},{9,5},{12,14},{13,9},{14,10},{15,13... | collective-permute-start | bytes 995336 | tf_op jit(solution)/shard_map/ppermute | solution.py:271
  26.8 10.9 %collective-permute-start.7 = (bf16[1296,128]{1,0:T(8,128)(2,1)S(1)}, bf16[1296,128]{1,0:T(8,128)(2,1)S(1)}, u32[]{:S(2)}, u32[]{:S(2)}) collective-permute-start(bf16[1296,128]{1,0:T(8,128)(2,1)S(1)} %collective-permute-done.6.part), channel_id=1, source_target_pairs={{0,2},{1,5},{4,0},{5,9},{8,4},{9,13},{12,8},{13,15},{14,12},{15,11... | collective-permute-start | bytes 995336 | tf_op jit(solution)/shard_map/ppermute | solution.py:271
  33.2 7.1 %collective-permute-start.8 = (bf16[1296,128]{1,0:T(8,128)(2,1)S(1)}, bf16[1296,128]{1,0:T(8,128)(2,1)S(1)}, u32[]{:S(2)}, u32[]{:S(2)}) collective-permute-start(bf16[1296,128]{1,0:T(8,128)(2,1)S(1)} %collective-permute-done.5.part), channel_id=1, source_target_pairs={{0,4},{1,3},{4,8},{5,1},{8,12},{9,5},{12,14},{13,9},{14,10},{15,13... | collective-permute-start | bytes 995336 | tf_op jit(solution)/shard_map/ppermute | solution.py:271

commit v6 on v5

--- a/solution.py
+++ b/solution.py
@@ -13,7 +13,7 @@
 SMEM = pltpu.SMEM
 LIMIT = 48 * 1024 * 1024
 WHOLE = 63 * 1024 * 1024
-BUSY = 5
+TIE = 3
 FOOT = 16
 
 
@@ -25,7 +25,8 @@
     return pl.CostEstimate(flops=flops, bytes_accessed=size, transcendentals=0)
 
 
-def pack_kernel(half, cols_hbm, b_hbm, o_ref, cols_ref, b_ref, sem, sems):
+def pack_kernel(half, cols_hbm, b_hbm, *refs):
+    *o_refs, cols_ref, b_ref, sem, sems = refs
     rows, slots, bs, _ = b_ref.shape
     copies = [pltpu.make_async_copy(b_hbm.at[r], b_ref.at[r], sems.at[r]) for r in range(rows)]
     fetch = pltpu.make_async_copy(cols_hbm, cols_ref, sem)
@@ -35,27 +36,27 @@
     row = lax.broadcasted_iota(jnp.int32, (FOOT, 2 * bs), 0)
     lane = lax.broadcasted_iota(jnp.int32, (FOOT, 2 * bs), 1)
     fetch.wait()
-    foot = jnp.full((FOOT, 2 * bs), slots, jnp.int32)
-    for r in range(rows):
-        for n in range(slots):
-            here = (row == r) & (lane == lax.rem(cols_ref[r, n], half))
-            foot = jnp.where(here, n, foot)
-    o_ref[rows // 2 * slots * bs :, :] = foot.astype(jnp.float32).astype(o_ref.dtype)
-    for p in range(rows // 2):
+    for p, o_ref in enumerate(o_refs):
+        foot = jnp.full((FOOT, 2 * bs), slots, jnp.int32)
+        for h in range(2):
+            for n in range(slots):
+                here = (row == h) & (lane == lax.rem(cols_ref[2 * p + h, n], half))
+                foot = jnp.where(here, n, foot)
+        o_ref[slots * bs :, :] = foot.astype(jnp.float32).astype(o_ref.dtype)
         copies[2 * p].wait()
         copies[2 * p + 1].wait()
         for n in range(slots):
-            at = (p * slots + n) * bs
-            o_ref[at : at + bs, :] = jnp.concatenate([b_ref[2 * p, n], b_ref[2 * p + 1, n]], axis=-1)
+            o_ref[n * bs : (n + 1) * bs, :] = jnp.concatenate([b_ref[2 * p, n], b_ref[2 * p + 1, n]], axis=-1)
 
 
 def pack(half, cols, b_vals):
     rows, slots, bs, _ = b_vals.shape
+    shapes = [(slots * bs + FOOT, 2 * bs)] * (rows // 2)
     return pl.pallas_call(
         functools.partial(pack_kernel, half),
-        out_shape=jax.ShapeDtypeStruct((rows // 2 * slots * bs + FOOT, 2 * bs), b_vals.dtype),
+        out_shape=[jax.ShapeDtypeStruct(shape, b_vals.dtype) for shape in shapes],
         in_specs=[pl.BlockSpec(memory_space=pl.ANY)] * 2,
-        out_specs=pl.BlockSpec(memory_space=VMEM),
+        out_specs=[pl.BlockSpec(memory_space=VMEM)] * len(shapes),
         scratch_shapes=[
             SMEM(cols.shape, cols.dtype),
             VMEM(b_vals.shape, b_vals.dtype),
@@ -111,7 +112,7 @@
             ],
         ),
         compiler_params=params(),
-        cost_estimate=cost(0, BUSY * 8 * own.size),
+        cost_estimate=cost(0, 8 * own.size),
     )(cols, others, own, other)
 
 
@@ -128,39 +129,39 @@
     return look_up(order, lax.rem(look_up(spots, lax.axis_index("row")) - ahead + len(order), len(order)))
 
 
-def add_products(a, part, total, first, feet, where, sem):
+def add_products(panels, parts, total, first, feet, where, sem):
     groups, bs = total.shape[0], total.shape[3] // 2
-    pairs = a.shape[0]
-    slots = (part.shape[0] - FOOT) // bs // pairs
-    feet[...] = part[pairs * slots * bs :, :].astype(jnp.float32).astype(jnp.int32)
+    slots = (parts[0].shape[0] - FOOT) // bs
+    for k, part in enumerate(parts):
+        feet[k] = part[slots * bs :, :].astype(jnp.float32).astype(jnp.int32)
     copy = pltpu.make_async_copy(feet, where, sem)
     copy.start()
     copy.wait()
     low = lax.broadcasted_iota(jnp.int32, (bs, 2 * bs), 1) < bs
-    panels = jnp.concatenate([a[p] for p in range(pairs)], axis=-1)
-
-    def block(p, slot):
-        at = pl.multiple_of((p * slots + jnp.minimum(slot, slots - 1)) * bs, bs)
+    left_side = jnp.concatenate([panel[...] for panel in panels], axis=-1)
+
+    def block(part, slot):
+        at = pl.multiple_of(jnp.minimum(slot, slots - 1) * bs, bs)
         return jnp.where(slot < slots, part[pl.ds(at, bs), :], jnp.zeros((bs, 2 * bs), part.dtype))
 
     def turn(x):
         return jnp.concatenate([x[:, bs:], x[:, :bs]], axis=-1)
 
     def body(g, carry):
-        panel = []
-        for p in range(pairs):
+        rows = []
+        for k, part in enumerate(parts):
             for h in range(2):
                 tiles = []
                 for q in (2 * g, 2 * g + 1):
-                    left = block(p, where[2 * p + h, 2 * q])
-                    right = block(p, where[2 * p + h, 2 * q + 1])
+                    left = block(part, where[k, h, 2 * q])
+                    right = block(part, where[k, h, 2 * q + 1])
                     if h == 0:
                         right = turn(right)
                     else:
                         left = turn(left)
                     tiles.append(jnp.where(low, left, right))
-                panel.append(jnp.concatenate(tiles, axis=-1))
-        sums = jnp.dot(panels, jnp.concatenate(panel, axis=0), preferred_element_type=jnp.float32)
+                rows.append(jnp.concatenate(tiles, axis=-1))
+        sums = jnp.dot(left_side, jnp.concatenate(rows, axis=0), preferred_element_type=jnp.float32)
         for t in range(2):
             piece = sums[:, t * 2 * bs : (t + 1) * 2 * bs]
             if first:
@@ -172,18 +173,25 @@
     lax.fori_loop(0, groups, body, 0, unroll=min(groups, 4))
 
 
-def first_kernel(source, a_ref, part, total, *scratch):
-    add_products(a_ref.at[source()], part, total, True, *scratch)
-
-
-def middle_kernel(source, a_ref, before, part, total, *scratch):
-    add_products(a_ref.at[source()], part, total, False, *scratch)
-
-
-def last_kernel(source, a_ref, total, cols_hbm, part, o_hbm, feet, where, sem, cols_ref, o_ref, cols_sem, sems):
+def split(a_ref, sources, parts):
+    return [a_ref.at[place, p] for place in [source() for source in sources] for p in range(a_ref.shape[1])], parts
+
+
+def first_kernel(sources, a_ref, *refs):
+    *parts, total, feet, where, sem = refs
+    add_products(*split(a_ref, sources, parts), total, True, feet, where, sem)
+
+
+def middle_kernel(sources, a_ref, before, *refs):
+    *parts, total, feet, where, sem = refs
+    add_products(*split(a_ref, sources, parts), total, False, feet, where, sem)
+
+
+def last_kernel(sources, a_ref, total, cols_hbm, *refs):
+    *parts, o_hbm, feet, where, sem, cols_ref, o_ref, cols_sem, sems = refs
     fetch = pltpu.make_async_copy(cols_hbm, cols_ref, cols_sem)
     fetch.start()
-    add_products(a_ref.at[source()], part, total, False, feet, where, sem)
+    add_products(*split(a_ref, sources, parts), total, False, feet, where, sem)
     fetch.wait()
     rows, slots, bs, _ = o_ref.shape
     half = total.shape[0] * 4
@@ -199,13 +207,13 @@
         copy.wait()
 
 
-def product(kernel, source, a, total, part, out, cols=None):
+def product(order, arrived, a, total, out, cols=None):
     hbm, vmem = pl.BlockSpec(memory_space=pl.ANY), pl.BlockSpec(memory_space=VMEM)
-    scratch = [
-        VMEM((FOOT, part.shape[1]), jnp.int32),
-        SMEM((FOOT, part.shape[1]), jnp.int32),
-        pltpu.SemaphoreType.DMA,
-    ]
+    kernel = first_kernel if total is None else middle_kernel if cols is None else last_kernel
+    sources = [functools.partial(arrived_from, order, way, steps) for way, steps, _ in arrived]
+    parts = [ref for _, _, refs in arrived for ref in refs]
+    feet = (len(arrived) * a.shape[1], FOOT, parts[0].shape[1])
+    scratch = [VMEM(feet, jnp.int32), SMEM(feet, jnp.int32), pltpu.SemaphoreType.DMA]
     arrays, specs = [a], [vmem]
     if total is not None:
         arrays, specs = arrays + [total], specs + [vmem]
@@ -218,15 +226,15 @@
             pltpu.SemaphoreType.DMA(out.shape[:1]),
         ]
     return pl.pallas_call(
-        functools.partial(kernel, source),
+        functools.partial(kernel, sources),
         out_shape=out,
-        in_specs=specs + [vmem],
+        in_specs=specs + [vmem] * len(parts),
         out_specs=vmem if cols is None else hbm,
         scratch_shapes=scratch,
         input_output_aliases={1: 0} if total is not None and cols is None else {},
         compiler_params=params(),
-        cost_estimate=cost(BUSY * 2 * a.shape[2] * math.prod(out.shape), 0),
-    )(*arrays, part)
+        cost_estimate=cost(2 * len(arrived) * a.shape[2] * math.prod(out.shape), 0),
+    )(*arrays, *parts)
 
 
 def local(order, a_vals, b_vals, cols):
@@ -242,42 +250,33 @@
             for c in range(2)
         ]
 
-    own = pack(half, cols, b_vals)
-    _, *mine = lax.optimization_barrier((own, a_vals, cols))
+    parts = pack(half, cols, b_vals)
+    _, *mine = lax.optimization_barrier((parts[0], a_vals, cols))
     swap = [(0, 1), (1, 0)]
     a_other, others = (lax.ppermute(x, "col", swap) for x in mine)
     a = dense_rows(sources, cols, others, a_vals, a_other)
     total_shape = jax.ShapeDtypeStruct((half // 4, 2, rows * bs, 2 * bs), jnp.float32)
-    waiting = [(0, 1, own)]
     total = None
-
-    def add():
-        step, way, part = waiting.pop(0)
-        kernel = first_kernel if total is None else middle_kernel
-        return product(kernel, functools.partial(arrived_from, order, way, step), a, total, part, total_shape)
-
-    held = {1: own, -1: own}
+    held = {way: parts for way in hops}
+    arrived = [(1, 0, parts)]
     for step in range(1, hops[1] + 1):
-        for way in hops:
-            if step > hops[way]:
-                continue
-            part = held[way]
-            if step > 1:
-                waiting.append((step - 1, way, part))
-                if total is None:
-                    part, a = lax.optimization_barrier((part, a))
-                else:
-                    part, total = lax.optimization_barrier((part, total))
-            held[way] = lax.ppermute(part, ("row", "col"), ring(way))
-            if step > 1:
-                total = add()
-    waiting += [(step - 1, -1, held[-1])] if hops[-1] < hops[1] else []
-    waiting += [(hops[-1], -1, held[-1])] if hops[-1] == hops[1] else []
-    while waiting:
-        total = add()
+        ways = [way for way in hops if step <= hops[way]]
+        for way in ways:
+            sent = list(held[way])
+            if step == TIE:
+                sent = [lax.optimization_barrier((part, a))[0] for part in sent]
+            elif total is not None and way == 1:
+                sent[0], total = lax.optimization_barrier((sent[0], total))
+            held[way] = [lax.ppermute(part, ("row", "col"), ring(way)) for part in sent]
+        if step == 1:
+            arrived += [(way, 1, held[way]) for way in ways]
+        elif step >= TIE:
+            total = product(order, arrived, a, total, total_shape)
+            arrived = before
+        before = [(way, step, held[way]) for way in ways]
+    total = product(order, arrived[:1], a, total, total_shape)
     out = jax.ShapeDtypeStruct(a_vals.shape, a_vals.dtype)
-    source = functools.partial(arrived_from, order, 1, hops[1])
-    return product(last_kernel, source, a, total, held[1], out, cols)
+    return product(order, arrived[1:] + before, a, total, out, cols)
 
 
 def ring_order(mesh):

time: 43 us -> 37.9 us (0.88)
  waiting for transfers between devices: 15.8 us -> 5.95 us
  starting transfers between devices: 12.5 us -> 19.3 us
  Pallas kernels: 14.4 us -> 12.4 us
    ppermute x7 -> x14, waiting for transfers between devices: 15 us -> 4.81 us  [local(): held[way] = [lax.ppermute(part, ('row', 'col'), ring(way)) for part in sent]]
    ppermute x7 -> x14, starting transfers between devices: 11.8 us -> 18.8 us  [local(): held[way] = [lax.ppermute(part, ('row', 'col'), ring(way)) for part in sent]]
    pallas_call x9 -> x5, Pallas kernels: 12.6 us -> 10.6 us  [the longest x4 8.54 us: product(): pl.pallas_call(functools.partial(kernel, sources), out_shape=out, in_spec...]
  transfers between devices with their start and end apart: 9 -> 16, of which waited for: 5 -> 4; matrix products, arithmetic and copies ran while one was open for 0% -> 0% of each run, Pallas kernels for 23% -> 19%
where the time goes in v6:
time: 37.9 us; the launch traced here: 37.8 us
  starting transfers between devices  19.3 us (51%)
  Pallas kernels  12.4 us (33%)
  waiting for transfers between devices  5.95 us (16%)
    ppermute x14, starting transfers between devices, local(): held[way] = [lax.ppermute(part, ('row', 'col'), ring(way)) for part in sent]  18.8 us
    pallas_call x4, Pallas kernels, product(): pl.pallas_call(functools.partial(kernel, sources), out_shape=out, in_spec...  8.54 us
    ppermute x14, waiting for transfers between devices, local(): held[way] = [lax.ppermute(part, ('row', 'col'), ring(way)) for part in sent]  4.81 us
    pallas_call x1, Pallas kernels, pack(): pl.pallas_call(functools.partial(pack_kernel, half), out_shape=[jax.Shape...  2.03 us
    pallas_call x1, Pallas kernels, dense_rows(): pl.pallas_call(dense_kernel, out_shape=jax.ShapeDtypeStruct((sources, row...  1.82 us
    ppermute x2, waiting for transfers between devices, local(): a_other, others = (lax.ppermute(x, 'col', swap) for x in mine)  1.14 us
  transfers between devices with their start and end apart: 16, of which 4 were waited for; matrix products, arithmetic and copies ran while one was open for 0% of the time, Pallas kernels for 19%

profile of v6, /device:TPU:0, one launch (start us, length us, event | category | flops | bytes accessed | tf_op | source)
XLA Modules:
  0.0 37.8 jit_solution(6356641712530546810)
XLA Ops:
  0.0 0.0 copy-start
  0.0 2.0 %shard_map.37 = (bf16[656,128]{1,0:T(8,128)(2,1)}, bf16[656,128]{1,0:T(8,128)(2,1)}) custom-call(s32[4,10]{1,0:T(4,128)} %cols_hbm.3, bf16[4,10,64,64]{3,2,1,0:T(8,128)(2,1)} %b_hbm.1), custom_call_target="tpu_custom_call" | custom-call | bytes 655360 | tf_op jit(solution)/shard_map/pallas_call | solution.py:55
  2.0 0.0 copy-start.3
  2.1 3.1 %collective-permute-start.2 = (bf16[656,128]{1,0:T(8,128)(2,1)}, bf16[656,128]{1,0:T(8,128)(2,1)S(1)}, u32[]{:S(2)}, u32[]{:S(2)}) collective-permute-start(bf16[656,128]{1,0:T(8,128)(2,1)} %get-tuple-element.15.refs_0_), channel_id=1, source_target_pairs={{0,4},{1,3},{4,8},{5,1},{8,12},{9,5},{12,14},{13,9},{14,10},{15,13... | collective-permute-start | bytes 503816 | tf_op jit(solution)/shard_map/ppermute | solution.py:270
  5.1 0.0 copy-start.1
  5.1 0.0 copy-start.2
  5.1 1.6 %collective-permute-start.5 = (bf16[656,128]{1,0:T(8,128)(2,1)}, bf16[656,128]{1,0:T(8,128)(2,1)S(1)}, u32[]{:S(2)}, u32[]{:S(2)}) collective-permute-start(bf16[656,128]{1,0:T(8,128)(2,1)} %get-tuple-element.19.refs_1_), channel_id=1, source_target_pairs={{0,4},{1,3},{4,8},{5,1},{8,12},{9,5},{12,14},{13,9},{14,10},{15,13... | collective-permute-start | bytes 503816 | tf_op jit(solution)/shard_map/ppermute | solution.py:270
  6.7 0.0 copy-done
  6.7 0.0 collective-permute-start.1
  6.7 0.0 copy-done.3
  6.7 0.5 %collective-permute-start = (s32[4,10]{1,0:T(4,128)S(1)}, s32[4,10]{1,0:T(4,128)S(1)}, u32[]{:S(2)}, u32[]{:S(2)}) collective-permute-start(s32[4,10]{1,0:T(4,128)S(1)} %copy-done.3), channel_id=1, source_target_pairs={{0,1},{1,0},{2,3},{3,2},{4,5},{5,4},{6,7},{7,6},{8,9},{9,8},{10,11... | collective-permute-start | bytes 488 | tf_op jit(solution)/shard_map/ppermute | solution.py:256
  7.2 0.4 %collective-permute-start.7 = (bf16[656,128]{1,0:T(8,128)(2,1)}, bf16[656,128]{1,0:T(8,128)(2,1)S(1)}, u32[]{:S(2)}, u32[]{:S(2)}) collective-permute-start(bf16[656,128]{1,0:T(8,128)(2,1)} %get-tuple-element.19.refs_1_), channel_id=1, source_target_pairs={{0,2},{1,5},{4,0},{5,9},{8,4},{9,13},{12,8},{13,15},{14,12},{15,11... | collective-permute-start | bytes 503816 | tf_op jit(solution)/shard_map/ppermute | solution.py:270
  7.7 1.1 %collective-permute-done.others_ref = s32[4,10]{1,0:T(4,128)S(1)} collective-permute-done((s32[4,10]{1,0:T(4,128)S(1)}, s32[4,10]{1,0:T(4,128)S(1)}, u32[]{:S(2)}, u32[]{:S(2)}) %collective-permute-start) | collective-permute-done | bytes 192 | tf_op jit(solution)/shard_map/ppermute | solution.py:256
  8.8 0.4 %collective-permute-start.6 = (bf16[656,128]{1,0:T(8,128)(2,1)}, bf16[656,128]{1,0:T(8,128)(2,1)S(1)}, u32[]{:S(2)}, u32[]{:S(2)}) collective-permute-start(bf16[656,128]{1,0:T(8,128)(2,1)} %get-tuple-element.15.refs_0_), channel_id=1, source_target_pairs={{0,2},{1,5},{4,0},{5,9},{8,4},{9,13},{12,8},{13,15},{14,12},{15,11... | collective-permute-start | bytes 503816 | tf_op jit(solution)/shard_map/ppermute | solution.py:270
  9.3 0.0 collective-permute-done.2.refs_2_
  9.3 1.6 %collective-permute-start.3 = (bf16[656,128]{1,0:T(8,128)(2,1)S(1)}, bf16[656,128]{1,0:T(8,128)(2,1)S(1)}, u32[]{:S(2)}, u32[]{:S(2)}) collective-permute-start(bf16[656,128]{1,0:T(8,128)(2,1)S(1)} %collective-permute-done.2.refs_2_), channel_id=1, source_target_pairs={{0,4},{1,3},{4,8},{5,1},{8,12},{9,5},{12,14},{13,9},{14,10},{15,13... | collective-permute-start | bytes 503816 | tf_op jit(solution)/shard_map/ppermute | solution.py:270
  10.8 0.4 %collective-permute-done.5.refs_3_ = bf16[656,128]{1,0:T(8,128)(2,1)S(1)} collective-permute-done((bf16[656,128]{1,0:T(8,128)(2,1)}, bf16[656,128]{1,0:T(8,128)(2,1)S(1)}, u32[]{:S(2)}, u32[]{:S(2)}) %collective-permute-start.5) | collective-permute-done | bytes 167968 | tf_op jit(solution)/shard_map/ppermute | solution.py:270
  11.3 2.0 %collective-permute-start.8 = (bf16[656,128]{1,0:T(8,128)(2,1)S(1)}, bf16[656,128]{1,0:T(8,128)(2,1)S(1)}, u32[]{:S(2)}, u32[]{:S(2)}) collective-permute-start(bf16[656,128]{1,0:T(8,128)(2,1)S(1)} %collective-permute-done.5.refs_3_), channel_id=1, source_target_pairs={{0,4},{1,3},{4,8},{5,1},{8,12},{9,5},{12,14},{13,9},{14,10},{15,13... | collective-permute-start | bytes 503816 | tf_op jit(solution)/shard_map/ppermute | solution.py:270
  13.3 0.0 collective-permute-done.7.refs_5_
  13.3 0.7 %collective-permute-start.10 = (bf16[656,128]{1,0:T(8,128)(2,1)S(1)}, bf16[656,128]{1,0:T(8,128)(2,1)S(1)}, u32[]{:S(2)}, u32[]{:S(2)}) collective-permute-start(bf16[656,128]{1,0:T(8,128)(2,1)S(1)} %collective-permute-done.7.refs_5_), channel_id=1, source_target_pairs={{0,2},{1,5},{4,0},{5,9},{8,4},{9,13},{12,8},{13,15},{14,12},{15,11... | collective-permute-start | bytes 503816 | tf_op jit(solution)/shard_map/ppermute | solution.py:270
  14.0 2.3 %collective-permute-done.6.refs_4_ = bf16[656,128]{1,0:T(8,128)(2,1)S(1)} collective-permute-done((bf16[656,128]{1,0:T(8,128)(2,1)}, bf16[656,128]{1,0:T(8,128)(2,1)S(1)}, u32[]{:S(2)}, u32[]{:S(2)}) %collective-permute-start.6) | collective-permute-done | bytes 167968 | tf_op jit(solution)/shard_map/ppermute | solution.py:270
  16.3 0.4 %collective-permute-start.9 = (bf16[656,128]{1,0:T(8,128)(2,1)S(1)}, bf16[656,128]{1,0:T(8,128)(2,1)S(1)}, u32[]{:S(2)}, u32[]{:S(2)}) collective-permute-start(bf16[656,128]{1,0:T(8,128)(2,1)S(1)} %collective-permute-done.6.refs_4_), channel_id=1, source_target_pairs={{0,2},{1,5},{4,0},{5,9},{8,4},{9,13},{12,8},{13,15},{14,12},{15,11... | collective-permute-start | bytes 503816 | tf_op jit(solution)/shard_map/ppermute | solution.py:270
  16.7 0.0 collective-permute-done.1.other_ref
  16.7 1.8 %shard_map.38.a_ref = bf16[8,2,256,128]{3,2,1,0:T(8,128)(2,1)S(1)} custom-call(s32[4,10]{1,0:T(4,128)S(1)} %copy-done.3, s32[4,10]{1,0:T(4,128)S(1)} %collective-permute-done.others_ref, bf16[4,10,64,64]{3,2,1,0:T(8,128)(2,1)S(1)} %copy-done, bf16[4,10,64,64]{3,2,1,0:T(8,128)(2,1)S(1)} %collective-permute-done.1.other_ref), custom_call_target="tpu_custom_call" | custom-call | bytes 1310720 | tf_op jit(solution)/shard_map/pallas_call | solution.py:101
  18.6 0.0 collective-permute-done.3.refs_0_
  18.6 1.6 %collective-permute-start.4 = (bf16[656,128]{1,0:T(8,128)(2,1)S(1)}, bf16[656,128]{1,0:T(8,128)(2,1)S(1)}, u32[]{:S(2)}, u32[]{:S(2)}) collective-permute-start(bf16[656,128]{1,0:T(8,128)(2,1)S(1)} %collective-permute-done.3.refs_0_), channel_id=1, source_target_pairs={{0,4},{1,3},{4,8},{5,1},{8,12},{9,5},{12,14},{13,9},{14,10},{15,13... | collective-permute-start | bytes 503816 | tf_op jit(solution)/shard_map/ppermute | solution.py:270
  20.2 0.0 collective-permute-done.8.refs_1_
  20.2 2.3 %collective-permute-start.11 = (bf16[656,128]{1,0:T(8,128)(2,1)S(1)}, bf16[656,128]{1,0:T(8,128)(2,1)S(1)}, u32[]{:S(2)}, u32[]{:S(2)}) collective-permute-start(bf16[656,128]{1,0:T(8,128)(2,1)S(1)} %collective-permute-done.8.refs_1_), channel_id=1, source_target_pairs={{0,4},{1,3},{4,8},{5,1},{8,12},{9,5},{12,14},{13,9},{14,10},{15,13... | collective-permute-start | bytes 503816 | tf_op jit(solution)/shard_map/ppermute | solution.py:270
  22.5 0.0 copy-done.1
  22.5 0.0 copy-done.2
  22.5 2.3 %shard_map.39.before = f32[4,2,256,128]{3,2,1,0:T(8,128)S(1)} custom-call(bf16[8,2,256,128]{3,2,1,0:T(8,128)(2,1)S(1)} %shard_map.38.a_ref, bf16[656,128]{1,0:T(8,128)(2,1)S(1)} %copy-done.1, bf16[656,128]{1,0:T(8,128)(2,1)S(1)} %copy-done.2, bf16[656,128]{1,0:T(8,128)(2,1)S(1)} %collective-permute-done.2.refs_2_, ...), custom_call_target="tpu_custom_call" | custom-call | flops 402653184 | tf_op jit(solution)/shard_map/pallas_call | solution.py:228
  24.8 0.0 collective-permute-done.10.refs_3_
  24.9 0.0 collective-permute-done.9.refs_2_
  24.9 0.1 collective-permute-start.12
  24.9 1.1 %collective-permute-start.13 = (bf16[656,128]{1,0:T(8,128)(2,1)S(1)}, bf16[656,128]{1,0:T(8,128)(2,1)S(1)}, u32[]{:S(2)}, u32[]{:S(2)}) collective-permute-start(bf16[656,128]{1,0:T(8,128)(2,1)S(1)} %collective-permute-done.10.refs_3_), channel_id=1, source_target_pairs={{0,2},{1,5},{4,0},{5,9},{8,4},{9,13},{12,8},{13,15},{14,12},{15,11... | collective-permute-start | bytes 503816 | tf_op jit(solution)/shard_map/ppermute | solution.py:270
  26.1 0.0 collective-permute-done.4.refs_0_
  26.1 1.0 %collective-permute-start.14 = (bf16[656,128]{1,0:T(8,128)(2,1)S(1)}, bf16[656,128]{1,0:T(8,128)(2,1)S(1)}, u32[]{:S(2)}, u32[]{:S(2)}) collective-permute-start(bf16[656,128]{1,0:T(8,128)(2,1)S(1)} %collective-permute-done.4.refs_0_), channel_id=1, source_target_pairs={{0,4},{1,3},{4,8},{5,1},{8,12},{9,5},{12,14},{13,9},{14,10},{15,13... | collective-permute-start | bytes 503816 | tf_op jit(solution)/shard_map/ppermute | solution.py:270
  27.1 0.0 collective-permute-done.11.refs_1_
  27.1 2.4 %collective-permute-start.15 = (bf16[656,128]{1,0:T(8,128)(2,1)S(1)}, bf16[656,128]{1,0:T(8,128)(2,1)S(1)}, u32[]{:S(2)}, u32[]{:S(2)}) collective-permute-start(bf16[656,128]{1,0:T(8,128)(2,1)S(1)} %collective-permute-done.11.refs_1_), channel_id=1, source_target_pairs={{0,4},{1,3},{4,8},{5,1},{8,12},{9,5},{12,14},{13,9},{14,10},{15,13... | collective-permute-start | bytes 503816 | tf_op jit(solution)/shard_map/ppermute | solution.py:270
  29.4 1.8 %shard_map.40.before = f32[4,2,256,128]{3,2,1,0:T(8,128)S(1)} custom-call(bf16[8,2,256,128]{3,2,1,0:T(8,128)(2,1)S(1)} %shard_map.38.a_ref, f32[4,2,256,128]{3,2,1,0:T(8,128)S(1)} %shard_map.39.before, bf16[656,128]{1,0:T(8,128)(2,1)S(1)} %collective-permute-done.3.refs_0_, ...), custom_call_target="tpu_custom_call", output_to_operand_aliasing={{}: (1, {})} | custom-call | flops 268435456 | tf_op jit(solution)/shard_map/pallas_call | solution.py:228
  31.2 1.3 %shard_map.41.total = f32[4,2,256,128]{3,2,1,0:T(8,128)S(1)} custom-call(bf16[8,2,256,128]{3,2,1,0:T(8,128)(2,1)S(1)} %shard_map.38.a_ref, f32[4,2,256,128]{3,2,1,0:T(8,128)S(1)} %shard_map.40.before, bf16[656,128]{1,0:T(8,128)(2,1)S(1)} %collective-permute-done.4.refs_0_, ...), custom_call_target="tpu_custom_call", output_to_operand_aliasing={{}: (1, {})} | custom-call | flops 134217728 | tf_op jit(solution)/shard_map/pallas_call | solution.py:228
  32.5 0.0 collective-permute-done.12.refs_0_
  32.5 2.1 %collective-permute-done.13.refs_1_ = bf16[656,128]{1,0:T(8,128)(2,1)S(1)} collective-permute-done((bf16[656,128]{1,0:T(8,128)(2,1)S(1)}, bf16[656,128]{1,0:T(8,128)(2,1)S(1)}, u32[]{:S(2)}, u32[]{:S(2)}) %collective-permute-start.13) | collective-permute-done | bytes 167968 | tf_op jit(solution)/shard_map/ppermute | solution.py:270
  34.6 0.0 collective-permute-done.14.refs_2_
  34.6 0.0 collective-permute-done.15.refs_3_
  34.6 3.2 %shard_map.42 = bf16[4,10,64,64]{3,2,1,0:T(8,128)(2,1)} custom-call(bf16[8,2,256,128]{3,2,1,0:T(8,128)(2,1)S(1)} %shard_map.38.a_ref, f32[4,2,256,128]{3,2,1,0:T(8,128)S(1)} %shard_map.41.total, s32[4,10]{1,0:T(4,128)S(1)} %copy-done.3, bf16[656,128]{1,0:T(8,128)(2,1)S(1)} %collective-permute-done.12.refs_0_, ...), custom_call_target="tpu_custom_call" | custom-call | flops 167772160 | tf_op jit(solution)/shard_map/pallas_call | solution.py:228
Async XLA Ops:
  0.0 6.7 %copy-start = (bf16[4,10,64,64]{3,2,1,0:T(8,128)(2,1)S(1)}, bf16[4,10,64,64]{3,2,1,0:T(8,128)(2,1)}, u32[]{:S(2)}) copy-start(bf16[4,10,64,64]{3,2,1,0:T(8,128)(2,1)} %own_ref.1) | copy-start | bytes 983044
  2.0 4.7 %copy-start.3 = (s32[4,10]{1,0:T(4,128)S(1)}, s32[4,10]{1,0:T(4,128)}, u32[]{:S(2)}) copy-start(s32[4,10]{1,0:T(4,128)} %cols_hbm.3) | copy-start | bytes 484
  2.1 7.2 %collective-permute-start.2 = (bf16[656,128]{1,0:T(8,128)(2,1)}, bf16[656,128]{1,0:T(8,128)(2,1)S(1)}, u32[]{:S(2)}, u32[]{:S(2)}) collective-permute-start(bf16[656,128]{1,0:T(8,128)(2,1)} %get-tuple-element.15.refs_0_), channel_id=1, source_target_pairs={{0,4},{1,3},{4,8},{5,1},{8,12},{9,5},{12,14},{13,9},{14,10},{15,13... | collective-permute-start | bytes 503816 | tf_op jit(solution)/shard_map/ppermute | solution.py:270
  5.1 17.4 %copy-start.1 = (bf16[656,128]{1,0:T(8,128)(2,1)S(1)}, bf16[656,128]{1,0:T(8,128)(2,1)}, u32[]{:S(2)}) copy-start(bf16[656,128]{1,0:T(8,128)(2,1)} %get-tuple-element.15.refs_0_) | copy-start | bytes 503812
  5.1 17.4 %copy-start.2 = (bf16[656,128]{1,0:T(8,128)(2,1)S(1)}, bf16[656,128]{1,0:T(8,128)(2,1)}, u32[]{:S(2)}) copy-start(bf16[656,128]{1,0:T(8,128)(2,1)} %get-tuple-element.19.refs_1_) | copy-start | bytes 503812
  5.1 6.1 %collective-permute-start.5 = (bf16[656,128]{1,0:T(8,128)(2,1)}, bf16[656,128]{1,0:T(8,128)(2,1)S(1)}, u32[]{:S(2)}, u32[]{:S(2)}) collective-permute-start(bf16[656,128]{1,0:T(8,128)(2,1)} %get-tuple-element.19.refs_1_), channel_id=1, source_target_pairs={{0,4},{1,3},{4,8},{5,1},{8,12},{9,5},{12,14},{13,9},{14,10},{15,13... | collective-permute-start | bytes 503816 | tf_op jit(solution)/shard_map/ppermute | solution.py:270
  6.7 10.0 %collective-permute-start.1 = (bf16[4,10,64,64]{3,2,1,0:T(8,128)(2,1)S(1)}, bf16[4,10,64,64]{3,2,1,0:T(8,128)(2,1)S(1)}, u32[]{:S(2)}, u32[]{:S(2)}) collective-permute-start(bf16[4,10,64,64]{3,2,1,0:T(8,128)(2,1)S(1)} %copy-done), channel_id=1, source_target_pairs={{0,1},{1,0},{2,3},{3,2},{4,5},{5,4},{6,7},{7,6},{8,9},{9,8},{10,11... | collective-permute-start | bytes 983048 | tf_op jit(solution)/shard_map/ppermute | solution.py:256
  6.7 2.1 %collective-permute-start = (s32[4,10]{1,0:T(4,128)S(1)}, s32[4,10]{1,0:T(4,128)S(1)}, u32[]{:S(2)}, u32[]{:S(2)}) collective-permute-start(s32[4,10]{1,0:T(4,128)S(1)} %copy-done.3), channel_id=1, source_target_pairs={{0,1},{1,0},{2,3},{3,2},{4,5},{5,4},{6,7},{7,6},{8,9},{9,8},{10,11... | collective-permute-start | bytes 488 | tf_op jit(solution)/shard_map/ppermute | solution.py:256
  7.2 6.0 %collective-permute-start.7 = (bf16[656,128]{1,0:T(8,128)(2,1)}, bf16[656,128]{1,0:T(8,128)(2,1)S(1)}, u32[]{:S(2)}, u32[]{:S(2)}) collective-permute-start(bf16[656,128]{1,0:T(8,128)(2,1)} %get-tuple-element.19.refs_1_), channel_id=1, source_target_pairs={{0,2},{1,5},{4,0},{5,9},{8,4},{9,13},{12,8},{13,15},{14,12},{15,11... | collective-permute-start | bytes 503816 | tf_op jit(solution)/shard_map/ppermute | solution.py:270
  8.8 7.5 %collective-permute-start.6 = (bf16[656,128]{1,0:T(8,128)(2,1)}, bf16[656,128]{1,0:T(8,128)(2,1)S(1)}, u32[]{:S(2)}, u32[]{:S(2)}) collective-permute-start(bf16[656,128]{1,0:T(8,128)(2,1)} %get-tuple-element.15.refs_0_), channel_id=1, source_target_pairs={{0,2},{1,5},{4,0},{5,9},{8,4},{9,13},{12,8},{13,15},{14,12},{15,11... | collective-permute-start | bytes 503816 | tf_op jit(solution)/shard_map/ppermute | solution.py:270
  9.3 9.3 %collective-permute-start.3 = (bf16[656,128]{1,0:T(8,128)(2,1)S(1)}, bf16[656,128]{1,0:T(8,128)(2,1)S(1)}, u32[]{:S(2)}, u32[]{:S(2)}) collective-permute-start(bf16[656,128]{1,0:T(8,128)(2,1)S(1)} %collective-permute-done.2.refs_2_), channel_id=1, source_target_pairs={{0,4},{1,3},{4,8},{5,1},{8,12},{9,5},{12,14},{13,9},{14,10},{15,13... | collective-permute-start | bytes 503816 | tf_op jit(solution)/shard_map/ppermute | solution.py:270
  11.3 8.9 %collective-permute-start.8 = (bf16[656,128]{1,0:T(8,128)(2,1)S(1)}, bf16[656,128]{1,0:T(8,128)(2,1)S(1)}, u32[]{:S(2)}, u32[]{:S(2)}) collective-permute-start(bf16[656,128]{1,0:T(8,128)(2,1)S(1)} %collective-permute-done.5.refs_3_), channel_id=1, source_target_pairs={{0,4},{1,3},{4,8},{5,1},{8,12},{9,5},{12,14},{13,9},{14,10},{15,13... | collective-permute-start | bytes 503816 | tf_op jit(solution)/shard_map/ppermute | solution.py:270
  13.3 11.6 %collective-permute-start.10 = (bf16[656,128]{1,0:T(8,128)(2,1)S(1)}, bf16[656,128]{1,0:T(8,128)(2,1)S(1)}, u32[]{:S(2)}, u32[]{:S(2)}) collective-permute-start(bf16[656,128]{1,0:T(8,128)(2,1)S(1)} %collective-permute-done.7.refs_5_), channel_id=1, source_target_pairs={{0,2},{1,5},{4,0},{5,9},{8,4},{9,13},{12,8},{13,15},{14,12},{15,11... | collective-permute-start | bytes 503816 | tf_op jit(solution)/shard_map/ppermute | solution.py:270
  16.3 8.6 %collective-permute-start.9 = (bf16[656,128]{1,0:T(8,128)(2,1)S(1)}, bf16[656,128]{1,0:T(8,128)(2,1)S(1)}, u32[]{:S(2)}, u32[]{:S(2)}) collective-permute-start(bf16[656,128]{1,0:T(8,128)(2,1)S(1)} %collective-permute-done.6.refs_4_), channel_id=1, source_target_pairs={{0,2},{1,5},{4,0},{5,9},{8,4},{9,13},{12,8},{13,15},{14,12},{15,11... | collective-permute-start | bytes 503816 | tf_op jit(solution)/shard_map/ppermute | solution.py:270
  18.6 7.5 %collective-permute-start.4 = (bf16[656,128]{1,0:T(8,128)(2,1)S(1)}, bf16[656,128]{1,0:T(8,128)(2,1)S(1)}, u32[]{:S(2)}, u32[]{:S(2)}) collective-permute-start(bf16[656,128]{1,0:T(8,128)(2,1)S(1)} %collective-permute-done.3.refs_0_), channel_id=1, source_target_pairs={{0,4},{1,3},{4,8},{5,1},{8,12},{9,5},{12,14},{13,9},{14,10},{15,13... | collective-permute-start | bytes 503816 | tf_op jit(solution)/shard_map/ppermute | solution.py:270
  20.2 6.9 %collective-permute-start.11 = (bf16[656,128]{1,0:T(8,128)(2,1)S(1)}, bf16[656,128]{1,0:T(8,128)(2,1)S(1)}, u32[]{:S(2)}, u32[]{:S(2)}) collective-permute-start(bf16[656,128]{1,0:T(8,128)(2,1)S(1)} %collective-permute-done.8.refs_1_), channel_id=1, source_target_pairs={{0,4},{1,3},{4,8},{5,1},{8,12},{9,5},{12,14},{13,9},{14,10},{15,13... | collective-permute-start | bytes 503816 | tf_op jit(solution)/shard_map/ppermute | solution.py:270
  24.9 7.6 %collective-permute-start.12 = (bf16[656,128]{1,0:T(8,128)(2,1)S(1)}, bf16[656,128]{1,0:T(8,128)(2,1)S(1)}, u32[]{:S(2)}, u32[]{:S(2)}) collective-permute-start(bf16[656,128]{1,0:T(8,128)(2,1)S(1)} %collective-permute-done.9.refs_2_), channel_id=1, source_target_pairs={{0,2},{1,5},{4,0},{5,9},{8,4},{9,13},{12,8},{13,15},{14,12},{15,11... | collective-permute-start | bytes 503816 | tf_op jit(solution)/shard_map/ppermute | solution.py:270
  24.9 9.6 %collective-permute-start.13 = (bf16[656,128]{1,0:T(8,128)(2,1)S(1)}, bf16[656,128]{1,0:T(8,128)(2,1)S(1)}, u32[]{:S(2)}, u32[]{:S(2)}) collective-permute-start(bf16[656,128]{1,0:T(8,128)(2,1)S(1)} %collective-permute-done.10.refs_3_), channel_id=1, source_target_pairs={{0,2},{1,5},{4,0},{5,9},{8,4},{9,13},{12,8},{13,15},{14,12},{15,11... | collective-permute-start | bytes 503816 | tf_op jit(solution)/shard_map/ppermute | solution.py:270
  26.1 8.5 %collective-permute-start.14 = (bf16[656,128]{1,0:T(8,128)(2,1)S(1)}, bf16[656,128]{1,0:T(8,128)(2,1)S(1)}, u32[]{:S(2)}, u32[]{:S(2)}) collective-permute-start(bf16[656,128]{1,0:T(8,128)(2,1)S(1)} %collective-permute-done.4.refs_0_), channel_id=1, source_target_pairs={{0,4},{1,3},{4,8},{5,1},{8,12},{9,5},{12,14},{13,9},{14,10},{15,13... | collective-permute-start | bytes 503816 | tf_op jit(solution)/shard_map/ppermute | solution.py:270
  27.1 7.5 %collective-permute-start.15 = (bf16[656,128]{1,0:T(8,128)(2,1)S(1)}, bf16[656,128]{1,0:T(8,128)(2,1)S(1)}, u32[]{:S(2)}, u32[]{:S(2)}) collective-permute-start(bf16[656,128]{1,0:T(8,128)(2,1)S(1)} %collective-permute-done.11.refs_1_), channel_id=1, source_target_pairs={{0,4},{1,3},{4,8},{5,1},{8,12},{9,5},{12,14},{13,9},{14,10},{15,13... | collective-permute-start | bytes 503816 | tf_op jit(solution)/shard_map/ppermute | solution.py:270

commit v7 on v6

--- a/solution.py
+++ b/solution.py
@@ -13,7 +13,6 @@
 SMEM = pltpu.SMEM
 LIMIT = 48 * 1024 * 1024
 WHOLE = 63 * 1024 * 1024
-TIE = 3
 FOOT = 16
 
 
@@ -144,9 +143,6 @@
         at = pl.multiple_of(jnp.minimum(slot, slots - 1) * bs, bs)
         return jnp.where(slot < slots, part[pl.ds(at, bs), :], jnp.zeros((bs, 2 * bs), part.dtype))
 
-    def turn(x):
-        return jnp.concatenate([x[:, bs:], x[:, :bs]], axis=-1)
-
     def body(g, carry):
         rows = []
         for k, part in enumerate(parts):
@@ -156,9 +152,9 @@
                     left = block(part, where[k, h, 2 * q])
                     right = block(part, where[k, h, 2 * q + 1])
                     if h == 0:
-                        right = turn(right)
+                        right = pltpu.roll(right, bs, 1)
                     else:
-                        left = turn(left)
+                        left = pltpu.roll(left, bs, 1)
                     tiles.append(jnp.where(low, left, right))
                 rows.append(jnp.concatenate(tiles, axis=-1))
         sums = jnp.dot(left_side, jnp.concatenate(rows, axis=0), preferred_element_type=jnp.float32)
@@ -199,9 +195,9 @@
     for i in range(rows):
         for k in range(slots):
             l = lax.rem(cols_ref[i, k], half)
-            tile = total[l // 4, (l // 2) % 2, i * bs : (i + 1) * bs, :]
+            tile = total[l // 4, (l // 2) % 2, i * bs : (i + 1) * bs, :].astype(o_ref.dtype)
             tile = jnp.where(l % 2 == 0, tile, pltpu.roll(tile, bs, 1))
-            o_ref[i, k] = tile[:, :bs].astype(o_ref.dtype)
+            o_ref[i, k] = tile[:, :bs]
         copies[i].start()
     for copy in copies:
         copy.wait()
@@ -258,25 +254,27 @@
     total_shape = jax.ShapeDtypeStruct((half // 4, 2, rows * bs, 2 * bs), jnp.float32)
     total = None
     held = {way: parts for way in hops}
-    arrived = [(1, 0, parts)]
+    rounds = [[(1, 0, parts)]]
     for step in range(1, hops[1] + 1):
         ways = [way for way in hops if step <= hops[way]]
         for way in ways:
             sent = list(held[way])
-            if step == TIE:
+            if (step, way) == (2, -1):
                 sent = [lax.optimization_barrier((part, a))[0] for part in sent]
-            elif total is not None and way == 1:
+            elif (step, way) == (3, 1):
+                total = product(order, rounds.pop(0), a, total, total_shape)
                 sent[0], total = lax.optimization_barrier((sent[0], total))
+            elif step > 2 and way == -1:
+                total = product(order, rounds.pop(0), a, total, total_shape)
+                for k, part in enumerate(sent):
+                    sent[k], total = lax.optimization_barrier((part, total))
             held[way] = [lax.ppermute(part, ("row", "col"), ring(way)) for part in sent]
-        if step == 1:
-            arrived += [(way, 1, held[way]) for way in ways]
-        elif step >= TIE:
-            total = product(order, arrived, a, total, total_shape)
-            arrived = before
-        before = [(way, step, held[way]) for way in ways]
-    total = product(order, arrived[:1], a, total, total_shape)
+        rounds.append([(way, step, held[way]) for way in ways])
+    *_, late, last = rounds
+    for some in [*rounds[:-2], late[:1]]:
+        total = product(order, some, a, total, total_shape)
     out = jax.ShapeDtypeStruct(a_vals.shape, a_vals.dtype)
-    return product(order, arrived[1:] + before, a, total, out, cols)
+    return product(order, late[1:] + last, a, total, out, cols)
 
 
 def ring_order(mesh):

time: 37.9 us -> 39.8 us (1.050); the launches traced: 37.8 us -> 39.3 us
  waiting for transfers between devices: 5.95 us -> 7.06 us
  Pallas kernels: 12.4 us -> 13.1 us
  starting transfers between devices: 19.3 us -> 18.9 us
    ppermute x14, waiting for transfers between devices: 4.81 us -> 5.91 us  [local(): held[way] = [lax.ppermute(part, ('row', 'col'), ring(way)) for part in sent]]
    pallas_call x4 -> x5, Pallas kernels: 8.54 us -> 9.28 us  [product(): pl.pallas_call(functools.partial(kernel, sources), out_shape=out, in_spec...]
    ppermute x14, starting transfers between devices: 18.8 us -> 18.4 us  [local(): held[way] = [lax.ppermute(part, ('row', 'col'), ring(way)) for part in sent]]
  transfers between devices with their start and end apart: 16 -> 16, of which waited for: 4 -> 5; matrix products, arithmetic and copies ran while one was open for 0% -> 0% of each run, Pallas kernels for 19% -> 20%
where the time goes in v7:
time: 39.8 us; the launch traced here: 39.3 us
  starting transfers between devices  18.9 us (47%)
  Pallas kernels  13.1 us (33%)
  waiting for transfers between devices  7.06 us (18%)
    ppermute x14, starting transfers between devices, local(): held[way] = [lax.ppermute(part, ('row', 'col'), ring(way)) for part in sent]  18.4 us
    pallas_call x5, Pallas kernels, product(): pl.pallas_call(functools.partial(kernel, sources), out_shape=out, in_spec...  9.28 us
    ppermute x14, waiting for transfers between devices, local(): held[way] = [lax.ppermute(part, ('row', 'col'), ring(way)) for part in sent]  5.91 us
    pallas_call x1, Pallas kernels, pack(): pl.pallas_call(functools.partial(pack_kernel, half), out_shape=[jax.Shape...  2.03 us
    pallas_call x1, Pallas kernels, dense_rows(): pl.pallas_call(dense_kernel, out_shape=jax.ShapeDtypeStruct((sources, row...  1.82 us
    ppermute x2, waiting for transfers between devices, local(): a_other, others = (lax.ppermute(x, 'col', swap) for x in mine)  1.16 us
  transfers between devices with their start and end apart: 16, of which 5 were waited for; matrix products, arithmetic and copies ran while one was open for 0% of the time, Pallas kernels for 20%

profile of v7, /device:TPU:0, one launch (start us, length us, event | category | flops | bytes accessed | tf_op | source)
XLA Modules:
  0.0 39.3 jit_solution(12602485667928585142)
XLA Ops:
  0.0 0.0 copy-start
  0.0 2.0 %shard_map.37 = (bf16[656,128]{1,0:T(8,128)(2,1)}, bf16[656,128]{1,0:T(8,128)(2,1)}) custom-call(s32[4,10]{1,0:T(4,128)} %cols_hbm.3, bf16[4,10,64,64]{3,2,1,0:T(8,128)(2,1)} %b_hbm.1), custom_call_target="tpu_custom_call" | custom-call | bytes 655360 | tf_op jit(solution)/shard_map/pallas_call | solution.py:54
  2.0 0.0 copy-start.3
  2.1 0.0 copy-done
  2.1 0.5 %collective-permute-start.1 = (bf16[4,10,64,64]{3,2,1,0:T(8,128)(2,1)S(1)}, bf16[4,10,64,64]{3,2,1,0:T(8,128)(2,1)S(1)}, u32[]{:S(2)}, u32[]{:S(2)}) collective-permute-start(bf16[4,10,64,64]{3,2,1,0:T(8,128)(2,1)S(1)} %copy-done), channel_id=1, source_target_pairs={{0,1},{1,0},{2,3},{3,2},{4,5},{5,4},{6,7},{7,6},{8,9},{9,8},{10,11... | collective-permute-start | bytes 983048 | tf_op jit(solution)/shard_map/ppermute | solution.py:252
  2.6 2.6 %collective-permute-start.6 = (bf16[656,128]{1,0:T(8,128)(2,1)}, bf16[656,128]{1,0:T(8,128)(2,1)S(1)}, u32[]{:S(2)}, u32[]{:S(2)}) collective-permute-start(bf16[656,128]{1,0:T(8,128)(2,1)} %get-tuple-element.17.refs_0_), channel_id=1, source_target_pairs={{0,4},{1,3},{4,8},{5,1},{8,12},{9,5},{12,14},{13,9},{14,10},{15,13... | collective-permute-start | bytes 503816 | tf_op jit(solution)/shard_map/ppermute | solution.py:271
  5.2 0.0 copy-start.1
  5.2 0.0 copy-start.2
  5.2 1.6 %collective-permute-start.8 = (bf16[656,128]{1,0:T(8,128)(2,1)}, bf16[656,128]{1,0:T(8,128)(2,1)S(1)}, u32[]{:S(2)}, u32[]{:S(2)}) collective-permute-start(bf16[656,128]{1,0:T(8,128)(2,1)} %get-tuple-element.20.refs_1_), channel_id=1, source_target_pairs={{0,4},{1,3},{4,8},{5,1},{8,12},{9,5},{12,14},{13,9},{14,10},{15,13... | collective-permute-start | bytes 503816 | tf_op jit(solution)/shard_map/ppermute | solution.py:271
  6.8 0.4 %collective-permute-start.4 = (bf16[656,128]{1,0:T(8,128)(2,1)}, bf16[656,128]{1,0:T(8,128)(2,1)S(1)}, u32[]{:S(2)}, u32[]{:S(2)}) collective-permute-start(bf16[656,128]{1,0:T(8,128)(2,1)} %get-tuple-element.17.refs_0_), channel_id=1, source_target_pairs={{0,2},{1,5},{4,0},{5,9},{8,4},{9,13},{12,8},{13,15},{14,12},{15,11... | collective-permute-start | bytes 503816 | tf_op jit(solution)/shard_map/ppermute | solution.py:271
  7.2 0.0 copy-done.3
  7.3 0.0 collective-permute-start
  7.3 1.2 %collective-permute-done.others_ref = s32[4,10]{1,0:T(4,128)S(1)} collective-permute-done((s32[4,10]{1,0:T(4,128)S(1)}, s32[4,10]{1,0:T(4,128)S(1)}, u32[]{:S(2)}, u32[]{:S(2)}) %collective-permute-start) | collective-permute-done | bytes 192 | tf_op jit(solution)/shard_map/ppermute | solution.py:252
  8.4 0.8 %collective-permute-start.2 = (bf16[656,128]{1,0:T(8,128)(2,1)}, bf16[656,128]{1,0:T(8,128)(2,1)S(1)}, u32[]{:S(2)}, u32[]{:S(2)}) collective-permute-start(bf16[656,128]{1,0:T(8,128)(2,1)} %get-tuple-element.20.refs_1_), channel_id=1, source_target_pairs={{0,2},{1,5},{4,0},{5,9},{8,4},{9,13},{12,8},{13,15},{14,12},{15,11... | collective-permute-start | bytes 503816 | tf_op jit(solution)/shard_map/ppermute | solution.py:271
  9.2 0.1 collective-permute-done.6.refs_0_
  9.3 2.4 %collective-permute-start.7 = (bf16[656,128]{1,0:T(8,128)(2,1)S(1)}, bf16[656,128]{1,0:T(8,128)(2,1)S(1)}, u32[]{:S(2)}, u32[]{:S(2)}) collective-permute-start(bf16[656,128]{1,0:T(8,128)(2,1)S(1)} %collective-permute-done.6.refs_0_), channel_id=1, source_target_pairs={{0,4},{1,3},{4,8},{5,1},{8,12},{9,5},{12,14},{13,9},{14,10},{15,13... | collective-permute-start | bytes 503816 | tf_op jit(solution)/shard_map/ppermute | solution.py:271
  11.7 1.2 %collective-permute-done.8.refs_1_ = bf16[656,128]{1,0:T(8,128)(2,1)S(1)} collective-permute-done((bf16[656,128]{1,0:T(8,128)(2,1)}, bf16[656,128]{1,0:T(8,128)(2,1)S(1)}, u32[]{:S(2)}, u32[]{:S(2)}) %collective-permute-start.8) | collective-permute-done | bytes 167968 | tf_op jit(solution)/shard_map/ppermute | solution.py:271
  12.9 2.4 %collective-permute-start.9 = (bf16[656,128]{1,0:T(8,128)(2,1)S(1)}, bf16[656,128]{1,0:T(8,128)(2,1)S(1)}, u32[]{:S(2)}, u32[]{:S(2)}) collective-permute-start(bf16[656,128]{1,0:T(8,128)(2,1)S(1)} %collective-permute-done.8.refs_1_), channel_id=1, source_target_pairs={{0,4},{1,3},{4,8},{5,1},{8,12},{9,5},{12,14},{13,9},{14,10},{15,13... | collective-permute-start | bytes 503816 | tf_op jit(solution)/shard_map/ppermute | solution.py:271
  15.3 0.0 collective-permute-done.1.other_ref
  15.3 1.8 %shard_map.38.a_ref = bf16[8,2,256,128]{3,2,1,0:T(8,128)(2,1)S(1)} custom-call(s32[4,10]{1,0:T(4,128)S(1)} %copy-done.3, s32[4,10]{1,0:T(4,128)S(1)} %collective-permute-done.others_ref, bf16[4,10,64,64]{3,2,1,0:T(8,128)(2,1)S(1)} %copy-done, bf16[4,10,64,64]{3,2,1,0:T(8,128)(2,1)S(1)} %collective-permute-done.1.other_ref), custom_call_target="tpu_custom_call" | custom-call | bytes 1310720 | tf_op jit(solution)/shard_map/pallas_call | solution.py:100
  17.1 0.0 collective-permute-done.4.refs_2_
  17.2 0.1 collective-permute-start.5
  17.2 0.0 collective-permute-done.2.refs_3_
  17.2 1.0 %collective-permute-start.3 = (bf16[656,128]{1,0:T(8,128)(2,1)S(1)}, bf16[656,128]{1,0:T(8,128)(2,1)S(1)}, u32[]{:S(2)}, u32[]{:S(2)}) collective-permute-start(bf16[656,128]{1,0:T(8,128)(2,1)S(1)} %collective-permute-done.2.refs_3_), channel_id=1, source_target_pairs={{0,2},{1,5},{4,0},{5,9},{8,4},{9,13},{12,8},{13,15},{14,12},{15,11... | collective-permute-start | bytes 503816 | tf_op jit(solution)/shard_map/ppermute | solution.py:271
  18.2 0.0 copy-done.1
  18.2 0.0 copy-done.2
  18.2 1.3 %shard_map.39.before = f32[4,2,256,128]{3,2,1,0:T(8,128)S(1)} custom-call(bf16[8,2,256,128]{3,2,1,0:T(8,128)(2,1)S(1)} %shard_map.38.a_ref, bf16[656,128]{1,0:T(8,128)(2,1)S(1)} %copy-done.1, bf16[656,128]{1,0:T(8,128)(2,1)S(1)} %copy-done.2), custom_call_target="tpu_custom_call" | custom-call | flops 134217728 | tf_op jit(solution)/shard_map/pallas_call | solution.py:224
  19.5 0.0 collective-permute-done.7.refs_0_
  19.5 1.1 %collective-permute-start.10 = (bf16[656,128]{1,0:T(8,128)(2,1)S(1)}, bf16[656,128]{1,0:T(8,128)(2,1)S(1)}, u32[]{:S(2)}, u32[]{:S(2)}) collective-permute-start(bf16[656,128]{1,0:T(8,128)(2,1)S(1)} %collective-permute-done.7.refs_0_), channel_id=1, source_target_pairs={{0,4},{1,3},{4,8},{5,1},{8,12},{9,5},{12,14},{13,9},{14,10},{15,13... | collective-permute-start | bytes 503816 | tf_op jit(solution)/shard_map/ppermute | solution.py:271
  20.7 0.0 collective-permute-done.9.refs_1_
  20.7 2.0 %collective-permute-start.11 = (bf16[656,128]{1,0:T(8,128)(2,1)S(1)}, bf16[656,128]{1,0:T(8,128)(2,1)S(1)}, u32[]{:S(2)}, u32[]{:S(2)}) collective-permute-start(bf16[656,128]{1,0:T(8,128)(2,1)S(1)} %collective-permute-done.9.refs_1_), channel_id=1, source_target_pairs={{0,4},{1,3},{4,8},{5,1},{8,12},{9,5},{12,14},{13,9},{14,10},{15,13... | collective-permute-start | bytes 503816 | tf_op jit(solution)/shard_map/ppermute | solution.py:271
  22.6 1.8 %shard_map.40.before = f32[4,2,256,128]{3,2,1,0:T(8,128)S(1)} custom-call(bf16[8,2,256,128]{3,2,1,0:T(8,128)(2,1)S(1)} %shard_map.38.a_ref, f32[4,2,256,128]{3,2,1,0:T(8,128)S(1)} %shard_map.39.before, bf16[656,128]{1,0:T(8,128)(2,1)S(1)} %collective-permute-done.6.refs_0_, ...), custom_call_target="tpu_custom_call", output_to_operand_aliasing={{}: (1, {})} | custom-call | flops 268435456 | tf_op jit(solution)/shard_map/pallas_call | solution.py:224
  24.4 0.0 collective-permute-done.5.refs_2_
  24.4 3.5 %collective-permute-done.3.refs_3_ = bf16[656,128]{1,0:T(8,128)(2,1)S(1)} collective-permute-done((bf16[656,128]{1,0:T(8,128)(2,1)S(1)}, bf16[656,128]{1,0:T(8,128)(2,1)S(1)}, u32[]{:S(2)}, u32[]{:S(2)}) %collective-permute-start.3) | collective-permute-done | bytes 167968 | tf_op jit(solution)/shard_map/ppermute | solution.py:271
  27.9 0.0 collective-permute-start.13
  27.9 0.0 collective-permute-start.12
  27.9 0.0 collective-permute-done.10.refs_0_
  27.9 2.1 %collective-permute-start.14 = (bf16[656,128]{1,0:T(8,128)(2,1)S(1)}, bf16[656,128]{1,0:T(8,128)(2,1)S(1)}, u32[]{:S(2)}, u32[]{:S(2)}) collective-permute-start(bf16[656,128]{1,0:T(8,128)(2,1)S(1)} %collective-permute-done.10.refs_0_), channel_id=1, source_target_pairs={{0,4},{1,3},{4,8},{5,1},{8,12},{9,5},{12,14},{13,9},{14,10},{15,13... | collective-permute-start | bytes 503816 | tf_op jit(solution)/shard_map/ppermute | solution.py:271
  30.0 0.0 collective-permute-done.11.refs_1_
  30.0 2.0 %collective-permute-start.15 = (bf16[656,128]{1,0:T(8,128)(2,1)S(1)}, bf16[656,128]{1,0:T(8,128)(2,1)S(1)}, u32[]{:S(2)}, u32[]{:S(2)}) collective-permute-start(bf16[656,128]{1,0:T(8,128)(2,1)S(1)} %collective-permute-done.11.refs_1_), channel_id=1, source_target_pairs={{0,4},{1,3},{4,8},{5,1},{8,12},{9,5},{12,14},{13,9},{14,10},{15,13... | collective-permute-start | bytes 503816 | tf_op jit(solution)/shard_map/ppermute | solution.py:271
  32.0 1.8 %shard_map.41.before = f32[4,2,256,128]{3,2,1,0:T(8,128)S(1)} custom-call(bf16[8,2,256,128]{3,2,1,0:T(8,128)(2,1)S(1)} %shard_map.38.a_ref, f32[4,2,256,128]{3,2,1,0:T(8,128)S(1)} %shard_map.40.before, bf16[656,128]{1,0:T(8,128)(2,1)S(1)} %collective-permute-done.7.refs_0_, ...), custom_call_target="tpu_custom_call", output_to_operand_aliasing={{}: (1, {})} | custom-call | flops 268435456 | tf_op jit(solution)/shard_map/pallas_call | solution.py:224
  33.8 1.3 %shard_map.42.total = f32[4,2,256,128]{3,2,1,0:T(8,128)S(1)} custom-call(bf16[8,2,256,128]{3,2,1,0:T(8,128)(2,1)S(1)} %shard_map.38.a_ref, f32[4,2,256,128]{3,2,1,0:T(8,128)S(1)} %shard_map.41.before, bf16[656,128]{1,0:T(8,128)(2,1)S(1)} %collective-permute-done.10.refs_0_, ...), custom_call_target="tpu_custom_call", output_to_operand_aliasing={{}: (1, {})} | custom-call | flops 134217728 | tf_op jit(solution)/shard_map/pallas_call | solution.py:224
  35.1 0.0 collective-permute-done.13.refs_1_
  35.1 1.0 %collective-permute-done.12.refs_0_ = bf16[656,128]{1,0:T(8,128)(2,1)S(1)} collective-permute-done((bf16[656,128]{1,0:T(8,128)(2,1)S(1)}, bf16[656,128]{1,0:T(8,128)(2,1)S(1)}, u32[]{:S(2)}, u32[]{:S(2)}) %collective-permute-start.12) | collective-permute-done | bytes 167968 | tf_op jit(solution)/shard_map/ppermute | solution.py:271
  36.1 0.0 collective-permute-done.14.refs_2_
  36.1 0.0 collective-permute-done.15.refs_3_
  36.1 3.2 %shard_map.43 = bf16[4,10,64,64]{3,2,1,0:T(8,128)(2,1)} custom-call(bf16[8,2,256,128]{3,2,1,0:T(8,128)(2,1)S(1)} %shard_map.38.a_ref, f32[4,2,256,128]{3,2,1,0:T(8,128)S(1)} %shard_map.42.total, s32[4,10]{1,0:T(4,128)S(1)} %copy-done.3, bf16[656,128]{1,0:T(8,128)(2,1)S(1)} %collective-permute-done.12.refs_0_, ...), custom_call_target="tpu_custom_call" | custom-call | flops 167772160 | tf_op jit(solution)/shard_map/pallas_call | solution.py:224
Async XLA Ops:
  0.0 2.1 %copy-start = (bf16[4,10,64,64]{3,2,1,0:T(8,128)(2,1)S(1)}, bf16[4,10,64,64]{3,2,1,0:T(8,128)(2,1)}, u32[]{:S(2)}) copy-start(bf16[4,10,64,64]{3,2,1,0:T(8,128)(2,1)} %own_ref.1) | copy-start | bytes 983044
  2.0 5.2 %copy-start.3 = (s32[4,10]{1,0:T(4,128)S(1)}, s32[4,10]{1,0:T(4,128)}, u32[]{:S(2)}) copy-start(s32[4,10]{1,0:T(4,128)} %cols_hbm.3) | copy-start | bytes 484
  2.1 13.3 %collective-permute-start.1 = (bf16[4,10,64,64]{3,2,1,0:T(8,128)(2,1)S(1)}, bf16[4,10,64,64]{3,2,1,0:T(8,128)(2,1)S(1)}, u32[]{:S(2)}, u32[]{:S(2)}) collective-permute-start(bf16[4,10,64,64]{3,2,1,0:T(8,128)(2,1)S(1)} %copy-done), channel_id=1, source_target_pairs={{0,1},{1,0},{2,3},{3,2},{4,5},{5,4},{6,7},{7,6},{8,9},{9,8},{10,11... | collective-permute-start | bytes 983048 | tf_op jit(solution)/shard_map/ppermute | solution.py:252
  2.6 6.8 %collective-permute-start.6 = (bf16[656,128]{1,0:T(8,128)(2,1)}, bf16[656,128]{1,0:T(8,128)(2,1)S(1)}, u32[]{:S(2)}, u32[]{:S(2)}) collective-permute-start(bf16[656,128]{1,0:T(8,128)(2,1)} %get-tuple-element.17.refs_0_), channel_id=1, source_target_pairs={{0,4},{1,3},{4,8},{5,1},{8,12},{9,5},{12,14},{13,9},{14,10},{15,13... | collective-permute-start | bytes 503816 | tf_op jit(solution)/shard_map/ppermute | solution.py:271
  5.2 13.0 %copy-start.1 = (bf16[656,128]{1,0:T(8,128)(2,1)S(1)}, bf16[656,128]{1,0:T(8,128)(2,1)}, u32[]{:S(2)}) copy-start(bf16[656,128]{1,0:T(8,128)(2,1)} %get-tuple-element.17.refs_0_) | copy-start | bytes 503812
  5.2 13.0 %copy-start.2 = (bf16[656,128]{1,0:T(8,128)(2,1)S(1)}, bf16[656,128]{1,0:T(8,128)(2,1)}, u32[]{:S(2)}) copy-start(bf16[656,128]{1,0:T(8,128)(2,1)} %get-tuple-element.20.refs_1_) | copy-start | bytes 503812
  5.2 7.7 %collective-permute-start.8 = (bf16[656,128]{1,0:T(8,128)(2,1)}, bf16[656,128]{1,0:T(8,128)(2,1)S(1)}, u32[]{:S(2)}, u32[]{:S(2)}) collective-permute-start(bf16[656,128]{1,0:T(8,128)(2,1)} %get-tuple-element.20.refs_1_), channel_id=1, source_target_pairs={{0,4},{1,3},{4,8},{5,1},{8,12},{9,5},{12,14},{13,9},{14,10},{15,13... | collective-permute-start | bytes 503816 | tf_op jit(solution)/shard_map/ppermute | solution.py:271
  6.8 10.4 %collective-permute-start.4 = (bf16[656,128]{1,0:T(8,128)(2,1)}, bf16[656,128]{1,0:T(8,128)(2,1)S(1)}, u32[]{:S(2)}, u32[]{:S(2)}) collective-permute-start(bf16[656,128]{1,0:T(8,128)(2,1)} %get-tuple-element.17.refs_0_), channel_id=1, source_target_pairs={{0,2},{1,5},{4,0},{5,9},{8,4},{9,13},{12,8},{13,15},{14,12},{15,11... | collective-permute-start | bytes 503816 | tf_op jit(solution)/shard_map/ppermute | solution.py:271
  7.3 1.2 %collective-permute-start = (s32[4,10]{1,0:T(4,128)S(1)}, s32[4,10]{1,0:T(4,128)S(1)}, u32[]{:S(2)}, u32[]{:S(2)}) collective-permute-start(s32[4,10]{1,0:T(4,128)S(1)} %copy-done.3), channel_id=1, source_target_pairs={{0,1},{1,0},{2,3},{3,2},{4,5},{5,4},{6,7},{7,6},{8,9},{9,8},{10,11... | collective-permute-start | bytes 488 | tf_op jit(solution)/shard_map/ppermute | solution.py:252
  8.4 8.8 %collective-permute-start.2 = (bf16[656,128]{1,0:T(8,128)(2,1)}, bf16[656,128]{1,0:T(8,128)(2,1)S(1)}, u32[]{:S(2)}, u32[]{:S(2)}) collective-permute-start(bf16[656,128]{1,0:T(8,128)(2,1)} %get-tuple-element.20.refs_1_), channel_id=1, source_target_pairs={{0,2},{1,5},{4,0},{5,9},{8,4},{9,13},{12,8},{13,15},{14,12},{15,11... | collective-permute-start | bytes 503816 | tf_op jit(solution)/shard_map/ppermute | solution.py:271
  9.3 10.2 %collective-permute-start.7 = (bf16[656,128]{1,0:T(8,128)(2,1)S(1)}, bf16[656,128]{1,0:T(8,128)(2,1)S(1)}, u32[]{:S(2)}, u32[]{:S(2)}) collective-permute-start(bf16[656,128]{1,0:T(8,128)(2,1)S(1)} %collective-permute-done.6.refs_0_), channel_id=1, source_target_pairs={{0,4},{1,3},{4,8},{5,1},{8,12},{9,5},{12,14},{13,9},{14,10},{15,13... | collective-permute-start | bytes 503816 | tf_op jit(solution)/shard_map/ppermute | solution.py:271
  12.9 7.7 %collective-permute-start.9 = (bf16[656,128]{1,0:T(8,128)(2,1)S(1)}, bf16[656,128]{1,0:T(8,128)(2,1)S(1)}, u32[]{:S(2)}, u32[]{:S(2)}) collective-permute-start(bf16[656,128]{1,0:T(8,128)(2,1)S(1)} %collective-permute-done.8.refs_1_), channel_id=1, source_target_pairs={{0,4},{1,3},{4,8},{5,1},{8,12},{9,5},{12,14},{13,9},{14,10},{15,13... | collective-permute-start | bytes 503816 | tf_op jit(solution)/shard_map/ppermute | solution.py:271
  17.2 7.2 %collective-permute-start.5 = (bf16[656,128]{1,0:T(8,128)(2,1)S(1)}, bf16[656,128]{1,0:T(8,128)(2,1)S(1)}, u32[]{:S(2)}, u32[]{:S(2)}) collective-permute-start(bf16[656,128]{1,0:T(8,128)(2,1)S(1)} %collective-permute-done.4.refs_2_), channel_id=1, source_target_pairs={{0,2},{1,5},{4,0},{5,9},{8,4},{9,13},{12,8},{13,15},{14,12},{15,11... | collective-permute-start | bytes 503816 | tf_op jit(solution)/shard_map/ppermute | solution.py:271
  17.2 10.7 %collective-permute-start.3 = (bf16[656,128]{1,0:T(8,128)(2,1)S(1)}, bf16[656,128]{1,0:T(8,128)(2,1)S(1)}, u32[]{:S(2)}, u32[]{:S(2)}) collective-permute-start(bf16[656,128]{1,0:T(8,128)(2,1)S(1)} %collective-permute-done.2.refs_3_), channel_id=1, source_target_pairs={{0,2},{1,5},{4,0},{5,9},{8,4},{9,13},{12,8},{13,15},{14,12},{15,11... | collective-permute-start | bytes 503816 | tf_op jit(solution)/shard_map/ppermute | solution.py:271
  19.5 8.4 %collective-permute-start.10 = (bf16[656,128]{1,0:T(8,128)(2,1)S(1)}, bf16[656,128]{1,0:T(8,128)(2,1)S(1)}, u32[]{:S(2)}, u32[]{:S(2)}) collective-permute-start(bf16[656,128]{1,0:T(8,128)(2,1)S(1)} %collective-permute-done.7.refs_0_), channel_id=1, source_target_pairs={{0,4},{1,3},{4,8},{5,1},{8,12},{9,5},{12,14},{13,9},{14,10},{15,13... | collective-permute-start | bytes 503816 | tf_op jit(solution)/shard_map/ppermute | solution.py:271
  20.7 9.3 %collective-permute-start.11 = (bf16[656,128]{1,0:T(8,128)(2,1)S(1)}, bf16[656,128]{1,0:T(8,128)(2,1)S(1)}, u32[]{:S(2)}, u32[]{:S(2)}) collective-permute-start(bf16[656,128]{1,0:T(8,128)(2,1)S(1)} %collective-permute-done.9.refs_1_), channel_id=1, source_target_pairs={{0,4},{1,3},{4,8},{5,1},{8,12},{9,5},{12,14},{13,9},{14,10},{15,13... | collective-permute-start | bytes 503816 | tf_op jit(solution)/shard_map/ppermute | solution.py:271
  27.9 7.1 %collective-permute-start.13 = (bf16[656,128]{1,0:T(8,128)(2,1)S(1)}, bf16[656,128]{1,0:T(8,128)(2,1)S(1)}, u32[]{:S(2)}, u32[]{:S(2)}) collective-permute-start(bf16[656,128]{1,0:T(8,128)(2,1)S(1)} %collective-permute-done.3.refs_3_), channel_id=1, source_target_pairs={{0,2},{1,5},{4,0},{5,9},{8,4},{9,13},{12,8},{13,15},{14,12},{15,11... | collective-permute-start | bytes 503816 | tf_op jit(solution)/shard_map/ppermute | solution.py:271
  27.9 8.2 %collective-permute-start.12 = (bf16[656,128]{1,0:T(8,128)(2,1)S(1)}, bf16[656,128]{1,0:T(8,128)(2,1)S(1)}, u32[]{:S(2)}, u32[]{:S(2)}) collective-permute-start(bf16[656,128]{1,0:T(8,128)(2,1)S(1)} %collective-permute-done.5.refs_2_), channel_id=1, source_target_pairs={{0,2},{1,5},{4,0},{5,9},{8,4},{9,13},{12,8},{13,15},{14,12},{15,11... | collective-permute-start | bytes 503816 | tf_op jit(solution)/shard_map/ppermute | solution.py:271
  27.9 8.2 %collective-permute-start.14 = (bf16[656,128]{1,0:T(8,128)(2,1)S(1)}, bf16[656,128]{1,0:T(8,128)(2,1)S(1)}, u32[]{:S(2)}, u32[]{:S(2)}) collective-permute-start(bf16[656,128]{1,0:T(8,128)(2,1)S(1)} %collective-permute-done.10.refs_0_), channel_id=1, source_target_pairs={{0,4},{1,3},{4,8},{5,1},{8,12},{9,5},{12,14},{13,9},{14,10},{15,13... | collective-permute-start | bytes 503816 | tf_op jit(solution)/shard_map/ppermute | solution.py:271
  30.0 6.1 %collective-permute-start.15 = (bf16[656,128]{1,0:T(8,128)(2,1)S(1)}, bf16[656,128]{1,0:T(8,128)(2,1)S(1)}, u32[]{:S(2)}, u32[]{:S(2)}) collective-permute-start(bf16[656,128]{1,0:T(8,128)(2,1)S(1)} %collective-permute-done.11.refs_1_), channel_id=1, source_target_pairs={{0,4},{1,3},{4,8},{5,1},{8,12},{9,5},{12,14},{13,9},{14,10},{15,13... | collective-permute-start | bytes 503816 | tf_op jit(solution)/shard_map/ppermute | solution.py:271

commit v8 on v7

--- a/solution.py
+++ b/solution.py
@@ -13,6 +13,7 @@
 SMEM = pltpu.SMEM
 LIMIT = 48 * 1024 * 1024
 WHOLE = 63 * 1024 * 1024
+STRIDE = 5
 FOOT = 16
 
 
@@ -25,7 +26,9 @@
 
 
 def pack_kernel(half, cols_hbm, b_hbm, *refs):
-    *o_refs, cols_ref, b_ref, sem, sems = refs
+    pairs = b_hbm.shape[0] // 2
+    o_hbms, refs = refs[:pairs], refs[pairs:]
+    o_refs, (cols_ref, b_ref, sem, sems, o_sems) = refs[:pairs], refs[pairs:]
     rows, slots, bs, _ = b_ref.shape
     copies = [pltpu.make_async_copy(b_hbm.at[r], b_ref.at[r], sems.at[r]) for r in range(rows)]
     fetch = pltpu.make_async_copy(cols_hbm, cols_ref, sem)
@@ -35,32 +38,38 @@
     row = lax.broadcasted_iota(jnp.int32, (FOOT, 2 * bs), 0)
     lane = lax.broadcasted_iota(jnp.int32, (FOOT, 2 * bs), 1)
     fetch.wait()
-    for p, o_ref in enumerate(o_refs):
-        foot = jnp.full((FOOT, 2 * bs), slots, jnp.int32)
-        for h in range(2):
-            for n in range(slots):
-                here = (row == h) & (lane == lax.rem(cols_ref[2 * p + h, n], half))
-                foot = jnp.where(here, n, foot)
-        o_ref[slots * bs :, :] = foot.astype(jnp.float32).astype(o_ref.dtype)
+    foot = jnp.full((FOOT, 2 * bs), slots, jnp.int32)
+    for r in range(rows):
+        for n in range(slots):
+            here = (row == r) & (lane == lax.rem(cols_ref[r, n], half))
+            foot = jnp.where(here, n, foot)
+    o_refs[0][slots * bs :, :] = foot.astype(jnp.float32).astype(b_ref.dtype)
+    writes = [pltpu.make_async_copy(o_refs[p], o_hbms[p], o_sems.at[p]) for p in range(pairs)]
+    for p in range(pairs):
         copies[2 * p].wait()
         copies[2 * p + 1].wait()
         for n in range(slots):
-            o_ref[n * bs : (n + 1) * bs, :] = jnp.concatenate([b_ref[2 * p, n], b_ref[2 * p + 1, n]], axis=-1)
+            o_refs[p][n * bs : (n + 1) * bs, :] = jnp.concatenate([b_ref[2 * p, n], b_ref[2 * p + 1, n]], axis=-1)
+        writes[p].start()
+    for write in writes:
+        write.wait()
 
 
 def pack(half, cols, b_vals):
     rows, slots, bs, _ = b_vals.shape
-    shapes = [(slots * bs + FOOT, 2 * bs)] * (rows // 2)
+    shapes = [(slots * bs + (FOOT if p == 0 else 0), 2 * bs) for p in range(rows // 2)]
     return pl.pallas_call(
         functools.partial(pack_kernel, half),
         out_shape=[jax.ShapeDtypeStruct(shape, b_vals.dtype) for shape in shapes],
         in_specs=[pl.BlockSpec(memory_space=pl.ANY)] * 2,
-        out_specs=[pl.BlockSpec(memory_space=VMEM)] * len(shapes),
+        out_specs=[pl.BlockSpec(memory_space=pl.ANY)] * len(shapes),
         scratch_shapes=[
+            *(VMEM(shape, b_vals.dtype) for shape in shapes),
             SMEM(cols.shape, cols.dtype),
             VMEM(b_vals.shape, b_vals.dtype),
             pltpu.SemaphoreType.DMA,
             pltpu.SemaphoreType.DMA((rows,)),
+            pltpu.SemaphoreType.DMA((len(shapes),)),
         ],
         compiler_params=params(WHOLE),
         cost_estimate=cost(0, 2 * b_vals.size * 2),
@@ -130,9 +139,10 @@
 
 def add_products(panels, parts, total, first, feet, where, sem):
     groups, bs = total.shape[0], total.shape[3] // 2
+    pairs = len(parts) // feet.shape[0]
     slots = (parts[0].shape[0] - FOOT) // bs
-    for k, part in enumerate(parts):
-        feet[k] = part[slots * bs :, :].astype(jnp.float32).astype(jnp.int32)
+    for k in range(feet.shape[0]):
+        feet[k] = parts[k * pairs][slots * bs :, :].astype(jnp.float32).astype(jnp.int32)
     copy = pltpu.make_async_copy(feet, where, sem)
     copy.start()
     copy.wait()
@@ -149,8 +159,8 @@
             for h in range(2):
                 tiles = []
                 for q in (2 * g, 2 * g + 1):
-                    left = block(part, where[k, h, 2 * q])
-                    right = block(part, where[k, h, 2 * q + 1])
+                    left = block(part, where[k // pairs, k % pairs * 2 + h, 2 * q])
+                    right = block(part, where[k // pairs, k % pairs * 2 + h, 2 * q + 1])
                     if h == 0:
                         right = pltpu.roll(right, bs, 1)
                     else:
@@ -191,14 +201,17 @@
     fetch.wait()
     rows, slots, bs, _ = o_ref.shape
     half = total.shape[0] * 4
-    copies = [pltpu.make_async_copy(o_ref.at[i], o_hbm.at[i], sems.at[i]) for i in range(rows)]
+    copies = []
     for i in range(rows):
         for k in range(slots):
             l = lax.rem(cols_ref[i, k], half)
             tile = total[l // 4, (l // 2) % 2, i * bs : (i + 1) * bs, :].astype(o_ref.dtype)
             tile = jnp.where(l % 2 == 0, tile, pltpu.roll(tile, bs, 1))
             o_ref[i, k] = tile[:, :bs]
-        copies[i].start()
+            if k % STRIDE == STRIDE - 1 or k == slots - 1:
+                some = pl.ds(k // STRIDE * STRIDE, k % STRIDE + 1)
+                copies.append(pltpu.make_async_copy(o_ref.at[i, some], o_hbm.at[i, some], sems.at[i, k // STRIDE]))
+                copies[-1].start()
     for copy in copies:
         copy.wait()
 
@@ -208,7 +221,7 @@
     kernel = first_kernel if total is None else middle_kernel if cols is None else last_kernel
     sources = [functools.partial(arrived_from, order, way, steps) for way, steps, _ in arrived]
     parts = [ref for _, _, refs in arrived for ref in refs]
-    feet = (len(arrived) * a.shape[1], FOOT, parts[0].shape[1])
+    feet = (len(arrived), FOOT, parts[0].shape[1])
     scratch = [VMEM(feet, jnp.int32), SMEM(feet, jnp.int32), pltpu.SemaphoreType.DMA]
     arrays, specs = [a], [vmem]
     if total is not None:
@@ -219,7 +232,7 @@
             SMEM(cols.shape, cols.dtype),
             VMEM(out.shape, out.dtype),
             pltpu.SemaphoreType.DMA,
-            pltpu.SemaphoreType.DMA(out.shape[:1]),
+            pltpu.SemaphoreType.DMA((out.shape[0], -(-out.shape[1] // STRIDE))),
         ]
     return pl.pallas_call(
         functools.partial(kernel, sources),
@@ -259,15 +272,14 @@
         ways = [way for way in hops if step <= hops[way]]
         for way in ways:
             sent = list(held[way])
-            if (step, way) == (2, -1):
+            if step == 3:
                 sent = [lax.optimization_barrier((part, a))[0] for part in sent]
-            elif (step, way) == (3, 1):
+            if (step, way) == (3, -1):
                 total = product(order, rounds.pop(0), a, total, total_shape)
                 sent[0], total = lax.optimization_barrier((sent[0], total))
-            elif step > 2 and way == -1:
+            elif step > 3 and way == 1:
                 total = product(order, rounds.pop(0), a, total, total_shape)
-                for k, part in enumerate(sent):
-                    sent[k], total = lax.optimization_barrier((part, total))
+                sent[-1], total = lax.optimization_barrier((sent[-1], total))
             held[way] = [lax.ppermute(part, ("row", "col"), ring(way)) for part in sent]
         rounds.append([(way, step, held[way]) for way in ways])
     *_, late, last = rounds

time: 39.8 us -> 37.4 us (0.940); the launches traced: 39.3 us -> 37.3 us
  Pallas kernels: 13.1 us -> 12.1 us
  waiting for transfers between devices: 7.06 us -> 6.28 us
    pallas_call x5, Pallas kernels: 9.28 us -> 8.19 us  [product(): pl.pallas_call(functools.partial(kernel, sources), out_shape=out, in_spec...]
    ppermute x14, waiting for transfers between devices: 5.91 us -> 5.12 us  [local(): held[way] = [lax.ppermute(part, ('row', 'col'), ring(way)) for part in sent]]
    ppermute x2, starting transfers between devices: 0.52 us -> 0.01 us  [local(): a_other, others = (lax.ppermute(x, 'col', swap) for x in mine)]
    ppermute x14, starting transfers between devices: 18.4 us -> 18.8 us  [local(): held[way] = [lax.ppermute(part, ('row', 'col'), ring(way)) for part in sent]]
  transfers between devices with their start and end apart: 16 -> 16, of which waited for: 5 -> 7; matrix products, arithmetic and copies ran while one was open for 0% -> 0% of each run, Pallas kernels for 20% -> 19%
where the time goes in v8:
time: 37.4 us; the launch traced here: 37.3 us
  starting transfers between devices  18.8 us (50%)
  Pallas kernels  12.1 us (32%)
  waiting for transfers between devices  6.28 us (17%)
    ppermute x14, starting transfers between devices, local(): held[way] = [lax.ppermute(part, ('row', 'col'), ring(way)) for part in sent]  18.8 us
    pallas_call x5, Pallas kernels, product(): pl.pallas_call(functools.partial(kernel, sources), out_shape=out, in_spec...  8.19 us
    ppermute x14, waiting for transfers between devices, local(): held[way] = [lax.ppermute(part, ('row', 'col'), ring(way)) for part in sent]  5.12 us
    pallas_call x1, Pallas kernels, pack(): pl.pallas_call(functools.partial(pack_kernel, half), out_shape=[jax.Shape...  2.05 us
    pallas_call x1, Pallas kernels, dense_rows(): pl.pallas_call(dense_kernel, out_shape=jax.ShapeDtypeStruct((sources, row...  1.82 us
    ppermute x2, waiting for transfers between devices, local(): a_other, others = (lax.ppermute(x, 'col', swap) for x in mine)  1.16 us
  transfers between devices with their start and end apart: 16, of which 7 were waited for; matrix products, arithmetic and copies ran while one was open for 0% of the time, Pallas kernels for 19%

profile of v8, /device:TPU:0, one launch (start us, length us, event | category | flops | bytes accessed | tf_op | source)
XLA Modules:
  0.0 37.3 jit_solution(13740590184381520972)
XLA Ops:
  0.0 0.0 copy-start
  0.0 2.0 %shard_map.37 = (bf16[656,128]{1,0:T(8,128)(2,1)}, bf16[640,128]{1,0:T(8,128)(2,1)}) custom-call(s32[4,10]{1,0:T(4,128)} %cols_hbm.3, bf16[4,10,64,64]{3,2,1,0:T(8,128)(2,1)} %b_hbm.1), custom_call_target="tpu_custom_call" | custom-call | bytes 655360 | tf_op jit(solution)/shard_map/pallas_call | solution.py:61
  2.1 0.0 copy-start.3
  2.1 3.1 %collective-permute-start.7 = (bf16[656,128]{1,0:T(8,128)(2,1)}, bf16[656,128]{1,0:T(8,128)(2,1)S(1)}, u32[]{:S(2)}, u32[]{:S(2)}) collective-permute-start(bf16[656,128]{1,0:T(8,128)(2,1)} %get-tuple-element.17.refs_0_), channel_id=1, source_target_pairs={{0,4},{1,3},{4,8},{5,1},{8,12},{9,5},{12,14},{13,9},{14,10},{15,13... | collective-permute-start | bytes 503816 | tf_op jit(solution)/shard_map/ppermute | solution.py:283
  5.1 0.0 copy-done
  5.1 0.0 collective-permute-start.1
  5.2 0.0 copy-start.1
  5.2 0.0 copy-start.2
  5.2 1.6 %collective-permute-start.2 = (bf16[640,128]{1,0:T(8,128)(2,1)}, bf16[640,128]{1,0:T(8,128)(2,1)S(1)}, u32[]{:S(2)}, u32[]{:S(2)}) collective-permute-start(bf16[640,128]{1,0:T(8,128)(2,1)} %get-tuple-element.20.refs_1_), channel_id=1, source_target_pairs={{0,4},{1,3},{4,8},{5,1},{8,12},{9,5},{12,14},{13,9},{14,10},{15,13... | collective-permute-start | bytes 491528 | tf_op jit(solution)/shard_map/ppermute | solution.py:283
  6.8 0.4 %collective-permute-start.8 = (bf16[640,128]{1,0:T(8,128)(2,1)}, bf16[640,128]{1,0:T(8,128)(2,1)S(1)}, u32[]{:S(2)}, u32[]{:S(2)}) collective-permute-start(bf16[640,128]{1,0:T(8,128)(2,1)} %get-tuple-element.20.refs_1_), channel_id=1, source_target_pairs={{0,2},{1,5},{4,0},{5,9},{8,4},{9,13},{12,8},{13,15},{14,12},{15,11... | collective-permute-start | bytes 491528 | tf_op jit(solution)/shard_map/ppermute | solution.py:283
  7.2 0.0 copy-done.3
  7.2 0.0 collective-permute-start
  7.2 1.2 %collective-permute-done.others_ref = s32[4,10]{1,0:T(4,128)S(1)} collective-permute-done((s32[4,10]{1,0:T(4,128)S(1)}, s32[4,10]{1,0:T(4,128)S(1)}, u32[]{:S(2)}, u32[]{:S(2)}) %collective-permute-start) | collective-permute-done | bytes 192 | tf_op jit(solution)/shard_map/ppermute | solution.py:265
  8.4 1.0 %collective-permute-start.5 = (bf16[656,128]{1,0:T(8,128)(2,1)}, bf16[656,128]{1,0:T(8,128)(2,1)S(1)}, u32[]{:S(2)}, u32[]{:S(2)}) collective-permute-start(bf16[656,128]{1,0:T(8,128)(2,1)} %get-tuple-element.17.refs_0_), channel_id=1, source_target_pairs={{0,2},{1,5},{4,0},{5,9},{8,4},{9,13},{12,8},{13,15},{14,12},{15,11... | collective-permute-start | bytes 503816 | tf_op jit(solution)/shard_map/ppermute | solution.py:283
  9.4 0.0 collective-permute-done.7.refs_0_
  9.4 1.8 %collective-permute-start.9 = (bf16[656,128]{1,0:T(8,128)(2,1)S(1)}, bf16[656,128]{1,0:T(8,128)(2,1)S(1)}, u32[]{:S(2)}, u32[]{:S(2)}) collective-permute-start(bf16[656,128]{1,0:T(8,128)(2,1)S(1)} %collective-permute-done.7.refs_0_), channel_id=1, source_target_pairs={{0,4},{1,3},{4,8},{5,1},{8,12},{9,5},{12,14},{13,9},{14,10},{15,13... | collective-permute-start | bytes 503816 | tf_op jit(solution)/shard_map/ppermute | solution.py:283
  11.2 1.3 %collective-permute-done.2.refs_1_ = bf16[640,128]{1,0:T(8,128)(2,1)S(1)} collective-permute-done((bf16[640,128]{1,0:T(8,128)(2,1)}, bf16[640,128]{1,0:T(8,128)(2,1)S(1)}, u32[]{:S(2)}, u32[]{:S(2)}) %collective-permute-start.2) | collective-permute-done | bytes 163872 | tf_op jit(solution)/shard_map/ppermute | solution.py:283
  12.5 2.2 %collective-permute-start.3 = (bf16[640,128]{1,0:T(8,128)(2,1)S(1)}, bf16[640,128]{1,0:T(8,128)(2,1)S(1)}, u32[]{:S(2)}, u32[]{:S(2)}) collective-permute-start(bf16[640,128]{1,0:T(8,128)(2,1)S(1)} %collective-permute-done.2.refs_1_), channel_id=1, source_target_pairs={{0,4},{1,3},{4,8},{5,1},{8,12},{9,5},{12,14},{13,9},{14,10},{15,13... | collective-permute-start | bytes 491528 | tf_op jit(solution)/shard_map/ppermute | solution.py:283
  14.7 0.0 collective-permute-done.8.refs_3_
  14.7 0.0 collective-permute-start.10
  14.7 1.0 %collective-permute-done.5.refs_2_ = bf16[656,128]{1,0:T(8,128)(2,1)S(1)} collective-permute-done((bf16[656,128]{1,0:T(8,128)(2,1)}, bf16[656,128]{1,0:T(8,128)(2,1)S(1)}, u32[]{:S(2)}, u32[]{:S(2)}) %collective-permute-start.5) | collective-permute-done | bytes 167968 | tf_op jit(solution)/shard_map/ppermute | solution.py:283
  15.7 1.1 %collective-permute-start.6 = (bf16[656,128]{1,0:T(8,128)(2,1)S(1)}, bf16[656,128]{1,0:T(8,128)(2,1)S(1)}, u32[]{:S(2)}, u32[]{:S(2)}) collective-permute-start(bf16[656,128]{1,0:T(8,128)(2,1)S(1)} %collective-permute-done.5.refs_2_), channel_id=1, source_target_pairs={{0,2},{1,5},{4,0},{5,9},{8,4},{9,13},{12,8},{13,15},{14,12},{15,11... | collective-permute-start | bytes 503816 | tf_op jit(solution)/shard_map/ppermute | solution.py:283
  16.8 0.0 collective-permute-done.1.other_ref
  16.8 1.8 %shard_map.38.a_ref = bf16[8,2,256,128]{3,2,1,0:T(8,128)(2,1)S(1)} custom-call(s32[4,10]{1,0:T(4,128)S(1)} %copy-done.3, s32[4,10]{1,0:T(4,128)S(1)} %collective-permute-done.others_ref, bf16[4,10,64,64]{3,2,1,0:T(8,128)(2,1)S(1)} %copy-done, bf16[4,10,64,64]{3,2,1,0:T(8,128)(2,1)S(1)} %collective-permute-done.1.other_ref), custom_call_target="tpu_custom_call" | custom-call | bytes 1310720 | tf_op jit(solution)/shard_map/pallas_call | solution.py:109
  18.6 0.0 collective-permute-done.9.refs_0_
  18.6 1.0 %collective-permute-start.11 = (bf16[656,128]{1,0:T(8,128)(2,1)S(1)}, bf16[656,128]{1,0:T(8,128)(2,1)S(1)}, u32[]{:S(2)}, u32[]{:S(2)}) collective-permute-start(bf16[656,128]{1,0:T(8,128)(2,1)S(1)} %collective-permute-done.9.refs_0_), channel_id=1, source_target_pairs={{0,4},{1,3},{4,8},{5,1},{8,12},{9,5},{12,14},{13,9},{14,10},{15,13... | collective-permute-start | bytes 503816 | tf_op jit(solution)/shard_map/ppermute | solution.py:283
  19.6 0.5 %collective-permute-done.3.refs_1_ = bf16[640,128]{1,0:T(8,128)(2,1)S(1)} collective-permute-done((bf16[640,128]{1,0:T(8,128)(2,1)S(1)}, bf16[640,128]{1,0:T(8,128)(2,1)S(1)}, u32[]{:S(2)}, u32[]{:S(2)}) %collective-permute-start.3) | collective-permute-done | bytes 163872 | tf_op jit(solution)/shard_map/ppermute | solution.py:283
  20.2 1.8 %collective-permute-start.4 = (bf16[640,128]{1,0:T(8,128)(2,1)S(1)}, bf16[640,128]{1,0:T(8,128)(2,1)S(1)}, u32[]{:S(2)}, u32[]{:S(2)}) collective-permute-start(bf16[640,128]{1,0:T(8,128)(2,1)S(1)} %collective-permute-done.3.refs_1_), channel_id=1, source_target_pairs={{0,4},{1,3},{4,8},{5,1},{8,12},{9,5},{12,14},{13,9},{14,10},{15,13... | collective-permute-start | bytes 491528 | tf_op jit(solution)/shard_map/ppermute | solution.py:283
  21.9 0.0 collective-permute-done.10.refs_3_
  21.9 0.3 collective-permute-start.13
  22.2 0.0 copy-done.1
  22.2 0.0 copy-done.2
  22.2 1.1 %shard_map.39.before = f32[4,2,256,128]{3,2,1,0:T(8,128)S(1)} custom-call(bf16[8,2,256,128]{3,2,1,0:T(8,128)(2,1)S(1)} %shard_map.38.a_ref, bf16[656,128]{1,0:T(8,128)(2,1)S(1)} %copy-done.1, bf16[640,128]{1,0:T(8,128)(2,1)S(1)} %copy-done.2), custom_call_target="tpu_custom_call" | custom-call | flops 134217728 | tf_op jit(solution)/shard_map/pallas_call | solution.py:237
  23.3 0.0 collective-permute-done.6.refs_2_
  23.4 1.6 %collective-permute-start.12 = (bf16[656,128]{1,0:T(8,128)(2,1)S(1)}, bf16[656,128]{1,0:T(8,128)(2,1)S(1)}, u32[]{:S(2)}, u32[]{:S(2)}) collective-permute-start(bf16[656,128]{1,0:T(8,128)(2,1)S(1)} %collective-permute-done.6.refs_2_), channel_id=1, source_target_pairs={{0,2},{1,5},{4,0},{5,9},{8,4},{9,13},{12,8},{13,15},{14,12},{15,11... | collective-permute-start | bytes 503816 | tf_op jit(solution)/shard_map/ppermute | solution.py:283
  25.0 0.1 collective-permute-done.11.refs_0_
  25.0 1.5 %collective-permute-start.14 = (bf16[656,128]{1,0:T(8,128)(2,1)S(1)}, bf16[656,128]{1,0:T(8,128)(2,1)S(1)}, u32[]{:S(2)}, u32[]{:S(2)}) collective-permute-start(bf16[656,128]{1,0:T(8,128)(2,1)S(1)} %collective-permute-done.11.refs_0_), channel_id=1, source_target_pairs={{0,4},{1,3},{4,8},{5,1},{8,12},{9,5},{12,14},{13,9},{14,10},{15,13... | collective-permute-start | bytes 503816 | tf_op jit(solution)/shard_map/ppermute | solution.py:283
  26.5 1.5 %shard_map.40.before = f32[4,2,256,128]{3,2,1,0:T(8,128)S(1)} custom-call(bf16[8,2,256,128]{3,2,1,0:T(8,128)(2,1)S(1)} %shard_map.38.a_ref, f32[4,2,256,128]{3,2,1,0:T(8,128)S(1)} %shard_map.39.before, bf16[656,128]{1,0:T(8,128)(2,1)S(1)} %collective-permute-done.7.refs_0_, ...), custom_call_target="tpu_custom_call", output_to_operand_aliasing={{}: (1, {})} | custom-call | flops 268435456 | tf_op jit(solution)/shard_map/pallas_call | solution.py:237
  28.0 0.5 %collective-permute-done.4.refs_1_ = bf16[640,128]{1,0:T(8,128)(2,1)S(1)} collective-permute-done((bf16[640,128]{1,0:T(8,128)(2,1)S(1)}, bf16[640,128]{1,0:T(8,128)(2,1)S(1)}, u32[]{:S(2)}, u32[]{:S(2)}) %collective-permute-start.4) | collective-permute-done | bytes 163872 | tf_op jit(solution)/shard_map/ppermute | solution.py:283
  28.6 1.5 %collective-permute-start.15 = (bf16[640,128]{1,0:T(8,128)(2,1)S(1)}, bf16[640,128]{1,0:T(8,128)(2,1)S(1)}, u32[]{:S(2)}, u32[]{:S(2)}) collective-permute-start(bf16[640,128]{1,0:T(8,128)(2,1)S(1)} %collective-permute-done.4.refs_1_), channel_id=1, source_target_pairs={{0,4},{1,3},{4,8},{5,1},{8,12},{9,5},{12,14},{13,9},{14,10},{15,13... | collective-permute-start | bytes 491528 | tf_op jit(solution)/shard_map/ppermute | solution.py:283
  30.0 1.5 %shard_map.41.before = f32[4,2,256,128]{3,2,1,0:T(8,128)S(1)} custom-call(bf16[8,2,256,128]{3,2,1,0:T(8,128)(2,1)S(1)} %shard_map.38.a_ref, f32[4,2,256,128]{3,2,1,0:T(8,128)S(1)} %shard_map.40.before, bf16[656,128]{1,0:T(8,128)(2,1)S(1)} %collective-permute-done.9.refs_0_, ...), custom_call_target="tpu_custom_call", output_to_operand_aliasing={{}: (1, {})} | custom-call | flops 268435456 | tf_op jit(solution)/shard_map/pallas_call | solution.py:237
  31.5 1.1 %shard_map.42.total = f32[4,2,256,128]{3,2,1,0:T(8,128)S(1)} custom-call(bf16[8,2,256,128]{3,2,1,0:T(8,128)(2,1)S(1)} %shard_map.38.a_ref, f32[4,2,256,128]{3,2,1,0:T(8,128)S(1)} %shard_map.41.before, bf16[656,128]{1,0:T(8,128)(2,1)S(1)} %collective-permute-done.11.refs_0_, ...), custom_call_target="tpu_custom_call", output_to_operand_aliasing={{}: (1, {})} | custom-call | flops 134217728 | tf_op jit(solution)/shard_map/pallas_call | solution.py:237
  32.7 0.0 collective-permute-done.13.refs_1_
  32.7 0.0 collective-permute-done.12.refs_0_
  32.7 1.7 %collective-permute-done.15.refs_3_ = bf16[640,128]{1,0:T(8,128)(2,1)S(1)} collective-permute-done((bf16[640,128]{1,0:T(8,128)(2,1)S(1)}, bf16[640,128]{1,0:T(8,128)(2,1)S(1)}, u32[]{:S(2)}, u32[]{:S(2)}) %collective-permute-start.15) | collective-permute-done | bytes 163872 | tf_op jit(solution)/shard_map/ppermute | solution.py:283
  34.4 0.0 collective-permute-done.14.refs_2_
  34.4 2.9 %shard_map.43 = bf16[4,10,64,64]{3,2,1,0:T(8,128)(2,1)} custom-call(bf16[8,2,256,128]{3,2,1,0:T(8,128)(2,1)S(1)} %shard_map.38.a_ref, f32[4,2,256,128]{3,2,1,0:T(8,128)S(1)} %shard_map.42.total, s32[4,10]{1,0:T(4,128)S(1)} %copy-done.3, bf16[656,128]{1,0:T(8,128)(2,1)S(1)} %collective-permute-done.12.refs_0_, ...), custom_call_target="tpu_custom_call" | custom-call | flops 167772160 | tf_op jit(solution)/shard_map/pallas_call | solution.py:237
Async XLA Ops:
  0.0 5.1 %copy-start = (bf16[4,10,64,64]{3,2,1,0:T(8,128)(2,1)S(1)}, bf16[4,10,64,64]{3,2,1,0:T(8,128)(2,1)}, u32[]{:S(2)}) copy-start(bf16[4,10,64,64]{3,2,1,0:T(8,128)(2,1)} %own_ref.1) | copy-start | bytes 983044
  2.1 5.2 %copy-start.3 = (s32[4,10]{1,0:T(4,128)S(1)}, s32[4,10]{1,0:T(4,128)}, u32[]{:S(2)}) copy-start(s32[4,10]{1,0:T(4,128)} %cols_hbm.3) | copy-start | bytes 484
  2.1 7.3 %collective-permute-start.7 = (bf16[656,128]{1,0:T(8,128)(2,1)}, bf16[656,128]{1,0:T(8,128)(2,1)S(1)}, u32[]{:S(2)}, u32[]{:S(2)}) collective-permute-start(bf16[656,128]{1,0:T(8,128)(2,1)} %get-tuple-element.17.refs_0_), channel_id=1, source_target_pairs={{0,4},{1,3},{4,8},{5,1},{8,12},{9,5},{12,14},{13,9},{14,10},{15,13... | collective-permute-start | bytes 503816 | tf_op jit(solution)/shard_map/ppermute | solution.py:283
  5.1 11.6 %collective-permute-start.1 = (bf16[4,10,64,64]{3,2,1,0:T(8,128)(2,1)S(1)}, bf16[4,10,64,64]{3,2,1,0:T(8,128)(2,1)S(1)}, u32[]{:S(2)}, u32[]{:S(2)}) collective-permute-start(bf16[4,10,64,64]{3,2,1,0:T(8,128)(2,1)S(1)} %copy-done), channel_id=1, source_target_pairs={{0,1},{1,0},{2,3},{3,2},{4,5},{5,4},{6,7},{7,6},{8,9},{9,8},{10,11... | collective-permute-start | bytes 983048 | tf_op jit(solution)/shard_map/ppermute | solution.py:265
  5.2 17.1 %copy-start.1 = (bf16[656,128]{1,0:T(8,128)(2,1)S(1)}, bf16[656,128]{1,0:T(8,128)(2,1)}, u32[]{:S(2)}) copy-start(bf16[656,128]{1,0:T(8,128)(2,1)} %get-tuple-element.17.refs_0_) | copy-start | bytes 503812
  5.2 17.1 %copy-start.2 = (bf16[640,128]{1,0:T(8,128)(2,1)S(1)}, bf16[640,128]{1,0:T(8,128)(2,1)}, u32[]{:S(2)}) copy-start(bf16[640,128]{1,0:T(8,128)(2,1)} %get-tuple-element.20.refs_1_) | copy-start | bytes 491524
  5.2 7.3 %collective-permute-start.2 = (bf16[640,128]{1,0:T(8,128)(2,1)}, bf16[640,128]{1,0:T(8,128)(2,1)S(1)}, u32[]{:S(2)}, u32[]{:S(2)}) collective-permute-start(bf16[640,128]{1,0:T(8,128)(2,1)} %get-tuple-element.20.refs_1_), channel_id=1, source_target_pairs={{0,4},{1,3},{4,8},{5,1},{8,12},{9,5},{12,14},{13,9},{14,10},{15,13... | collective-permute-start | bytes 491528 | tf_op jit(solution)/shard_map/ppermute | solution.py:283
  6.8 7.9 %collective-permute-start.8 = (bf16[640,128]{1,0:T(8,128)(2,1)}, bf16[640,128]{1,0:T(8,128)(2,1)S(1)}, u32[]{:S(2)}, u32[]{:S(2)}) collective-permute-start(bf16[640,128]{1,0:T(8,128)(2,1)} %get-tuple-element.20.refs_1_), channel_id=1, source_target_pairs={{0,2},{1,5},{4,0},{5,9},{8,4},{9,13},{12,8},{13,15},{14,12},{15,11... | collective-permute-start | bytes 491528 | tf_op jit(solution)/shard_map/ppermute | solution.py:283
  7.2 1.2 %collective-permute-start = (s32[4,10]{1,0:T(4,128)S(1)}, s32[4,10]{1,0:T(4,128)S(1)}, u32[]{:S(2)}, u32[]{:S(2)}) collective-permute-start(s32[4,10]{1,0:T(4,128)S(1)} %copy-done.3), channel_id=1, source_target_pairs={{0,1},{1,0},{2,3},{3,2},{4,5},{5,4},{6,7},{7,6},{8,9},{9,8},{10,11... | collective-permute-start | bytes 488 | tf_op jit(solution)/shard_map/ppermute | solution.py:265
  8.4 7.3 %collective-permute-start.5 = (bf16[656,128]{1,0:T(8,128)(2,1)}, bf16[656,128]{1,0:T(8,128)(2,1)S(1)}, u32[]{:S(2)}, u32[]{:S(2)}) collective-permute-start(bf16[656,128]{1,0:T(8,128)(2,1)} %get-tuple-element.17.refs_0_), channel_id=1, source_target_pairs={{0,2},{1,5},{4,0},{5,9},{8,4},{9,13},{12,8},{13,15},{14,12},{15,11... | collective-permute-start | bytes 503816 | tf_op jit(solution)/shard_map/ppermute | solution.py:283
  9.4 9.2 %collective-permute-start.9 = (bf16[656,128]{1,0:T(8,128)(2,1)S(1)}, bf16[656,128]{1,0:T(8,128)(2,1)S(1)}, u32[]{:S(2)}, u32[]{:S(2)}) collective-permute-start(bf16[656,128]{1,0:T(8,128)(2,1)S(1)} %collective-permute-done.7.refs_0_), channel_id=1, source_target_pairs={{0,4},{1,3},{4,8},{5,1},{8,12},{9,5},{12,14},{13,9},{14,10},{15,13... | collective-permute-start | bytes 503816 | tf_op jit(solution)/shard_map/ppermute | solution.py:283
  12.5 7.7 %collective-permute-start.3 = (bf16[640,128]{1,0:T(8,128)(2,1)S(1)}, bf16[640,128]{1,0:T(8,128)(2,1)S(1)}, u32[]{:S(2)}, u32[]{:S(2)}) collective-permute-start(bf16[640,128]{1,0:T(8,128)(2,1)S(1)} %collective-permute-done.2.refs_1_), channel_id=1, source_target_pairs={{0,4},{1,3},{4,8},{5,1},{8,12},{9,5},{12,14},{13,9},{14,10},{15,13... | collective-permute-start | bytes 491528 | tf_op jit(solution)/shard_map/ppermute | solution.py:283
  14.7 7.2 %collective-permute-start.10 = (bf16[640,128]{1,0:T(8,128)(2,1)S(1)}, bf16[640,128]{1,0:T(8,128)(2,1)S(1)}, u32[]{:S(2)}, u32[]{:S(2)}) collective-permute-start(bf16[640,128]{1,0:T(8,128)(2,1)S(1)} %collective-permute-done.8.refs_3_), channel_id=1, source_target_pairs={{0,2},{1,5},{4,0},{5,9},{8,4},{9,13},{12,8},{13,15},{14,12},{15,11... | collective-permute-start | bytes 491528 | tf_op jit(solution)/shard_map/ppermute | solution.py:283
  15.7 7.6 %collective-permute-start.6 = (bf16[656,128]{1,0:T(8,128)(2,1)S(1)}, bf16[656,128]{1,0:T(8,128)(2,1)S(1)}, u32[]{:S(2)}, u32[]{:S(2)}) collective-permute-start(bf16[656,128]{1,0:T(8,128)(2,1)S(1)} %collective-permute-done.5.refs_2_), channel_id=1, source_target_pairs={{0,2},{1,5},{4,0},{5,9},{8,4},{9,13},{12,8},{13,15},{14,12},{15,11... | collective-permute-start | bytes 503816 | tf_op jit(solution)/shard_map/ppermute | solution.py:283
  18.6 6.4 %collective-permute-start.11 = (bf16[656,128]{1,0:T(8,128)(2,1)S(1)}, bf16[656,128]{1,0:T(8,128)(2,1)S(1)}, u32[]{:S(2)}, u32[]{:S(2)}) collective-permute-start(bf16[656,128]{1,0:T(8,128)(2,1)S(1)} %collective-permute-done.9.refs_0_), channel_id=1, source_target_pairs={{0,4},{1,3},{4,8},{5,1},{8,12},{9,5},{12,14},{13,9},{14,10},{15,13... | collective-permute-start | bytes 503816 | tf_op jit(solution)/shard_map/ppermute | solution.py:283
  20.2 8.4 %collective-permute-start.4 = (bf16[640,128]{1,0:T(8,128)(2,1)S(1)}, bf16[640,128]{1,0:T(8,128)(2,1)S(1)}, u32[]{:S(2)}, u32[]{:S(2)}) collective-permute-start(bf16[640,128]{1,0:T(8,128)(2,1)S(1)} %collective-permute-done.3.refs_1_), channel_id=1, source_target_pairs={{0,4},{1,3},{4,8},{5,1},{8,12},{9,5},{12,14},{13,9},{14,10},{15,13... | collective-permute-start | bytes 491528 | tf_op jit(solution)/shard_map/ppermute | solution.py:283
  21.9 10.8 %collective-permute-start.13 = (bf16[640,128]{1,0:T(8,128)(2,1)S(1)}, bf16[640,128]{1,0:T(8,128)(2,1)S(1)}, u32[]{:S(2)}, u32[]{:S(2)}) collective-permute-start(bf16[640,128]{1,0:T(8,128)(2,1)S(1)} %collective-permute-done.10.refs_3_), channel_id=1, source_target_pairs={{0,2},{1,5},{4,0},{5,9},{8,4},{9,13},{12,8},{13,15},{14,12},{15,11... | collective-permute-start | bytes 491528 | tf_op jit(solution)/shard_map/ppermute | solution.py:283
  23.4 9.3 %collective-permute-start.12 = (bf16[656,128]{1,0:T(8,128)(2,1)S(1)}, bf16[656,128]{1,0:T(8,128)(2,1)S(1)}, u32[]{:S(2)}, u32[]{:S(2)}) collective-permute-start(bf16[656,128]{1,0:T(8,128)(2,1)S(1)} %collective-permute-done.6.refs_2_), channel_id=1, source_target_pairs={{0,2},{1,5},{4,0},{5,9},{8,4},{9,13},{12,8},{13,15},{14,12},{15,11... | collective-permute-start | bytes 503816 | tf_op jit(solution)/shard_map/ppermute | solution.py:283
  25.0 9.3 %collective-permute-start.14 = (bf16[656,128]{1,0:T(8,128)(2,1)S(1)}, bf16[656,128]{1,0:T(8,128)(2,1)S(1)}, u32[]{:S(2)}, u32[]{:S(2)}) collective-permute-start(bf16[656,128]{1,0:T(8,128)(2,1)S(1)} %collective-permute-done.11.refs_0_), channel_id=1, source_target_pairs={{0,4},{1,3},{4,8},{5,1},{8,12},{9,5},{12,14},{13,9},{14,10},{15,13... | collective-permute-start | bytes 503816 | tf_op jit(solution)/shard_map/ppermute | solution.py:283
  28.6 5.8 %collective-permute-start.15 = (bf16[640,128]{1,0:T(8,128)(2,1)S(1)}, bf16[640,128]{1,0:T(8,128)(2,1)S(1)}, u32[]{:S(2)}, u32[]{:S(2)}) collective-permute-start(bf16[640,128]{1,0:T(8,128)(2,1)S(1)} %collective-permute-done.4.refs_1_), channel_id=1, source_target_pairs={{0,4},{1,3},{4,8},{5,1},{8,12},{9,5},{12,14},{13,9},{14,10},{15,13... | collective-permute-start | bytes 491528 | tf_op jit(solution)/shard_map/ppermute | solution.py:283

commit v9 on v8

--- a/solution.py
+++ b/solution.py
@@ -19,6 +19,10 @@
 
 def params(limit=LIMIT):
     return pltpu.CompilerParams(vmem_limit_bytes=limit)
+
+
+def within(col, half):
+    return jnp.where(col >= half, col - half, col)
 
 
 def cost(flops, size):
@@ -41,7 +45,7 @@
     foot = jnp.full((FOOT, 2 * bs), slots, jnp.int32)
     for r in range(rows):
         for n in range(slots):
-            here = (row == r) & (lane == lax.rem(cols_ref[r, n], half))
+            here = (row == r) & (lane == within(cols_ref[r, n], half))
             foot = jnp.where(here, n, foot)
     o_refs[0][slots * bs :, :] = foot.astype(jnp.float32).astype(b_ref.dtype)
     writes = [pltpu.make_async_copy(o_refs[p], o_hbms[p], o_sems.at[p]) for p in range(pairs)]
@@ -204,9 +208,9 @@
     copies = []
     for i in range(rows):
         for k in range(slots):
-            l = lax.rem(cols_ref[i, k], half)
-            tile = total[l // 4, (l // 2) % 2, i * bs : (i + 1) * bs, :].astype(o_ref.dtype)
-            tile = jnp.where(l % 2 == 0, tile, pltpu.roll(tile, bs, 1))
+            l = within(cols_ref[i, k], half)
+            tile = total[l >> 2, (l >> 1) & 1, i * bs : (i + 1) * bs, :].astype(o_ref.dtype)
+            tile = jnp.where(l & 1 == 0, tile, pltpu.roll(tile, bs, 1))
             o_ref[i, k] = tile[:, :bs]
             if k % STRIDE == STRIDE - 1 or k == slots - 1:
                 some = pl.ds(k // STRIDE * STRIDE, k % STRIDE + 1)
@@ -272,19 +276,17 @@
         ways = [way for way in hops if step <= hops[way]]
         for way in ways:
             sent = list(held[way])
+            if (step, way) == (1, -1):
+                sent = [lax.optimization_barrier((part, others))[0] for part in sent]
             if step == 3:
                 sent = [lax.optimization_barrier((part, a))[0] for part in sent]
-            if (step, way) == (3, -1):
+            if step > 2 and way == -1:
                 total = product(order, rounds.pop(0), a, total, total_shape)
                 sent[0], total = lax.optimization_barrier((sent[0], total))
-            elif step > 3 and way == 1:
-                total = product(order, rounds.pop(0), a, total, total_shape)
-                sent[-1], total = lax.optimization_barrier((sent[-1], total))
             held[way] = [lax.ppermute(part, ("row", "col"), ring(way)) for part in sent]
         rounds.append([(way, step, held[way]) for way in ways])
     *_, late, last = rounds
-    for some in [*rounds[:-2], late[:1]]:
-        total = product(order, some, a, total, total_shape)
+    total = product(order, sum(rounds[:-2], late[:1]), a, total, total_shape)
     out = jax.ShapeDtypeStruct(a_vals.shape, a_vals.dtype)
     return product(order, late[1:] + last, a, total, out, cols)
 

time: 37.4 us -> 35.8 us (0.957)
  Pallas kernels: 12.1 us -> 10.2 us
  waiting for transfers between devices: 6.28 us -> 7.75 us
  starting transfers between devices: 18.8 us -> 17.5 us
    pallas_call x5 -> x3, Pallas kernels: 8.19 us -> 6.37 us  [product(): pl.pallas_call(functools.partial(kernel, sources), out_shape=out, in_spec...]
    ppermute x14, waiting for transfers between devices: 5.12 us -> 6.6 us  [local(): held[way] = [lax.ppermute(part, ('row', 'col'), ring(way)) for part in sent]]
    ppermute x14, starting transfers between devices: 18.8 us -> 17.5 us  [local(): held[way] = [lax.ppermute(part, ('row', 'col'), ring(way)) for part in sent]]
  transfers between devices with their start and end apart: 16 -> 16, of which waited for: 7 -> 7; matrix products, arithmetic and copies ran while one was open for 0% -> 0% of each run, Pallas kernels for 19% -> 16%
where the time goes in v9:
time: 35.8 us; the launch traced here: 35.6 us
  starting transfers between devices  17.5 us (49%)
  Pallas kernels  10.2 us (28%)
  waiting for transfers between devices  7.75 us (22%)
    ppermute x14, starting transfers between devices, local(): held[way] = [lax.ppermute(part, ('row', 'col'), ring(way)) for part in sent]  17.5 us
    ppermute x14, waiting for transfers between devices, local(): held[way] = [lax.ppermute(part, ('row', 'col'), ring(way)) for part in sent]  6.6 us
    pallas_call x3, Pallas kernels, product(): pl.pallas_call(functools.partial(kernel, sources), out_shape=out, in_spec...  6.37 us
    pallas_call x1, Pallas kernels, pack(): pl.pallas_call(functools.partial(pack_kernel, half), out_shape=[jax.Shape...  2.05 us
    pallas_call x1, Pallas kernels, dense_rows(): pl.pallas_call(dense_kernel, out_shape=jax.ShapeDtypeStruct((sources, row...  1.82 us
    ppermute x2, waiting for transfers between devices, local(): a_other, others = (lax.ppermute(x, 'col', swap) for x in mine)  1.16 us
  transfers between devices with their start and end apart: 16, of which 7 were waited for; matrix products, arithmetic and copies ran while one was open for 0% of the time, Pallas kernels for 16%

profile of v9, /device:TPU:0, one launch (start us, length us, event | category | flops | bytes accessed | tf_op | source)
XLA Modules:
  0.0 35.6 jit_solution(16852833882411825577)
XLA Ops:
  0.0 0.0 copy-start
  0.0 2.0 %shard_map.37 = (bf16[656,128]{1,0:T(8,128)(2,1)}, bf16[640,128]{1,0:T(8,128)(2,1)}) custom-call(s32[4,10]{1,0:T(4,128)} %cols_hbm.3, bf16[4,10,64,64]{3,2,1,0:T(8,128)(2,1)} %b_hbm.1), custom_call_target="tpu_custom_call" | custom-call | bytes 655360 | tf_op jit(solution)/shard_map/pallas_call | solution.py:65
  2.1 0.0 copy-start.3
  2.1 3.1 %collective-permute-start.4 = (bf16[656,128]{1,0:T(8,128)(2,1)}, bf16[656,128]{1,0:T(8,128)(2,1)S(1)}, u32[]{:S(2)}, u32[]{:S(2)}) collective-permute-start(bf16[656,128]{1,0:T(8,128)(2,1)} %get-tuple-element.20.refs_0_), channel_id=1, source_target_pairs={{0,4},{1,3},{4,8},{5,1},{8,12},{9,5},{12,14},{13,9},{14,10},{15,13... | collective-permute-start | bytes 503816 | tf_op jit(solution)/shard_map/ppermute | solution.py:286
  5.1 0.0 copy-done
  5.1 0.0 collective-permute-start.1
  5.2 0.0 copy-start.1
  5.2 0.0 copy-start.2
  5.2 1.6 %collective-permute-start.7 = (bf16[640,128]{1,0:T(8,128)(2,1)}, bf16[640,128]{1,0:T(8,128)(2,1)S(1)}, u32[]{:S(2)}, u32[]{:S(2)}) collective-permute-start(bf16[640,128]{1,0:T(8,128)(2,1)} %get-tuple-element.26.refs_1_), channel_id=1, source_target_pairs={{0,4},{1,3},{4,8},{5,1},{8,12},{9,5},{12,14},{13,9},{14,10},{15,13... | collective-permute-start | bytes 491528 | tf_op jit(solution)/shard_map/ppermute | solution.py:286
  6.8 0.0 copy-done.3
  6.8 0.0 collective-permute-start
  6.8 1.2 %collective-permute-done.others_ref = s32[4,10]{1,0:T(4,128)S(1)} collective-permute-done((s32[4,10]{1,0:T(4,128)S(1)}, s32[4,10]{1,0:T(4,128)S(1)}, u32[]{:S(2)}, u32[]{:S(2)}) %collective-permute-start) | collective-permute-done | bytes 192 | tf_op jit(solution)/shard_map/ppermute | solution.py:269
  7.9 0.5 %collective-permute-start.2 = (bf16[656,128]{1,0:T(8,128)(2,1)}, bf16[656,128]{1,0:T(8,128)(2,1)S(1)}, u32[]{:S(2)}, u32[]{:S(2)}) collective-permute-start(bf16[656,128]{1,0:T(8,128)(2,1)} %get-tuple-element.20.refs_0_), channel_id=1, source_target_pairs={{0,2},{1,5},{4,0},{5,9},{8,4},{9,13},{12,8},{13,15},{14,12},{15,11... | collective-permute-start | bytes 503816 | tf_op jit(solution)/shard_map/ppermute | solution.py:286
  8.4 0.2 collective-permute-done.4.refs_2_
  8.6 2.1 %collective-permute-start.5 = (bf16[656,128]{1,0:T(8,128)(2,1)S(1)}, bf16[656,128]{1,0:T(8,128)(2,1)S(1)}, u32[]{:S(2)}, u32[]{:S(2)}) collective-permute-start(bf16[656,128]{1,0:T(8,128)(2,1)S(1)} %collective-permute-done.4.refs_2_), channel_id=1, source_target_pairs={{0,4},{1,3},{4,8},{5,1},{8,12},{9,5},{12,14},{13,9},{14,10},{15,13... | collective-permute-start | bytes 503816 | tf_op jit(solution)/shard_map/ppermute | solution.py:286
  10.7 0.0 collective-permute-start.10
  10.7 0.0 collective-permute-done.7.refs_3_
  10.7 2.0 %collective-permute-start.8 = (bf16[640,128]{1,0:T(8,128)(2,1)S(1)}, bf16[640,128]{1,0:T(8,128)(2,1)S(1)}, u32[]{:S(2)}, u32[]{:S(2)}) collective-permute-start(bf16[640,128]{1,0:T(8,128)(2,1)S(1)} %collective-permute-done.7.refs_3_), channel_id=1, source_target_pairs={{0,4},{1,3},{4,8},{5,1},{8,12},{9,5},{12,14},{13,9},{14,10},{15,13... | collective-permute-start | bytes 491528 | tf_op jit(solution)/shard_map/ppermute | solution.py:286
  12.8 2.3 %collective-permute-done.2.refs_4_ = bf16[656,128]{1,0:T(8,128)(2,1)S(1)} collective-permute-done((bf16[656,128]{1,0:T(8,128)(2,1)}, bf16[656,128]{1,0:T(8,128)(2,1)S(1)}, u32[]{:S(2)}, u32[]{:S(2)}) %collective-permute-start.2) | collective-permute-done | bytes 167968 | tf_op jit(solution)/shard_map/ppermute | solution.py:286
  15.0 0.5 %collective-permute-start.3 = (bf16[656,128]{1,0:T(8,128)(2,1)S(1)}, bf16[656,128]{1,0:T(8,128)(2,1)S(1)}, u32[]{:S(2)}, u32[]{:S(2)}) collective-permute-start(bf16[656,128]{1,0:T(8,128)(2,1)S(1)} %collective-permute-done.2.refs_4_), channel_id=1, source_target_pairs={{0,2},{1,5},{4,0},{5,9},{8,4},{9,13},{12,8},{13,15},{14,12},{15,11... | collective-permute-start | bytes 503816 | tf_op jit(solution)/shard_map/ppermute | solution.py:286
  15.5 0.0 collective-permute-done.1.other_ref
  15.5 1.8 %shard_map.38.a_ref = bf16[8,2,256,128]{3,2,1,0:T(8,128)(2,1)S(1)} custom-call(s32[4,10]{1,0:T(4,128)S(1)} %copy-done.3, s32[4,10]{1,0:T(4,128)S(1)} %collective-permute-done.others_ref, bf16[4,10,64,64]{3,2,1,0:T(8,128)(2,1)S(1)} %copy-done, bf16[4,10,64,64]{3,2,1,0:T(8,128)(2,1)S(1)} %collective-permute-done.1.other_ref), custom_call_target="tpu_custom_call" | custom-call | bytes 1310720 | tf_op jit(solution)/shard_map/pallas_call | solution.py:113
  17.3 0.0 collective-permute-done.5.refs_6_
  17.3 1.6 %collective-permute-start.6 = (bf16[656,128]{1,0:T(8,128)(2,1)S(1)}, bf16[656,128]{1,0:T(8,128)(2,1)S(1)}, u32[]{:S(2)}, u32[]{:S(2)}) collective-permute-start(bf16[656,128]{1,0:T(8,128)(2,1)S(1)} %collective-permute-done.5.refs_6_), channel_id=1, source_target_pairs={{0,4},{1,3},{4,8},{5,1},{8,12},{9,5},{12,14},{13,9},{14,10},{15,13... | collective-permute-start | bytes 503816 | tf_op jit(solution)/shard_map/ppermute | solution.py:286
  19.0 0.0 collective-permute-done.10.refs_5_
  19.0 0.5 %collective-permute-start.11 = (bf16[640,128]{1,0:T(8,128)(2,1)S(1)}, bf16[640,128]{1,0:T(8,128)(2,1)S(1)}, u32[]{:S(2)}, u32[]{:S(2)}) collective-permute-start(bf16[640,128]{1,0:T(8,128)(2,1)S(1)} %collective-permute-done.10.refs_5_), channel_id=1, source_target_pairs={{0,2},{1,5},{4,0},{5,9},{8,4},{9,13},{12,8},{13,15},{14,12},{15,11... | collective-permute-start | bytes 491528 | tf_op jit(solution)/shard_map/ppermute | solution.py:286
  19.4 0.0 collective-permute-done.8.refs_7_
  19.4 2.0 %collective-permute-start.9 = (bf16[640,128]{1,0:T(8,128)(2,1)S(1)}, bf16[640,128]{1,0:T(8,128)(2,1)S(1)}, u32[]{:S(2)}, u32[]{:S(2)}) collective-permute-start(bf16[640,128]{1,0:T(8,128)(2,1)S(1)} %collective-permute-done.8.refs_7_), channel_id=1, source_target_pairs={{0,4},{1,3},{4,8},{5,1},{8,12},{9,5},{12,14},{13,9},{14,10},{15,13... | collective-permute-start | bytes 491528 | tf_op jit(solution)/shard_map/ppermute | solution.py:286
  21.5 0.0 copy-done.1
  21.5 0.0 copy-done.2
  21.5 1.1 %shard_map.39.before = f32[4,2,256,128]{3,2,1,0:T(8,128)S(1)} custom-call(bf16[8,2,256,128]{3,2,1,0:T(8,128)(2,1)S(1)} %shard_map.38.a_ref, bf16[656,128]{1,0:T(8,128)(2,1)S(1)} %copy-done.1, bf16[640,128]{1,0:T(8,128)(2,1)S(1)} %copy-done.2), custom_call_target="tpu_custom_call" | custom-call | flops 134217728 | tf_op jit(solution)/shard_map/pallas_call | solution.py:241
  22.6 0.0 collective-permute-done.3.refs_8_
  22.6 0.1 collective-permute-start.12
  22.7 0.9 %collective-permute-done.6.refs_0_ = bf16[656,128]{1,0:T(8,128)(2,1)S(1)} collective-permute-done((bf16[656,128]{1,0:T(8,128)(2,1)S(1)}, bf16[656,128]{1,0:T(8,128)(2,1)S(1)}, u32[]{:S(2)}, u32[]{:S(2)}) %collective-permute-start.6) | collective-permute-done | bytes 167968 | tf_op jit(solution)/shard_map/ppermute | solution.py:286
  23.6 1.6 %collective-permute-start.14 = (bf16[656,128]{1,0:T(8,128)(2,1)S(1)}, bf16[656,128]{1,0:T(8,128)(2,1)S(1)}, u32[]{:S(2)}, u32[]{:S(2)}) collective-permute-start(bf16[656,128]{1,0:T(8,128)(2,1)S(1)} %collective-permute-done.6.refs_0_), channel_id=1, source_target_pairs={{0,4},{1,3},{4,8},{5,1},{8,12},{9,5},{12,14},{13,9},{14,10},{15,13... | collective-permute-start | bytes 503816 | tf_op jit(solution)/shard_map/ppermute | solution.py:286
  25.2 0.9 %collective-permute-done.11.refs_9_ = bf16[640,128]{1,0:T(8,128)(2,1)S(1)} collective-permute-done((bf16[640,128]{1,0:T(8,128)(2,1)S(1)}, bf16[640,128]{1,0:T(8,128)(2,1)S(1)}, u32[]{:S(2)}, u32[]{:S(2)}) %collective-permute-start.11) | collective-permute-done | bytes 163872 | tf_op jit(solution)/shard_map/ppermute | solution.py:286
  26.1 0.5 %collective-permute-start.13 = (bf16[640,128]{1,0:T(8,128)(2,1)S(1)}, bf16[640,128]{1,0:T(8,128)(2,1)S(1)}, u32[]{:S(2)}, u32[]{:S(2)}) collective-permute-start(bf16[640,128]{1,0:T(8,128)(2,1)S(1)} %collective-permute-done.11.refs_9_), channel_id=1, source_target_pairs={{0,2},{1,5},{4,0},{5,9},{8,4},{9,13},{12,8},{13,15},{14,12},{15,11... | collective-permute-start | bytes 491528 | tf_op jit(solution)/shard_map/ppermute | solution.py:286
  26.6 0.6 %collective-permute-done.9.refs_1_ = bf16[640,128]{1,0:T(8,128)(2,1)S(1)} collective-permute-done((bf16[640,128]{1,0:T(8,128)(2,1)S(1)}, bf16[640,128]{1,0:T(8,128)(2,1)S(1)}, u32[]{:S(2)}, u32[]{:S(2)}) %collective-permute-start.9) | collective-permute-done | bytes 163872 | tf_op jit(solution)/shard_map/ppermute | solution.py:286
  27.1 1.6 %collective-permute-start.15 = (bf16[640,128]{1,0:T(8,128)(2,1)S(1)}, bf16[640,128]{1,0:T(8,128)(2,1)S(1)}, u32[]{:S(2)}, u32[]{:S(2)}) collective-permute-start(bf16[640,128]{1,0:T(8,128)(2,1)S(1)} %collective-permute-done.9.refs_1_), channel_id=1, source_target_pairs={{0,4},{1,3},{4,8},{5,1},{8,12},{9,5},{12,14},{13,9},{14,10},{15,13... | collective-permute-start | bytes 491528 | tf_op jit(solution)/shard_map/ppermute | solution.py:286
  28.7 2.7 %shard_map.40.total = f32[4,2,256,128]{3,2,1,0:T(8,128)S(1)} custom-call(bf16[8,2,256,128]{3,2,1,0:T(8,128)(2,1)S(1)} %shard_map.38.a_ref, f32[4,2,256,128]{3,2,1,0:T(8,128)S(1)} %shard_map.39.before, bf16[656,128]{1,0:T(8,128)(2,1)S(1)} %collective-permute-done.6.refs_0_, ...), custom_call_target="tpu_custom_call", output_to_operand_aliasing={{}: (1, {})} | custom-call | flops 671088640 | tf_op jit(solution)/shard_map/pallas_call | solution.py:241
  31.4 1.6 %collective-permute-done.13.refs_1_ = bf16[640,128]{1,0:T(8,128)(2,1)S(1)} collective-permute-done((bf16[640,128]{1,0:T(8,128)(2,1)S(1)}, bf16[640,128]{1,0:T(8,128)(2,1)S(1)}, u32[]{:S(2)}, u32[]{:S(2)}) %collective-permute-start.13) | collective-permute-done | bytes 163872 | tf_op jit(solution)/shard_map/ppermute | solution.py:286
  33.1 0.0 collective-permute-done.12.refs_0_
  33.1 0.0 collective-permute-done.15.refs_3_
  33.1 0.0 collective-permute-done.14.refs_2_
  33.1 2.6 %shard_map.41 = bf16[4,10,64,64]{3,2,1,0:T(8,128)(2,1)} custom-call(bf16[8,2,256,128]{3,2,1,0:T(8,128)(2,1)S(1)} %shard_map.38.a_ref, f32[4,2,256,128]{3,2,1,0:T(8,128)S(1)} %shard_map.40.total, s32[4,10]{1,0:T(4,128)S(1)} %copy-done.3, bf16[656,128]{1,0:T(8,128)(2,1)S(1)} %collective-permute-done.12.refs_0_, ...), custom_call_target="tpu_custom_call" | custom-call | flops 167772160 | tf_op jit(solution)/shard_map/pallas_call | solution.py:241
Async XLA Ops:
  0.0 5.1 %copy-start = (bf16[4,10,64,64]{3,2,1,0:T(8,128)(2,1)S(1)}, bf16[4,10,64,64]{3,2,1,0:T(8,128)(2,1)}, u32[]{:S(2)}) copy-start(bf16[4,10,64,64]{3,2,1,0:T(8,128)(2,1)} %own_ref.1) | copy-start | bytes 983044
  2.1 4.7 %copy-start.3 = (s32[4,10]{1,0:T(4,128)S(1)}, s32[4,10]{1,0:T(4,128)}, u32[]{:S(2)}) copy-start(s32[4,10]{1,0:T(4,128)} %cols_hbm.3) | copy-start | bytes 484
  2.1 6.6 %collective-permute-start.4 = (bf16[656,128]{1,0:T(8,128)(2,1)}, bf16[656,128]{1,0:T(8,128)(2,1)S(1)}, u32[]{:S(2)}, u32[]{:S(2)}) collective-permute-start(bf16[656,128]{1,0:T(8,128)(2,1)} %get-tuple-element.20.refs_0_), channel_id=1, source_target_pairs={{0,4},{1,3},{4,8},{5,1},{8,12},{9,5},{12,14},{13,9},{14,10},{15,13... | collective-permute-start | bytes 503816 | tf_op jit(solution)/shard_map/ppermute | solution.py:286
  5.1 10.3 %collective-permute-start.1 = (bf16[4,10,64,64]{3,2,1,0:T(8,128)(2,1)S(1)}, bf16[4,10,64,64]{3,2,1,0:T(8,128)(2,1)S(1)}, u32[]{:S(2)}, u32[]{:S(2)}) collective-permute-start(bf16[4,10,64,64]{3,2,1,0:T(8,128)(2,1)S(1)} %copy-done), channel_id=1, source_target_pairs={{0,1},{1,0},{2,3},{3,2},{4,5},{5,4},{6,7},{7,6},{8,9},{9,8},{10,11... | collective-permute-start | bytes 983048 | tf_op jit(solution)/shard_map/ppermute | solution.py:269
  5.2 16.3 %copy-start.1 = (bf16[656,128]{1,0:T(8,128)(2,1)S(1)}, bf16[656,128]{1,0:T(8,128)(2,1)}, u32[]{:S(2)}) copy-start(bf16[656,128]{1,0:T(8,128)(2,1)} %get-tuple-element.20.refs_0_) | copy-start | bytes 503812
  5.2 16.3 %copy-start.2 = (bf16[640,128]{1,0:T(8,128)(2,1)S(1)}, bf16[640,128]{1,0:T(8,128)(2,1)}, u32[]{:S(2)}) copy-start(bf16[640,128]{1,0:T(8,128)(2,1)} %get-tuple-element.26.refs_1_) | copy-start | bytes 491524
  5.2 5.6 %collective-permute-start.7 = (bf16[640,128]{1,0:T(8,128)(2,1)}, bf16[640,128]{1,0:T(8,128)(2,1)S(1)}, u32[]{:S(2)}, u32[]{:S(2)}) collective-permute-start(bf16[640,128]{1,0:T(8,128)(2,1)} %get-tuple-element.26.refs_1_), channel_id=1, source_target_pairs={{0,4},{1,3},{4,8},{5,1},{8,12},{9,5},{12,14},{13,9},{14,10},{15,13... | collective-permute-start | bytes 491528 | tf_op jit(solution)/shard_map/ppermute | solution.py:286
  6.8 1.2 %collective-permute-start = (s32[4,10]{1,0:T(4,128)S(1)}, s32[4,10]{1,0:T(4,128)S(1)}, u32[]{:S(2)}, u32[]{:S(2)}) collective-permute-start(s32[4,10]{1,0:T(4,128)S(1)} %copy-done.3), channel_id=1, source_target_pairs={{0,1},{1,0},{2,3},{3,2},{4,5},{5,4},{6,7},{7,6},{8,9},{9,8},{10,11... | collective-permute-start | bytes 488 | tf_op jit(solution)/shard_map/ppermute | solution.py:269
  7.9 7.1 %collective-permute-start.2 = (bf16[656,128]{1,0:T(8,128)(2,1)}, bf16[656,128]{1,0:T(8,128)(2,1)S(1)}, u32[]{:S(2)}, u32[]{:S(2)}) collective-permute-start(bf16[656,128]{1,0:T(8,128)(2,1)} %get-tuple-element.20.refs_0_), channel_id=1, source_target_pairs={{0,2},{1,5},{4,0},{5,9},{8,4},{9,13},{12,8},{13,15},{14,12},{15,11... | collective-permute-start | bytes 503816 | tf_op jit(solution)/shard_map/ppermute | solution.py:286
  8.6 8.7 %collective-permute-start.5 = (bf16[656,128]{1,0:T(8,128)(2,1)S(1)}, bf16[656,128]{1,0:T(8,128)(2,1)S(1)}, u32[]{:S(2)}, u32[]{:S(2)}) collective-permute-start(bf16[656,128]{1,0:T(8,128)(2,1)S(1)} %collective-permute-done.4.refs_2_), channel_id=1, source_target_pairs={{0,4},{1,3},{4,8},{5,1},{8,12},{9,5},{12,14},{13,9},{14,10},{15,13... | collective-permute-start | bytes 503816 | tf_op jit(solution)/shard_map/ppermute | solution.py:286
  10.7 8.2 %collective-permute-start.10 = (bf16[640,128]{1,0:T(8,128)(2,1)}, bf16[640,128]{1,0:T(8,128)(2,1)S(1)}, u32[]{:S(2)}, u32[]{:S(2)}) collective-permute-start(bf16[640,128]{1,0:T(8,128)(2,1)} %get-tuple-element.26.refs_1_), channel_id=1, source_target_pairs={{0,2},{1,5},{4,0},{5,9},{8,4},{9,13},{12,8},{13,15},{14,12},{15,11... | collective-permute-start | bytes 491528 | tf_op jit(solution)/shard_map/ppermute | solution.py:286
  10.7 8.7 %collective-permute-start.8 = (bf16[640,128]{1,0:T(8,128)(2,1)S(1)}, bf16[640,128]{1,0:T(8,128)(2,1)S(1)}, u32[]{:S(2)}, u32[]{:S(2)}) collective-permute-start(bf16[640,128]{1,0:T(8,128)(2,1)S(1)} %collective-permute-done.7.refs_3_), channel_id=1, source_target_pairs={{0,4},{1,3},{4,8},{5,1},{8,12},{9,5},{12,14},{13,9},{14,10},{15,13... | collective-permute-start | bytes 491528 | tf_op jit(solution)/shard_map/ppermute | solution.py:286
  15.0 7.6 %collective-permute-start.3 = (bf16[656,128]{1,0:T(8,128)(2,1)S(1)}, bf16[656,128]{1,0:T(8,128)(2,1)S(1)}, u32[]{:S(2)}, u32[]{:S(2)}) collective-permute-start(bf16[656,128]{1,0:T(8,128)(2,1)S(1)} %collective-permute-done.2.refs_4_), channel_id=1, source_target_pairs={{0,2},{1,5},{4,0},{5,9},{8,4},{9,13},{12,8},{13,15},{14,12},{15,11... | collective-permute-start | bytes 503816 | tf_op jit(solution)/shard_map/ppermute | solution.py:286
  17.3 6.3 %collective-permute-start.6 = (bf16[656,128]{1,0:T(8,128)(2,1)S(1)}, bf16[656,128]{1,0:T(8,128)(2,1)S(1)}, u32[]{:S(2)}, u32[]{:S(2)}) collective-permute-start(bf16[656,128]{1,0:T(8,128)(2,1)S(1)} %collective-permute-done.5.refs_6_), channel_id=1, source_target_pairs={{0,4},{1,3},{4,8},{5,1},{8,12},{9,5},{12,14},{13,9},{14,10},{15,13... | collective-permute-start | bytes 503816 | tf_op jit(solution)/shard_map/ppermute | solution.py:286
  19.0 7.1 %collective-permute-start.11 = (bf16[640,128]{1,0:T(8,128)(2,1)S(1)}, bf16[640,128]{1,0:T(8,128)(2,1)S(1)}, u32[]{:S(2)}, u32[]{:S(2)}) collective-permute-start(bf16[640,128]{1,0:T(8,128)(2,1)S(1)} %collective-permute-done.10.refs_5_), channel_id=1, source_target_pairs={{0,2},{1,5},{4,0},{5,9},{8,4},{9,13},{12,8},{13,15},{14,12},{15,11... | collective-permute-start | bytes 491528 | tf_op jit(solution)/shard_map/ppermute | solution.py:286
  19.4 7.7 %collective-permute-start.9 = (bf16[640,128]{1,0:T(8,128)(2,1)S(1)}, bf16[640,128]{1,0:T(8,128)(2,1)S(1)}, u32[]{:S(2)}, u32[]{:S(2)}) collective-permute-start(bf16[640,128]{1,0:T(8,128)(2,1)S(1)} %collective-permute-done.8.refs_7_), channel_id=1, source_target_pairs={{0,4},{1,3},{4,8},{5,1},{8,12},{9,5},{12,14},{13,9},{14,10},{15,13... | collective-permute-start | bytes 491528 | tf_op jit(solution)/shard_map/ppermute | solution.py:286
  22.6 10.4 %collective-permute-start.12 = (bf16[656,128]{1,0:T(8,128)(2,1)S(1)}, bf16[656,128]{1,0:T(8,128)(2,1)S(1)}, u32[]{:S(2)}, u32[]{:S(2)}) collective-permute-start(bf16[656,128]{1,0:T(8,128)(2,1)S(1)} %collective-permute-done.3.refs_8_), channel_id=1, source_target_pairs={{0,2},{1,5},{4,0},{5,9},{8,4},{9,13},{12,8},{13,15},{14,12},{15,11... | collective-permute-start | bytes 503816 | tf_op jit(solution)/shard_map/ppermute | solution.py:286
  23.6 9.4 %collective-permute-start.14 = (bf16[656,128]{1,0:T(8,128)(2,1)S(1)}, bf16[656,128]{1,0:T(8,128)(2,1)S(1)}, u32[]{:S(2)}, u32[]{:S(2)}) collective-permute-start(bf16[656,128]{1,0:T(8,128)(2,1)S(1)} %collective-permute-done.6.refs_0_), channel_id=1, source_target_pairs={{0,4},{1,3},{4,8},{5,1},{8,12},{9,5},{12,14},{13,9},{14,10},{15,13... | collective-permute-start | bytes 503816 | tf_op jit(solution)/shard_map/ppermute | solution.py:286
  26.1 7.0 %collective-permute-start.13 = (bf16[640,128]{1,0:T(8,128)(2,1)S(1)}, bf16[640,128]{1,0:T(8,128)(2,1)S(1)}, u32[]{:S(2)}, u32[]{:S(2)}) collective-permute-start(bf16[640,128]{1,0:T(8,128)(2,1)S(1)} %collective-permute-done.11.refs_9_), channel_id=1, source_target_pairs={{0,2},{1,5},{4,0},{5,9},{8,4},{9,13},{12,8},{13,15},{14,12},{15,11... | collective-permute-start | bytes 491528 | tf_op jit(solution)/shard_map/ppermute | solution.py:286
  27.1 5.9 %collective-permute-start.15 = (bf16[640,128]{1,0:T(8,128)(2,1)S(1)}, bf16[640,128]{1,0:T(8,128)(2,1)S(1)}, u32[]{:S(2)}, u32[]{:S(2)}) collective-permute-start(bf16[640,128]{1,0:T(8,128)(2,1)S(1)} %collective-permute-done.9.refs_1_), channel_id=1, source_target_pairs={{0,4},{1,3},{4,8},{5,1},{8,12},{9,5},{12,14},{13,9},{14,10},{15,13... | collective-permute-start | bytes 491528 | tf_op jit(solution)/shard_map/ppermute | solution.py:286

commit v10 on v9

--- a/solution.py
+++ b/solution.py
@@ -12,13 +12,12 @@
 VMEM = pltpu.VMEM
 SMEM = pltpu.SMEM
 LIMIT = 48 * 1024 * 1024
-WHOLE = 63 * 1024 * 1024
 STRIDE = 5
 FOOT = 16
 
 
-def params(limit=LIMIT):
-    return pltpu.CompilerParams(vmem_limit_bytes=limit)
+def params():
+    return pltpu.CompilerParams(vmem_limit_bytes=LIMIT)
 
 
 def within(col, half):
@@ -30,9 +29,7 @@
 
 
 def pack_kernel(half, cols_hbm, b_hbm, *refs):
-    pairs = b_hbm.shape[0] // 2
-    o_hbms, refs = refs[:pairs], refs[pairs:]
-    o_refs, (cols_ref, b_ref, sem, sems, o_sems) = refs[:pairs], refs[pairs:]
+    *o_refs, cols_ref, b_ref, sem, sems = refs
     rows, slots, bs, _ = b_ref.shape
     copies = [pltpu.make_async_copy(b_hbm.at[r], b_ref.at[r], sems.at[r]) for r in range(rows)]
     fetch = pltpu.make_async_copy(cols_hbm, cols_ref, sem)
@@ -48,34 +45,29 @@
             here = (row == r) & (lane == within(cols_ref[r, n], half))
             foot = jnp.where(here, n, foot)
     o_refs[0][slots * bs :, :] = foot.astype(jnp.float32).astype(b_ref.dtype)
-    writes = [pltpu.make_async_copy(o_refs[p], o_hbms[p], o_sems.at[p]) for p in range(pairs)]
-    for p in range(pairs):
+    for p, o_ref in enumerate(o_refs):
         copies[2 * p].wait()
         copies[2 * p + 1].wait()
         for n in range(slots):
-            o_refs[p][n * bs : (n + 1) * bs, :] = jnp.concatenate([b_ref[2 * p, n], b_ref[2 * p + 1, n]], axis=-1)
-        writes[p].start()
-    for write in writes:
-        write.wait()
+            o_ref[n * bs : (n + 1) * bs, :] = jnp.concatenate([b_ref[2 * p, n], b_ref[2 * p + 1, n]], axis=-1)
 
 
 def pack(half, cols, b_vals):
     rows, slots, bs, _ = b_vals.shape
     shapes = [(slots * bs + (FOOT if p == 0 else 0), 2 * bs) for p in range(rows // 2)]
+    cols, b_vals = (pltpu.with_memory_space_constraint(x, pltpu.HBM) for x in (cols, b_vals))
     return pl.pallas_call(
         functools.partial(pack_kernel, half),
         out_shape=[jax.ShapeDtypeStruct(shape, b_vals.dtype) for shape in shapes],
         in_specs=[pl.BlockSpec(memory_space=pl.ANY)] * 2,
-        out_specs=[pl.BlockSpec(memory_space=pl.ANY)] * len(shapes),
+        out_specs=[pl.BlockSpec(memory_space=VMEM)] * len(shapes),
         scratch_shapes=[
-            *(VMEM(shape, b_vals.dtype) for shape in shapes),
             SMEM(cols.shape, cols.dtype),
             VMEM(b_vals.shape, b_vals.dtype),
             pltpu.SemaphoreType.DMA,
             pltpu.SemaphoreType.DMA((rows,)),
-            pltpu.SemaphoreType.DMA((len(shapes),)),
         ],
-        compiler_params=params(WHOLE),
+        compiler_params=params(),
         cost_estimate=cost(0, 2 * b_vals.size * 2),
     )(cols, b_vals)
 

time: 35.8 us -> 34.8 us (0.972)
  Pallas kernels: 10.2 us -> 9.55 us
  waiting for transfers between devices: 7.75 us -> 7.35 us
    pallas_call x1, Pallas kernels: 2.05 us -> 1.37 us  [pack(): pl.pallas_call(functools.partial(pack_kernel, half), out_shape=[jax.Shape...]
    ppermute x14, waiting for transfers between devices: 6.6 us -> 6.2 us  [local(): held[way] = [lax.ppermute(part, ('row', 'col'), ring(way)) for part in sent]]
  transfers between devices with their start and end apart: 16 -> 16, of which waited for: 7 -> 8; matrix products, arithmetic and copies ran while one was open for 0% -> 0% of each run, Pallas kernels for 16% -> 16%
where the time goes in v10:
time: 34.8 us; the launch traced here: 34.7 us
  starting transfers between devices  17.7 us (51%)
  Pallas kernels  9.55 us (27%)
  waiting for transfers between devices  7.35 us (21%)
    ppermute x14, starting transfers between devices, local(): held[way] = [lax.ppermute(part, ('row', 'col'), ring(way)) for part in sent]  17.7 us
    pallas_call x3, Pallas kernels, product(): pl.pallas_call(functools.partial(kernel, sources), out_shape=out, in_spec...  6.36 us
    ppermute x14, waiting for transfers between devices, local(): held[way] = [lax.ppermute(part, ('row', 'col'), ring(way)) for part in sent]  6.2 us
    pallas_call x1, Pallas kernels, dense_rows(): pl.pallas_call(dense_kernel, out_shape=jax.ShapeDtypeStruct((sources, row...  1.82 us
    pallas_call x1, Pallas kernels, pack(): pl.pallas_call(functools.partial(pack_kernel, half), out_shape=[jax.Shape...  1.37 us
    ppermute x2, waiting for transfers between devices, local(): a_other, others = (lax.ppermute(x, 'col', swap) for x in mine)  1.16 us
  transfers between devices with their start and end apart: 16, of which 8 were waited for; matrix products, arithmetic and copies ran while one was open for 0% of the time, Pallas kernels for 16%

profile of v10, /device:TPU:0, one launch (start us, length us, event | category | flops | bytes accessed | tf_op | source)
XLA Modules:
  0.0 34.7 jit_solution(15914605818665772351)
XLA Ops:
  0.0 0.0 copy-start
  0.0 1.4 %shard_map.37 = (bf16[656,128]{1,0:T(8,128)(2,1)S(1)}, bf16[640,128]{1,0:T(8,128)(2,1)S(1)}) custom-call(s32[4,10]{1,0:T(4,128)} %cols_hbm.3, bf16[4,10,64,64]{3,2,1,0:T(8,128)(2,1)} %b_hbm.1), custom_call_target="tpu_custom_call" | custom-call | bytes 655360 | tf_op jit(solution)/shard_map/pallas_call | solution.py:59
  1.4 0.0 copy-start.1
  1.4 3.1 %collective-permute-start.4 = (bf16[656,128]{1,0:T(8,128)(2,1)S(1)}, bf16[656,128]{1,0:T(8,128)(2,1)S(1)}, u32[]{:S(2)}, u32[]{:S(2)}) collective-permute-start(bf16[656,128]{1,0:T(8,128)(2,1)S(1)} %get-tuple-element.20.refs_0_), channel_id=1, source_target_pairs={{0,4},{1,3},{4,8},{5,1},{8,12},{9,5},{12,14},{13,9},{14,10},{15,13... | collective-permute-start | bytes 503816 | tf_op jit(solution)/shard_map/ppermute | solution.py:278
  4.5 0.0 copy-done
  4.5 0.0 collective-permute-start.1
  4.5 1.6 %collective-permute-start.7 = (bf16[640,128]{1,0:T(8,128)(2,1)S(1)}, bf16[640,128]{1,0:T(8,128)(2,1)S(1)}, u32[]{:S(2)}, u32[]{:S(2)}) collective-permute-start(bf16[640,128]{1,0:T(8,128)(2,1)S(1)} %get-tuple-element.26.refs_1_), channel_id=1, source_target_pairs={{0,4},{1,3},{4,8},{5,1},{8,12},{9,5},{12,14},{13,9},{14,10},{15,13... | collective-permute-start | bytes 491528 | tf_op jit(solution)/shard_map/ppermute | solution.py:278
  6.1 0.0 copy-done.1
  6.1 0.0 collective-permute-start
  6.1 1.2 %collective-permute-done.others_ref = s32[4,10]{1,0:T(4,128)S(1)} collective-permute-done((s32[4,10]{1,0:T(4,128)S(1)}, s32[4,10]{1,0:T(4,128)S(1)}, u32[]{:S(2)}, u32[]{:S(2)}) %collective-permute-start) | collective-permute-done | bytes 192 | tf_op jit(solution)/shard_map/ppermute | solution.py:261
  7.2 0.5 %collective-permute-start.2 = (bf16[656,128]{1,0:T(8,128)(2,1)S(1)}, bf16[656,128]{1,0:T(8,128)(2,1)S(1)}, u32[]{:S(2)}, u32[]{:S(2)}) collective-permute-start(bf16[656,128]{1,0:T(8,128)(2,1)S(1)} %get-tuple-element.20.refs_0_), channel_id=1, source_target_pairs={{0,2},{1,5},{4,0},{5,9},{8,4},{9,13},{12,8},{13,15},{14,12},{15,11... | collective-permute-start | bytes 503816 | tf_op jit(solution)/shard_map/ppermute | solution.py:278
  7.7 0.1 collective-permute-done.4.refs_2_
  7.8 2.1 %collective-permute-start.5 = (bf16[656,128]{1,0:T(8,128)(2,1)S(1)}, bf16[656,128]{1,0:T(8,128)(2,1)S(1)}, u32[]{:S(2)}, u32[]{:S(2)}) collective-permute-start(bf16[656,128]{1,0:T(8,128)(2,1)S(1)} %collective-permute-done.4.refs_2_), channel_id=1, source_target_pairs={{0,4},{1,3},{4,8},{5,1},{8,12},{9,5},{12,14},{13,9},{14,10},{15,13... | collective-permute-start | bytes 503816 | tf_op jit(solution)/shard_map/ppermute | solution.py:278
  9.8 0.0 collective-permute-start.10
  9.8 0.0 collective-permute-done.7.refs_3_
  9.8 2.0 %collective-permute-start.8 = (bf16[640,128]{1,0:T(8,128)(2,1)S(1)}, bf16[640,128]{1,0:T(8,128)(2,1)S(1)}, u32[]{:S(2)}, u32[]{:S(2)}) collective-permute-start(bf16[640,128]{1,0:T(8,128)(2,1)S(1)} %collective-permute-done.7.refs_3_), channel_id=1, source_target_pairs={{0,4},{1,3},{4,8},{5,1},{8,12},{9,5},{12,14},{13,9},{14,10},{15,13... | collective-permute-start | bytes 491528 | tf_op jit(solution)/shard_map/ppermute | solution.py:278
  11.9 2.1 %collective-permute-done.2.refs_4_ = bf16[656,128]{1,0:T(8,128)(2,1)S(1)} collective-permute-done((bf16[656,128]{1,0:T(8,128)(2,1)S(1)}, bf16[656,128]{1,0:T(8,128)(2,1)S(1)}, u32[]{:S(2)}, u32[]{:S(2)}) %collective-permute-start.2) | collective-permute-done | bytes 167968 | tf_op jit(solution)/shard_map/ppermute | solution.py:278
  13.9 0.5 %collective-permute-start.3 = (bf16[656,128]{1,0:T(8,128)(2,1)S(1)}, bf16[656,128]{1,0:T(8,128)(2,1)S(1)}, u32[]{:S(2)}, u32[]{:S(2)}) collective-permute-start(bf16[656,128]{1,0:T(8,128)(2,1)S(1)} %collective-permute-done.2.refs_4_), channel_id=1, source_target_pairs={{0,2},{1,5},{4,0},{5,9},{8,4},{9,13},{12,8},{13,15},{14,12},{15,11... | collective-permute-start | bytes 503816 | tf_op jit(solution)/shard_map/ppermute | solution.py:278
  14.4 0.0 collective-permute-done.1.other_ref
  14.4 1.8 %shard_map.38.a_ref = bf16[8,2,256,128]{3,2,1,0:T(8,128)(2,1)S(1)} custom-call(s32[4,10]{1,0:T(4,128)S(1)} %copy-done.1, s32[4,10]{1,0:T(4,128)S(1)} %collective-permute-done.others_ref, bf16[4,10,64,64]{3,2,1,0:T(8,128)(2,1)S(1)} %copy-done, bf16[4,10,64,64]{3,2,1,0:T(8,128)(2,1)S(1)} %collective-permute-done.1.other_ref), custom_call_target="tpu_custom_call" | custom-call | bytes 1310720 | tf_op jit(solution)/shard_map/pallas_call | solution.py:105
  16.2 0.0 collective-permute-done.5.refs_6_
  16.3 1.6 %collective-permute-start.6 = (bf16[656,128]{1,0:T(8,128)(2,1)S(1)}, bf16[656,128]{1,0:T(8,128)(2,1)S(1)}, u32[]{:S(2)}, u32[]{:S(2)}) collective-permute-start(bf16[656,128]{1,0:T(8,128)(2,1)S(1)} %collective-permute-done.5.refs_6_), channel_id=1, source_target_pairs={{0,4},{1,3},{4,8},{5,1},{8,12},{9,5},{12,14},{13,9},{14,10},{15,13... | collective-permute-start | bytes 503816 | tf_op jit(solution)/shard_map/ppermute | solution.py:278
  17.9 0.0 collective-permute-done.10.refs_5_
  17.9 0.5 %collective-permute-start.11 = (bf16[640,128]{1,0:T(8,128)(2,1)S(1)}, bf16[640,128]{1,0:T(8,128)(2,1)S(1)}, u32[]{:S(2)}, u32[]{:S(2)}) collective-permute-start(bf16[640,128]{1,0:T(8,128)(2,1)S(1)} %collective-permute-done.10.refs_5_), channel_id=1, source_target_pairs={{0,2},{1,5},{4,0},{5,9},{8,4},{9,13},{12,8},{13,15},{14,12},{15,11... | collective-permute-start | bytes 491528 | tf_op jit(solution)/shard_map/ppermute | solution.py:278
  18.3 0.1 collective-permute-done.8.refs_7_
  18.5 2.1 %collective-permute-start.9 = (bf16[640,128]{1,0:T(8,128)(2,1)S(1)}, bf16[640,128]{1,0:T(8,128)(2,1)S(1)}, u32[]{:S(2)}, u32[]{:S(2)}) collective-permute-start(bf16[640,128]{1,0:T(8,128)(2,1)S(1)} %collective-permute-done.8.refs_7_), channel_id=1, source_target_pairs={{0,4},{1,3},{4,8},{5,1},{8,12},{9,5},{12,14},{13,9},{14,10},{15,13... | collective-permute-start | bytes 491528 | tf_op jit(solution)/shard_map/ppermute | solution.py:278
  20.6 1.1 %shard_map.39.before = f32[4,2,256,128]{3,2,1,0:T(8,128)S(1)} custom-call(bf16[8,2,256,128]{3,2,1,0:T(8,128)(2,1)S(1)} %shard_map.38.a_ref, bf16[656,128]{1,0:T(8,128)(2,1)S(1)} %get-tuple-element.20.refs_0_, bf16[640,128]{1,0:T(8,128)(2,1)S(1)} %get-tuple-element.26.refs_1_), custom_call_target="tpu_custom_call" | custom-call | flops 134217728 | tf_op jit(solution)/shard_map/pallas_call | solution.py:233
  21.7 0.0 collective-permute-done.3.refs_8_
  21.7 0.1 collective-permute-start.12
  21.8 0.8 %collective-permute-done.6.refs_0_ = bf16[656,128]{1,0:T(8,128)(2,1)S(1)} collective-permute-done((bf16[656,128]{1,0:T(8,128)(2,1)S(1)}, bf16[656,128]{1,0:T(8,128)(2,1)S(1)}, u32[]{:S(2)}, u32[]{:S(2)}) %collective-permute-start.6) | collective-permute-done | bytes 167968 | tf_op jit(solution)/shard_map/ppermute | solution.py:278
  22.5 1.6 %collective-permute-start.14 = (bf16[656,128]{1,0:T(8,128)(2,1)S(1)}, bf16[656,128]{1,0:T(8,128)(2,1)S(1)}, u32[]{:S(2)}, u32[]{:S(2)}) collective-permute-start(bf16[656,128]{1,0:T(8,128)(2,1)S(1)} %collective-permute-done.6.refs_0_), channel_id=1, source_target_pairs={{0,4},{1,3},{4,8},{5,1},{8,12},{9,5},{12,14},{13,9},{14,10},{15,13... | collective-permute-start | bytes 503816 | tf_op jit(solution)/shard_map/ppermute | solution.py:278
  24.2 0.8 %collective-permute-done.11.refs_9_ = bf16[640,128]{1,0:T(8,128)(2,1)S(1)} collective-permute-done((bf16[640,128]{1,0:T(8,128)(2,1)S(1)}, bf16[640,128]{1,0:T(8,128)(2,1)S(1)}, u32[]{:S(2)}, u32[]{:S(2)}) %collective-permute-start.11) | collective-permute-done | bytes 163872 | tf_op jit(solution)/shard_map/ppermute | solution.py:278
  25.0 0.5 %collective-permute-start.13 = (bf16[640,128]{1,0:T(8,128)(2,1)S(1)}, bf16[640,128]{1,0:T(8,128)(2,1)S(1)}, u32[]{:S(2)}, u32[]{:S(2)}) collective-permute-start(bf16[640,128]{1,0:T(8,128)(2,1)S(1)} %collective-permute-done.11.refs_9_), channel_id=1, source_target_pairs={{0,2},{1,5},{4,0},{5,9},{8,4},{9,13},{12,8},{13,15},{14,12},{15,11... | collective-permute-start | bytes 491528 | tf_op jit(solution)/shard_map/ppermute | solution.py:278
  25.5 0.6 %collective-permute-done.9.refs_1_ = bf16[640,128]{1,0:T(8,128)(2,1)S(1)} collective-permute-done((bf16[640,128]{1,0:T(8,128)(2,1)S(1)}, bf16[640,128]{1,0:T(8,128)(2,1)S(1)}, u32[]{:S(2)}, u32[]{:S(2)}) %collective-permute-start.9) | collective-permute-done | bytes 163872 | tf_op jit(solution)/shard_map/ppermute | solution.py:278
  26.0 1.6 %collective-permute-start.15 = (bf16[640,128]{1,0:T(8,128)(2,1)S(1)}, bf16[640,128]{1,0:T(8,128)(2,1)S(1)}, u32[]{:S(2)}, u32[]{:S(2)}) collective-permute-start(bf16[640,128]{1,0:T(8,128)(2,1)S(1)} %collective-permute-done.9.refs_1_), channel_id=1, source_target_pairs={{0,4},{1,3},{4,8},{5,1},{8,12},{9,5},{12,14},{13,9},{14,10},{15,13... | collective-permute-start | bytes 491528 | tf_op jit(solution)/shard_map/ppermute | solution.py:278
  27.7 2.7 %shard_map.40.total = f32[4,2,256,128]{3,2,1,0:T(8,128)S(1)} custom-call(bf16[8,2,256,128]{3,2,1,0:T(8,128)(2,1)S(1)} %shard_map.38.a_ref, f32[4,2,256,128]{3,2,1,0:T(8,128)S(1)} %shard_map.39.before, bf16[656,128]{1,0:T(8,128)(2,1)S(1)} %collective-permute-done.6.refs_0_, ...), custom_call_target="tpu_custom_call", output_to_operand_aliasing={{}: (1, {})} | custom-call | flops 671088640 | tf_op jit(solution)/shard_map/pallas_call | solution.py:233
  30.4 1.7 %collective-permute-done.13.refs_1_ = bf16[640,128]{1,0:T(8,128)(2,1)S(1)} collective-permute-done((bf16[640,128]{1,0:T(8,128)(2,1)S(1)}, bf16[640,128]{1,0:T(8,128)(2,1)S(1)}, u32[]{:S(2)}, u32[]{:S(2)}) %collective-permute-start.13) | collective-permute-done | bytes 163872 | tf_op jit(solution)/shard_map/ppermute | solution.py:278
  32.1 0.0 collective-permute-done.12.refs_0_
  32.1 0.0 collective-permute-done.15.refs_3_
  32.1 0.0 collective-permute-done.14.refs_2_
  32.1 2.6 %shard_map.41 = bf16[4,10,64,64]{3,2,1,0:T(8,128)(2,1)} custom-call(bf16[8,2,256,128]{3,2,1,0:T(8,128)(2,1)S(1)} %shard_map.38.a_ref, f32[4,2,256,128]{3,2,1,0:T(8,128)S(1)} %shard_map.40.total, s32[4,10]{1,0:T(4,128)S(1)} %copy-done.1, bf16[656,128]{1,0:T(8,128)(2,1)S(1)} %collective-permute-done.12.refs_0_, ...), custom_call_target="tpu_custom_call" | custom-call | flops 167772160 | tf_op jit(solution)/shard_map/pallas_call | solution.py:233
Async XLA Ops:
  0.0 4.5 %copy-start = (bf16[4,10,64,64]{3,2,1,0:T(8,128)(2,1)S(1)}, bf16[4,10,64,64]{3,2,1,0:T(8,128)(2,1)}, u32[]{:S(2)}) copy-start(bf16[4,10,64,64]{3,2,1,0:T(8,128)(2,1)} %own_ref.1) | copy-start | bytes 983044
  1.4 4.7 %copy-start.1 = (s32[4,10]{1,0:T(4,128)S(1)}, s32[4,10]{1,0:T(4,128)}, u32[]{:S(2)}) copy-start(s32[4,10]{1,0:T(4,128)} %cols_hbm.3) | copy-start | bytes 484
  1.4 6.4 %collective-permute-start.4 = (bf16[656,128]{1,0:T(8,128)(2,1)S(1)}, bf16[656,128]{1,0:T(8,128)(2,1)S(1)}, u32[]{:S(2)}, u32[]{:S(2)}) collective-permute-start(bf16[656,128]{1,0:T(8,128)(2,1)S(1)} %get-tuple-element.20.refs_0_), channel_id=1, source_target_pairs={{0,4},{1,3},{4,8},{5,1},{8,12},{9,5},{12,14},{13,9},{14,10},{15,13... | collective-permute-start | bytes 503816 | tf_op jit(solution)/shard_map/ppermute | solution.py:278
  4.5 9.9 %collective-permute-start.1 = (bf16[4,10,64,64]{3,2,1,0:T(8,128)(2,1)S(1)}, bf16[4,10,64,64]{3,2,1,0:T(8,128)(2,1)S(1)}, u32[]{:S(2)}, u32[]{:S(2)}) collective-permute-start(bf16[4,10,64,64]{3,2,1,0:T(8,128)(2,1)S(1)} %copy-done), channel_id=1, source_target_pairs={{0,1},{1,0},{2,3},{3,2},{4,5},{5,4},{6,7},{7,6},{8,9},{9,8},{10,11... | collective-permute-start | bytes 983048 | tf_op jit(solution)/shard_map/ppermute | solution.py:261
  4.5 5.4 %collective-permute-start.7 = (bf16[640,128]{1,0:T(8,128)(2,1)S(1)}, bf16[640,128]{1,0:T(8,128)(2,1)S(1)}, u32[]{:S(2)}, u32[]{:S(2)}) collective-permute-start(bf16[640,128]{1,0:T(8,128)(2,1)S(1)} %get-tuple-element.26.refs_1_), channel_id=1, source_target_pairs={{0,4},{1,3},{4,8},{5,1},{8,12},{9,5},{12,14},{13,9},{14,10},{15,13... | collective-permute-start | bytes 491528 | tf_op jit(solution)/shard_map/ppermute | solution.py:278
  6.1 1.2 %collective-permute-start = (s32[4,10]{1,0:T(4,128)S(1)}, s32[4,10]{1,0:T(4,128)S(1)}, u32[]{:S(2)}, u32[]{:S(2)}) collective-permute-start(s32[4,10]{1,0:T(4,128)S(1)} %copy-done.1), channel_id=1, source_target_pairs={{0,1},{1,0},{2,3},{3,2},{4,5},{5,4},{6,7},{7,6},{8,9},{9,8},{10,11... | collective-permute-start | bytes 488 | tf_op jit(solution)/shard_map/ppermute | solution.py:261
  7.2 6.7 %collective-permute-start.2 = (bf16[656,128]{1,0:T(8,128)(2,1)S(1)}, bf16[656,128]{1,0:T(8,128)(2,1)S(1)}, u32[]{:S(2)}, u32[]{:S(2)}) collective-permute-start(bf16[656,128]{1,0:T(8,128)(2,1)S(1)} %get-tuple-element.20.refs_0_), channel_id=1, source_target_pairs={{0,2},{1,5},{4,0},{5,9},{8,4},{9,13},{12,8},{13,15},{14,12},{15,11... | collective-permute-start | bytes 503816 | tf_op jit(solution)/shard_map/ppermute | solution.py:278
  7.8 8.5 %collective-permute-start.5 = (bf16[656,128]{1,0:T(8,128)(2,1)S(1)}, bf16[656,128]{1,0:T(8,128)(2,1)S(1)}, u32[]{:S(2)}, u32[]{:S(2)}) collective-permute-start(bf16[656,128]{1,0:T(8,128)(2,1)S(1)} %collective-permute-done.4.refs_2_), channel_id=1, source_target_pairs={{0,4},{1,3},{4,8},{5,1},{8,12},{9,5},{12,14},{13,9},{14,10},{15,13... | collective-permute-start | bytes 503816 | tf_op jit(solution)/shard_map/ppermute | solution.py:278
  9.8 8.0 %collective-permute-start.10 = (bf16[640,128]{1,0:T(8,128)(2,1)S(1)}, bf16[640,128]{1,0:T(8,128)(2,1)S(1)}, u32[]{:S(2)}, u32[]{:S(2)}) collective-permute-start(bf16[640,128]{1,0:T(8,128)(2,1)S(1)} %get-tuple-element.26.refs_1_), channel_id=1, source_target_pairs={{0,2},{1,5},{4,0},{5,9},{8,4},{9,13},{12,8},{13,15},{14,12},{15,11... | collective-permute-start | bytes 491528 | tf_op jit(solution)/shard_map/ppermute | solution.py:278
  9.8 8.6 %collective-permute-start.8 = (bf16[640,128]{1,0:T(8,128)(2,1)S(1)}, bf16[640,128]{1,0:T(8,128)(2,1)S(1)}, u32[]{:S(2)}, u32[]{:S(2)}) collective-permute-start(bf16[640,128]{1,0:T(8,128)(2,1)S(1)} %collective-permute-done.7.refs_3_), channel_id=1, source_target_pairs={{0,4},{1,3},{4,8},{5,1},{8,12},{9,5},{12,14},{13,9},{14,10},{15,13... | collective-permute-start | bytes 491528 | tf_op jit(solution)/shard_map/ppermute | solution.py:278
  13.9 7.8 %collective-permute-start.3 = (bf16[656,128]{1,0:T(8,128)(2,1)S(1)}, bf16[656,128]{1,0:T(8,128)(2,1)S(1)}, u32[]{:S(2)}, u32[]{:S(2)}) collective-permute-start(bf16[656,128]{1,0:T(8,128)(2,1)S(1)} %collective-permute-done.2.refs_4_), channel_id=1, source_target_pairs={{0,2},{1,5},{4,0},{5,9},{8,4},{9,13},{12,8},{13,15},{14,12},{15,11... | collective-permute-start | bytes 503816 | tf_op jit(solution)/shard_map/ppermute | solution.py:278
  16.3 6.3 %collective-permute-start.6 = (bf16[656,128]{1,0:T(8,128)(2,1)S(1)}, bf16[656,128]{1,0:T(8,128)(2,1)S(1)}, u32[]{:S(2)}, u32[]{:S(2)}) collective-permute-start(bf16[656,128]{1,0:T(8,128)(2,1)S(1)} %collective-permute-done.5.refs_6_), channel_id=1, source_target_pairs={{0,4},{1,3},{4,8},{5,1},{8,12},{9,5},{12,14},{13,9},{14,10},{15,13... | collective-permute-start | bytes 503816 | tf_op jit(solution)/shard_map/ppermute | solution.py:278
  17.9 7.1 %collective-permute-start.11 = (bf16[640,128]{1,0:T(8,128)(2,1)S(1)}, bf16[640,128]{1,0:T(8,128)(2,1)S(1)}, u32[]{:S(2)}, u32[]{:S(2)}) collective-permute-start(bf16[640,128]{1,0:T(8,128)(2,1)S(1)} %collective-permute-done.10.refs_5_), channel_id=1, source_target_pairs={{0,2},{1,5},{4,0},{5,9},{8,4},{9,13},{12,8},{13,15},{14,12},{15,11... | collective-permute-start | bytes 491528 | tf_op jit(solution)/shard_map/ppermute | solution.py:278
  18.5 7.6 %collective-permute-start.9 = (bf16[640,128]{1,0:T(8,128)(2,1)S(1)}, bf16[640,128]{1,0:T(8,128)(2,1)S(1)}, u32[]{:S(2)}, u32[]{:S(2)}) collective-permute-start(bf16[640,128]{1,0:T(8,128)(2,1)S(1)} %collective-permute-done.8.refs_7_), channel_id=1, source_target_pairs={{0,4},{1,3},{4,8},{5,1},{8,12},{9,5},{12,14},{13,9},{14,10},{15,13... | collective-permute-start | bytes 491528 | tf_op jit(solution)/shard_map/ppermute | solution.py:278
  21.7 10.4 %collective-permute-start.12 = (bf16[656,128]{1,0:T(8,128)(2,1)S(1)}, bf16[656,128]{1,0:T(8,128)(2,1)S(1)}, u32[]{:S(2)}, u32[]{:S(2)}) collective-permute-start(bf16[656,128]{1,0:T(8,128)(2,1)S(1)} %collective-permute-done.3.refs_8_), channel_id=1, source_target_pairs={{0,2},{1,5},{4,0},{5,9},{8,4},{9,13},{12,8},{13,15},{14,12},{15,11... | collective-permute-start | bytes 503816 | tf_op jit(solution)/shard_map/ppermute | solution.py:278
  22.5 9.6 %collective-permute-start.14 = (bf16[656,128]{1,0:T(8,128)(2,1)S(1)}, bf16[656,128]{1,0:T(8,128)(2,1)S(1)}, u32[]{:S(2)}, u32[]{:S(2)}) collective-permute-start(bf16[656,128]{1,0:T(8,128)(2,1)S(1)} %collective-permute-done.6.refs_0_), channel_id=1, source_target_pairs={{0,4},{1,3},{4,8},{5,1},{8,12},{9,5},{12,14},{13,9},{14,10},{15,13... | collective-permute-start | bytes 503816 | tf_op jit(solution)/shard_map/ppermute | solution.py:278
  25.0 7.1 %collective-permute-start.13 = (bf16[640,128]{1,0:T(8,128)(2,1)S(1)}, bf16[640,128]{1,0:T(8,128)(2,1)S(1)}, u32[]{:S(2)}, u32[]{:S(2)}) collective-permute-start(bf16[640,128]{1,0:T(8,128)(2,1)S(1)} %collective-permute-done.11.refs_9_), channel_id=1, source_target_pairs={{0,2},{1,5},{4,0},{5,9},{8,4},{9,13},{12,8},{13,15},{14,12},{15,11... | collective-permute-start | bytes 491528 | tf_op jit(solution)/shard_map/ppermute | solution.py:278
  26.0 6.1 %collective-permute-start.15 = (bf16[640,128]{1,0:T(8,128)(2,1)S(1)}, bf16[640,128]{1,0:T(8,128)(2,1)S(1)}, u32[]{:S(2)}, u32[]{:S(2)}) collective-permute-start(bf16[640,128]{1,0:T(8,128)(2,1)S(1)} %collective-permute-done.9.refs_1_), channel_id=1, source_target_pairs={{0,4},{1,3},{4,8},{5,1},{8,12},{9,5},{12,14},{13,9},{14,10},{15,13... | collective-permute-start | bytes 491528 | tf_op jit(solution)/shard_map/ppermute | solution.py:278

commit v11 on v10

--- a/solution.py
+++ b/solution.py
@@ -270,8 +270,8 @@
             sent = list(held[way])
             if (step, way) == (1, -1):
                 sent = [lax.optimization_barrier((part, others))[0] for part in sent]
-            if step == 3:
-                sent = [lax.optimization_barrier((part, a))[0] for part in sent]
+            if (step, way) == (2, -1):
+                sent[-1], _ = lax.optimization_barrier((sent[-1], a))
             if step > 2 and way == -1:
                 total = product(order, rounds.pop(0), a, total, total_shape)
                 sent[0], total = lax.optimization_barrier((sent[0], total))

time: 34.8 us -> 34.8 us (level)
  starting transfers between devices: 17.7 us -> 18.3 us
  waiting for transfers between devices: 7.35 us -> 6.75 us
    ppermute x14, waiting for transfers between devices: 6.2 us -> 5.6 us  [local(): held[way] = [lax.ppermute(part, ('row', 'col'), ring(way)) for part in sent]]
    ppermute x14, starting transfers between devices: 17.7 us -> 18.3 us  [local(): held[way] = [lax.ppermute(part, ('row', 'col'), ring(way)) for part in sent]]
  transfers between devices with their start and end apart: 16 -> 16, of which waited for: 8 -> 7; matrix products, arithmetic and copies ran while one was open for 0% -> 0% of each run, Pallas kernels for 16% -> 16%
where the time goes in v11:
time: 34.8 us; the launch traced here: 34.7 us
  starting transfers between devices  18.3 us (53%)
  Pallas kernels  9.55 us (27%)
  waiting for transfers between devices  6.75 us (19%)
    ppermute x14, starting transfers between devices, local(): held[way] = [lax.ppermute(part, ('row', 'col'), ring(way)) for part in sent]  18.3 us
    pallas_call x3, Pallas kernels, product(): pl.pallas_call(functools.partial(kernel, sources), out_shape=out, in_spec...  6.36 us
    ppermute x14, waiting for transfers between devices, local(): held[way] = [lax.ppermute(part, ('row', 'col'), ring(way)) for part in sent]  5.6 us
    pallas_call x1, Pallas kernels, dense_rows(): pl.pallas_call(dense_kernel, out_shape=jax.ShapeDtypeStruct((sources, row...  1.82 us
    pallas_call x1, Pallas kernels, pack(): pl.pallas_call(functools.partial(pack_kernel, half), out_shape=[jax.Shape...  1.37 us
    ppermute x2, waiting for transfers between devices, local(): a_other, others = (lax.ppermute(x, 'col', swap) for x in mine)  1.16 us
  transfers between devices with their start and end apart: 16, of which 7 were waited for; matrix products, arithmetic and copies ran while one was open for 0% of the time, Pallas kernels for 16%

profile of v11, /device:TPU:0, one launch (start us, length us, event | category | flops | bytes accessed | tf_op | source)
XLA Modules:
  0.0 34.7 jit_solution(7521954648726841948)
XLA Ops:
  0.0 0.0 copy-start
  0.0 1.4 %shard_map.37 = (bf16[656,128]{1,0:T(8,128)(2,1)S(1)}, bf16[640,128]{1,0:T(8,128)(2,1)S(1)}) custom-call(s32[4,10]{1,0:T(4,128)} %cols_hbm.3, bf16[4,10,64,64]{3,2,1,0:T(8,128)(2,1)} %b_hbm.1), custom_call_target="tpu_custom_call" | custom-call | bytes 655360 | tf_op jit(solution)/shard_map/pallas_call | solution.py:59
  1.4 0.0 copy-start.1
  1.4 3.1 %collective-permute-start.4 = (bf16[656,128]{1,0:T(8,128)(2,1)S(1)}, bf16[656,128]{1,0:T(8,128)(2,1)S(1)}, u32[]{:S(2)}, u32[]{:S(2)}) collective-permute-start(bf16[656,128]{1,0:T(8,128)(2,1)S(1)} %get-tuple-element.17.refs_0_), channel_id=1, source_target_pairs={{0,4},{1,3},{4,8},{5,1},{8,12},{9,5},{12,14},{13,9},{14,10},{15,13... | collective-permute-start | bytes 503816 | tf_op jit(solution)/shard_map/ppermute | solution.py:278
  4.5 0.0 copy-done
  4.5 0.0 collective-permute-start.1
  4.5 1.6 %collective-permute-start.7 = (bf16[640,128]{1,0:T(8,128)(2,1)S(1)}, bf16[640,128]{1,0:T(8,128)(2,1)S(1)}, u32[]{:S(2)}, u32[]{:S(2)}) collective-permute-start(bf16[640,128]{1,0:T(8,128)(2,1)S(1)} %get-tuple-element.20.refs_1_), channel_id=1, source_target_pairs={{0,4},{1,3},{4,8},{5,1},{8,12},{9,5},{12,14},{13,9},{14,10},{15,13... | collective-permute-start | bytes 491528 | tf_op jit(solution)/shard_map/ppermute | solution.py:278
  6.1 0.0 copy-done.1
  6.1 0.0 collective-permute-start
  6.1 1.2 %collective-permute-done.others_ref = s32[4,10]{1,0:T(4,128)S(1)} collective-permute-done((s32[4,10]{1,0:T(4,128)S(1)}, s32[4,10]{1,0:T(4,128)S(1)}, u32[]{:S(2)}, u32[]{:S(2)}) %collective-permute-start) | collective-permute-done | bytes 192 | tf_op jit(solution)/shard_map/ppermute | solution.py:261
  7.2 0.5 %collective-permute-start.2 = (bf16[656,128]{1,0:T(8,128)(2,1)S(1)}, bf16[656,128]{1,0:T(8,128)(2,1)S(1)}, u32[]{:S(2)}, u32[]{:S(2)}) collective-permute-start(bf16[656,128]{1,0:T(8,128)(2,1)S(1)} %get-tuple-element.17.refs_0_), channel_id=1, source_target_pairs={{0,2},{1,5},{4,0},{5,9},{8,4},{9,13},{12,8},{13,15},{14,12},{15,11... | collective-permute-start | bytes 503816 | tf_op jit(solution)/shard_map/ppermute | solution.py:278
  7.7 0.1 collective-permute-done.4.refs_2_
  7.8 2.1 %collective-permute-start.5 = (bf16[656,128]{1,0:T(8,128)(2,1)S(1)}, bf16[656,128]{1,0:T(8,128)(2,1)S(1)}, u32[]{:S(2)}, u32[]{:S(2)}) collective-permute-start(bf16[656,128]{1,0:T(8,128)(2,1)S(1)} %collective-permute-done.4.refs_2_), channel_id=1, source_target_pairs={{0,4},{1,3},{4,8},{5,1},{8,12},{9,5},{12,14},{13,9},{14,10},{15,13... | collective-permute-start | bytes 503816 | tf_op jit(solution)/shard_map/ppermute | solution.py:278
  9.8 0.0 collective-permute-start.10
  9.8 0.0 collective-permute-done.7.refs_3_
  9.8 2.0 %collective-permute-start.8 = (bf16[640,128]{1,0:T(8,128)(2,1)S(1)}, bf16[640,128]{1,0:T(8,128)(2,1)S(1)}, u32[]{:S(2)}, u32[]{:S(2)}) collective-permute-start(bf16[640,128]{1,0:T(8,128)(2,1)S(1)} %collective-permute-done.7.refs_3_), channel_id=1, source_target_pairs={{0,4},{1,3},{4,8},{5,1},{8,12},{9,5},{12,14},{13,9},{14,10},{15,13... | collective-permute-start | bytes 491528 | tf_op jit(solution)/shard_map/ppermute | solution.py:278
  11.9 2.1 %collective-permute-done.2.refs_4_ = bf16[656,128]{1,0:T(8,128)(2,1)S(1)} collective-permute-done((bf16[656,128]{1,0:T(8,128)(2,1)S(1)}, bf16[656,128]{1,0:T(8,128)(2,1)S(1)}, u32[]{:S(2)}, u32[]{:S(2)}) %collective-permute-start.2) | collective-permute-done | bytes 167968 | tf_op jit(solution)/shard_map/ppermute | solution.py:278
  13.9 0.5 %collective-permute-start.3 = (bf16[656,128]{1,0:T(8,128)(2,1)S(1)}, bf16[656,128]{1,0:T(8,128)(2,1)S(1)}, u32[]{:S(2)}, u32[]{:S(2)}) collective-permute-start(bf16[656,128]{1,0:T(8,128)(2,1)S(1)} %collective-permute-done.2.refs_4_), channel_id=1, source_target_pairs={{0,2},{1,5},{4,0},{5,9},{8,4},{9,13},{12,8},{13,15},{14,12},{15,11... | collective-permute-start | bytes 503816 | tf_op jit(solution)/shard_map/ppermute | solution.py:278
  14.4 0.6 %collective-permute-done.5.refs_6_ = bf16[656,128]{1,0:T(8,128)(2,1)S(1)} collective-permute-done((bf16[656,128]{1,0:T(8,128)(2,1)S(1)}, bf16[656,128]{1,0:T(8,128)(2,1)S(1)}, u32[]{:S(2)}, u32[]{:S(2)}) %collective-permute-start.5) | collective-permute-done | bytes 167968 | tf_op jit(solution)/shard_map/ppermute | solution.py:278
  15.0 2.1 %collective-permute-start.6 = (bf16[656,128]{1,0:T(8,128)(2,1)S(1)}, bf16[656,128]{1,0:T(8,128)(2,1)S(1)}, u32[]{:S(2)}, u32[]{:S(2)}) collective-permute-start(bf16[656,128]{1,0:T(8,128)(2,1)S(1)} %collective-permute-done.5.refs_6_), channel_id=1, source_target_pairs={{0,4},{1,3},{4,8},{5,1},{8,12},{9,5},{12,14},{13,9},{14,10},{15,13... | collective-permute-start | bytes 503816 | tf_op jit(solution)/shard_map/ppermute | solution.py:278
  17.1 0.0 collective-permute-done.1.other_ref
  17.1 1.8 %shard_map.38.a_ref = bf16[8,2,256,128]{3,2,1,0:T(8,128)(2,1)S(1)} custom-call(s32[4,10]{1,0:T(4,128)S(1)} %copy-done.1, s32[4,10]{1,0:T(4,128)S(1)} %collective-permute-done.others_ref, bf16[4,10,64,64]{3,2,1,0:T(8,128)(2,1)S(1)} %copy-done, bf16[4,10,64,64]{3,2,1,0:T(8,128)(2,1)S(1)} %collective-permute-done.1.other_ref), custom_call_target="tpu_custom_call" | custom-call | bytes 1310720 | tf_op jit(solution)/shard_map/pallas_call | solution.py:105
  18.9 0.0 collective-permute-done.10.refs_5_
  18.9 0.1 collective-permute-start.11
  19.0 0.0 collective-permute-done.8.refs_7_
  19.0 2.0 %collective-permute-start.9 = (bf16[640,128]{1,0:T(8,128)(2,1)S(1)}, bf16[640,128]{1,0:T(8,128)(2,1)S(1)}, u32[]{:S(2)}, u32[]{:S(2)}) collective-permute-start(bf16[640,128]{1,0:T(8,128)(2,1)S(1)} %collective-permute-done.8.refs_7_), channel_id=1, source_target_pairs={{0,4},{1,3},{4,8},{5,1},{8,12},{9,5},{12,14},{13,9},{14,10},{15,13... | collective-permute-start | bytes 491528 | tf_op jit(solution)/shard_map/ppermute | solution.py:278
  21.0 1.1 %shard_map.39.before = f32[4,2,256,128]{3,2,1,0:T(8,128)S(1)} custom-call(bf16[8,2,256,128]{3,2,1,0:T(8,128)(2,1)S(1)} %shard_map.38.a_ref, bf16[656,128]{1,0:T(8,128)(2,1)S(1)} %get-tuple-element.17.refs_0_, bf16[640,128]{1,0:T(8,128)(2,1)S(1)} %get-tuple-element.20.refs_1_), custom_call_target="tpu_custom_call" | custom-call | flops 134217728 | tf_op jit(solution)/shard_map/pallas_call | solution.py:233
  22.1 0.0 collective-permute-done.3.refs_8_
  22.1 0.1 collective-permute-start.12
  22.3 0.0 collective-permute-done.6.refs_0_
  22.3 2.0 %collective-permute-start.14 = (bf16[656,128]{1,0:T(8,128)(2,1)S(1)}, bf16[656,128]{1,0:T(8,128)(2,1)S(1)}, u32[]{:S(2)}, u32[]{:S(2)}) collective-permute-start(bf16[656,128]{1,0:T(8,128)(2,1)S(1)} %collective-permute-done.6.refs_0_), channel_id=1, source_target_pairs={{0,4},{1,3},{4,8},{5,1},{8,12},{9,5},{12,14},{13,9},{14,10},{15,13... | collective-permute-start | bytes 503816 | tf_op jit(solution)/shard_map/ppermute | solution.py:278
  24.2 1.5 %collective-permute-done.11.refs_9_ = bf16[640,128]{1,0:T(8,128)(2,1)S(1)} collective-permute-done((bf16[640,128]{1,0:T(8,128)(2,1)S(1)}, bf16[640,128]{1,0:T(8,128)(2,1)S(1)}, u32[]{:S(2)}, u32[]{:S(2)}) %collective-permute-start.11) | collective-permute-done | bytes 163872 | tf_op jit(solution)/shard_map/ppermute | solution.py:278
  25.7 0.4 %collective-permute-start.13 = (bf16[640,128]{1,0:T(8,128)(2,1)S(1)}, bf16[640,128]{1,0:T(8,128)(2,1)S(1)}, u32[]{:S(2)}, u32[]{:S(2)}) collective-permute-start(bf16[640,128]{1,0:T(8,128)(2,1)S(1)} %collective-permute-done.11.refs_9_), channel_id=1, source_target_pairs={{0,2},{1,5},{4,0},{5,9},{8,4},{9,13},{12,8},{13,15},{14,12},{15,11... | collective-permute-start | bytes 491528 | tf_op jit(solution)/shard_map/ppermute | solution.py:278
  26.1 0.1 collective-permute-done.9.refs_1_
  26.2 2.0 %collective-permute-start.15 = (bf16[640,128]{1,0:T(8,128)(2,1)S(1)}, bf16[640,128]{1,0:T(8,128)(2,1)S(1)}, u32[]{:S(2)}, u32[]{:S(2)}) collective-permute-start(bf16[640,128]{1,0:T(8,128)(2,1)S(1)} %collective-permute-done.9.refs_1_), channel_id=1, source_target_pairs={{0,4},{1,3},{4,8},{5,1},{8,12},{9,5},{12,14},{13,9},{14,10},{15,13... | collective-permute-start | bytes 491528 | tf_op jit(solution)/shard_map/ppermute | solution.py:278
  28.1 2.7 %shard_map.40.total = f32[4,2,256,128]{3,2,1,0:T(8,128)S(1)} custom-call(bf16[8,2,256,128]{3,2,1,0:T(8,128)(2,1)S(1)} %shard_map.38.a_ref, f32[4,2,256,128]{3,2,1,0:T(8,128)S(1)} %shard_map.39.before, bf16[656,128]{1,0:T(8,128)(2,1)S(1)} %collective-permute-done.6.refs_0_, ...), custom_call_target="tpu_custom_call", output_to_operand_aliasing={{}: (1, {})} | custom-call | flops 671088640 | tf_op jit(solution)/shard_map/pallas_call | solution.py:233
  30.8 0.0 collective-permute-done.12.refs_0_
  30.8 1.3 %collective-permute-done.13.refs_1_ = bf16[640,128]{1,0:T(8,128)(2,1)S(1)} collective-permute-done((bf16[640,128]{1,0:T(8,128)(2,1)S(1)}, bf16[640,128]{1,0:T(8,128)(2,1)S(1)}, u32[]{:S(2)}, u32[]{:S(2)}) %collective-permute-start.13) | collective-permute-done | bytes 163872 | tf_op jit(solution)/shard_map/ppermute | solution.py:278
  32.1 0.0 collective-permute-done.15.refs_3_
  32.1 0.0 collective-permute-done.14.refs_2_
  32.1 2.6 %shard_map.41 = bf16[4,10,64,64]{3,2,1,0:T(8,128)(2,1)} custom-call(bf16[8,2,256,128]{3,2,1,0:T(8,128)(2,1)S(1)} %shard_map.38.a_ref, f32[4,2,256,128]{3,2,1,0:T(8,128)S(1)} %shard_map.40.total, s32[4,10]{1,0:T(4,128)S(1)} %copy-done.1, bf16[656,128]{1,0:T(8,128)(2,1)S(1)} %collective-permute-done.12.refs_0_, ...), custom_call_target="tpu_custom_call" | custom-call | flops 167772160 | tf_op jit(solution)/shard_map/pallas_call | solution.py:233
Async XLA Ops:
  0.0 4.5 %copy-start = (bf16[4,10,64,64]{3,2,1,0:T(8,128)(2,1)S(1)}, bf16[4,10,64,64]{3,2,1,0:T(8,128)(2,1)}, u32[]{:S(2)}) copy-start(bf16[4,10,64,64]{3,2,1,0:T(8,128)(2,1)} %own_ref.1) | copy-start | bytes 983044
  1.4 4.7 %copy-start.1 = (s32[4,10]{1,0:T(4,128)S(1)}, s32[4,10]{1,0:T(4,128)}, u32[]{:S(2)}) copy-start(s32[4,10]{1,0:T(4,128)} %cols_hbm.3) | copy-start | bytes 484
  1.4 6.4 %collective-permute-start.4 = (bf16[656,128]{1,0:T(8,128)(2,1)S(1)}, bf16[656,128]{1,0:T(8,128)(2,1)S(1)}, u32[]{:S(2)}, u32[]{:S(2)}) collective-permute-start(bf16[656,128]{1,0:T(8,128)(2,1)S(1)} %get-tuple-element.17.refs_0_), channel_id=1, source_target_pairs={{0,4},{1,3},{4,8},{5,1},{8,12},{9,5},{12,14},{13,9},{14,10},{15,13... | collective-permute-start | bytes 503816 | tf_op jit(solution)/shard_map/ppermute | solution.py:278
  4.5 12.6 %collective-permute-start.1 = (bf16[4,10,64,64]{3,2,1,0:T(8,128)(2,1)S(1)}, bf16[4,10,64,64]{3,2,1,0:T(8,128)(2,1)S(1)}, u32[]{:S(2)}, u32[]{:S(2)}) collective-permute-start(bf16[4,10,64,64]{3,2,1,0:T(8,128)(2,1)S(1)} %copy-done), channel_id=1, source_target_pairs={{0,1},{1,0},{2,3},{3,2},{4,5},{5,4},{6,7},{7,6},{8,9},{9,8},{10,11... | collective-permute-start | bytes 983048 | tf_op jit(solution)/shard_map/ppermute | solution.py:261
  4.5 5.4 %collective-permute-start.7 = (bf16[640,128]{1,0:T(8,128)(2,1)S(1)}, bf16[640,128]{1,0:T(8,128)(2,1)S(1)}, u32[]{:S(2)}, u32[]{:S(2)}) collective-permute-start(bf16[640,128]{1,0:T(8,128)(2,1)S(1)} %get-tuple-element.20.refs_1_), channel_id=1, source_target_pairs={{0,4},{1,3},{4,8},{5,1},{8,12},{9,5},{12,14},{13,9},{14,10},{15,13... | collective-permute-start | bytes 491528 | tf_op jit(solution)/shard_map/ppermute | solution.py:278
  6.1 1.2 %collective-permute-start = (s32[4,10]{1,0:T(4,128)S(1)}, s32[4,10]{1,0:T(4,128)S(1)}, u32[]{:S(2)}, u32[]{:S(2)}) collective-permute-start(s32[4,10]{1,0:T(4,128)S(1)} %copy-done.1), channel_id=1, source_target_pairs={{0,1},{1,0},{2,3},{3,2},{4,5},{5,4},{6,7},{7,6},{8,9},{9,8},{10,11... | collective-permute-start | bytes 488 | tf_op jit(solution)/shard_map/ppermute | solution.py:261
  7.2 6.7 %collective-permute-start.2 = (bf16[656,128]{1,0:T(8,128)(2,1)S(1)}, bf16[656,128]{1,0:T(8,128)(2,1)S(1)}, u32[]{:S(2)}, u32[]{:S(2)}) collective-permute-start(bf16[656,128]{1,0:T(8,128)(2,1)S(1)} %get-tuple-element.17.refs_0_), channel_id=1, source_target_pairs={{0,2},{1,5},{4,0},{5,9},{8,4},{9,13},{12,8},{13,15},{14,12},{15,11... | collective-permute-start | bytes 503816 | tf_op jit(solution)/shard_map/ppermute | solution.py:278
  7.8 7.2 %collective-permute-start.5 = (bf16[656,128]{1,0:T(8,128)(2,1)S(1)}, bf16[656,128]{1,0:T(8,128)(2,1)S(1)}, u32[]{:S(2)}, u32[]{:S(2)}) collective-permute-start(bf16[656,128]{1,0:T(8,128)(2,1)S(1)} %collective-permute-done.4.refs_2_), channel_id=1, source_target_pairs={{0,4},{1,3},{4,8},{5,1},{8,12},{9,5},{12,14},{13,9},{14,10},{15,13... | collective-permute-start | bytes 503816 | tf_op jit(solution)/shard_map/ppermute | solution.py:278
  9.8 9.1 %collective-permute-start.10 = (bf16[640,128]{1,0:T(8,128)(2,1)S(1)}, bf16[640,128]{1,0:T(8,128)(2,1)S(1)}, u32[]{:S(2)}, u32[]{:S(2)}) collective-permute-start(bf16[640,128]{1,0:T(8,128)(2,1)S(1)} %get-tuple-element.20.refs_1_), channel_id=1, source_target_pairs={{0,2},{1,5},{4,0},{5,9},{8,4},{9,13},{12,8},{13,15},{14,12},{15,11... | collective-permute-start | bytes 491528 | tf_op jit(solution)/shard_map/ppermute | solution.py:278
  9.8 9.1 %collective-permute-start.8 = (bf16[640,128]{1,0:T(8,128)(2,1)S(1)}, bf16[640,128]{1,0:T(8,128)(2,1)S(1)}, u32[]{:S(2)}, u32[]{:S(2)}) collective-permute-start(bf16[640,128]{1,0:T(8,128)(2,1)S(1)} %collective-permute-done.7.refs_3_), channel_id=1, source_target_pairs={{0,4},{1,3},{4,8},{5,1},{8,12},{9,5},{12,14},{13,9},{14,10},{15,13... | collective-permute-start | bytes 491528 | tf_op jit(solution)/shard_map/ppermute | solution.py:278
  13.9 8.2 %collective-permute-start.3 = (bf16[656,128]{1,0:T(8,128)(2,1)S(1)}, bf16[656,128]{1,0:T(8,128)(2,1)S(1)}, u32[]{:S(2)}, u32[]{:S(2)}) collective-permute-start(bf16[656,128]{1,0:T(8,128)(2,1)S(1)} %collective-permute-done.2.refs_4_), channel_id=1, source_target_pairs={{0,2},{1,5},{4,0},{5,9},{8,4},{9,13},{12,8},{13,15},{14,12},{15,11... | collective-permute-start | bytes 503816 | tf_op jit(solution)/shard_map/ppermute | solution.py:278
  15.0 7.3 %collective-permute-start.6 = (bf16[656,128]{1,0:T(8,128)(2,1)S(1)}, bf16[656,128]{1,0:T(8,128)(2,1)S(1)}, u32[]{:S(2)}, u32[]{:S(2)}) collective-permute-start(bf16[656,128]{1,0:T(8,128)(2,1)S(1)} %collective-permute-done.5.refs_6_), channel_id=1, source_target_pairs={{0,4},{1,3},{4,8},{5,1},{8,12},{9,5},{12,14},{13,9},{14,10},{15,13... | collective-permute-start | bytes 503816 | tf_op jit(solution)/shard_map/ppermute | solution.py:278
  18.9 6.8 %collective-permute-start.11 = (bf16[640,128]{1,0:T(8,128)(2,1)S(1)}, bf16[640,128]{1,0:T(8,128)(2,1)S(1)}, u32[]{:S(2)}, u32[]{:S(2)}) collective-permute-start(bf16[640,128]{1,0:T(8,128)(2,1)S(1)} %collective-permute-done.10.refs_5_), channel_id=1, source_target_pairs={{0,2},{1,5},{4,0},{5,9},{8,4},{9,13},{12,8},{13,15},{14,12},{15,11... | collective-permute-start | bytes 491528 | tf_op jit(solution)/shard_map/ppermute | solution.py:278
  19.0 7.2 %collective-permute-start.9 = (bf16[640,128]{1,0:T(8,128)(2,1)S(1)}, bf16[640,128]{1,0:T(8,128)(2,1)S(1)}, u32[]{:S(2)}, u32[]{:S(2)}) collective-permute-start(bf16[640,128]{1,0:T(8,128)(2,1)S(1)} %collective-permute-done.8.refs_7_), channel_id=1, source_target_pairs={{0,4},{1,3},{4,8},{5,1},{8,12},{9,5},{12,14},{13,9},{14,10},{15,13... | collective-permute-start | bytes 491528 | tf_op jit(solution)/shard_map/ppermute | solution.py:278
  22.1 8.7 %collective-permute-start.12 = (bf16[656,128]{1,0:T(8,128)(2,1)S(1)}, bf16[656,128]{1,0:T(8,128)(2,1)S(1)}, u32[]{:S(2)}, u32[]{:S(2)}) collective-permute-start(bf16[656,128]{1,0:T(8,128)(2,1)S(1)} %collective-permute-done.3.refs_8_), channel_id=1, source_target_pairs={{0,2},{1,5},{4,0},{5,9},{8,4},{9,13},{12,8},{13,15},{14,12},{15,11... | collective-permute-start | bytes 503816 | tf_op jit(solution)/shard_map/ppermute | solution.py:278
  22.3 9.9 %collective-permute-start.14 = (bf16[656,128]{1,0:T(8,128)(2,1)S(1)}, bf16[656,128]{1,0:T(8,128)(2,1)S(1)}, u32[]{:S(2)}, u32[]{:S(2)}) collective-permute-start(bf16[656,128]{1,0:T(8,128)(2,1)S(1)} %collective-permute-done.6.refs_0_), channel_id=1, source_target_pairs={{0,4},{1,3},{4,8},{5,1},{8,12},{9,5},{12,14},{13,9},{14,10},{15,13... | collective-permute-start | bytes 503816 | tf_op jit(solution)/shard_map/ppermute | solution.py:278
  25.7 6.4 %collective-permute-start.13 = (bf16[640,128]{1,0:T(8,128)(2,1)S(1)}, bf16[640,128]{1,0:T(8,128)(2,1)S(1)}, u32[]{:S(2)}, u32[]{:S(2)}) collective-permute-start(bf16[640,128]{1,0:T(8,128)(2,1)S(1)} %collective-permute-done.11.refs_9_), channel_id=1, source_target_pairs={{0,2},{1,5},{4,0},{5,9},{8,4},{9,13},{12,8},{13,15},{14,12},{15,11... | collective-permute-start | bytes 491528 | tf_op jit(solution)/shard_map/ppermute | solution.py:278
  26.2 5.9 %collective-permute-start.15 = (bf16[640,128]{1,0:T(8,128)(2,1)S(1)}, bf16[640,128]{1,0:T(8,128)(2,1)S(1)}, u32[]{:S(2)}, u32[]{:S(2)}) collective-permute-start(bf16[640,128]{1,0:T(8,128)(2,1)S(1)} %collective-permute-done.9.refs_1_), channel_id=1, source_target_pairs={{0,4},{1,3},{4,8},{5,1},{8,12},{9,5},{12,14},{13,9},{14,10},{15,13... | collective-permute-start | bytes 491528 | tf_op jit(solution)/shard_map/ppermute | solution.py:278

commit v12 on v11

--- a/solution.py
+++ b/solution.py
@@ -271,7 +271,7 @@
             if (step, way) == (1, -1):
                 sent = [lax.optimization_barrier((part, others))[0] for part in sent]
             if (step, way) == (2, -1):
-                sent[-1], _ = lax.optimization_barrier((sent[-1], a))
+                sent[0], _ = lax.optimization_barrier((sent[0], a))
             if step > 2 and way == -1:
                 total = product(order, rounds.pop(0), a, total, total_shape)
                 sent[0], total = lax.optimization_barrier((sent[0], total))

time: 34.8 us -> 34.8 us (level)
  waiting for transfers between devices: 6.75 us -> 6.21 us
  starting transfers between devices: 18.3 us -> 18.8 us
    ppermute x14, starting transfers between devices: 18.3 us -> 18.8 us  [local(): held[way] = [lax.ppermute(part, ('row', 'col'), ring(way)) for part in sent]]
    ppermute x14, waiting for transfers between devices: 5.6 us -> 5.05 us  [local(): held[way] = [lax.ppermute(part, ('row', 'col'), ring(way)) for part in sent]]
  transfers between devices with their start and end apart: 16 -> 16, of which waited for: 7 -> 10; matrix products, arithmetic and copies ran while one was open for 0% -> 0% of each run, Pallas kernels for 16% -> 16%
where the time goes in v12:
time: 34.8 us; the launch traced here: 34.7 us
  starting transfers between devices  18.8 us (54%)
  Pallas kernels  9.55 us (27%)
  waiting for transfers between devices  6.21 us (18%)
    ppermute x14, starting transfers between devices, local(): held[way] = [lax.ppermute(part, ('row', 'col'), ring(way)) for part in sent]  18.8 us
    pallas_call x3, Pallas kernels, product(): pl.pallas_call(functools.partial(kernel, sources), out_shape=out, in_spec...  6.36 us
    ppermute x14, waiting for transfers between devices, local(): held[way] = [lax.ppermute(part, ('row', 'col'), ring(way)) for part in sent]  5.05 us
    pallas_call x1, Pallas kernels, dense_rows(): pl.pallas_call(dense_kernel, out_shape=jax.ShapeDtypeStruct((sources, row...  1.82 us
    pallas_call x1, Pallas kernels, pack(): pl.pallas_call(functools.partial(pack_kernel, half), out_shape=[jax.Shape...  1.37 us
    ppermute x2, waiting for transfers between devices, local(): a_other, others = (lax.ppermute(x, 'col', swap) for x in mine)  1.16 us
  transfers between devices with their start and end apart: 16, of which 10 were waited for; matrix products, arithmetic and copies ran while one was open for 0% of the time, Pallas kernels for 16%

profile of v12, /device:TPU:0, one launch (start us, length us, event | category | flops | bytes accessed | tf_op | source)
XLA Modules:
  0.0 34.7 jit_solution(1861582140827427268)
XLA Ops:
  0.0 0.0 copy-start
  0.0 1.4 %shard_map.37 = (bf16[656,128]{1,0:T(8,128)(2,1)S(1)}, bf16[640,128]{1,0:T(8,128)(2,1)S(1)}) custom-call(s32[4,10]{1,0:T(4,128)} %cols_hbm.3, bf16[4,10,64,64]{3,2,1,0:T(8,128)(2,1)} %b_hbm.1), custom_call_target="tpu_custom_call" | custom-call | bytes 655360 | tf_op jit(solution)/shard_map/pallas_call | solution.py:59
  1.4 0.0 copy-start.1
  1.4 3.1 %collective-permute-start.4 = (bf16[656,128]{1,0:T(8,128)(2,1)S(1)}, bf16[656,128]{1,0:T(8,128)(2,1)S(1)}, u32[]{:S(2)}, u32[]{:S(2)}) collective-permute-start(bf16[656,128]{1,0:T(8,128)(2,1)S(1)} %get-tuple-element.17.refs_0_), channel_id=1, source_target_pairs={{0,4},{1,3},{4,8},{5,1},{8,12},{9,5},{12,14},{13,9},{14,10},{15,13... | collective-permute-start | bytes 503816 | tf_op jit(solution)/shard_map/ppermute | solution.py:278
  4.5 0.0 copy-done
  4.5 0.0 collective-permute-start.1
  4.5 1.6 %collective-permute-start.7 = (bf16[640,128]{1,0:T(8,128)(2,1)S(1)}, bf16[640,128]{1,0:T(8,128)(2,1)S(1)}, u32[]{:S(2)}, u32[]{:S(2)}) collective-permute-start(bf16[640,128]{1,0:T(8,128)(2,1)S(1)} %get-tuple-element.21.refs_1_), channel_id=1, source_target_pairs={{0,4},{1,3},{4,8},{5,1},{8,12},{9,5},{12,14},{13,9},{14,10},{15,13... | collective-permute-start | bytes 491528 | tf_op jit(solution)/shard_map/ppermute | solution.py:278
  6.1 0.0 copy-done.1
  6.1 0.0 collective-permute-start
  6.1 1.2 %collective-permute-done.others_ref = s32[4,10]{1,0:T(4,128)S(1)} collective-permute-done((s32[4,10]{1,0:T(4,128)S(1)}, s32[4,10]{1,0:T(4,128)S(1)}, u32[]{:S(2)}, u32[]{:S(2)}) %collective-permute-start) | collective-permute-done | bytes 192 | tf_op jit(solution)/shard_map/ppermute | solution.py:261
  7.2 0.5 %collective-permute-start.2 = (bf16[656,128]{1,0:T(8,128)(2,1)S(1)}, bf16[656,128]{1,0:T(8,128)(2,1)S(1)}, u32[]{:S(2)}, u32[]{:S(2)}) collective-permute-start(bf16[656,128]{1,0:T(8,128)(2,1)S(1)} %get-tuple-element.17.refs_0_), channel_id=1, source_target_pairs={{0,2},{1,5},{4,0},{5,9},{8,4},{9,13},{12,8},{13,15},{14,12},{15,11... | collective-permute-start | bytes 503816 | tf_op jit(solution)/shard_map/ppermute | solution.py:278
  7.7 0.1 collective-permute-done.4.refs_2_
  7.8 2.1 %collective-permute-start.5 = (bf16[656,128]{1,0:T(8,128)(2,1)S(1)}, bf16[656,128]{1,0:T(8,128)(2,1)S(1)}, u32[]{:S(2)}, u32[]{:S(2)}) collective-permute-start(bf16[656,128]{1,0:T(8,128)(2,1)S(1)} %collective-permute-done.4.refs_2_), channel_id=1, source_target_pairs={{0,4},{1,3},{4,8},{5,1},{8,12},{9,5},{12,14},{13,9},{14,10},{15,13... | collective-permute-start | bytes 503816 | tf_op jit(solution)/shard_map/ppermute | solution.py:278
  9.8 0.0 collective-permute-start.10
  9.8 0.0 collective-permute-done.7.refs_3_
  9.8 2.0 %collective-permute-start.8 = (bf16[640,128]{1,0:T(8,128)(2,1)S(1)}, bf16[640,128]{1,0:T(8,128)(2,1)S(1)}, u32[]{:S(2)}, u32[]{:S(2)}) collective-permute-start(bf16[640,128]{1,0:T(8,128)(2,1)S(1)} %collective-permute-done.7.refs_3_), channel_id=1, source_target_pairs={{0,4},{1,3},{4,8},{5,1},{8,12},{9,5},{12,14},{13,9},{14,10},{15,13... | collective-permute-start | bytes 491528 | tf_op jit(solution)/shard_map/ppermute | solution.py:278
  11.9 0.0 collective-permute-done.1.other_ref
  11.9 1.8 %shard_map.38.a_ref = bf16[8,2,256,128]{3,2,1,0:T(8,128)(2,1)S(1)} custom-call(s32[4,10]{1,0:T(4,128)S(1)} %copy-done.1, s32[4,10]{1,0:T(4,128)S(1)} %collective-permute-done.others_ref, bf16[4,10,64,64]{3,2,1,0:T(8,128)(2,1)S(1)} %copy-done, bf16[4,10,64,64]{3,2,1,0:T(8,128)(2,1)S(1)} %collective-permute-done.1.other_ref), custom_call_target="tpu_custom_call" | custom-call | bytes 1310720 | tf_op jit(solution)/shard_map/pallas_call | solution.py:105
  13.7 0.2 collective-permute-done.2.refs_4_
  13.9 0.5 %collective-permute-start.3 = (bf16[656,128]{1,0:T(8,128)(2,1)S(1)}, bf16[656,128]{1,0:T(8,128)(2,1)S(1)}, u32[]{:S(2)}, u32[]{:S(2)}) collective-permute-start(bf16[656,128]{1,0:T(8,128)(2,1)S(1)} %collective-permute-done.2.refs_4_), channel_id=1, source_target_pairs={{0,2},{1,5},{4,0},{5,9},{8,4},{9,13},{12,8},{13,15},{14,12},{15,11... | collective-permute-start | bytes 503816 | tf_op jit(solution)/shard_map/ppermute | solution.py:278
  14.4 0.6 %collective-permute-done.5.refs_6_ = bf16[656,128]{1,0:T(8,128)(2,1)S(1)} collective-permute-done((bf16[656,128]{1,0:T(8,128)(2,1)S(1)}, bf16[656,128]{1,0:T(8,128)(2,1)S(1)}, u32[]{:S(2)}, u32[]{:S(2)}) %collective-permute-start.5) | collective-permute-done | bytes 167968 | tf_op jit(solution)/shard_map/ppermute | solution.py:278
  15.0 2.1 %collective-permute-start.6 = (bf16[656,128]{1,0:T(8,128)(2,1)S(1)}, bf16[656,128]{1,0:T(8,128)(2,1)S(1)}, u32[]{:S(2)}, u32[]{:S(2)}) collective-permute-start(bf16[656,128]{1,0:T(8,128)(2,1)S(1)} %collective-permute-done.5.refs_6_), channel_id=1, source_target_pairs={{0,4},{1,3},{4,8},{5,1},{8,12},{9,5},{12,14},{13,9},{14,10},{15,13... | collective-permute-start | bytes 503816 | tf_op jit(solution)/shard_map/ppermute | solution.py:278
  17.1 0.4 %collective-permute-done.10.refs_5_ = bf16[640,128]{1,0:T(8,128)(2,1)S(1)} collective-permute-done((bf16[640,128]{1,0:T(8,128)(2,1)S(1)}, bf16[640,128]{1,0:T(8,128)(2,1)S(1)}, u32[]{:S(2)}, u32[]{:S(2)}) %collective-permute-start.10) | collective-permute-done | bytes 163872 | tf_op jit(solution)/shard_map/ppermute | solution.py:278
  17.4 0.5 %collective-permute-start.11 = (bf16[640,128]{1,0:T(8,128)(2,1)S(1)}, bf16[640,128]{1,0:T(8,128)(2,1)S(1)}, u32[]{:S(2)}, u32[]{:S(2)}) collective-permute-start(bf16[640,128]{1,0:T(8,128)(2,1)S(1)} %collective-permute-done.10.refs_5_), channel_id=1, source_target_pairs={{0,2},{1,5},{4,0},{5,9},{8,4},{9,13},{12,8},{13,15},{14,12},{15,11... | collective-permute-start | bytes 491528 | tf_op jit(solution)/shard_map/ppermute | solution.py:278
  17.9 0.6 %collective-permute-done.8.refs_7_ = bf16[640,128]{1,0:T(8,128)(2,1)S(1)} collective-permute-done((bf16[640,128]{1,0:T(8,128)(2,1)S(1)}, bf16[640,128]{1,0:T(8,128)(2,1)S(1)}, u32[]{:S(2)}, u32[]{:S(2)}) %collective-permute-start.8) | collective-permute-done | bytes 163872 | tf_op jit(solution)/shard_map/ppermute | solution.py:278
  18.5 2.1 %collective-permute-start.9 = (bf16[640,128]{1,0:T(8,128)(2,1)S(1)}, bf16[640,128]{1,0:T(8,128)(2,1)S(1)}, u32[]{:S(2)}, u32[]{:S(2)}) collective-permute-start(bf16[640,128]{1,0:T(8,128)(2,1)S(1)} %collective-permute-done.8.refs_7_), channel_id=1, source_target_pairs={{0,4},{1,3},{4,8},{5,1},{8,12},{9,5},{12,14},{13,9},{14,10},{15,13... | collective-permute-start | bytes 491528 | tf_op jit(solution)/shard_map/ppermute | solution.py:278
  20.6 1.1 %shard_map.39.before = f32[4,2,256,128]{3,2,1,0:T(8,128)S(1)} custom-call(bf16[8,2,256,128]{3,2,1,0:T(8,128)(2,1)S(1)} %shard_map.38.a_ref, bf16[656,128]{1,0:T(8,128)(2,1)S(1)} %get-tuple-element.17.refs_0_, bf16[640,128]{1,0:T(8,128)(2,1)S(1)} %get-tuple-element.21.refs_1_), custom_call_target="tpu_custom_call" | custom-call | flops 134217728 | tf_op jit(solution)/shard_map/pallas_call | solution.py:233
  21.7 0.0 collective-permute-done.3.refs_8_
  21.7 0.1 collective-permute-start.12
  21.8 0.4 %collective-permute-done.6.refs_0_ = bf16[656,128]{1,0:T(8,128)(2,1)S(1)} collective-permute-done((bf16[656,128]{1,0:T(8,128)(2,1)S(1)}, bf16[656,128]{1,0:T(8,128)(2,1)S(1)}, u32[]{:S(2)}, u32[]{:S(2)}) %collective-permute-start.6) | collective-permute-done | bytes 167968 | tf_op jit(solution)/shard_map/ppermute | solution.py:278
  22.2 2.0 %collective-permute-start.14 = (bf16[656,128]{1,0:T(8,128)(2,1)S(1)}, bf16[656,128]{1,0:T(8,128)(2,1)S(1)}, u32[]{:S(2)}, u32[]{:S(2)}) collective-permute-start(bf16[656,128]{1,0:T(8,128)(2,1)S(1)} %collective-permute-done.6.refs_0_), channel_id=1, source_target_pairs={{0,4},{1,3},{4,8},{5,1},{8,12},{9,5},{12,14},{13,9},{14,10},{15,13... | collective-permute-start | bytes 503816 | tf_op jit(solution)/shard_map/ppermute | solution.py:278
  24.2 0.5 %collective-permute-done.11.refs_9_ = bf16[640,128]{1,0:T(8,128)(2,1)S(1)} collective-permute-done((bf16[640,128]{1,0:T(8,128)(2,1)S(1)}, bf16[640,128]{1,0:T(8,128)(2,1)S(1)}, u32[]{:S(2)}, u32[]{:S(2)}) %collective-permute-start.11) | collective-permute-done | bytes 163872 | tf_op jit(solution)/shard_map/ppermute | solution.py:278
  24.7 0.5 %collective-permute-start.13 = (bf16[640,128]{1,0:T(8,128)(2,1)S(1)}, bf16[640,128]{1,0:T(8,128)(2,1)S(1)}, u32[]{:S(2)}, u32[]{:S(2)}) collective-permute-start(bf16[640,128]{1,0:T(8,128)(2,1)S(1)} %collective-permute-done.11.refs_9_), channel_id=1, source_target_pairs={{0,2},{1,5},{4,0},{5,9},{8,4},{9,13},{12,8},{13,15},{14,12},{15,11... | collective-permute-start | bytes 491528 | tf_op jit(solution)/shard_map/ppermute | solution.py:278
  25.1 0.6 %collective-permute-done.9.refs_1_ = bf16[640,128]{1,0:T(8,128)(2,1)S(1)} collective-permute-done((bf16[640,128]{1,0:T(8,128)(2,1)S(1)}, bf16[640,128]{1,0:T(8,128)(2,1)S(1)}, u32[]{:S(2)}, u32[]{:S(2)}) %collective-permute-start.9) | collective-permute-done | bytes 163872 | tf_op jit(solution)/shard_map/ppermute | solution.py:278
  25.7 2.0 %collective-permute-start.15 = (bf16[640,128]{1,0:T(8,128)(2,1)S(1)}, bf16[640,128]{1,0:T(8,128)(2,1)S(1)}, u32[]{:S(2)}, u32[]{:S(2)}) collective-permute-start(bf16[640,128]{1,0:T(8,128)(2,1)S(1)} %collective-permute-done.9.refs_1_), channel_id=1, source_target_pairs={{0,4},{1,3},{4,8},{5,1},{8,12},{9,5},{12,14},{13,9},{14,10},{15,13... | collective-permute-start | bytes 491528 | tf_op jit(solution)/shard_map/ppermute | solution.py:278
  27.7 2.7 %shard_map.40.total = f32[4,2,256,128]{3,2,1,0:T(8,128)S(1)} custom-call(bf16[8,2,256,128]{3,2,1,0:T(8,128)(2,1)S(1)} %shard_map.38.a_ref, f32[4,2,256,128]{3,2,1,0:T(8,128)S(1)} %shard_map.39.before, bf16[656,128]{1,0:T(8,128)(2,1)S(1)} %collective-permute-done.6.refs_0_, ...), custom_call_target="tpu_custom_call", output_to_operand_aliasing={{}: (1, {})} | custom-call | flops 671088640 | tf_op jit(solution)/shard_map/pallas_call | solution.py:233
  30.4 1.7 %collective-permute-done.13.refs_1_ = bf16[640,128]{1,0:T(8,128)(2,1)S(1)} collective-permute-done((bf16[640,128]{1,0:T(8,128)(2,1)S(1)}, bf16[640,128]{1,0:T(8,128)(2,1)S(1)}, u32[]{:S(2)}, u32[]{:S(2)}) %collective-permute-start.13) | collective-permute-done | bytes 163872 | tf_op jit(solution)/shard_map/ppermute | solution.py:278
  32.1 0.0 collective-permute-done.15.refs_3_
  32.1 0.0 collective-permute-done.12.refs_0_
  32.1 0.0 collective-permute-done.14.refs_2_
  32.1 2.6 %shard_map.41 = bf16[4,10,64,64]{3,2,1,0:T(8,128)(2,1)} custom-call(bf16[8,2,256,128]{3,2,1,0:T(8,128)(2,1)S(1)} %shard_map.38.a_ref, f32[4,2,256,128]{3,2,1,0:T(8,128)S(1)} %shard_map.40.total, s32[4,10]{1,0:T(4,128)S(1)} %copy-done.1, bf16[656,128]{1,0:T(8,128)(2,1)S(1)} %collective-permute-done.12.refs_0_, ...), custom_call_target="tpu_custom_call" | custom-call | flops 167772160 | tf_op jit(solution)/shard_map/pallas_call | solution.py:233
Async XLA Ops:
  0.0 4.5 %copy-start = (bf16[4,10,64,64]{3,2,1,0:T(8,128)(2,1)S(1)}, bf16[4,10,64,64]{3,2,1,0:T(8,128)(2,1)}, u32[]{:S(2)}) copy-start(bf16[4,10,64,64]{3,2,1,0:T(8,128)(2,1)} %own_ref.1) | copy-start | bytes 983044
  1.4 4.7 %copy-start.1 = (s32[4,10]{1,0:T(4,128)S(1)}, s32[4,10]{1,0:T(4,128)}, u32[]{:S(2)}) copy-start(s32[4,10]{1,0:T(4,128)} %cols_hbm.3) | copy-start | bytes 484
  1.4 6.4 %collective-permute-start.4 = (bf16[656,128]{1,0:T(8,128)(2,1)S(1)}, bf16[656,128]{1,0:T(8,128)(2,1)S(1)}, u32[]{:S(2)}, u32[]{:S(2)}) collective-permute-start(bf16[656,128]{1,0:T(8,128)(2,1)S(1)} %get-tuple-element.17.refs_0_), channel_id=1, source_target_pairs={{0,4},{1,3},{4,8},{5,1},{8,12},{9,5},{12,14},{13,9},{14,10},{15,13... | collective-permute-start | bytes 503816 | tf_op jit(solution)/shard_map/ppermute | solution.py:278
  4.5 7.4 %collective-permute-start.1 = (bf16[4,10,64,64]{3,2,1,0:T(8,128)(2,1)S(1)}, bf16[4,10,64,64]{3,2,1,0:T(8,128)(2,1)S(1)}, u32[]{:S(2)}, u32[]{:S(2)}) collective-permute-start(bf16[4,10,64,64]{3,2,1,0:T(8,128)(2,1)S(1)} %copy-done), channel_id=1, source_target_pairs={{0,1},{1,0},{2,3},{3,2},{4,5},{5,4},{6,7},{7,6},{8,9},{9,8},{10,11... | collective-permute-start | bytes 983048 | tf_op jit(solution)/shard_map/ppermute | solution.py:261
  4.5 5.4 %collective-permute-start.7 = (bf16[640,128]{1,0:T(8,128)(2,1)S(1)}, bf16[640,128]{1,0:T(8,128)(2,1)S(1)}, u32[]{:S(2)}, u32[]{:S(2)}) collective-permute-start(bf16[640,128]{1,0:T(8,128)(2,1)S(1)} %get-tuple-element.21.refs_1_), channel_id=1, source_target_pairs={{0,4},{1,3},{4,8},{5,1},{8,12},{9,5},{12,14},{13,9},{14,10},{15,13... | collective-permute-start | bytes 491528 | tf_op jit(solution)/shard_map/ppermute | solution.py:278
  6.1 1.2 %collective-permute-start = (s32[4,10]{1,0:T(4,128)S(1)}, s32[4,10]{1,0:T(4,128)S(1)}, u32[]{:S(2)}, u32[]{:S(2)}) collective-permute-start(s32[4,10]{1,0:T(4,128)S(1)} %copy-done.1), channel_id=1, source_target_pairs={{0,1},{1,0},{2,3},{3,2},{4,5},{5,4},{6,7},{7,6},{8,9},{9,8},{10,11... | collective-permute-start | bytes 488 | tf_op jit(solution)/shard_map/ppermute | solution.py:261
  7.2 6.7 %collective-permute-start.2 = (bf16[656,128]{1,0:T(8,128)(2,1)S(1)}, bf16[656,128]{1,0:T(8,128)(2,1)S(1)}, u32[]{:S(2)}, u32[]{:S(2)}) collective-permute-start(bf16[656,128]{1,0:T(8,128)(2,1)S(1)} %get-tuple-element.17.refs_0_), channel_id=1, source_target_pairs={{0,2},{1,5},{4,0},{5,9},{8,4},{9,13},{12,8},{13,15},{14,12},{15,11... | collective-permute-start | bytes 503816 | tf_op jit(solution)/shard_map/ppermute | solution.py:278
  7.8 7.2 %collective-permute-start.5 = (bf16[656,128]{1,0:T(8,128)(2,1)S(1)}, bf16[656,128]{1,0:T(8,128)(2,1)S(1)}, u32[]{:S(2)}, u32[]{:S(2)}) collective-permute-start(bf16[656,128]{1,0:T(8,128)(2,1)S(1)} %collective-permute-done.4.refs_2_), channel_id=1, source_target_pairs={{0,4},{1,3},{4,8},{5,1},{8,12},{9,5},{12,14},{13,9},{14,10},{15,13... | collective-permute-start | bytes 503816 | tf_op jit(solution)/shard_map/ppermute | solution.py:278
  9.8 7.6 %collective-permute-start.10 = (bf16[640,128]{1,0:T(8,128)(2,1)S(1)}, bf16[640,128]{1,0:T(8,128)(2,1)S(1)}, u32[]{:S(2)}, u32[]{:S(2)}) collective-permute-start(bf16[640,128]{1,0:T(8,128)(2,1)S(1)} %get-tuple-element.21.refs_1_), channel_id=1, source_target_pairs={{0,2},{1,5},{4,0},{5,9},{8,4},{9,13},{12,8},{13,15},{14,12},{15,11... | collective-permute-start | bytes 491528 | tf_op jit(solution)/shard_map/ppermute | solution.py:278
  9.8 8.6 %collective-permute-start.8 = (bf16[640,128]{1,0:T(8,128)(2,1)S(1)}, bf16[640,128]{1,0:T(8,128)(2,1)S(1)}, u32[]{:S(2)}, u32[]{:S(2)}) collective-permute-start(bf16[640,128]{1,0:T(8,128)(2,1)S(1)} %collective-permute-done.7.refs_3_), channel_id=1, source_target_pairs={{0,4},{1,3},{4,8},{5,1},{8,12},{9,5},{12,14},{13,9},{14,10},{15,13... | collective-permute-start | bytes 491528 | tf_op jit(solution)/shard_map/ppermute | solution.py:278
  13.9 7.8 %collective-permute-start.3 = (bf16[656,128]{1,0:T(8,128)(2,1)S(1)}, bf16[656,128]{1,0:T(8,128)(2,1)S(1)}, u32[]{:S(2)}, u32[]{:S(2)}) collective-permute-start(bf16[656,128]{1,0:T(8,128)(2,1)S(1)} %collective-permute-done.2.refs_4_), channel_id=1, source_target_pairs={{0,2},{1,5},{4,0},{5,9},{8,4},{9,13},{12,8},{13,15},{14,12},{15,11... | collective-permute-start | bytes 503816 | tf_op jit(solution)/shard_map/ppermute | solution.py:278
  15.0 7.2 %collective-permute-start.6 = (bf16[656,128]{1,0:T(8,128)(2,1)S(1)}, bf16[656,128]{1,0:T(8,128)(2,1)S(1)}, u32[]{:S(2)}, u32[]{:S(2)}) collective-permute-start(bf16[656,128]{1,0:T(8,128)(2,1)S(1)} %collective-permute-done.5.refs_6_), channel_id=1, source_target_pairs={{0,4},{1,3},{4,8},{5,1},{8,12},{9,5},{12,14},{13,9},{14,10},{15,13... | collective-permute-start | bytes 503816 | tf_op jit(solution)/shard_map/ppermute | solution.py:278
  17.4 7.2 %collective-permute-start.11 = (bf16[640,128]{1,0:T(8,128)(2,1)S(1)}, bf16[640,128]{1,0:T(8,128)(2,1)S(1)}, u32[]{:S(2)}, u32[]{:S(2)}) collective-permute-start(bf16[640,128]{1,0:T(8,128)(2,1)S(1)} %collective-permute-done.10.refs_5_), channel_id=1, source_target_pairs={{0,2},{1,5},{4,0},{5,9},{8,4},{9,13},{12,8},{13,15},{14,12},{15,11... | collective-permute-start | bytes 491528 | tf_op jit(solution)/shard_map/ppermute | solution.py:278
  18.5 7.2 %collective-permute-start.9 = (bf16[640,128]{1,0:T(8,128)(2,1)S(1)}, bf16[640,128]{1,0:T(8,128)(2,1)S(1)}, u32[]{:S(2)}, u32[]{:S(2)}) collective-permute-start(bf16[640,128]{1,0:T(8,128)(2,1)S(1)} %collective-permute-done.8.refs_7_), channel_id=1, source_target_pairs={{0,4},{1,3},{4,8},{5,1},{8,12},{9,5},{12,14},{13,9},{14,10},{15,13... | collective-permute-start | bytes 491528 | tf_op jit(solution)/shard_map/ppermute | solution.py:278
  21.7 10.4 %collective-permute-start.12 = (bf16[656,128]{1,0:T(8,128)(2,1)S(1)}, bf16[656,128]{1,0:T(8,128)(2,1)S(1)}, u32[]{:S(2)}, u32[]{:S(2)}) collective-permute-start(bf16[656,128]{1,0:T(8,128)(2,1)S(1)} %collective-permute-done.3.refs_8_), channel_id=1, source_target_pairs={{0,2},{1,5},{4,0},{5,9},{8,4},{9,13},{12,8},{13,15},{14,12},{15,11... | collective-permute-start | bytes 503816 | tf_op jit(solution)/shard_map/ppermute | solution.py:278
  22.2 9.9 %collective-permute-start.14 = (bf16[656,128]{1,0:T(8,128)(2,1)S(1)}, bf16[656,128]{1,0:T(8,128)(2,1)S(1)}, u32[]{:S(2)}, u32[]{:S(2)}) collective-permute-start(bf16[656,128]{1,0:T(8,128)(2,1)S(1)} %collective-permute-done.6.refs_0_), channel_id=1, source_target_pairs={{0,4},{1,3},{4,8},{5,1},{8,12},{9,5},{12,14},{13,9},{14,10},{15,13... | collective-permute-start | bytes 503816 | tf_op jit(solution)/shard_map/ppermute | solution.py:278
  24.7 7.4 %collective-permute-start.13 = (bf16[640,128]{1,0:T(8,128)(2,1)S(1)}, bf16[640,128]{1,0:T(8,128)(2,1)S(1)}, u32[]{:S(2)}, u32[]{:S(2)}) collective-permute-start(bf16[640,128]{1,0:T(8,128)(2,1)S(1)} %collective-permute-done.11.refs_9_), channel_id=1, source_target_pairs={{0,2},{1,5},{4,0},{5,9},{8,4},{9,13},{12,8},{13,15},{14,12},{15,11... | collective-permute-start | bytes 491528 | tf_op jit(solution)/shard_map/ppermute | solution.py:278
  25.7 6.4 %collective-permute-start.15 = (bf16[640,128]{1,0:T(8,128)(2,1)S(1)}, bf16[640,128]{1,0:T(8,128)(2,1)S(1)}, u32[]{:S(2)}, u32[]{:S(2)}) collective-permute-start(bf16[640,128]{1,0:T(8,128)(2,1)S(1)} %collective-permute-done.9.refs_1_), channel_id=1, source_target_pairs={{0,4},{1,3},{4,8},{5,1},{8,12},{9,5},{12,14},{13,9},{14,10},{15,13... | collective-permute-start | bytes 491528 | tf_op jit(solution)/shard_map/ppermute | solution.py:278

commit v13 on v12

--- a/solution.py
+++ b/solution.py
@@ -268,8 +268,6 @@
         ways = [way for way in hops if step <= hops[way]]
         for way in ways:
             sent = list(held[way])
-            if (step, way) == (1, -1):
-                sent = [lax.optimization_barrier((part, others))[0] for part in sent]
             if (step, way) == (2, -1):
                 sent[0], _ = lax.optimization_barrier((sent[0], a))
             if step > 2 and way == -1:

time: 34.8 us -> 35.8 us (1.029)
  waiting for transfers between devices: 6.21 us -> 8.41 us
  starting transfers between devices: 18.8 us -> 17.6 us
    ppermute x14, waiting for transfers between devices: 5.05 us -> 7.25 us  [local(): held[way] = [lax.ppermute(part, ('row', 'col'), ring(way)) for part in sent]]
    ppermute x14, starting transfers between devices: 18.8 us -> 17.6 us  [local(): held[way] = [lax.ppermute(part, ('row', 'col'), ring(way)) for part in sent]]
  transfers between devices with their start and end apart: 16 -> 16, of which waited for: 10 -> 8; matrix products, arithmetic and copies ran while one was open for 0% -> 0% of each run, Pallas kernels for 16% -> 16%
where the time goes in v13:
time: 35.8 us; the launch traced here: 35.7 us
  starting transfers between devices  17.6 us (49%)
  Pallas kernels  9.56 us (27%)
  waiting for transfers between devices  8.41 us (23%)
    ppermute x14, starting transfers between devices, local(): held[way] = [lax.ppermute(part, ('row', 'col'), ring(way)) for part in sent]  17.6 us
    ppermute x14, waiting for transfers between devices, local(): held[way] = [lax.ppermute(part, ('row', 'col'), ring(way)) for part in sent]  7.25 us
    pallas_call x3, Pallas kernels, product(): pl.pallas_call(functools.partial(kernel, sources), out_shape=out, in_spec...  6.37 us
    pallas_call x1, Pallas kernels, dense_rows(): pl.pallas_call(dense_kernel, out_shape=jax.ShapeDtypeStruct((sources, row...  1.82 us
    pallas_call x1, Pallas kernels, pack(): pl.pallas_call(functools.partial(pack_kernel, half), out_shape=[jax.Shape...  1.37 us
    ppermute x2, waiting for transfers between devices, local(): a_other, others = (lax.ppermute(x, 'col', swap) for x in mine)  1.16 us
  transfers between devices with their start and end apart: 16, of which 8 were waited for; matrix products, arithmetic and copies ran while one was open for 0% of the time, Pallas kernels for 16%

profile of v13, /device:TPU:0, one launch (start us, length us, event | category | flops | bytes accessed | tf_op | source)
XLA Modules:
  0.0 35.7 jit_solution(8534875745273025953)
XLA Ops:
  0.0 0.0 copy-start
  0.0 1.4 %shard_map.37 = (bf16[656,128]{1,0:T(8,128)(2,1)S(1)}, bf16[640,128]{1,0:T(8,128)(2,1)S(1)}) custom-call(s32[4,10]{1,0:T(4,128)} %cols_hbm.3, bf16[4,10,64,64]{3,2,1,0:T(8,128)(2,1)} %b_hbm.1), custom_call_target="tpu_custom_call" | custom-call | bytes 655360 | tf_op jit(solution)/shard_map/pallas_call | solution.py:59
  1.4 0.0 copy-start.1
  1.4 3.1 %collective-permute-start.4 = (bf16[656,128]{1,0:T(8,128)(2,1)S(1)}, bf16[656,128]{1,0:T(8,128)(2,1)S(1)}, u32[]{:S(2)}, u32[]{:S(2)}) collective-permute-start(bf16[656,128]{1,0:T(8,128)(2,1)S(1)} %get-tuple-element.12.refs_0_), channel_id=1, source_target_pairs={{0,4},{1,3},{4,8},{5,1},{8,12},{9,5},{12,14},{13,9},{14,10},{15,13... | collective-permute-start | bytes 503816 | tf_op jit(solution)/shard_map/ppermute | solution.py:276
  4.5 0.0 copy-done
  4.5 0.0 collective-permute-start.1
  4.5 1.6 %collective-permute-start.7 = (bf16[640,128]{1,0:T(8,128)(2,1)S(1)}, bf16[640,128]{1,0:T(8,128)(2,1)S(1)}, u32[]{:S(2)}, u32[]{:S(2)}) collective-permute-start(bf16[640,128]{1,0:T(8,128)(2,1)S(1)} %get-tuple-element.16.refs_1_), channel_id=1, source_target_pairs={{0,4},{1,3},{4,8},{5,1},{8,12},{9,5},{12,14},{13,9},{14,10},{15,13... | collective-permute-start | bytes 491528 | tf_op jit(solution)/shard_map/ppermute | solution.py:276
  6.1 0.4 %collective-permute-start.2 = (bf16[656,128]{1,0:T(8,128)(2,1)S(1)}, bf16[656,128]{1,0:T(8,128)(2,1)S(1)}, u32[]{:S(2)}, u32[]{:S(2)}) collective-permute-start(bf16[656,128]{1,0:T(8,128)(2,1)S(1)} %get-tuple-element.12.refs_0_), channel_id=1, source_target_pairs={{0,2},{1,5},{4,0},{5,9},{8,4},{9,13},{12,8},{13,15},{14,12},{15,11... | collective-permute-start | bytes 503816 | tf_op jit(solution)/shard_map/ppermute | solution.py:276
  6.5 1.3 %collective-permute-done.4.refs_2_ = bf16[656,128]{1,0:T(8,128)(2,1)S(1)} collective-permute-done((bf16[656,128]{1,0:T(8,128)(2,1)S(1)}, bf16[656,128]{1,0:T(8,128)(2,1)S(1)}, u32[]{:S(2)}, u32[]{:S(2)}) %collective-permute-start.4) | collective-permute-done | bytes 167968 | tf_op jit(solution)/shard_map/ppermute | solution.py:276
  7.8 2.5 %collective-permute-start.5 = (bf16[656,128]{1,0:T(8,128)(2,1)S(1)}, bf16[656,128]{1,0:T(8,128)(2,1)S(1)}, u32[]{:S(2)}, u32[]{:S(2)}) collective-permute-start(bf16[656,128]{1,0:T(8,128)(2,1)S(1)} %collective-permute-done.4.refs_2_), channel_id=1, source_target_pairs={{0,4},{1,3},{4,8},{5,1},{8,12},{9,5},{12,14},{13,9},{14,10},{15,13... | collective-permute-start | bytes 503816 | tf_op jit(solution)/shard_map/ppermute | solution.py:276
  10.3 0.0 copy-done.1
  10.3 0.0 collective-permute-start
  10.3 1.2 %collective-permute-done.others_ref = s32[4,10]{1,0:T(4,128)S(1)} collective-permute-done((s32[4,10]{1,0:T(4,128)S(1)}, s32[4,10]{1,0:T(4,128)S(1)}, u32[]{:S(2)}, u32[]{:S(2)}) %collective-permute-start) | collective-permute-done | bytes 192 | tf_op jit(solution)/shard_map/ppermute | solution.py:261
  11.5 0.0 collective-permute-start.10
  11.5 0.0 collective-permute-done.7.refs_3_
  11.5 2.0 %collective-permute-start.8 = (bf16[640,128]{1,0:T(8,128)(2,1)S(1)}, bf16[640,128]{1,0:T(8,128)(2,1)S(1)}, u32[]{:S(2)}, u32[]{:S(2)}) collective-permute-start(bf16[640,128]{1,0:T(8,128)(2,1)S(1)} %collective-permute-done.7.refs_3_), channel_id=1, source_target_pairs={{0,4},{1,3},{4,8},{5,1},{8,12},{9,5},{12,14},{13,9},{14,10},{15,13... | collective-permute-start | bytes 491528 | tf_op jit(solution)/shard_map/ppermute | solution.py:276
  13.5 0.0 collective-permute-done.1.other_ref
  13.5 1.8 %shard_map.38.a_ref = bf16[8,2,256,128]{3,2,1,0:T(8,128)(2,1)S(1)} custom-call(s32[4,10]{1,0:T(4,128)S(1)} %copy-done.1, s32[4,10]{1,0:T(4,128)S(1)} %collective-permute-done.others_ref, bf16[4,10,64,64]{3,2,1,0:T(8,128)(2,1)S(1)} %copy-done, bf16[4,10,64,64]{3,2,1,0:T(8,128)(2,1)S(1)} %collective-permute-done.1.other_ref), custom_call_target="tpu_custom_call" | custom-call | bytes 1310720 | tf_op jit(solution)/shard_map/pallas_call | solution.py:105
  15.3 0.0 collective-permute-done.2.refs_4_
  15.3 0.1 collective-permute-start.3
  15.4 0.0 collective-permute-done.5.refs_6_
  15.4 2.0 %collective-permute-start.6 = (bf16[656,128]{1,0:T(8,128)(2,1)S(1)}, bf16[656,128]{1,0:T(8,128)(2,1)S(1)}, u32[]{:S(2)}, u32[]{:S(2)}) collective-permute-start(bf16[656,128]{1,0:T(8,128)(2,1)S(1)} %collective-permute-done.5.refs_6_), channel_id=1, source_target_pairs={{0,4},{1,3},{4,8},{5,1},{8,12},{9,5},{12,14},{13,9},{14,10},{15,13... | collective-permute-start | bytes 503816 | tf_op jit(solution)/shard_map/ppermute | solution.py:276
  17.4 0.7 %collective-permute-done.10.refs_5_ = bf16[640,128]{1,0:T(8,128)(2,1)S(1)} collective-permute-done((bf16[640,128]{1,0:T(8,128)(2,1)S(1)}, bf16[640,128]{1,0:T(8,128)(2,1)S(1)}, u32[]{:S(2)}, u32[]{:S(2)}) %collective-permute-start.10) | collective-permute-done | bytes 163872 | tf_op jit(solution)/shard_map/ppermute | solution.py:276
  18.1 0.0 collective-permute-start.11
  18.1 0.0 collective-permute-done.8.refs_7_
  18.1 2.0 %collective-permute-start.9 = (bf16[640,128]{1,0:T(8,128)(2,1)S(1)}, bf16[640,128]{1,0:T(8,128)(2,1)S(1)}, u32[]{:S(2)}, u32[]{:S(2)}) collective-permute-start(bf16[640,128]{1,0:T(8,128)(2,1)S(1)} %collective-permute-done.8.refs_7_), channel_id=1, source_target_pairs={{0,4},{1,3},{4,8},{5,1},{8,12},{9,5},{12,14},{13,9},{14,10},{15,13... | collective-permute-start | bytes 491528 | tf_op jit(solution)/shard_map/ppermute | solution.py:276
  20.1 1.1 %shard_map.39.before = f32[4,2,256,128]{3,2,1,0:T(8,128)S(1)} custom-call(bf16[8,2,256,128]{3,2,1,0:T(8,128)(2,1)S(1)} %shard_map.38.a_ref, bf16[656,128]{1,0:T(8,128)(2,1)S(1)} %get-tuple-element.12.refs_0_, bf16[640,128]{1,0:T(8,128)(2,1)S(1)} %get-tuple-element.16.refs_1_), custom_call_target="tpu_custom_call" | custom-call | flops 134217728 | tf_op jit(solution)/shard_map/pallas_call | solution.py:233
  21.3 1.3 %collective-permute-done.3.refs_8_ = bf16[656,128]{1,0:T(8,128)(2,1)S(1)} collective-permute-done((bf16[656,128]{1,0:T(8,128)(2,1)S(1)}, bf16[656,128]{1,0:T(8,128)(2,1)S(1)}, u32[]{:S(2)}, u32[]{:S(2)}) %collective-permute-start.3) | collective-permute-done | bytes 167968 | tf_op jit(solution)/shard_map/ppermute | solution.py:276
  22.5 0.0 collective-permute-start.12
  22.5 0.1 collective-permute-done.6.refs_0_
  22.7 2.0 %collective-permute-start.14 = (bf16[656,128]{1,0:T(8,128)(2,1)S(1)}, bf16[656,128]{1,0:T(8,128)(2,1)S(1)}, u32[]{:S(2)}, u32[]{:S(2)}) collective-permute-start(bf16[656,128]{1,0:T(8,128)(2,1)S(1)} %collective-permute-done.6.refs_0_), channel_id=1, source_target_pairs={{0,4},{1,3},{4,8},{5,1},{8,12},{9,5},{12,14},{13,9},{14,10},{15,13... | collective-permute-start | bytes 503816 | tf_op jit(solution)/shard_map/ppermute | solution.py:276
  24.6 1.4 %collective-permute-done.11.refs_9_ = bf16[640,128]{1,0:T(8,128)(2,1)S(1)} collective-permute-done((bf16[640,128]{1,0:T(8,128)(2,1)S(1)}, bf16[640,128]{1,0:T(8,128)(2,1)S(1)}, u32[]{:S(2)}, u32[]{:S(2)}) %collective-permute-start.11) | collective-permute-done | bytes 163872 | tf_op jit(solution)/shard_map/ppermute | solution.py:276
  26.1 0.0 collective-permute-start.13
  26.1 0.1 collective-permute-done.9.refs_1_
  26.2 2.0 %collective-permute-start.15 = (bf16[640,128]{1,0:T(8,128)(2,1)S(1)}, bf16[640,128]{1,0:T(8,128)(2,1)S(1)}, u32[]{:S(2)}, u32[]{:S(2)}) collective-permute-start(bf16[640,128]{1,0:T(8,128)(2,1)S(1)} %collective-permute-done.9.refs_1_), channel_id=1, source_target_pairs={{0,4},{1,3},{4,8},{5,1},{8,12},{9,5},{12,14},{13,9},{14,10},{15,13... | collective-permute-start | bytes 491528 | tf_op jit(solution)/shard_map/ppermute | solution.py:276
  28.2 2.7 %shard_map.40.total = f32[4,2,256,128]{3,2,1,0:T(8,128)S(1)} custom-call(bf16[8,2,256,128]{3,2,1,0:T(8,128)(2,1)S(1)} %shard_map.38.a_ref, f32[4,2,256,128]{3,2,1,0:T(8,128)S(1)} %shard_map.39.before, bf16[656,128]{1,0:T(8,128)(2,1)S(1)} %collective-permute-done.6.refs_0_, ...), custom_call_target="tpu_custom_call", output_to_operand_aliasing={{}: (1, {})} | custom-call | flops 671088640 | tf_op jit(solution)/shard_map/pallas_call | solution.py:233
  30.8 2.3 %collective-permute-done.13.refs_1_ = bf16[640,128]{1,0:T(8,128)(2,1)S(1)} collective-permute-done((bf16[640,128]{1,0:T(8,128)(2,1)S(1)}, bf16[640,128]{1,0:T(8,128)(2,1)S(1)}, u32[]{:S(2)}, u32[]{:S(2)}) %collective-permute-start.13) | collective-permute-done | bytes 163872 | tf_op jit(solution)/shard_map/ppermute | solution.py:276
  33.1 0.0 collective-permute-done.15.refs_3_
  33.1 0.0 collective-permute-done.12.refs_0_
  33.1 0.0 collective-permute-done.14.refs_2_
  33.1 2.6 %shard_map.41 = bf16[4,10,64,64]{3,2,1,0:T(8,128)(2,1)} custom-call(bf16[8,2,256,128]{3,2,1,0:T(8,128)(2,1)S(1)} %shard_map.38.a_ref, f32[4,2,256,128]{3,2,1,0:T(8,128)S(1)} %shard_map.40.total, s32[4,10]{1,0:T(4,128)S(1)} %copy-done.1, bf16[656,128]{1,0:T(8,128)(2,1)S(1)} %collective-permute-done.12.refs_0_, ...), custom_call_target="tpu_custom_call" | custom-call | flops 167772160 | tf_op jit(solution)/shard_map/pallas_call | solution.py:233
Async XLA Ops:
  0.0 4.5 %copy-start = (bf16[4,10,64,64]{3,2,1,0:T(8,128)(2,1)S(1)}, bf16[4,10,64,64]{3,2,1,0:T(8,128)(2,1)}, u32[]{:S(2)}) copy-start(bf16[4,10,64,64]{3,2,1,0:T(8,128)(2,1)} %own_ref.1) | copy-start | bytes 983044
  1.4 8.9 %copy-start.1 = (s32[4,10]{1,0:T(4,128)S(1)}, s32[4,10]{1,0:T(4,128)}, u32[]{:S(2)}) copy-start(s32[4,10]{1,0:T(4,128)} %cols_hbm.3) | copy-start | bytes 484
  1.4 6.4 %collective-permute-start.4 = (bf16[656,128]{1,0:T(8,128)(2,1)S(1)}, bf16[656,128]{1,0:T(8,128)(2,1)S(1)}, u32[]{:S(2)}, u32[]{:S(2)}) collective-permute-start(bf16[656,128]{1,0:T(8,128)(2,1)S(1)} %get-tuple-element.12.refs_0_), channel_id=1, source_target_pairs={{0,4},{1,3},{4,8},{5,1},{8,12},{9,5},{12,14},{13,9},{14,10},{15,13... | collective-permute-start | bytes 503816 | tf_op jit(solution)/shard_map/ppermute | solution.py:276
  4.5 9.0 %collective-permute-start.1 = (bf16[4,10,64,64]{3,2,1,0:T(8,128)(2,1)S(1)}, bf16[4,10,64,64]{3,2,1,0:T(8,128)(2,1)S(1)}, u32[]{:S(2)}, u32[]{:S(2)}) collective-permute-start(bf16[4,10,64,64]{3,2,1,0:T(8,128)(2,1)S(1)} %copy-done), channel_id=1, source_target_pairs={{0,1},{1,0},{2,3},{3,2},{4,5},{5,4},{6,7},{7,6},{8,9},{9,8},{10,11... | collective-permute-start | bytes 983048 | tf_op jit(solution)/shard_map/ppermute | solution.py:261
  4.5 7.0 %collective-permute-start.7 = (bf16[640,128]{1,0:T(8,128)(2,1)S(1)}, bf16[640,128]{1,0:T(8,128)(2,1)S(1)}, u32[]{:S(2)}, u32[]{:S(2)}) collective-permute-start(bf16[640,128]{1,0:T(8,128)(2,1)S(1)} %get-tuple-element.16.refs_1_), channel_id=1, source_target_pairs={{0,4},{1,3},{4,8},{5,1},{8,12},{9,5},{12,14},{13,9},{14,10},{15,13... | collective-permute-start | bytes 491528 | tf_op jit(solution)/shard_map/ppermute | solution.py:276
  6.1 9.3 %collective-permute-start.2 = (bf16[656,128]{1,0:T(8,128)(2,1)S(1)}, bf16[656,128]{1,0:T(8,128)(2,1)S(1)}, u32[]{:S(2)}, u32[]{:S(2)}) collective-permute-start(bf16[656,128]{1,0:T(8,128)(2,1)S(1)} %get-tuple-element.12.refs_0_), channel_id=1, source_target_pairs={{0,2},{1,5},{4,0},{5,9},{8,4},{9,13},{12,8},{13,15},{14,12},{15,11... | collective-permute-start | bytes 503816 | tf_op jit(solution)/shard_map/ppermute | solution.py:276
  7.8 7.6 %collective-permute-start.5 = (bf16[656,128]{1,0:T(8,128)(2,1)S(1)}, bf16[656,128]{1,0:T(8,128)(2,1)S(1)}, u32[]{:S(2)}, u32[]{:S(2)}) collective-permute-start(bf16[656,128]{1,0:T(8,128)(2,1)S(1)} %collective-permute-done.4.refs_2_), channel_id=1, source_target_pairs={{0,4},{1,3},{4,8},{5,1},{8,12},{9,5},{12,14},{13,9},{14,10},{15,13... | collective-permute-start | bytes 503816 | tf_op jit(solution)/shard_map/ppermute | solution.py:276
  10.3 1.2 %collective-permute-start = (s32[4,10]{1,0:T(4,128)S(1)}, s32[4,10]{1,0:T(4,128)S(1)}, u32[]{:S(2)}, u32[]{:S(2)}) collective-permute-start(s32[4,10]{1,0:T(4,128)S(1)} %copy-done.1), channel_id=1, source_target_pairs={{0,1},{1,0},{2,3},{3,2},{4,5},{5,4},{6,7},{7,6},{8,9},{9,8},{10,11... | collective-permute-start | bytes 488 | tf_op jit(solution)/shard_map/ppermute | solution.py:261
  11.5 6.6 %collective-permute-start.10 = (bf16[640,128]{1,0:T(8,128)(2,1)S(1)}, bf16[640,128]{1,0:T(8,128)(2,1)S(1)}, u32[]{:S(2)}, u32[]{:S(2)}) collective-permute-start(bf16[640,128]{1,0:T(8,128)(2,1)S(1)} %get-tuple-element.16.refs_1_), channel_id=1, source_target_pairs={{0,2},{1,5},{4,0},{5,9},{8,4},{9,13},{12,8},{13,15},{14,12},{15,11... | collective-permute-start | bytes 491528 | tf_op jit(solution)/shard_map/ppermute | solution.py:276
  11.5 6.6 %collective-permute-start.8 = (bf16[640,128]{1,0:T(8,128)(2,1)S(1)}, bf16[640,128]{1,0:T(8,128)(2,1)S(1)}, u32[]{:S(2)}, u32[]{:S(2)}) collective-permute-start(bf16[640,128]{1,0:T(8,128)(2,1)S(1)} %collective-permute-done.7.refs_3_), channel_id=1, source_target_pairs={{0,4},{1,3},{4,8},{5,1},{8,12},{9,5},{12,14},{13,9},{14,10},{15,13... | collective-permute-start | bytes 491528 | tf_op jit(solution)/shard_map/ppermute | solution.py:276
  15.3 7.2 %collective-permute-start.3 = (bf16[656,128]{1,0:T(8,128)(2,1)S(1)}, bf16[656,128]{1,0:T(8,128)(2,1)S(1)}, u32[]{:S(2)}, u32[]{:S(2)}) collective-permute-start(bf16[656,128]{1,0:T(8,128)(2,1)S(1)} %collective-permute-done.2.refs_4_), channel_id=1, source_target_pairs={{0,2},{1,5},{4,0},{5,9},{8,4},{9,13},{12,8},{13,15},{14,12},{15,11... | collective-permute-start | bytes 503816 | tf_op jit(solution)/shard_map/ppermute | solution.py:276
  15.4 7.3 %collective-permute-start.6 = (bf16[656,128]{1,0:T(8,128)(2,1)S(1)}, bf16[656,128]{1,0:T(8,128)(2,1)S(1)}, u32[]{:S(2)}, u32[]{:S(2)}) collective-permute-start(bf16[656,128]{1,0:T(8,128)(2,1)S(1)} %collective-permute-done.5.refs_6_), channel_id=1, source_target_pairs={{0,4},{1,3},{4,8},{5,1},{8,12},{9,5},{12,14},{13,9},{14,10},{15,13... | collective-permute-start | bytes 503816 | tf_op jit(solution)/shard_map/ppermute | solution.py:276
  18.1 8.0 %collective-permute-start.11 = (bf16[640,128]{1,0:T(8,128)(2,1)S(1)}, bf16[640,128]{1,0:T(8,128)(2,1)S(1)}, u32[]{:S(2)}, u32[]{:S(2)}) collective-permute-start(bf16[640,128]{1,0:T(8,128)(2,1)S(1)} %collective-permute-done.10.refs_5_), channel_id=1, source_target_pairs={{0,2},{1,5},{4,0},{5,9},{8,4},{9,13},{12,8},{13,15},{14,12},{15,11... | collective-permute-start | bytes 491528 | tf_op jit(solution)/shard_map/ppermute | solution.py:276
  18.1 8.1 %collective-permute-start.9 = (bf16[640,128]{1,0:T(8,128)(2,1)S(1)}, bf16[640,128]{1,0:T(8,128)(2,1)S(1)}, u32[]{:S(2)}, u32[]{:S(2)}) collective-permute-start(bf16[640,128]{1,0:T(8,128)(2,1)S(1)} %collective-permute-done.8.refs_7_), channel_id=1, source_target_pairs={{0,4},{1,3},{4,8},{5,1},{8,12},{9,5},{12,14},{13,9},{14,10},{15,13... | collective-permute-start | bytes 491528 | tf_op jit(solution)/shard_map/ppermute | solution.py:276
  22.5 10.6 %collective-permute-start.12 = (bf16[656,128]{1,0:T(8,128)(2,1)S(1)}, bf16[656,128]{1,0:T(8,128)(2,1)S(1)}, u32[]{:S(2)}, u32[]{:S(2)}) collective-permute-start(bf16[656,128]{1,0:T(8,128)(2,1)S(1)} %collective-permute-done.3.refs_8_), channel_id=1, source_target_pairs={{0,2},{1,5},{4,0},{5,9},{8,4},{9,13},{12,8},{13,15},{14,12},{15,11... | collective-permute-start | bytes 503816 | tf_op jit(solution)/shard_map/ppermute | solution.py:276
  22.7 10.4 %collective-permute-start.14 = (bf16[656,128]{1,0:T(8,128)(2,1)S(1)}, bf16[656,128]{1,0:T(8,128)(2,1)S(1)}, u32[]{:S(2)}, u32[]{:S(2)}) collective-permute-start(bf16[656,128]{1,0:T(8,128)(2,1)S(1)} %collective-permute-done.6.refs_0_), channel_id=1, source_target_pairs={{0,4},{1,3},{4,8},{5,1},{8,12},{9,5},{12,14},{13,9},{14,10},{15,13... | collective-permute-start | bytes 503816 | tf_op jit(solution)/shard_map/ppermute | solution.py:276
  26.1 7.1 %collective-permute-start.13 = (bf16[640,128]{1,0:T(8,128)(2,1)S(1)}, bf16[640,128]{1,0:T(8,128)(2,1)S(1)}, u32[]{:S(2)}, u32[]{:S(2)}) collective-permute-start(bf16[640,128]{1,0:T(8,128)(2,1)S(1)} %collective-permute-done.11.refs_9_), channel_id=1, source_target_pairs={{0,2},{1,5},{4,0},{5,9},{8,4},{9,13},{12,8},{13,15},{14,12},{15,11... | collective-permute-start | bytes 491528 | tf_op jit(solution)/shard_map/ppermute | solution.py:276
  26.2 6.9 %collective-permute-start.15 = (bf16[640,128]{1,0:T(8,128)(2,1)S(1)}, bf16[640,128]{1,0:T(8,128)(2,1)S(1)}, u32[]{:S(2)}, u32[]{:S(2)}) collective-permute-start(bf16[640,128]{1,0:T(8,128)(2,1)S(1)} %collective-permute-done.9.refs_1_), channel_id=1, source_target_pairs={{0,4},{1,3},{4,8},{5,1},{8,12},{9,5},{12,14},{13,9},{14,10},{15,13... | collective-permute-start | bytes 491528 | tf_op jit(solution)/shard_map/ppermute | solution.py:276

commit v14 on v13

--- a/solution.py
+++ b/solution.py
@@ -268,11 +268,13 @@
         ways = [way for way in hops if step <= hops[way]]
         for way in ways:
             sent = list(held[way])
-            if (step, way) == (2, -1):
-                sent[0], _ = lax.optimization_barrier((sent[0], a))
+            if (step, way) == (3, 1):
+                sent[-1], _, _ = lax.optimization_barrier((sent[-1], a, held[-1][-1]))
             if step > 2 and way == -1:
                 total = product(order, rounds.pop(0), a, total, total_shape)
                 sent[0], total = lax.optimization_barrier((sent[0], total))
+            if (step, way) == (2, 1):
+                sent[-1], _ = lax.optimization_barrier((sent[-1], rounds[1][1][2][-1]))
             held[way] = [lax.ppermute(part, ("row", "col"), ring(way)) for part in sent]
         rounds.append([(way, step, held[way]) for way in ways])
     *_, late, last = rounds

time: 35.8 us -> 35.7 us (level)
  waiting for transfers between devices: 8.41 us -> 7.63 us
  starting transfers between devices: 17.6 us -> 18.3 us
    ppermute x2, waiting for transfers between devices: 1.16 us -> 0.01 us  [local(): a_other, others = (lax.ppermute(x, 'col', swap) for x in mine)]
    ppermute x14, starting transfers between devices: 17.6 us -> 18.3 us  [local(): held[way] = [lax.ppermute(part, ('row', 'col'), ring(way)) for part in sent]]
    ppermute x14, waiting for transfers between devices: 7.25 us -> 7.62 us  [local(): held[way] = [lax.ppermute(part, ('row', 'col'), ring(way)) for part in sent]]
  transfers between devices with their start and end apart: 16 -> 16, of which waited for: 8 -> 6; matrix products, arithmetic and copies ran while one was open for 0% -> 0% of each run, Pallas kernels for 16% -> 16%
where the time goes in v14:
time: 35.7 us; the launch traced here: 35.5 us
  starting transfers between devices  18.3 us (51%)
  Pallas kernels  9.55 us (27%)
  waiting for transfers between devices  7.63 us (21%)
    ppermute x14, starting transfers between devices, local(): held[way] = [lax.ppermute(part, ('row', 'col'), ring(way)) for part in sent]  18.3 us
    ppermute x14, waiting for transfers between devices, local(): held[way] = [lax.ppermute(part, ('row', 'col'), ring(way)) for part in sent]  7.62 us
    pallas_call x3, Pallas kernels, product(): pl.pallas_call(functools.partial(kernel, sources), out_shape=out, in_spec...  6.35 us
    pallas_call x1, Pallas kernels, dense_rows(): pl.pallas_call(dense_kernel, out_shape=jax.ShapeDtypeStruct((sources, row...  1.83 us
    pallas_call x1, Pallas kernels, pack(): pl.pallas_call(functools.partial(pack_kernel, half), out_shape=[jax.Shape...  1.37 us
  transfers between devices with their start and end apart: 16, of which 6 were waited for; matrix products, arithmetic and copies ran while one was open for 0% of the time, Pallas kernels for 16%

profile of v14, /device:TPU:0, one launch (start us, length us, event | category | flops | bytes accessed | tf_op | source)
XLA Modules:
  0.0 35.5 jit_solution(6646464571421644142)
XLA Ops:
  0.0 0.0 copy-start
  0.0 1.4 %shard_map.37 = (bf16[656,128]{1,0:T(8,128)(2,1)S(1)}, bf16[640,128]{1,0:T(8,128)(2,1)S(1)}) custom-call(s32[4,10]{1,0:T(4,128)} %cols_hbm.3, bf16[4,10,64,64]{3,2,1,0:T(8,128)(2,1)} %b_hbm.1), custom_call_target="tpu_custom_call" | custom-call | bytes 655360 | tf_op jit(solution)/shard_map/pallas_call | solution.py:59
  1.4 0.0 copy-start.1
  1.4 3.1 %collective-permute-start.4 = (bf16[656,128]{1,0:T(8,128)(2,1)S(1)}, bf16[656,128]{1,0:T(8,128)(2,1)S(1)}, u32[]{:S(2)}, u32[]{:S(2)}) collective-permute-start(bf16[656,128]{1,0:T(8,128)(2,1)S(1)} %get-tuple-element.13.refs_0_), channel_id=1, source_target_pairs={{0,4},{1,3},{4,8},{5,1},{8,12},{9,5},{12,14},{13,9},{14,10},{15,13... | collective-permute-start | bytes 503816 | tf_op jit(solution)/shard_map/ppermute | solution.py:278
  4.5 0.0 collective-permute-start.8
  4.5 2.0 %collective-permute-start.7 = (bf16[640,128]{1,0:T(8,128)(2,1)S(1)}, bf16[640,128]{1,0:T(8,128)(2,1)S(1)}, u32[]{:S(2)}, u32[]{:S(2)}) collective-permute-start(bf16[640,128]{1,0:T(8,128)(2,1)S(1)} %get-tuple-element.16.refs_1_), channel_id=1, source_target_pairs={{0,4},{1,3},{4,8},{5,1},{8,12},{9,5},{12,14},{13,9},{14,10},{15,13... | collective-permute-start | bytes 491528 | tf_op jit(solution)/shard_map/ppermute | solution.py:278
  6.5 0.0 copy-done
  6.5 0.0 collective-permute-start.1
  6.5 0.5 %collective-permute-start.2 = (bf16[656,128]{1,0:T(8,128)(2,1)S(1)}, bf16[656,128]{1,0:T(8,128)(2,1)S(1)}, u32[]{:S(2)}, u32[]{:S(2)}) collective-permute-start(bf16[656,128]{1,0:T(8,128)(2,1)S(1)} %get-tuple-element.13.refs_0_), channel_id=1, source_target_pairs={{0,2},{1,5},{4,0},{5,9},{8,4},{9,13},{12,8},{13,15},{14,12},{15,11... | collective-permute-start | bytes 503816 | tf_op jit(solution)/shard_map/ppermute | solution.py:278
  7.0 2.0 %collective-permute-done.4.refs_2_ = bf16[656,128]{1,0:T(8,128)(2,1)S(1)} collective-permute-done((bf16[656,128]{1,0:T(8,128)(2,1)S(1)}, bf16[656,128]{1,0:T(8,128)(2,1)S(1)}, u32[]{:S(2)}, u32[]{:S(2)}) %collective-permute-start.4) | collective-permute-done | bytes 167968 | tf_op jit(solution)/shard_map/ppermute | solution.py:278
  9.0 1.5 %collective-permute-start.5 = (bf16[656,128]{1,0:T(8,128)(2,1)S(1)}, bf16[656,128]{1,0:T(8,128)(2,1)S(1)}, u32[]{:S(2)}, u32[]{:S(2)}) collective-permute-start(bf16[656,128]{1,0:T(8,128)(2,1)S(1)} %collective-permute-done.4.refs_2_), channel_id=1, source_target_pairs={{0,4},{1,3},{4,8},{5,1},{8,12},{9,5},{12,14},{13,9},{14,10},{15,13... | collective-permute-start | bytes 503816 | tf_op jit(solution)/shard_map/ppermute | solution.py:278
  10.5 0.0 collective-permute-done.8.refs_5_
  10.5 0.0 copy-done.1
  10.5 0.0 collective-permute-start
  10.5 2.0 %collective-permute-done.7.refs_3_ = bf16[640,128]{1,0:T(8,128)(2,1)S(1)} collective-permute-done((bf16[640,128]{1,0:T(8,128)(2,1)S(1)}, bf16[640,128]{1,0:T(8,128)(2,1)S(1)}, u32[]{:S(2)}, u32[]{:S(2)}) %collective-permute-start.7) | collective-permute-done | bytes 163872 | tf_op jit(solution)/shard_map/ppermute | solution.py:278
  12.5 0.8 %collective-permute-start.9 = (bf16[640,128]{1,0:T(8,128)(2,1)S(1)}, bf16[640,128]{1,0:T(8,128)(2,1)S(1)}, u32[]{:S(2)}, u32[]{:S(2)}) collective-permute-start(bf16[640,128]{1,0:T(8,128)(2,1)S(1)} %collective-permute-done.7.refs_3_), channel_id=1, source_target_pairs={{0,4},{1,3},{4,8},{5,1},{8,12},{9,5},{12,14},{13,9},{14,10},{15,13... | collective-permute-start | bytes 491528 | tf_op jit(solution)/shard_map/ppermute | solution.py:278
  13.3 0.0 collective-permute-done.others_ref
  13.3 1.6 %collective-permute-start.10 = (bf16[640,128]{1,0:T(8,128)(2,1)S(1)}, bf16[640,128]{1,0:T(8,128)(2,1)S(1)}, u32[]{:S(2)}, u32[]{:S(2)}) collective-permute-start(bf16[640,128]{1,0:T(8,128)(2,1)S(1)} %collective-permute-done.8.refs_5_), channel_id=1, source_target_pairs={{0,2},{1,5},{4,0},{5,9},{8,4},{9,13},{12,8},{13,15},{14,12},{15,11... | collective-permute-start | bytes 491528 | tf_op jit(solution)/shard_map/ppermute | solution.py:278
  14.9 0.0 collective-permute-done.2.refs_4_
  14.9 2.0 %collective-permute-start.3 = (bf16[656,128]{1,0:T(8,128)(2,1)S(1)}, bf16[656,128]{1,0:T(8,128)(2,1)S(1)}, u32[]{:S(2)}, u32[]{:S(2)}) collective-permute-start(bf16[656,128]{1,0:T(8,128)(2,1)S(1)} %collective-permute-done.2.refs_4_), channel_id=1, source_target_pairs={{0,2},{1,5},{4,0},{5,9},{8,4},{9,13},{12,8},{13,15},{14,12},{15,11... | collective-permute-start | bytes 503816 | tf_op jit(solution)/shard_map/ppermute | solution.py:278
  17.0 0.0 collective-permute-done.5.refs_6_
  17.0 0.0 collective-permute-start.6
  17.0 0.0 collective-permute-done.1.other_ref
  17.0 1.8 %shard_map.38.a_ref = bf16[8,2,256,128]{3,2,1,0:T(8,128)(2,1)S(1)} custom-call(s32[4,10]{1,0:T(4,128)S(1)} %copy-done.1, s32[4,10]{1,0:T(4,128)S(1)} %collective-permute-done.others_ref, bf16[4,10,64,64]{3,2,1,0:T(8,128)(2,1)S(1)} %copy-done, bf16[4,10,64,64]{3,2,1,0:T(8,128)(2,1)S(1)} %collective-permute-done.1.other_ref), custom_call_target="tpu_custom_call" | custom-call | bytes 1310720 | tf_op jit(solution)/shard_map/pallas_call | solution.py:105
  18.8 1.2 %collective-permute-done.9.refs_7_ = bf16[640,128]{1,0:T(8,128)(2,1)S(1)} collective-permute-done((bf16[640,128]{1,0:T(8,128)(2,1)S(1)}, bf16[640,128]{1,0:T(8,128)(2,1)S(1)}, u32[]{:S(2)}, u32[]{:S(2)}) %collective-permute-start.9) | collective-permute-done | bytes 163872 | tf_op jit(solution)/shard_map/ppermute | solution.py:278
  20.0 0.0 collective-permute-done.10.refs_9_
  20.0 1.4 %collective-permute-start.11 = (bf16[640,128]{1,0:T(8,128)(2,1)S(1)}, bf16[640,128]{1,0:T(8,128)(2,1)S(1)}, u32[]{:S(2)}, u32[]{:S(2)}) collective-permute-start(bf16[640,128]{1,0:T(8,128)(2,1)S(1)} %collective-permute-done.9.refs_7_), channel_id=1, source_target_pairs={{0,4},{1,3},{4,8},{5,1},{8,12},{9,5},{12,14},{13,9},{14,10},{15,13... | collective-permute-start | bytes 491528 | tf_op jit(solution)/shard_map/ppermute | solution.py:278
  21.4 1.1 %shard_map.39.before = f32[4,2,256,128]{3,2,1,0:T(8,128)S(1)} custom-call(bf16[8,2,256,128]{3,2,1,0:T(8,128)(2,1)S(1)} %shard_map.38.a_ref, bf16[656,128]{1,0:T(8,128)(2,1)S(1)} %get-tuple-element.13.refs_0_, bf16[640,128]{1,0:T(8,128)(2,1)S(1)} %get-tuple-element.16.refs_1_), custom_call_target="tpu_custom_call" | custom-call | flops 134217728 | tf_op jit(solution)/shard_map/pallas_call | solution.py:233
  22.5 0.6 %collective-permute-done.3.refs_8_ = bf16[656,128]{1,0:T(8,128)(2,1)S(1)} collective-permute-done((bf16[656,128]{1,0:T(8,128)(2,1)S(1)}, bf16[656,128]{1,0:T(8,128)(2,1)S(1)}, u32[]{:S(2)}, u32[]{:S(2)}) %collective-permute-start.3) | collective-permute-done | bytes 167968 | tf_op jit(solution)/shard_map/ppermute | solution.py:278
  23.1 2.5 %collective-permute-start.12 = (bf16[656,128]{1,0:T(8,128)(2,1)S(1)}, bf16[656,128]{1,0:T(8,128)(2,1)S(1)}, u32[]{:S(2)}, u32[]{:S(2)}) collective-permute-start(bf16[656,128]{1,0:T(8,128)(2,1)S(1)} %collective-permute-done.3.refs_8_), channel_id=1, source_target_pairs={{0,2},{1,5},{4,0},{5,9},{8,4},{9,13},{12,8},{13,15},{14,12},{15,11... | collective-permute-start | bytes 503816 | tf_op jit(solution)/shard_map/ppermute | solution.py:278
  25.6 0.0 collective-permute-done.6.refs_0_
  25.6 0.0 collective-permute-start.14
  25.6 2.0 %collective-permute-start.13 = (bf16[640,128]{1,0:T(8,128)(2,1)S(1)}, bf16[640,128]{1,0:T(8,128)(2,1)S(1)}, u32[]{:S(2)}, u32[]{:S(2)}) collective-permute-start(bf16[640,128]{1,0:T(8,128)(2,1)S(1)} %collective-permute-done.10.refs_9_), channel_id=1, source_target_pairs={{0,2},{1,5},{4,0},{5,9},{8,4},{9,13},{12,8},{13,15},{14,12},{15,11... | collective-permute-start | bytes 491528 | tf_op jit(solution)/shard_map/ppermute | solution.py:278
  27.6 0.0 collective-permute-done.11.refs_1_
  27.6 0.8 %collective-permute-start.15 = (bf16[640,128]{1,0:T(8,128)(2,1)S(1)}, bf16[640,128]{1,0:T(8,128)(2,1)S(1)}, u32[]{:S(2)}, u32[]{:S(2)}) collective-permute-start(bf16[640,128]{1,0:T(8,128)(2,1)S(1)} %collective-permute-done.11.refs_1_), channel_id=1, source_target_pairs={{0,4},{1,3},{4,8},{5,1},{8,12},{9,5},{12,14},{13,9},{14,10},{15,13... | collective-permute-start | bytes 491528 | tf_op jit(solution)/shard_map/ppermute | solution.py:278
  28.5 2.7 %shard_map.40.total = f32[4,2,256,128]{3,2,1,0:T(8,128)S(1)} custom-call(bf16[8,2,256,128]{3,2,1,0:T(8,128)(2,1)S(1)} %shard_map.38.a_ref, f32[4,2,256,128]{3,2,1,0:T(8,128)S(1)} %shard_map.39.before, bf16[656,128]{1,0:T(8,128)(2,1)S(1)} %collective-permute-done.6.refs_0_, ...), custom_call_target="tpu_custom_call", output_to_operand_aliasing={{}: (1, {})} | custom-call | flops 671088640 | tf_op jit(solution)/shard_map/pallas_call | solution.py:233
  31.2 1.0 %collective-permute-done.13.refs_1_ = bf16[640,128]{1,0:T(8,128)(2,1)S(1)} collective-permute-done((bf16[640,128]{1,0:T(8,128)(2,1)S(1)}, bf16[640,128]{1,0:T(8,128)(2,1)S(1)}, u32[]{:S(2)}, u32[]{:S(2)}) %collective-permute-start.13) | collective-permute-done | bytes 163872 | tf_op jit(solution)/shard_map/ppermute | solution.py:278
  32.2 0.0 collective-permute-done.12.refs_0_
  32.2 0.8 %collective-permute-done.15.refs_3_ = bf16[640,128]{1,0:T(8,128)(2,1)S(1)} collective-permute-done((bf16[640,128]{1,0:T(8,128)(2,1)S(1)}, bf16[640,128]{1,0:T(8,128)(2,1)S(1)}, u32[]{:S(2)}, u32[]{:S(2)}) %collective-permute-start.15) | collective-permute-done | bytes 163872 | tf_op jit(solution)/shard_map/ppermute | solution.py:278
  33.0 0.0 collective-permute-done.14.refs_2_
  33.0 2.6 %shard_map.41 = bf16[4,10,64,64]{3,2,1,0:T(8,128)(2,1)} custom-call(bf16[8,2,256,128]{3,2,1,0:T(8,128)(2,1)S(1)} %shard_map.38.a_ref, f32[4,2,256,128]{3,2,1,0:T(8,128)S(1)} %shard_map.40.total, s32[4,10]{1,0:T(4,128)S(1)} %copy-done.1, bf16[656,128]{1,0:T(8,128)(2,1)S(1)} %collective-permute-done.12.refs_0_, ...), custom_call_target="tpu_custom_call" | custom-call | flops 167772160 | tf_op jit(solution)/shard_map/pallas_call | solution.py:233
Async XLA Ops:
  0.0 6.5 %copy-start = (bf16[4,10,64,64]{3,2,1,0:T(8,128)(2,1)S(1)}, bf16[4,10,64,64]{3,2,1,0:T(8,128)(2,1)}, u32[]{:S(2)}) copy-start(bf16[4,10,64,64]{3,2,1,0:T(8,128)(2,1)} %own_ref.1) | copy-start | bytes 983044
  1.4 9.1 %copy-start.1 = (s32[4,10]{1,0:T(4,128)S(1)}, s32[4,10]{1,0:T(4,128)}, u32[]{:S(2)}) copy-start(s32[4,10]{1,0:T(4,128)} %cols_hbm.3) | copy-start | bytes 484
  1.4 7.6 %collective-permute-start.4 = (bf16[656,128]{1,0:T(8,128)(2,1)S(1)}, bf16[656,128]{1,0:T(8,128)(2,1)S(1)}, u32[]{:S(2)}, u32[]{:S(2)}) collective-permute-start(bf16[656,128]{1,0:T(8,128)(2,1)S(1)} %get-tuple-element.13.refs_0_), channel_id=1, source_target_pairs={{0,4},{1,3},{4,8},{5,1},{8,12},{9,5},{12,14},{13,9},{14,10},{15,13... | collective-permute-start | bytes 503816 | tf_op jit(solution)/shard_map/ppermute | solution.py:278
  4.5 6.1 %collective-permute-start.8 = (bf16[640,128]{1,0:T(8,128)(2,1)S(1)}, bf16[640,128]{1,0:T(8,128)(2,1)S(1)}, u32[]{:S(2)}, u32[]{:S(2)}) collective-permute-start(bf16[640,128]{1,0:T(8,128)(2,1)S(1)} %get-tuple-element.16.refs_1_), channel_id=1, source_target_pairs={{0,2},{1,5},{4,0},{5,9},{8,4},{9,13},{12,8},{13,15},{14,12},{15,11... | collective-permute-start | bytes 491528 | tf_op jit(solution)/shard_map/ppermute | solution.py:278
  4.5 8.0 %collective-permute-start.7 = (bf16[640,128]{1,0:T(8,128)(2,1)S(1)}, bf16[640,128]{1,0:T(8,128)(2,1)S(1)}, u32[]{:S(2)}, u32[]{:S(2)}) collective-permute-start(bf16[640,128]{1,0:T(8,128)(2,1)S(1)} %get-tuple-element.16.refs_1_), channel_id=1, source_target_pairs={{0,4},{1,3},{4,8},{5,1},{8,12},{9,5},{12,14},{13,9},{14,10},{15,13... | collective-permute-start | bytes 491528 | tf_op jit(solution)/shard_map/ppermute | solution.py:278
  6.5 10.5 %collective-permute-start.1 = (bf16[4,10,64,64]{3,2,1,0:T(8,128)(2,1)S(1)}, bf16[4,10,64,64]{3,2,1,0:T(8,128)(2,1)S(1)}, u32[]{:S(2)}, u32[]{:S(2)}) collective-permute-start(bf16[4,10,64,64]{3,2,1,0:T(8,128)(2,1)S(1)} %copy-done), channel_id=1, source_target_pairs={{0,1},{1,0},{2,3},{3,2},{4,5},{5,4},{6,7},{7,6},{8,9},{9,8},{10,11... | collective-permute-start | bytes 983048 | tf_op jit(solution)/shard_map/ppermute | solution.py:261
  6.5 8.4 %collective-permute-start.2 = (bf16[656,128]{1,0:T(8,128)(2,1)S(1)}, bf16[656,128]{1,0:T(8,128)(2,1)S(1)}, u32[]{:S(2)}, u32[]{:S(2)}) collective-permute-start(bf16[656,128]{1,0:T(8,128)(2,1)S(1)} %get-tuple-element.13.refs_0_), channel_id=1, source_target_pairs={{0,2},{1,5},{4,0},{5,9},{8,4},{9,13},{12,8},{13,15},{14,12},{15,11... | collective-permute-start | bytes 503816 | tf_op jit(solution)/shard_map/ppermute | solution.py:278
  9.0 8.0 %collective-permute-start.5 = (bf16[656,128]{1,0:T(8,128)(2,1)S(1)}, bf16[656,128]{1,0:T(8,128)(2,1)S(1)}, u32[]{:S(2)}, u32[]{:S(2)}) collective-permute-start(bf16[656,128]{1,0:T(8,128)(2,1)S(1)} %collective-permute-done.4.refs_2_), channel_id=1, source_target_pairs={{0,4},{1,3},{4,8},{5,1},{8,12},{9,5},{12,14},{13,9},{14,10},{15,13... | collective-permute-start | bytes 503816 | tf_op jit(solution)/shard_map/ppermute | solution.py:278
  10.5 2.8 %collective-permute-start = (s32[4,10]{1,0:T(4,128)S(1)}, s32[4,10]{1,0:T(4,128)S(1)}, u32[]{:S(2)}, u32[]{:S(2)}) collective-permute-start(s32[4,10]{1,0:T(4,128)S(1)} %copy-done.1), channel_id=1, source_target_pairs={{0,1},{1,0},{2,3},{3,2},{4,5},{5,4},{6,7},{7,6},{8,9},{9,8},{10,11... | collective-permute-start | bytes 488 | tf_op jit(solution)/shard_map/ppermute | solution.py:261
  12.5 7.5 %collective-permute-start.9 = (bf16[640,128]{1,0:T(8,128)(2,1)S(1)}, bf16[640,128]{1,0:T(8,128)(2,1)S(1)}, u32[]{:S(2)}, u32[]{:S(2)}) collective-permute-start(bf16[640,128]{1,0:T(8,128)(2,1)S(1)} %collective-permute-done.7.refs_3_), channel_id=1, source_target_pairs={{0,4},{1,3},{4,8},{5,1},{8,12},{9,5},{12,14},{13,9},{14,10},{15,13... | collective-permute-start | bytes 491528 | tf_op jit(solution)/shard_map/ppermute | solution.py:278
  13.3 6.7 %collective-permute-start.10 = (bf16[640,128]{1,0:T(8,128)(2,1)S(1)}, bf16[640,128]{1,0:T(8,128)(2,1)S(1)}, u32[]{:S(2)}, u32[]{:S(2)}) collective-permute-start(bf16[640,128]{1,0:T(8,128)(2,1)S(1)} %collective-permute-done.8.refs_5_), channel_id=1, source_target_pairs={{0,2},{1,5},{4,0},{5,9},{8,4},{9,13},{12,8},{13,15},{14,12},{15,11... | collective-permute-start | bytes 491528 | tf_op jit(solution)/shard_map/ppermute | solution.py:278
  14.9 8.2 %collective-permute-start.3 = (bf16[656,128]{1,0:T(8,128)(2,1)S(1)}, bf16[656,128]{1,0:T(8,128)(2,1)S(1)}, u32[]{:S(2)}, u32[]{:S(2)}) collective-permute-start(bf16[656,128]{1,0:T(8,128)(2,1)S(1)} %collective-permute-done.2.refs_4_), channel_id=1, source_target_pairs={{0,2},{1,5},{4,0},{5,9},{8,4},{9,13},{12,8},{13,15},{14,12},{15,11... | collective-permute-start | bytes 503816 | tf_op jit(solution)/shard_map/ppermute | solution.py:278
  17.0 8.6 %collective-permute-start.6 = (bf16[656,128]{1,0:T(8,128)(2,1)S(1)}, bf16[656,128]{1,0:T(8,128)(2,1)S(1)}, u32[]{:S(2)}, u32[]{:S(2)}) collective-permute-start(bf16[656,128]{1,0:T(8,128)(2,1)S(1)} %collective-permute-done.5.refs_6_), channel_id=1, source_target_pairs={{0,4},{1,3},{4,8},{5,1},{8,12},{9,5},{12,14},{13,9},{14,10},{15,13... | collective-permute-start | bytes 503816 | tf_op jit(solution)/shard_map/ppermute | solution.py:278
  20.0 7.6 %collective-permute-start.11 = (bf16[640,128]{1,0:T(8,128)(2,1)S(1)}, bf16[640,128]{1,0:T(8,128)(2,1)S(1)}, u32[]{:S(2)}, u32[]{:S(2)}) collective-permute-start(bf16[640,128]{1,0:T(8,128)(2,1)S(1)} %collective-permute-done.9.refs_7_), channel_id=1, source_target_pairs={{0,4},{1,3},{4,8},{5,1},{8,12},{9,5},{12,14},{13,9},{14,10},{15,13... | collective-permute-start | bytes 491528 | tf_op jit(solution)/shard_map/ppermute | solution.py:278
  23.1 9.1 %collective-permute-start.12 = (bf16[656,128]{1,0:T(8,128)(2,1)S(1)}, bf16[656,128]{1,0:T(8,128)(2,1)S(1)}, u32[]{:S(2)}, u32[]{:S(2)}) collective-permute-start(bf16[656,128]{1,0:T(8,128)(2,1)S(1)} %collective-permute-done.3.refs_8_), channel_id=1, source_target_pairs={{0,2},{1,5},{4,0},{5,9},{8,4},{9,13},{12,8},{13,15},{14,12},{15,11... | collective-permute-start | bytes 503816 | tf_op jit(solution)/shard_map/ppermute | solution.py:278
  25.6 7.4 %collective-permute-start.14 = (bf16[656,128]{1,0:T(8,128)(2,1)S(1)}, bf16[656,128]{1,0:T(8,128)(2,1)S(1)}, u32[]{:S(2)}, u32[]{:S(2)}) collective-permute-start(bf16[656,128]{1,0:T(8,128)(2,1)S(1)} %collective-permute-done.6.refs_0_), channel_id=1, source_target_pairs={{0,4},{1,3},{4,8},{5,1},{8,12},{9,5},{12,14},{13,9},{14,10},{15,13... | collective-permute-start | bytes 503816 | tf_op jit(solution)/shard_map/ppermute | solution.py:278
  25.6 6.6 %collective-permute-start.13 = (bf16[640,128]{1,0:T(8,128)(2,1)S(1)}, bf16[640,128]{1,0:T(8,128)(2,1)S(1)}, u32[]{:S(2)}, u32[]{:S(2)}) collective-permute-start(bf16[640,128]{1,0:T(8,128)(2,1)S(1)} %collective-permute-done.10.refs_9_), channel_id=1, source_target_pairs={{0,2},{1,5},{4,0},{5,9},{8,4},{9,13},{12,8},{13,15},{14,12},{15,11... | collective-permute-start | bytes 491528 | tf_op jit(solution)/shard_map/ppermute | solution.py:278
  27.6 5.3 %collective-permute-start.15 = (bf16[640,128]{1,0:T(8,128)(2,1)S(1)}, bf16[640,128]{1,0:T(8,128)(2,1)S(1)}, u32[]{:S(2)}, u32[]{:S(2)}) collective-permute-start(bf16[640,128]{1,0:T(8,128)(2,1)S(1)} %collective-permute-done.11.refs_1_), channel_id=1, source_target_pairs={{0,4},{1,3},{4,8},{5,1},{8,12},{9,5},{12,14},{13,9},{14,10},{15,13... | collective-permute-start | bytes 491528 | tf_op jit(solution)/shard_map/ppermute | solution.py:278

commit v15 on v12

--- a/solution.py
+++ b/solution.py
@@ -133,17 +133,20 @@
     return look_up(order, lax.rem(look_up(spots, lax.axis_index("row")) - ahead + len(order), len(order)))
 
 
-def add_products(panels, parts, total, first, feet, where, sem):
+def add_products(a_ref, sources, refs, total, first, feet, where, sem):
     groups, bs = total.shape[0], total.shape[3] // 2
-    pairs = len(parts) // feet.shape[0]
-    slots = (parts[0].shape[0] - FOOT) // bs
-    for k in range(feet.shape[0]):
-        feet[k] = parts[k * pairs][slots * bs :, :].astype(jnp.float32).astype(jnp.int32)
+    parts, panels, refs = [], [], list(refs)
+    for k, (place, start, stop) in enumerate(sources):
+        mine, refs, place = refs[:stop], refs[stop:], place()
+        slots = (mine[0].shape[0] - FOOT) // bs
+        feet[k] = mine[0][slots * bs :, :].astype(jnp.float32).astype(jnp.int32)
+        parts += [(mine[p], k, 2 * p) for p in range(start, stop)]
+        panels += [a_ref[place, p] for p in range(start, stop)]
     copy = pltpu.make_async_copy(feet, where, sem)
     copy.start()
     copy.wait()
     low = lax.broadcasted_iota(jnp.int32, (bs, 2 * bs), 1) < bs
-    left_side = jnp.concatenate([panel[...] for panel in panels], axis=-1)
+    left_side = jnp.concatenate(panels, axis=-1)
 
     def block(part, slot):
         at = pl.multiple_of(jnp.minimum(slot, slots - 1) * bs, bs)
@@ -151,12 +154,12 @@
 
     def body(g, carry):
         rows = []
-        for k, part in enumerate(parts):
+        for part, k, r in parts:
             for h in range(2):
                 tiles = []
                 for q in (2 * g, 2 * g + 1):
-                    left = block(part, where[k // pairs, k % pairs * 2 + h, 2 * q])
-                    right = block(part, where[k // pairs, k % pairs * 2 + h, 2 * q + 1])
+                    left = block(part, where[k, r + h, 2 * q])
+                    right = block(part, where[k, r + h, 2 * q + 1])
                     if h == 0:
                         right = pltpu.roll(right, bs, 1)
                     else:
@@ -175,25 +178,21 @@
     lax.fori_loop(0, groups, body, 0, unroll=min(groups, 4))
 
 
-def split(a_ref, sources, parts):
-    return [a_ref.at[place, p] for place in [source() for source in sources] for p in range(a_ref.shape[1])], parts
-
-
 def first_kernel(sources, a_ref, *refs):
     *parts, total, feet, where, sem = refs
-    add_products(*split(a_ref, sources, parts), total, True, feet, where, sem)
+    add_products(a_ref, sources, parts, total, True, feet, where, sem)
 
 
 def middle_kernel(sources, a_ref, before, *refs):
     *parts, total, feet, where, sem = refs
-    add_products(*split(a_ref, sources, parts), total, False, feet, where, sem)
+    add_products(a_ref, sources, parts, total, False, feet, where, sem)
 
 
 def last_kernel(sources, a_ref, total, cols_hbm, *refs):
     *parts, o_hbm, feet, where, sem, cols_ref, o_ref, cols_sem, sems = refs
     fetch = pltpu.make_async_copy(cols_hbm, cols_ref, cols_sem)
     fetch.start()
-    add_products(*split(a_ref, sources, parts), total, False, feet, where, sem)
+    add_products(a_ref, sources, parts, total, False, feet, where, sem)
     fetch.wait()
     rows, slots, bs, _ = o_ref.shape
     half = total.shape[0] * 4
@@ -215,8 +214,10 @@
 def product(order, arrived, a, total, out, cols=None):
     hbm, vmem = pl.BlockSpec(memory_space=pl.ANY), pl.BlockSpec(memory_space=VMEM)
     kernel = first_kernel if total is None else middle_kernel if cols is None else last_kernel
-    sources = [functools.partial(arrived_from, order, way, steps) for way, steps, _ in arrived]
-    parts = [ref for _, _, refs in arrived for ref in refs]
+    sources = [
+        (functools.partial(arrived_from, order, way, steps), start, len(refs)) for way, steps, refs, start in arrived
+    ]
+    parts = [ref for _, _, refs, _ in arrived for ref in refs]
     feet = (len(arrived), FOOT, parts[0].shape[1])
     scratch = [VMEM(feet, jnp.int32), SMEM(feet, jnp.int32), pltpu.SemaphoreType.DMA]
     arrays, specs = [a], [vmem]
@@ -263,7 +264,7 @@
     total_shape = jax.ShapeDtypeStruct((half // 4, 2, rows * bs, 2 * bs), jnp.float32)
     total = None
     held = {way: parts for way in hops}
-    rounds = [[(1, 0, parts)]]
+    rounds = [[(1, 0, parts, 0)]]
     for step in range(1, hops[1] + 1):
         ways = [way for way in hops if step <= hops[way]]
         for way in ways:
@@ -276,11 +277,13 @@
                 total = product(order, rounds.pop(0), a, total, total_shape)
                 sent[0], total = lax.optimization_barrier((sent[0], total))
             held[way] = [lax.ppermute(part, ("row", "col"), ring(way)) for part in sent]
-        rounds.append([(way, step, held[way]) for way in ways])
+        rounds.append([(way, step, held[way], 0) for way in ways])
     *_, late, last = rounds
     total = product(order, sum(rounds[:-2], late[:1]), a, total, total_shape)
+    late = late[1:] + last
+    total = product(order, [(*what, refs[:1], 0) for *what, refs, _ in late], a, total, total_shape)
     out = jax.ShapeDtypeStruct(a_vals.shape, a_vals.dtype)
-    return product(order, late[1:] + last, a, total, out, cols)
+    return product(order, [(*what, refs, 1) for *what, refs, _ in late], a, total, out, cols)
 
 
 def ring_order(mesh):

time: 34.8 us -> 34.6 us (level)
  waiting for transfers between devices: 6.21 us -> 4.81 us
  Pallas kernels: 9.55 us -> 10.7 us
    ppermute x14, waiting for transfers between devices: 5.05 us -> 3.65 us  [local(): held[way] = [lax.ppermute(part, ('row', 'col'), ring(way)) for part in sent]]
    pallas_call x3 -> x4, Pallas kernels: 6.36 us -> 7.47 us  [product(): pl.pallas_call(functools.partial(kernel, sources), out_shape=out, in_spec...]
  transfers between devices with their start and end apart: 16 -> 16, of which waited for: 10 -> 10; matrix products, arithmetic and copies ran while one was open for 0% -> 0% of each run, Pallas kernels for 16% -> 20%
where the time goes in v15:
time: 34.6 us; the launch traced here: 34.4 us
  starting transfers between devices  18.8 us (54%)
  Pallas kernels  10.7 us (31%)
  waiting for transfers between devices  4.81 us (14%)
    ppermute x14, starting transfers between devices, local(): held[way] = [lax.ppermute(part, ('row', 'col'), ring(way)) for part in sent]  18.8 us
    pallas_call x4, Pallas kernels, product(): pl.pallas_call(functools.partial(kernel, sources), out_shape=out, in_spec...  7.47 us
    ppermute x14, waiting for transfers between devices, local(): held[way] = [lax.ppermute(part, ('row', 'col'), ring(way)) for part in sent]  3.65 us
    pallas_call x1, Pallas kernels, dense_rows(): pl.pallas_call(dense_kernel, out_shape=jax.ShapeDtypeStruct((sources, row...  1.82 us
    pallas_call x1, Pallas kernels, pack(): pl.pallas_call(functools.partial(pack_kernel, half), out_shape=[jax.Shape...  1.37 us
    ppermute x2, waiting for transfers between devices, local(): a_other, others = (lax.ppermute(x, 'col', swap) for x in mine)  1.16 us
  transfers between devices with their start and end apart: 16, of which 10 were waited for; matrix products, arithmetic and copies ran while one was open for 0% of the time, Pallas kernels for 20%

profile of v15, /device:TPU:0, one launch (start us, length us, event | category | flops | bytes accessed | tf_op | source)
XLA Modules:
  0.0 34.4 jit_solution(1328762938079076597)
XLA Ops:
  0.0 0.0 copy-start
  0.0 1.4 %shard_map.37 = (bf16[656,128]{1,0:T(8,128)(2,1)S(1)}, bf16[640,128]{1,0:T(8,128)(2,1)S(1)}) custom-call(s32[4,10]{1,0:T(4,128)} %cols_hbm.3, bf16[4,10,64,64]{3,2,1,0:T(8,128)(2,1)} %b_hbm.1), custom_call_target="tpu_custom_call" | custom-call | bytes 655360 | tf_op jit(solution)/shard_map/pallas_call | solution.py:59
  1.4 0.0 copy-start.1
  1.4 3.1 %collective-permute-start.4 = (bf16[656,128]{1,0:T(8,128)(2,1)S(1)}, bf16[656,128]{1,0:T(8,128)(2,1)S(1)}, u32[]{:S(2)}, u32[]{:S(2)}) collective-permute-start(bf16[656,128]{1,0:T(8,128)(2,1)S(1)} %get-tuple-element.17.refs_0_), channel_id=1, source_target_pairs={{0,4},{1,3},{4,8},{5,1},{8,12},{9,5},{12,14},{13,9},{14,10},{15,13... | collective-permute-start | bytes 503816 | tf_op jit(solution)/shard_map/ppermute | solution.py:279
  4.5 0.0 copy-done
  4.5 0.0 collective-permute-start.1
  4.5 1.6 %collective-permute-start.7 = (bf16[640,128]{1,0:T(8,128)(2,1)S(1)}, bf16[640,128]{1,0:T(8,128)(2,1)S(1)}, u32[]{:S(2)}, u32[]{:S(2)}) collective-permute-start(bf16[640,128]{1,0:T(8,128)(2,1)S(1)} %get-tuple-element.21.refs_1_), channel_id=1, source_target_pairs={{0,4},{1,3},{4,8},{5,1},{8,12},{9,5},{12,14},{13,9},{14,10},{15,13... | collective-permute-start | bytes 491528 | tf_op jit(solution)/shard_map/ppermute | solution.py:279
  6.1 0.0 copy-done.1
  6.1 0.0 collective-permute-start
  6.1 1.2 %collective-permute-done.others_ref = s32[4,10]{1,0:T(4,128)S(1)} collective-permute-done((s32[4,10]{1,0:T(4,128)S(1)}, s32[4,10]{1,0:T(4,128)S(1)}, u32[]{:S(2)}, u32[]{:S(2)}) %collective-permute-start) | collective-permute-done | bytes 192 | tf_op jit(solution)/shard_map/ppermute | solution.py:262
  7.2 0.5 %collective-permute-start.2 = (bf16[656,128]{1,0:T(8,128)(2,1)S(1)}, bf16[656,128]{1,0:T(8,128)(2,1)S(1)}, u32[]{:S(2)}, u32[]{:S(2)}) collective-permute-start(bf16[656,128]{1,0:T(8,128)(2,1)S(1)} %get-tuple-element.17.refs_0_), channel_id=1, source_target_pairs={{0,2},{1,5},{4,0},{5,9},{8,4},{9,13},{12,8},{13,15},{14,12},{15,11... | collective-permute-start | bytes 503816 | tf_op jit(solution)/shard_map/ppermute | solution.py:279
  7.7 0.1 collective-permute-done.4.refs_2_
  7.8 2.1 %collective-permute-start.5 = (bf16[656,128]{1,0:T(8,128)(2,1)S(1)}, bf16[656,128]{1,0:T(8,128)(2,1)S(1)}, u32[]{:S(2)}, u32[]{:S(2)}) collective-permute-start(bf16[656,128]{1,0:T(8,128)(2,1)S(1)} %collective-permute-done.4.refs_2_), channel_id=1, source_target_pairs={{0,4},{1,3},{4,8},{5,1},{8,12},{9,5},{12,14},{13,9},{14,10},{15,13... | collective-permute-start | bytes 503816 | tf_op jit(solution)/shard_map/ppermute | solution.py:279
  9.8 0.0 collective-permute-start.10
  9.8 0.0 collective-permute-done.7.refs_3_
  9.8 2.0 %collective-permute-start.8 = (bf16[640,128]{1,0:T(8,128)(2,1)S(1)}, bf16[640,128]{1,0:T(8,128)(2,1)S(1)}, u32[]{:S(2)}, u32[]{:S(2)}) collective-permute-start(bf16[640,128]{1,0:T(8,128)(2,1)S(1)} %collective-permute-done.7.refs_3_), channel_id=1, source_target_pairs={{0,4},{1,3},{4,8},{5,1},{8,12},{9,5},{12,14},{13,9},{14,10},{15,13... | collective-permute-start | bytes 491528 | tf_op jit(solution)/shard_map/ppermute | solution.py:279
  11.9 0.0 collective-permute-done.1.other_ref
  11.9 1.8 %shard_map.38.a_ref = bf16[8,2,256,128]{3,2,1,0:T(8,128)(2,1)S(1)} custom-call(s32[4,10]{1,0:T(4,128)S(1)} %copy-done.1, s32[4,10]{1,0:T(4,128)S(1)} %collective-permute-done.others_ref, bf16[4,10,64,64]{3,2,1,0:T(8,128)(2,1)S(1)} %copy-done, bf16[4,10,64,64]{3,2,1,0:T(8,128)(2,1)S(1)} %collective-permute-done.1.other_ref), custom_call_target="tpu_custom_call" | custom-call | bytes 1310720 | tf_op jit(solution)/shard_map/pallas_call | solution.py:105
  13.7 0.2 collective-permute-done.2.refs_4_
  13.9 0.5 %collective-permute-start.3 = (bf16[656,128]{1,0:T(8,128)(2,1)S(1)}, bf16[656,128]{1,0:T(8,128)(2,1)S(1)}, u32[]{:S(2)}, u32[]{:S(2)}) collective-permute-start(bf16[656,128]{1,0:T(8,128)(2,1)S(1)} %collective-permute-done.2.refs_4_), channel_id=1, source_target_pairs={{0,2},{1,5},{4,0},{5,9},{8,4},{9,13},{12,8},{13,15},{14,12},{15,11... | collective-permute-start | bytes 503816 | tf_op jit(solution)/shard_map/ppermute | solution.py:279
  14.4 0.6 %collective-permute-done.5.refs_6_ = bf16[656,128]{1,0:T(8,128)(2,1)S(1)} collective-permute-done((bf16[656,128]{1,0:T(8,128)(2,1)S(1)}, bf16[656,128]{1,0:T(8,128)(2,1)S(1)}, u32[]{:S(2)}, u32[]{:S(2)}) %collective-permute-start.5) | collective-permute-done | bytes 167968 | tf_op jit(solution)/shard_map/ppermute | solution.py:279
  15.0 2.1 %collective-permute-start.6 = (bf16[656,128]{1,0:T(8,128)(2,1)S(1)}, bf16[656,128]{1,0:T(8,128)(2,1)S(1)}, u32[]{:S(2)}, u32[]{:S(2)}) collective-permute-start(bf16[656,128]{1,0:T(8,128)(2,1)S(1)} %collective-permute-done.5.refs_6_), channel_id=1, source_target_pairs={{0,4},{1,3},{4,8},{5,1},{8,12},{9,5},{12,14},{13,9},{14,10},{15,13... | collective-permute-start | bytes 503816 | tf_op jit(solution)/shard_map/ppermute | solution.py:279
  17.1 0.4 %collective-permute-done.10.refs_5_ = bf16[640,128]{1,0:T(8,128)(2,1)S(1)} collective-permute-done((bf16[640,128]{1,0:T(8,128)(2,1)S(1)}, bf16[640,128]{1,0:T(8,128)(2,1)S(1)}, u32[]{:S(2)}, u32[]{:S(2)}) %collective-permute-start.10) | collective-permute-done | bytes 163872 | tf_op jit(solution)/shard_map/ppermute | solution.py:279
  17.4 0.5 %collective-permute-start.11 = (bf16[640,128]{1,0:T(8,128)(2,1)S(1)}, bf16[640,128]{1,0:T(8,128)(2,1)S(1)}, u32[]{:S(2)}, u32[]{:S(2)}) collective-permute-start(bf16[640,128]{1,0:T(8,128)(2,1)S(1)} %collective-permute-done.10.refs_5_), channel_id=1, source_target_pairs={{0,2},{1,5},{4,0},{5,9},{8,4},{9,13},{12,8},{13,15},{14,12},{15,11... | collective-permute-start | bytes 491528 | tf_op jit(solution)/shard_map/ppermute | solution.py:279
  17.9 0.6 %collective-permute-done.8.refs_7_ = bf16[640,128]{1,0:T(8,128)(2,1)S(1)} collective-permute-done((bf16[640,128]{1,0:T(8,128)(2,1)S(1)}, bf16[640,128]{1,0:T(8,128)(2,1)S(1)}, u32[]{:S(2)}, u32[]{:S(2)}) %collective-permute-start.8) | collective-permute-done | bytes 163872 | tf_op jit(solution)/shard_map/ppermute | solution.py:279
  18.5 2.1 %collective-permute-start.9 = (bf16[640,128]{1,0:T(8,128)(2,1)S(1)}, bf16[640,128]{1,0:T(8,128)(2,1)S(1)}, u32[]{:S(2)}, u32[]{:S(2)}) collective-permute-start(bf16[640,128]{1,0:T(8,128)(2,1)S(1)} %collective-permute-done.8.refs_7_), channel_id=1, source_target_pairs={{0,4},{1,3},{4,8},{5,1},{8,12},{9,5},{12,14},{13,9},{14,10},{15,13... | collective-permute-start | bytes 491528 | tf_op jit(solution)/shard_map/ppermute | solution.py:279
  20.6 1.1 %shard_map.39.before = f32[4,2,256,128]{3,2,1,0:T(8,128)S(1)} custom-call(bf16[8,2,256,128]{3,2,1,0:T(8,128)(2,1)S(1)} %shard_map.38.a_ref, bf16[656,128]{1,0:T(8,128)(2,1)S(1)} %get-tuple-element.17.refs_0_, bf16[640,128]{1,0:T(8,128)(2,1)S(1)} %get-tuple-element.21.refs_1_), custom_call_target="tpu_custom_call" | custom-call | flops 134217728 | tf_op jit(solution)/shard_map/pallas_call | solution.py:234
  21.7 0.0 collective-permute-done.3.refs_8_
  21.7 0.1 collective-permute-start.12
  21.8 0.4 %collective-permute-done.6.refs_0_ = bf16[656,128]{1,0:T(8,128)(2,1)S(1)} collective-permute-done((bf16[656,128]{1,0:T(8,128)(2,1)S(1)}, bf16[656,128]{1,0:T(8,128)(2,1)S(1)}, u32[]{:S(2)}, u32[]{:S(2)}) %collective-permute-start.6) | collective-permute-done | bytes 167968 | tf_op jit(solution)/shard_map/ppermute | solution.py:279
  22.2 2.0 %collective-permute-start.13 = (bf16[656,128]{1,0:T(8,128)(2,1)S(1)}, bf16[656,128]{1,0:T(8,128)(2,1)S(1)}, u32[]{:S(2)}, u32[]{:S(2)}) collective-permute-start(bf16[656,128]{1,0:T(8,128)(2,1)S(1)} %collective-permute-done.6.refs_0_), channel_id=1, source_target_pairs={{0,4},{1,3},{4,8},{5,1},{8,12},{9,5},{12,14},{13,9},{14,10},{15,13... | collective-permute-start | bytes 503816 | tf_op jit(solution)/shard_map/ppermute | solution.py:279
  24.2 0.5 %collective-permute-done.11.refs_9_ = bf16[640,128]{1,0:T(8,128)(2,1)S(1)} collective-permute-done((bf16[640,128]{1,0:T(8,128)(2,1)S(1)}, bf16[640,128]{1,0:T(8,128)(2,1)S(1)}, u32[]{:S(2)}, u32[]{:S(2)}) %collective-permute-start.11) | collective-permute-done | bytes 163872 | tf_op jit(solution)/shard_map/ppermute | solution.py:279
  24.7 0.5 %collective-permute-start.14 = (bf16[640,128]{1,0:T(8,128)(2,1)S(1)}, bf16[640,128]{1,0:T(8,128)(2,1)S(1)}, u32[]{:S(2)}, u32[]{:S(2)}) collective-permute-start(bf16[640,128]{1,0:T(8,128)(2,1)S(1)} %collective-permute-done.11.refs_9_), channel_id=1, source_target_pairs={{0,2},{1,5},{4,0},{5,9},{8,4},{9,13},{12,8},{13,15},{14,12},{15,11... | collective-permute-start | bytes 491528 | tf_op jit(solution)/shard_map/ppermute | solution.py:279
  25.1 0.6 %collective-permute-done.9.refs_1_ = bf16[640,128]{1,0:T(8,128)(2,1)S(1)} collective-permute-done((bf16[640,128]{1,0:T(8,128)(2,1)S(1)}, bf16[640,128]{1,0:T(8,128)(2,1)S(1)}, u32[]{:S(2)}, u32[]{:S(2)}) %collective-permute-start.9) | collective-permute-done | bytes 163872 | tf_op jit(solution)/shard_map/ppermute | solution.py:279
  25.7 2.0 %collective-permute-start.15 = (bf16[640,128]{1,0:T(8,128)(2,1)S(1)}, bf16[640,128]{1,0:T(8,128)(2,1)S(1)}, u32[]{:S(2)}, u32[]{:S(2)}) collective-permute-start(bf16[640,128]{1,0:T(8,128)(2,1)S(1)} %collective-permute-done.9.refs_1_), channel_id=1, source_target_pairs={{0,4},{1,3},{4,8},{5,1},{8,12},{9,5},{12,14},{13,9},{14,10},{15,13... | collective-permute-start | bytes 491528 | tf_op jit(solution)/shard_map/ppermute | solution.py:279
  27.7 2.8 %shard_map.40.before = f32[4,2,256,128]{3,2,1,0:T(8,128)S(1)} custom-call(bf16[8,2,256,128]{3,2,1,0:T(8,128)(2,1)S(1)} %shard_map.38.a_ref, f32[4,2,256,128]{3,2,1,0:T(8,128)S(1)} %shard_map.39.before, bf16[656,128]{1,0:T(8,128)(2,1)S(1)} %collective-permute-done.6.refs_0_, ...), custom_call_target="tpu_custom_call", output_to_operand_aliasing={{}: (1, {})} | custom-call | flops 671088640 | tf_op jit(solution)/shard_map/pallas_call | solution.py:234
  30.5 0.0 collective-permute-done.12.refs_0_
  30.5 0.0 collective-permute-done.13.refs_1_.refs_2_
  30.5 1.3 %shard_map.41.total = f32[4,2,256,128]{3,2,1,0:T(8,128)S(1)} custom-call(bf16[8,2,256,128]{3,2,1,0:T(8,128)(2,1)S(1)} %shard_map.38.a_ref, f32[4,2,256,128]{3,2,1,0:T(8,128)S(1)} %shard_map.40.before, bf16[656,128]{1,0:T(8,128)(2,1)S(1)} %collective-permute-done.12.refs_0_, ...), custom_call_target="tpu_custom_call", output_to_operand_aliasing={{}: (1, {})} | custom-call | flops 268435456 | tf_op jit(solution)/shard_map/pallas_call | solution.py:234
  31.8 0.3 collective-permute-done.14.refs_1_
  32.1 0.0 collective-permute-done.15.refs_3_
  32.1 2.3 %shard_map.42 = bf16[4,10,64,64]{3,2,1,0:T(8,128)(2,1)} custom-call(bf16[8,2,256,128]{3,2,1,0:T(8,128)(2,1)S(1)} %shard_map.38.a_ref, f32[4,2,256,128]{3,2,1,0:T(8,128)S(1)} %shard_map.41.total, s32[4,10]{1,0:T(4,128)S(1)} %copy-done.1, bf16[656,128]{1,0:T(8,128)(2,1)S(1)} %collective-permute-done.12.refs_0_, ...), custom_call_target="tpu_custom_call" | custom-call | flops 167772160 | tf_op jit(solution)/shard_map/pallas_call | solution.py:234
Async XLA Ops:
  0.0 4.5 %copy-start = (bf16[4,10,64,64]{3,2,1,0:T(8,128)(2,1)S(1)}, bf16[4,10,64,64]{3,2,1,0:T(8,128)(2,1)}, u32[]{:S(2)}) copy-start(bf16[4,10,64,64]{3,2,1,0:T(8,128)(2,1)} %own_ref.1) | copy-start | bytes 983044
  1.4 4.7 %copy-start.1 = (s32[4,10]{1,0:T(4,128)S(1)}, s32[4,10]{1,0:T(4,128)}, u32[]{:S(2)}) copy-start(s32[4,10]{1,0:T(4,128)} %cols_hbm.3) | copy-start | bytes 484
  1.4 6.4 %collective-permute-start.4 = (bf16[656,128]{1,0:T(8,128)(2,1)S(1)}, bf16[656,128]{1,0:T(8,128)(2,1)S(1)}, u32[]{:S(2)}, u32[]{:S(2)}) collective-permute-start(bf16[656,128]{1,0:T(8,128)(2,1)S(1)} %get-tuple-element.17.refs_0_), channel_id=1, source_target_pairs={{0,4},{1,3},{4,8},{5,1},{8,12},{9,5},{12,14},{13,9},{14,10},{15,13... | collective-permute-start | bytes 503816 | tf_op jit(solution)/shard_map/ppermute | solution.py:279
  4.5 7.4 %collective-permute-start.1 = (bf16[4,10,64,64]{3,2,1,0:T(8,128)(2,1)S(1)}, bf16[4,10,64,64]{3,2,1,0:T(8,128)(2,1)S(1)}, u32[]{:S(2)}, u32[]{:S(2)}) collective-permute-start(bf16[4,10,64,64]{3,2,1,0:T(8,128)(2,1)S(1)} %copy-done), channel_id=1, source_target_pairs={{0,1},{1,0},{2,3},{3,2},{4,5},{5,4},{6,7},{7,6},{8,9},{9,8},{10,11... | collective-permute-start | bytes 983048 | tf_op jit(solution)/shard_map/ppermute | solution.py:262
  4.5 5.4 %collective-permute-start.7 = (bf16[640,128]{1,0:T(8,128)(2,1)S(1)}, bf16[640,128]{1,0:T(8,128)(2,1)S(1)}, u32[]{:S(2)}, u32[]{:S(2)}) collective-permute-start(bf16[640,128]{1,0:T(8,128)(2,1)S(1)} %get-tuple-element.21.refs_1_), channel_id=1, source_target_pairs={{0,4},{1,3},{4,8},{5,1},{8,12},{9,5},{12,14},{13,9},{14,10},{15,13... | collective-permute-start | bytes 491528 | tf_op jit(solution)/shard_map/ppermute | solution.py:279
  6.1 1.2 %collective-permute-start = (s32[4,10]{1,0:T(4,128)S(1)}, s32[4,10]{1,0:T(4,128)S(1)}, u32[]{:S(2)}, u32[]{:S(2)}) collective-permute-start(s32[4,10]{1,0:T(4,128)S(1)} %copy-done.1), channel_id=1, source_target_pairs={{0,1},{1,0},{2,3},{3,2},{4,5},{5,4},{6,7},{7,6},{8,9},{9,8},{10,11... | collective-permute-start | bytes 488 | tf_op jit(solution)/shard_map/ppermute | solution.py:262
  7.2 6.7 %collective-permute-start.2 = (bf16[656,128]{1,0:T(8,128)(2,1)S(1)}, bf16[656,128]{1,0:T(8,128)(2,1)S(1)}, u32[]{:S(2)}, u32[]{:S(2)}) collective-permute-start(bf16[656,128]{1,0:T(8,128)(2,1)S(1)} %get-tuple-element.17.refs_0_), channel_id=1, source_target_pairs={{0,2},{1,5},{4,0},{5,9},{8,4},{9,13},{12,8},{13,15},{14,12},{15,11... | collective-permute-start | bytes 503816 | tf_op jit(solution)/shard_map/ppermute | solution.py:279
  7.8 7.2 %collective-permute-start.5 = (bf16[656,128]{1,0:T(8,128)(2,1)S(1)}, bf16[656,128]{1,0:T(8,128)(2,1)S(1)}, u32[]{:S(2)}, u32[]{:S(2)}) collective-permute-start(bf16[656,128]{1,0:T(8,128)(2,1)S(1)} %collective-permute-done.4.refs_2_), channel_id=1, source_target_pairs={{0,4},{1,3},{4,8},{5,1},{8,12},{9,5},{12,14},{13,9},{14,10},{15,13... | collective-permute-start | bytes 503816 | tf_op jit(solution)/shard_map/ppermute | solution.py:279
  9.8 7.6 %collective-permute-start.10 = (bf16[640,128]{1,0:T(8,128)(2,1)S(1)}, bf16[640,128]{1,0:T(8,128)(2,1)S(1)}, u32[]{:S(2)}, u32[]{:S(2)}) collective-permute-start(bf16[640,128]{1,0:T(8,128)(2,1)S(1)} %get-tuple-element.21.refs_1_), channel_id=1, source_target_pairs={{0,2},{1,5},{4,0},{5,9},{8,4},{9,13},{12,8},{13,15},{14,12},{15,11... | collective-permute-start | bytes 491528 | tf_op jit(solution)/shard_map/ppermute | solution.py:279
  9.8 8.6 %collective-permute-start.8 = (bf16[640,128]{1,0:T(8,128)(2,1)S(1)}, bf16[640,128]{1,0:T(8,128)(2,1)S(1)}, u32[]{:S(2)}, u32[]{:S(2)}) collective-permute-start(bf16[640,128]{1,0:T(8,128)(2,1)S(1)} %collective-permute-done.7.refs_3_), channel_id=1, source_target_pairs={{0,4},{1,3},{4,8},{5,1},{8,12},{9,5},{12,14},{13,9},{14,10},{15,13... | collective-permute-start | bytes 491528 | tf_op jit(solution)/shard_map/ppermute | solution.py:279
  13.9 7.8 %collective-permute-start.3 = (bf16[656,128]{1,0:T(8,128)(2,1)S(1)}, bf16[656,128]{1,0:T(8,128)(2,1)S(1)}, u32[]{:S(2)}, u32[]{:S(2)}) collective-permute-start(bf16[656,128]{1,0:T(8,128)(2,1)S(1)} %collective-permute-done.2.refs_4_), channel_id=1, source_target_pairs={{0,2},{1,5},{4,0},{5,9},{8,4},{9,13},{12,8},{13,15},{14,12},{15,11... | collective-permute-start | bytes 503816 | tf_op jit(solution)/shard_map/ppermute | solution.py:279
  15.0 7.2 %collective-permute-start.6 = (bf16[656,128]{1,0:T(8,128)(2,1)S(1)}, bf16[656,128]{1,0:T(8,128)(2,1)S(1)}, u32[]{:S(2)}, u32[]{:S(2)}) collective-permute-start(bf16[656,128]{1,0:T(8,128)(2,1)S(1)} %collective-permute-done.5.refs_6_), channel_id=1, source_target_pairs={{0,4},{1,3},{4,8},{5,1},{8,12},{9,5},{12,14},{13,9},{14,10},{15,13... | collective-permute-start | bytes 503816 | tf_op jit(solution)/shard_map/ppermute | solution.py:279
  17.4 7.2 %collective-permute-start.11 = (bf16[640,128]{1,0:T(8,128)(2,1)S(1)}, bf16[640,128]{1,0:T(8,128)(2,1)S(1)}, u32[]{:S(2)}, u32[]{:S(2)}) collective-permute-start(bf16[640,128]{1,0:T(8,128)(2,1)S(1)} %collective-permute-done.10.refs_5_), channel_id=1, source_target_pairs={{0,2},{1,5},{4,0},{5,9},{8,4},{9,13},{12,8},{13,15},{14,12},{15,11... | collective-permute-start | bytes 491528 | tf_op jit(solution)/shard_map/ppermute | solution.py:279
  18.5 7.2 %collective-permute-start.9 = (bf16[640,128]{1,0:T(8,128)(2,1)S(1)}, bf16[640,128]{1,0:T(8,128)(2,1)S(1)}, u32[]{:S(2)}, u32[]{:S(2)}) collective-permute-start(bf16[640,128]{1,0:T(8,128)(2,1)S(1)} %collective-permute-done.8.refs_7_), channel_id=1, source_target_pairs={{0,4},{1,3},{4,8},{5,1},{8,12},{9,5},{12,14},{13,9},{14,10},{15,13... | collective-permute-start | bytes 491528 | tf_op jit(solution)/shard_map/ppermute | solution.py:279
  21.7 8.7 %collective-permute-start.12 = (bf16[656,128]{1,0:T(8,128)(2,1)S(1)}, bf16[656,128]{1,0:T(8,128)(2,1)S(1)}, u32[]{:S(2)}, u32[]{:S(2)}) collective-permute-start(bf16[656,128]{1,0:T(8,128)(2,1)S(1)} %collective-permute-done.3.refs_8_), channel_id=1, source_target_pairs={{0,2},{1,5},{4,0},{5,9},{8,4},{9,13},{12,8},{13,15},{14,12},{15,11... | collective-permute-start | bytes 503816 | tf_op jit(solution)/shard_map/ppermute | solution.py:279
  22.2 8.3 %collective-permute-start.13 = (bf16[656,128]{1,0:T(8,128)(2,1)S(1)}, bf16[656,128]{1,0:T(8,128)(2,1)S(1)}, u32[]{:S(2)}, u32[]{:S(2)}) collective-permute-start(bf16[656,128]{1,0:T(8,128)(2,1)S(1)} %collective-permute-done.6.refs_0_), channel_id=1, source_target_pairs={{0,4},{1,3},{4,8},{5,1},{8,12},{9,5},{12,14},{13,9},{14,10},{15,13... | collective-permute-start | bytes 503816 | tf_op jit(solution)/shard_map/ppermute | solution.py:279
  24.7 7.4 %collective-permute-start.14 = (bf16[640,128]{1,0:T(8,128)(2,1)S(1)}, bf16[640,128]{1,0:T(8,128)(2,1)S(1)}, u32[]{:S(2)}, u32[]{:S(2)}) collective-permute-start(bf16[640,128]{1,0:T(8,128)(2,1)S(1)} %collective-permute-done.11.refs_9_), channel_id=1, source_target_pairs={{0,2},{1,5},{4,0},{5,9},{8,4},{9,13},{12,8},{13,15},{14,12},{15,11... | collective-permute-start | bytes 491528 | tf_op jit(solution)/shard_map/ppermute | solution.py:279
  25.7 6.4 %collective-permute-start.15 = (bf16[640,128]{1,0:T(8,128)(2,1)S(1)}, bf16[640,128]{1,0:T(8,128)(2,1)S(1)}, u32[]{:S(2)}, u32[]{:S(2)}) collective-permute-start(bf16[640,128]{1,0:T(8,128)(2,1)S(1)} %collective-permute-done.9.refs_1_), channel_id=1, source_target_pairs={{0,4},{1,3},{4,8},{5,1},{8,12},{9,5},{12,14},{13,9},{14,10},{15,13... | collective-permute-start | bytes 491528 | tf_op jit(solution)/shard_map/ppermute | solution.py:279

commit v16 on v15

--- a/solution.py
+++ b/solution.py
@@ -12,7 +12,7 @@
 VMEM = pltpu.VMEM
 SMEM = pltpu.SMEM
 LIMIT = 48 * 1024 * 1024
-STRIDE = 5
+STRIDE = 2
 FOOT = 16
 
 
@@ -31,11 +31,14 @@
 def pack_kernel(half, cols_hbm, b_hbm, *refs):
     *o_refs, cols_ref, b_ref, sem, sems = refs
     rows, slots, bs, _ = b_ref.shape
-    copies = [pltpu.make_async_copy(b_hbm.at[r], b_ref.at[r], sems.at[r]) for r in range(rows)]
     fetch = pltpu.make_async_copy(cols_hbm, cols_ref, sem)
     fetch.start()
-    for copy in copies:
-        copy.start()
+    copies = {}
+    for r in range(rows):
+        for k in range(0, slots, STRIDE):
+            some = pl.ds(k, min(STRIDE, slots - k))
+            copies[r, k] = pltpu.make_async_copy(b_hbm.at[r, some], b_ref.at[r, some], sems.at[r, k // STRIDE])
+            copies[r, k].start()
     row = lax.broadcasted_iota(jnp.int32, (FOOT, 2 * bs), 0)
     lane = lax.broadcasted_iota(jnp.int32, (FOOT, 2 * bs), 1)
     fetch.wait()
@@ -46,9 +49,10 @@
             foot = jnp.where(here, n, foot)
     o_refs[0][slots * bs :, :] = foot.astype(jnp.float32).astype(b_ref.dtype)
     for p, o_ref in enumerate(o_refs):
-        copies[2 * p].wait()
-        copies[2 * p + 1].wait()
         for n in range(slots):
+            if n % STRIDE == 0:
+                copies[2 * p, n].wait()
+                copies[2 * p + 1, n].wait()
             o_ref[n * bs : (n + 1) * bs, :] = jnp.concatenate([b_ref[2 * p, n], b_ref[2 * p + 1, n]], axis=-1)
 
 
@@ -65,7 +69,7 @@
             SMEM(cols.shape, cols.dtype),
             VMEM(b_vals.shape, b_vals.dtype),
             pltpu.SemaphoreType.DMA,
-            pltpu.SemaphoreType.DMA((rows,)),
+            pltpu.SemaphoreType.DMA((rows, -(-slots // STRIDE))),
         ],
         compiler_params=params(),
         cost_estimate=cost(0, 2 * b_vals.size * 2),

time: 34.6 us -> 35.2 us (1.017)
  Pallas kernels: 10.7 us -> 11.3 us
    pallas_call x1, Pallas kernels: 1.37 us -> 1.88 us  [pack(): pl.pallas_call(functools.partial(pack_kernel, half), out_shape=[jax.Shape...]
where the time goes in v16:
time: 35.2 us; the launch traced here: 35 us
  starting transfers between devices  18.8 us (53%)
  Pallas kernels  11.3 us (32%)
  waiting for transfers between devices  4.82 us (14%)
    ppermute x14, starting transfers between devices, local(): held[way] = [lax.ppermute(part, ('row', 'col'), ring(way)) for part in sent]  18.8 us
    pallas_call x4, Pallas kernels, product(): pl.pallas_call(functools.partial(kernel, sources), out_shape=out, in_spec...  7.55 us
    ppermute x14, waiting for transfers between devices, local(): held[way] = [lax.ppermute(part, ('row', 'col'), ring(way)) for part in sent]  3.67 us
    pallas_call x1, Pallas kernels, pack(): pl.pallas_call(functools.partial(pack_kernel, half), out_shape=[jax.Shape...  1.88 us
    pallas_call x1, Pallas kernels, dense_rows(): pl.pallas_call(dense_kernel, out_shape=jax.ShapeDtypeStruct((sources, row...  1.82 us
    ppermute x2, waiting for transfers between devices, local(): a_other, others = (lax.ppermute(x, 'col', swap) for x in mine)  1.16 us
  transfers between devices with their start and end apart: 16, of which 10 were waited for; matrix products, arithmetic and copies ran while one was open for 0% of the time, Pallas kernels for 20%

profile of v16, /device:TPU:0, one launch (start us, length us, event | category | flops | bytes accessed | tf_op | source)
XLA Modules:
  0.0 35.0 jit_solution(12957430803396785152)
XLA Ops:
  0.0 0.0 copy-start
  0.0 1.9 %shard_map.37 = (bf16[656,128]{1,0:T(8,128)(2,1)S(1)}, bf16[640,128]{1,0:T(8,128)(2,1)S(1)}) custom-call(s32[4,10]{1,0:T(4,128)} %cols_hbm.3, bf16[4,10,64,64]{3,2,1,0:T(8,128)(2,1)} %b_hbm.1), custom_call_target="tpu_custom_call" | custom-call | bytes 655360 | tf_op jit(solution)/shard_map/pallas_call | solution.py:63
  1.9 0.0 copy-start.1
  1.9 3.1 %collective-permute-start.4 = (bf16[656,128]{1,0:T(8,128)(2,1)S(1)}, bf16[656,128]{1,0:T(8,128)(2,1)S(1)}, u32[]{:S(2)}, u32[]{:S(2)}) collective-permute-start(bf16[656,128]{1,0:T(8,128)(2,1)S(1)} %get-tuple-element.17.refs_0_), channel_id=1, source_target_pairs={{0,4},{1,3},{4,8},{5,1},{8,12},{9,5},{12,14},{13,9},{14,10},{15,13... | collective-permute-start | bytes 503816 | tf_op jit(solution)/shard_map/ppermute | solution.py:283
  5.0 0.0 copy-done
  5.0 0.0 collective-permute-start.1
  5.0 1.6 %collective-permute-start.7 = (bf16[640,128]{1,0:T(8,128)(2,1)S(1)}, bf16[640,128]{1,0:T(8,128)(2,1)S(1)}, u32[]{:S(2)}, u32[]{:S(2)}) collective-permute-start(bf16[640,128]{1,0:T(8,128)(2,1)S(1)} %get-tuple-element.21.refs_1_), channel_id=1, source_target_pairs={{0,4},{1,3},{4,8},{5,1},{8,12},{9,5},{12,14},{13,9},{14,10},{15,13... | collective-permute-start | bytes 491528 | tf_op jit(solution)/shard_map/ppermute | solution.py:283
  6.6 0.0 copy-done.1
  6.6 0.0 collective-permute-start
  6.6 1.2 %collective-permute-done.others_ref = s32[4,10]{1,0:T(4,128)S(1)} collective-permute-done((s32[4,10]{1,0:T(4,128)S(1)}, s32[4,10]{1,0:T(4,128)S(1)}, u32[]{:S(2)}, u32[]{:S(2)}) %collective-permute-start) | collective-permute-done | bytes 192 | tf_op jit(solution)/shard_map/ppermute | solution.py:266
  7.7 0.5 %collective-permute-start.2 = (bf16[656,128]{1,0:T(8,128)(2,1)S(1)}, bf16[656,128]{1,0:T(8,128)(2,1)S(1)}, u32[]{:S(2)}, u32[]{:S(2)}) collective-permute-start(bf16[656,128]{1,0:T(8,128)(2,1)S(1)} %get-tuple-element.17.refs_0_), channel_id=1, source_target_pairs={{0,2},{1,5},{4,0},{5,9},{8,4},{9,13},{12,8},{13,15},{14,12},{15,11... | collective-permute-start | bytes 503816 | tf_op jit(solution)/shard_map/ppermute | solution.py:283
  8.2 0.1 collective-permute-done.4.refs_2_
  8.3 2.1 %collective-permute-start.5 = (bf16[656,128]{1,0:T(8,128)(2,1)S(1)}, bf16[656,128]{1,0:T(8,128)(2,1)S(1)}, u32[]{:S(2)}, u32[]{:S(2)}) collective-permute-start(bf16[656,128]{1,0:T(8,128)(2,1)S(1)} %collective-permute-done.4.refs_2_), channel_id=1, source_target_pairs={{0,4},{1,3},{4,8},{5,1},{8,12},{9,5},{12,14},{13,9},{14,10},{15,13... | collective-permute-start | bytes 503816 | tf_op jit(solution)/shard_map/ppermute | solution.py:283
  10.3 0.0 collective-permute-start.10
  10.3 0.0 collective-permute-done.7.refs_3_
  10.4 2.0 %collective-permute-start.8 = (bf16[640,128]{1,0:T(8,128)(2,1)S(1)}, bf16[640,128]{1,0:T(8,128)(2,1)S(1)}, u32[]{:S(2)}, u32[]{:S(2)}) collective-permute-start(bf16[640,128]{1,0:T(8,128)(2,1)S(1)} %collective-permute-done.7.refs_3_), channel_id=1, source_target_pairs={{0,4},{1,3},{4,8},{5,1},{8,12},{9,5},{12,14},{13,9},{14,10},{15,13... | collective-permute-start | bytes 491528 | tf_op jit(solution)/shard_map/ppermute | solution.py:283
  12.4 0.0 collective-permute-done.1.other_ref
  12.4 1.8 %shard_map.38.a_ref = bf16[8,2,256,128]{3,2,1,0:T(8,128)(2,1)S(1)} custom-call(s32[4,10]{1,0:T(4,128)S(1)} %copy-done.1, s32[4,10]{1,0:T(4,128)S(1)} %collective-permute-done.others_ref, bf16[4,10,64,64]{3,2,1,0:T(8,128)(2,1)S(1)} %copy-done, bf16[4,10,64,64]{3,2,1,0:T(8,128)(2,1)S(1)} %collective-permute-done.1.other_ref), custom_call_target="tpu_custom_call" | custom-call | bytes 1310720 | tf_op jit(solution)/shard_map/pallas_call | solution.py:109
  14.2 0.2 collective-permute-done.2.refs_4_
  14.4 0.5 %collective-permute-start.3 = (bf16[656,128]{1,0:T(8,128)(2,1)S(1)}, bf16[656,128]{1,0:T(8,128)(2,1)S(1)}, u32[]{:S(2)}, u32[]{:S(2)}) collective-permute-start(bf16[656,128]{1,0:T(8,128)(2,1)S(1)} %collective-permute-done.2.refs_4_), channel_id=1, source_target_pairs={{0,2},{1,5},{4,0},{5,9},{8,4},{9,13},{12,8},{13,15},{14,12},{15,11... | collective-permute-start | bytes 503816 | tf_op jit(solution)/shard_map/ppermute | solution.py:283
  14.9 0.6 %collective-permute-done.5.refs_6_ = bf16[656,128]{1,0:T(8,128)(2,1)S(1)} collective-permute-done((bf16[656,128]{1,0:T(8,128)(2,1)S(1)}, bf16[656,128]{1,0:T(8,128)(2,1)S(1)}, u32[]{:S(2)}, u32[]{:S(2)}) %collective-permute-start.5) | collective-permute-done | bytes 167968 | tf_op jit(solution)/shard_map/ppermute | solution.py:283
  15.5 2.1 %collective-permute-start.6 = (bf16[656,128]{1,0:T(8,128)(2,1)S(1)}, bf16[656,128]{1,0:T(8,128)(2,1)S(1)}, u32[]{:S(2)}, u32[]{:S(2)}) collective-permute-start(bf16[656,128]{1,0:T(8,128)(2,1)S(1)} %collective-permute-done.5.refs_6_), channel_id=1, source_target_pairs={{0,4},{1,3},{4,8},{5,1},{8,12},{9,5},{12,14},{13,9},{14,10},{15,13... | collective-permute-start | bytes 503816 | tf_op jit(solution)/shard_map/ppermute | solution.py:283
  17.6 0.4 %collective-permute-done.10.refs_5_ = bf16[640,128]{1,0:T(8,128)(2,1)S(1)} collective-permute-done((bf16[640,128]{1,0:T(8,128)(2,1)S(1)}, bf16[640,128]{1,0:T(8,128)(2,1)S(1)}, u32[]{:S(2)}, u32[]{:S(2)}) %collective-permute-start.10) | collective-permute-done | bytes 163872 | tf_op jit(solution)/shard_map/ppermute | solution.py:283
  18.0 0.5 %collective-permute-start.11 = (bf16[640,128]{1,0:T(8,128)(2,1)S(1)}, bf16[640,128]{1,0:T(8,128)(2,1)S(1)}, u32[]{:S(2)}, u32[]{:S(2)}) collective-permute-start(bf16[640,128]{1,0:T(8,128)(2,1)S(1)} %collective-permute-done.10.refs_5_), channel_id=1, source_target_pairs={{0,2},{1,5},{4,0},{5,9},{8,4},{9,13},{12,8},{13,15},{14,12},{15,11... | collective-permute-start | bytes 491528 | tf_op jit(solution)/shard_map/ppermute | solution.py:283
  18.4 0.6 %collective-permute-done.8.refs_7_ = bf16[640,128]{1,0:T(8,128)(2,1)S(1)} collective-permute-done((bf16[640,128]{1,0:T(8,128)(2,1)S(1)}, bf16[640,128]{1,0:T(8,128)(2,1)S(1)}, u32[]{:S(2)}, u32[]{:S(2)}) %collective-permute-start.8) | collective-permute-done | bytes 163872 | tf_op jit(solution)/shard_map/ppermute | solution.py:283
  19.0 2.1 %collective-permute-start.9 = (bf16[640,128]{1,0:T(8,128)(2,1)S(1)}, bf16[640,128]{1,0:T(8,128)(2,1)S(1)}, u32[]{:S(2)}, u32[]{:S(2)}) collective-permute-start(bf16[640,128]{1,0:T(8,128)(2,1)S(1)} %collective-permute-done.8.refs_7_), channel_id=1, source_target_pairs={{0,4},{1,3},{4,8},{5,1},{8,12},{9,5},{12,14},{13,9},{14,10},{15,13... | collective-permute-start | bytes 491528 | tf_op jit(solution)/shard_map/ppermute | solution.py:283
  21.1 1.1 %shard_map.39.before = f32[4,2,256,128]{3,2,1,0:T(8,128)S(1)} custom-call(bf16[8,2,256,128]{3,2,1,0:T(8,128)(2,1)S(1)} %shard_map.38.a_ref, bf16[656,128]{1,0:T(8,128)(2,1)S(1)} %get-tuple-element.17.refs_0_, bf16[640,128]{1,0:T(8,128)(2,1)S(1)} %get-tuple-element.21.refs_1_), custom_call_target="tpu_custom_call" | custom-call | flops 134217728 | tf_op jit(solution)/shard_map/pallas_call | solution.py:238
  22.2 0.0 collective-permute-done.3.refs_8_
  22.2 0.1 collective-permute-start.12
  22.3 0.4 %collective-permute-done.6.refs_0_ = bf16[656,128]{1,0:T(8,128)(2,1)S(1)} collective-permute-done((bf16[656,128]{1,0:T(8,128)(2,1)S(1)}, bf16[656,128]{1,0:T(8,128)(2,1)S(1)}, u32[]{:S(2)}, u32[]{:S(2)}) %collective-permute-start.6) | collective-permute-done | bytes 167968 | tf_op jit(solution)/shard_map/ppermute | solution.py:283
  22.7 2.0 %collective-permute-start.13 = (bf16[656,128]{1,0:T(8,128)(2,1)S(1)}, bf16[656,128]{1,0:T(8,128)(2,1)S(1)}, u32[]{:S(2)}, u32[]{:S(2)}) collective-permute-start(bf16[656,128]{1,0:T(8,128)(2,1)S(1)} %collective-permute-done.6.refs_0_), channel_id=1, source_target_pairs={{0,4},{1,3},{4,8},{5,1},{8,12},{9,5},{12,14},{13,9},{14,10},{15,13... | collective-permute-start | bytes 503816 | tf_op jit(solution)/shard_map/ppermute | solution.py:283
  24.7 0.5 %collective-permute-done.11.refs_9_ = bf16[640,128]{1,0:T(8,128)(2,1)S(1)} collective-permute-done((bf16[640,128]{1,0:T(8,128)(2,1)S(1)}, bf16[640,128]{1,0:T(8,128)(2,1)S(1)}, u32[]{:S(2)}, u32[]{:S(2)}) %collective-permute-start.11) | collective-permute-done | bytes 163872 | tf_op jit(solution)/shard_map/ppermute | solution.py:283
  25.2 0.5 %collective-permute-start.14 = (bf16[640,128]{1,0:T(8,128)(2,1)S(1)}, bf16[640,128]{1,0:T(8,128)(2,1)S(1)}, u32[]{:S(2)}, u32[]{:S(2)}) collective-permute-start(bf16[640,128]{1,0:T(8,128)(2,1)S(1)} %collective-permute-done.11.refs_9_), channel_id=1, source_target_pairs={{0,2},{1,5},{4,0},{5,9},{8,4},{9,13},{12,8},{13,15},{14,12},{15,11... | collective-permute-start | bytes 491528 | tf_op jit(solution)/shard_map/ppermute | solution.py:283
  25.7 0.6 %collective-permute-done.9.refs_1_ = bf16[640,128]{1,0:T(8,128)(2,1)S(1)} collective-permute-done((bf16[640,128]{1,0:T(8,128)(2,1)S(1)}, bf16[640,128]{1,0:T(8,128)(2,1)S(1)}, u32[]{:S(2)}, u32[]{:S(2)}) %collective-permute-start.9) | collective-permute-done | bytes 163872 | tf_op jit(solution)/shard_map/ppermute | solution.py:283
  26.2 2.0 %collective-permute-start.15 = (bf16[640,128]{1,0:T(8,128)(2,1)S(1)}, bf16[640,128]{1,0:T(8,128)(2,1)S(1)}, u32[]{:S(2)}, u32[]{:S(2)}) collective-permute-start(bf16[640,128]{1,0:T(8,128)(2,1)S(1)} %collective-permute-done.9.refs_1_), channel_id=1, source_target_pairs={{0,4},{1,3},{4,8},{5,1},{8,12},{9,5},{12,14},{13,9},{14,10},{15,13... | collective-permute-start | bytes 491528 | tf_op jit(solution)/shard_map/ppermute | solution.py:283
  28.2 2.8 %shard_map.40.before = f32[4,2,256,128]{3,2,1,0:T(8,128)S(1)} custom-call(bf16[8,2,256,128]{3,2,1,0:T(8,128)(2,1)S(1)} %shard_map.38.a_ref, f32[4,2,256,128]{3,2,1,0:T(8,128)S(1)} %shard_map.39.before, bf16[656,128]{1,0:T(8,128)(2,1)S(1)} %collective-permute-done.6.refs_0_, ...), custom_call_target="tpu_custom_call", output_to_operand_aliasing={{}: (1, {})} | custom-call | flops 671088640 | tf_op jit(solution)/shard_map/pallas_call | solution.py:238
  31.0 0.0 collective-permute-done.12.refs_0_
  31.0 0.0 collective-permute-done.13.refs_1_.refs_2_
  31.0 1.3 %shard_map.41.total = f32[4,2,256,128]{3,2,1,0:T(8,128)S(1)} custom-call(bf16[8,2,256,128]{3,2,1,0:T(8,128)(2,1)S(1)} %shard_map.38.a_ref, f32[4,2,256,128]{3,2,1,0:T(8,128)S(1)} %shard_map.40.before, bf16[656,128]{1,0:T(8,128)(2,1)S(1)} %collective-permute-done.12.refs_0_, ...), custom_call_target="tpu_custom_call", output_to_operand_aliasing={{}: (1, {})} | custom-call | flops 268435456 | tf_op jit(solution)/shard_map/pallas_call | solution.py:238
  32.3 0.3 collective-permute-done.14.refs_1_
  32.6 0.0 collective-permute-done.15.refs_3_
  32.6 2.4 %shard_map.42 = bf16[4,10,64,64]{3,2,1,0:T(8,128)(2,1)} custom-call(bf16[8,2,256,128]{3,2,1,0:T(8,128)(2,1)S(1)} %shard_map.38.a_ref, f32[4,2,256,128]{3,2,1,0:T(8,128)S(1)} %shard_map.41.total, s32[4,10]{1,0:T(4,128)S(1)} %copy-done.1, bf16[656,128]{1,0:T(8,128)(2,1)S(1)} %collective-permute-done.12.refs_0_, ...), custom_call_target="tpu_custom_call" | custom-call | flops 167772160 | tf_op jit(solution)/shard_map/pallas_call | solution.py:238
Async XLA Ops:
  0.0 5.0 %copy-start = (bf16[4,10,64,64]{3,2,1,0:T(8,128)(2,1)S(1)}, bf16[4,10,64,64]{3,2,1,0:T(8,128)(2,1)}, u32[]{:S(2)}) copy-start(bf16[4,10,64,64]{3,2,1,0:T(8,128)(2,1)} %own_ref.1) | copy-start | bytes 983044
  1.9 4.7 %copy-start.1 = (s32[4,10]{1,0:T(4,128)S(1)}, s32[4,10]{1,0:T(4,128)}, u32[]{:S(2)}) copy-start(s32[4,10]{1,0:T(4,128)} %cols_hbm.3) | copy-start | bytes 484
  1.9 6.4 %collective-permute-start.4 = (bf16[656,128]{1,0:T(8,128)(2,1)S(1)}, bf16[656,128]{1,0:T(8,128)(2,1)S(1)}, u32[]{:S(2)}, u32[]{:S(2)}) collective-permute-start(bf16[656,128]{1,0:T(8,128)(2,1)S(1)} %get-tuple-element.17.refs_0_), channel_id=1, source_target_pairs={{0,4},{1,3},{4,8},{5,1},{8,12},{9,5},{12,14},{13,9},{14,10},{15,13... | collective-permute-start | bytes 503816 | tf_op jit(solution)/shard_map/ppermute | solution.py:283
  5.0 7.4 %collective-permute-start.1 = (bf16[4,10,64,64]{3,2,1,0:T(8,128)(2,1)S(1)}, bf16[4,10,64,64]{3,2,1,0:T(8,128)(2,1)S(1)}, u32[]{:S(2)}, u32[]{:S(2)}) collective-permute-start(bf16[4,10,64,64]{3,2,1,0:T(8,128)(2,1)S(1)} %copy-done), channel_id=1, source_target_pairs={{0,1},{1,0},{2,3},{3,2},{4,5},{5,4},{6,7},{7,6},{8,9},{9,8},{10,11... | collective-permute-start | bytes 983048 | tf_op jit(solution)/shard_map/ppermute | solution.py:266
  5.0 5.4 %collective-permute-start.7 = (bf16[640,128]{1,0:T(8,128)(2,1)S(1)}, bf16[640,128]{1,0:T(8,128)(2,1)S(1)}, u32[]{:S(2)}, u32[]{:S(2)}) collective-permute-start(bf16[640,128]{1,0:T(8,128)(2,1)S(1)} %get-tuple-element.21.refs_1_), channel_id=1, source_target_pairs={{0,4},{1,3},{4,8},{5,1},{8,12},{9,5},{12,14},{13,9},{14,10},{15,13... | collective-permute-start | bytes 491528 | tf_op jit(solution)/shard_map/ppermute | solution.py:283
  6.6 1.2 %collective-permute-start = (s32[4,10]{1,0:T(4,128)S(1)}, s32[4,10]{1,0:T(4,128)S(1)}, u32[]{:S(2)}, u32[]{:S(2)}) collective-permute-start(s32[4,10]{1,0:T(4,128)S(1)} %copy-done.1), channel_id=1, source_target_pairs={{0,1},{1,0},{2,3},{3,2},{4,5},{5,4},{6,7},{7,6},{8,9},{9,8},{10,11... | collective-permute-start | bytes 488 | tf_op jit(solution)/shard_map/ppermute | solution.py:266
  7.7 6.7 %collective-permute-start.2 = (bf16[656,128]{1,0:T(8,128)(2,1)S(1)}, bf16[656,128]{1,0:T(8,128)(2,1)S(1)}, u32[]{:S(2)}, u32[]{:S(2)}) collective-permute-start(bf16[656,128]{1,0:T(8,128)(2,1)S(1)} %get-tuple-element.17.refs_0_), channel_id=1, source_target_pairs={{0,2},{1,5},{4,0},{5,9},{8,4},{9,13},{12,8},{13,15},{14,12},{15,11... | collective-permute-start | bytes 503816 | tf_op jit(solution)/shard_map/ppermute | solution.py:283
  8.3 7.2 %collective-permute-start.5 = (bf16[656,128]{1,0:T(8,128)(2,1)S(1)}, bf16[656,128]{1,0:T(8,128)(2,1)S(1)}, u32[]{:S(2)}, u32[]{:S(2)}) collective-permute-start(bf16[656,128]{1,0:T(8,128)(2,1)S(1)} %collective-permute-done.4.refs_2_), channel_id=1, source_target_pairs={{0,4},{1,3},{4,8},{5,1},{8,12},{9,5},{12,14},{13,9},{14,10},{15,13... | collective-permute-start | bytes 503816 | tf_op jit(solution)/shard_map/ppermute | solution.py:283
  10.3 7.6 %collective-permute-start.10 = (bf16[640,128]{1,0:T(8,128)(2,1)S(1)}, bf16[640,128]{1,0:T(8,128)(2,1)S(1)}, u32[]{:S(2)}, u32[]{:S(2)}) collective-permute-start(bf16[640,128]{1,0:T(8,128)(2,1)S(1)} %get-tuple-element.21.refs_1_), channel_id=1, source_target_pairs={{0,2},{1,5},{4,0},{5,9},{8,4},{9,13},{12,8},{13,15},{14,12},{15,11... | collective-permute-start | bytes 491528 | tf_op jit(solution)/shard_map/ppermute | solution.py:283
  10.4 8.6 %collective-permute-start.8 = (bf16[640,128]{1,0:T(8,128)(2,1)S(1)}, bf16[640,128]{1,0:T(8,128)(2,1)S(1)}, u32[]{:S(2)}, u32[]{:S(2)}) collective-permute-start(bf16[640,128]{1,0:T(8,128)(2,1)S(1)} %collective-permute-done.7.refs_3_), channel_id=1, source_target_pairs={{0,4},{1,3},{4,8},{5,1},{8,12},{9,5},{12,14},{13,9},{14,10},{15,13... | collective-permute-start | bytes 491528 | tf_op jit(solution)/shard_map/ppermute | solution.py:283
  14.4 7.8 %collective-permute-start.3 = (bf16[656,128]{1,0:T(8,128)(2,1)S(1)}, bf16[656,128]{1,0:T(8,128)(2,1)S(1)}, u32[]{:S(2)}, u32[]{:S(2)}) collective-permute-start(bf16[656,128]{1,0:T(8,128)(2,1)S(1)} %collective-permute-done.2.refs_4_), channel_id=1, source_target_pairs={{0,2},{1,5},{4,0},{5,9},{8,4},{9,13},{12,8},{13,15},{14,12},{15,11... | collective-permute-start | bytes 503816 | tf_op jit(solution)/shard_map/ppermute | solution.py:283
  15.5 7.2 %collective-permute-start.6 = (bf16[656,128]{1,0:T(8,128)(2,1)S(1)}, bf16[656,128]{1,0:T(8,128)(2,1)S(1)}, u32[]{:S(2)}, u32[]{:S(2)}) collective-permute-start(bf16[656,128]{1,0:T(8,128)(2,1)S(1)} %collective-permute-done.5.refs_6_), channel_id=1, source_target_pairs={{0,4},{1,3},{4,8},{5,1},{8,12},{9,5},{12,14},{13,9},{14,10},{15,13... | collective-permute-start | bytes 503816 | tf_op jit(solution)/shard_map/ppermute | solution.py:283
  18.0 7.2 %collective-permute-start.11 = (bf16[640,128]{1,0:T(8,128)(2,1)S(1)}, bf16[640,128]{1,0:T(8,128)(2,1)S(1)}, u32[]{:S(2)}, u32[]{:S(2)}) collective-permute-start(bf16[640,128]{1,0:T(8,128)(2,1)S(1)} %collective-permute-done.10.refs_5_), channel_id=1, source_target_pairs={{0,2},{1,5},{4,0},{5,9},{8,4},{9,13},{12,8},{13,15},{14,12},{15,11... | collective-permute-start | bytes 491528 | tf_op jit(solution)/shard_map/ppermute | solution.py:283
  19.0 7.2 %collective-permute-start.9 = (bf16[640,128]{1,0:T(8,128)(2,1)S(1)}, bf16[640,128]{1,0:T(8,128)(2,1)S(1)}, u32[]{:S(2)}, u32[]{:S(2)}) collective-permute-start(bf16[640,128]{1,0:T(8,128)(2,1)S(1)} %collective-permute-done.8.refs_7_), channel_id=1, source_target_pairs={{0,4},{1,3},{4,8},{5,1},{8,12},{9,5},{12,14},{13,9},{14,10},{15,13... | collective-permute-start | bytes 491528 | tf_op jit(solution)/shard_map/ppermute | solution.py:283
  22.2 8.7 %collective-permute-start.12 = (bf16[656,128]{1,0:T(8,128)(2,1)S(1)}, bf16[656,128]{1,0:T(8,128)(2,1)S(1)}, u32[]{:S(2)}, u32[]{:S(2)}) collective-permute-start(bf16[656,128]{1,0:T(8,128)(2,1)S(1)} %collective-permute-done.3.refs_8_), channel_id=1, source_target_pairs={{0,2},{1,5},{4,0},{5,9},{8,4},{9,13},{12,8},{13,15},{14,12},{15,11... | collective-permute-start | bytes 503816 | tf_op jit(solution)/shard_map/ppermute | solution.py:283
  22.7 8.3 %collective-permute-start.13 = (bf16[656,128]{1,0:T(8,128)(2,1)S(1)}, bf16[656,128]{1,0:T(8,128)(2,1)S(1)}, u32[]{:S(2)}, u32[]{:S(2)}) collective-permute-start(bf16[656,128]{1,0:T(8,128)(2,1)S(1)} %collective-permute-done.6.refs_0_), channel_id=1, source_target_pairs={{0,4},{1,3},{4,8},{5,1},{8,12},{9,5},{12,14},{13,9},{14,10},{15,13... | collective-permute-start | bytes 503816 | tf_op jit(solution)/shard_map/ppermute | solution.py:283
  25.2 7.4 %collective-permute-start.14 = (bf16[640,128]{1,0:T(8,128)(2,1)S(1)}, bf16[640,128]{1,0:T(8,128)(2,1)S(1)}, u32[]{:S(2)}, u32[]{:S(2)}) collective-permute-start(bf16[640,128]{1,0:T(8,128)(2,1)S(1)} %collective-permute-done.11.refs_9_), channel_id=1, source_target_pairs={{0,2},{1,5},{4,0},{5,9},{8,4},{9,13},{12,8},{13,15},{14,12},{15,11... | collective-permute-start | bytes 491528 | tf_op jit(solution)/shard_map/ppermute | solution.py:283
  26.2 6.4 %collective-permute-start.15 = (bf16[640,128]{1,0:T(8,128)(2,1)S(1)}, bf16[640,128]{1,0:T(8,128)(2,1)S(1)}, u32[]{:S(2)}, u32[]{:S(2)}) collective-permute-start(bf16[640,128]{1,0:T(8,128)(2,1)S(1)} %collective-permute-done.9.refs_1_), channel_id=1, source_target_pairs={{0,4},{1,3},{4,8},{5,1},{8,12},{9,5},{12,14},{13,9},{14,10},{15,13... | collective-permute-start | bytes 491528 | tf_op jit(solution)/shard_map/ppermute | solution.py:283

commit v17 on v15

--- a/solution.py
+++ b/solution.py
@@ -3,7 +3,6 @@
 
 import jax
 import jax.numpy as jnp
-import numpy as np
 from jax import lax
 from jax.experimental import pallas as pl
 from jax.experimental.pallas import tpu as pltpu
@@ -31,7 +30,8 @@
 def pack_kernel(half, cols_hbm, b_hbm, *refs):
     *o_refs, cols_ref, b_ref, sem, sems = refs
     rows, slots, bs, _ = b_ref.shape
-    copies = [pltpu.make_async_copy(b_hbm.at[r], b_ref.at[r], sems.at[r]) for r in range(rows)]
+    pairs = [pl.ds(2 * p, 2) for p in range(rows // 2)]
+    copies = [pltpu.make_async_copy(b_hbm.at[pair], b_ref.at[pair], sems.at[p]) for p, pair in enumerate(pairs)]
     fetch = pltpu.make_async_copy(cols_hbm, cols_ref, sem)
     fetch.start()
     for copy in copies:
@@ -46,8 +46,7 @@
             foot = jnp.where(here, n, foot)
     o_refs[0][slots * bs :, :] = foot.astype(jnp.float32).astype(b_ref.dtype)
     for p, o_ref in enumerate(o_refs):
-        copies[2 * p].wait()
-        copies[2 * p + 1].wait()
+        copies[p].wait()
         for n in range(slots):
             o_ref[n * bs : (n + 1) * bs, :] = jnp.concatenate([b_ref[2 * p, n], b_ref[2 * p + 1, n]], axis=-1)
 
@@ -65,7 +64,7 @@
             SMEM(cols.shape, cols.dtype),
             VMEM(b_vals.shape, b_vals.dtype),
             pltpu.SemaphoreType.DMA,
-            pltpu.SemaphoreType.DMA((rows,)),
+            pltpu.SemaphoreType.DMA((rows // 2,)),
         ],
         compiler_params=params(),
         cost_estimate=cost(0, 2 * b_vals.size * 2),
@@ -129,7 +128,7 @@
 
 def arrived_from(order, way, steps):
     spots = [order.index(r) for r in range(len(order))]
-    ahead = jnp.where(lax.axis_index("col") == 0, way, -way) * steps
+    ahead = jnp.where(lax.axis_index("col") == 1, way, -way) * steps
     return look_up(order, lax.rem(look_up(spots, lax.axis_index("row")) - ahead + len(order), len(order)))
 
 
@@ -251,7 +250,7 @@
 
     def ring(way):
         return [
-            (order[r] * 2 + c, order[(r + (way if c == 0 else -way)) % sources] * 2 + c)
+            (order[r] * 2 + c, order[(r + (way if c == 1 else -way)) % sources] * 2 + c)
             for r in range(sources)
             for c in range(2)
         ]

time: 34.6 us -> 34.4 us (level)
  starting transfers between devices: 18.8 us -> 19.2 us
  waiting for transfers between devices: 4.81 us -> 4.44 us
    ppermute x14, waiting for transfers between devices: 3.65 us -> 3.28 us  [local(): held[way] = [lax.ppermute(part, ('row', 'col'), ring(way)) for part in sent]]
where the time goes in v17:
time: 34.4 us; the launch traced here: 34.3 us
  starting transfers between devices  19.2 us (56%)
  Pallas kernels  10.6 us (31%)
  waiting for transfers between devices  4.44 us (13%)
    ppermute x14, starting transfers between devices, local(): held[way] = [lax.ppermute(part, ('row', 'col'), ring(way)) for part in sent]  19.1 us
    pallas_call x4, Pallas kernels, product(): pl.pallas_call(functools.partial(kernel, sources), out_shape=out, in_spec...  7.48 us
    ppermute x14, waiting for transfers between devices, local(): held[way] = [lax.ppermute(part, ('row', 'col'), ring(way)) for part in sent]  3.28 us
    pallas_call x1, Pallas kernels, dense_rows(): pl.pallas_call(dense_kernel, out_shape=jax.ShapeDtypeStruct((sources, row...  1.82 us
    pallas_call x1, Pallas kernels, pack(): pl.pallas_call(functools.partial(pack_kernel, half), out_shape=[jax.Shape...  1.29 us
    ppermute x2, waiting for transfers between devices, local(): a_other, others = (lax.ppermute(x, 'col', swap) for x in mine)  1.16 us
  transfers between devices with their start and end apart: 16, of which 10 were waited for; matrix products, arithmetic and copies ran while one was open for 0% of the time, Pallas kernels for 20%

profile of v17, /device:TPU:0, one launch (start us, length us, event | category | flops | bytes accessed | tf_op | source)
XLA Modules:
  0.0 34.3 jit_solution(13141150099924322726)
XLA Ops:
  0.0 0.0 copy-start
  0.0 1.3 %shard_map.37 = (bf16[656,128]{1,0:T(8,128)(2,1)S(1)}, bf16[640,128]{1,0:T(8,128)(2,1)S(1)}) custom-call(s32[4,10]{1,0:T(4,128)} %cols_hbm.3, bf16[4,10,64,64]{3,2,1,0:T(8,128)(2,1)} %b_hbm.1), custom_call_target="tpu_custom_call" | custom-call | bytes 655360 | tf_op jit(solution)/shard_map/pallas_call | solution.py:58
  1.3 0.0 copy-start.1
  1.3 3.0 %collective-permute-start.4 = (bf16[656,128]{1,0:T(8,128)(2,1)S(1)}, bf16[656,128]{1,0:T(8,128)(2,1)S(1)}, u32[]{:S(2)}, u32[]{:S(2)}) collective-permute-start(bf16[656,128]{1,0:T(8,128)(2,1)S(1)} %get-tuple-element.17.refs_0_), channel_id=1, source_target_pairs={{0,2},{1,5},{4,0},{5,9},{8,4},{9,13},{12,8},{13,15},{14,12},{15,11... | collective-permute-start | bytes 503816 | tf_op jit(solution)/shard_map/ppermute | solution.py:278
  4.3 0.0 copy-done
  4.3 0.0 collective-permute-start.1
  4.3 1.6 %collective-permute-start.7 = (bf16[640,128]{1,0:T(8,128)(2,1)S(1)}, bf16[640,128]{1,0:T(8,128)(2,1)S(1)}, u32[]{:S(2)}, u32[]{:S(2)}) collective-permute-start(bf16[640,128]{1,0:T(8,128)(2,1)S(1)} %get-tuple-element.21.refs_1_), channel_id=1, source_target_pairs={{0,2},{1,5},{4,0},{5,9},{8,4},{9,13},{12,8},{13,15},{14,12},{15,11... | collective-permute-start | bytes 491528 | tf_op jit(solution)/shard_map/ppermute | solution.py:278
  5.9 0.0 copy-done.1
  5.9 0.0 collective-permute-start
  5.9 1.2 %collective-permute-done.others_ref = s32[4,10]{1,0:T(4,128)S(1)} collective-permute-done((s32[4,10]{1,0:T(4,128)S(1)}, s32[4,10]{1,0:T(4,128)S(1)}, u32[]{:S(2)}, u32[]{:S(2)}) %collective-permute-start) | collective-permute-done | bytes 192 | tf_op jit(solution)/shard_map/ppermute | solution.py:261
  7.1 0.6 %collective-permute-start.2 = (bf16[656,128]{1,0:T(8,128)(2,1)S(1)}, bf16[656,128]{1,0:T(8,128)(2,1)S(1)}, u32[]{:S(2)}, u32[]{:S(2)}) collective-permute-start(bf16[656,128]{1,0:T(8,128)(2,1)S(1)} %get-tuple-element.17.refs_0_), channel_id=1, source_target_pairs={{0,4},{1,3},{4,8},{5,1},{8,12},{9,5},{12,14},{13,9},{14,10},{15,13... | collective-permute-start | bytes 503816 | tf_op jit(solution)/shard_map/ppermute | solution.py:278
  7.6 0.1 collective-permute-done.4.refs_2_
  7.7 2.0 %collective-permute-start.5 = (bf16[656,128]{1,0:T(8,128)(2,1)S(1)}, bf16[656,128]{1,0:T(8,128)(2,1)S(1)}, u32[]{:S(2)}, u32[]{:S(2)}) collective-permute-start(bf16[656,128]{1,0:T(8,128)(2,1)S(1)} %collective-permute-done.4.refs_2_), channel_id=1, source_target_pairs={{0,2},{1,5},{4,0},{5,9},{8,4},{9,13},{12,8},{13,15},{14,12},{15,11... | collective-permute-start | bytes 503816 | tf_op jit(solution)/shard_map/ppermute | solution.py:278
  9.7 0.1 collective-permute-start.10
  9.8 0.0 collective-permute-done.7.refs_3_
  9.8 2.0 %collective-permute-start.8 = (bf16[640,128]{1,0:T(8,128)(2,1)S(1)}, bf16[640,128]{1,0:T(8,128)(2,1)S(1)}, u32[]{:S(2)}, u32[]{:S(2)}) collective-permute-start(bf16[640,128]{1,0:T(8,128)(2,1)S(1)} %collective-permute-done.7.refs_3_), channel_id=1, source_target_pairs={{0,2},{1,5},{4,0},{5,9},{8,4},{9,13},{12,8},{13,15},{14,12},{15,11... | collective-permute-start | bytes 491528 | tf_op jit(solution)/shard_map/ppermute | solution.py:278
  11.7 0.0 collective-permute-done.1.other_ref
  11.7 1.8 %shard_map.38.a_ref = bf16[8,2,256,128]{3,2,1,0:T(8,128)(2,1)S(1)} custom-call(s32[4,10]{1,0:T(4,128)S(1)} %copy-done.1, s32[4,10]{1,0:T(4,128)S(1)} %collective-permute-done.others_ref, bf16[4,10,64,64]{3,2,1,0:T(8,128)(2,1)S(1)} %copy-done, bf16[4,10,64,64]{3,2,1,0:T(8,128)(2,1)S(1)} %collective-permute-done.1.other_ref), custom_call_target="tpu_custom_call" | custom-call | bytes 1310720 | tf_op jit(solution)/shard_map/pallas_call | solution.py:104
  13.6 0.2 collective-permute-done.2.refs_4_
  13.8 0.7 %collective-permute-start.3 = (bf16[656,128]{1,0:T(8,128)(2,1)S(1)}, bf16[656,128]{1,0:T(8,128)(2,1)S(1)}, u32[]{:S(2)}, u32[]{:S(2)}) collective-permute-start(bf16[656,128]{1,0:T(8,128)(2,1)S(1)} %collective-permute-done.2.refs_4_), channel_id=1, source_target_pairs={{0,4},{1,3},{4,8},{5,1},{8,12},{9,5},{12,14},{13,9},{14,10},{15,13... | collective-permute-start | bytes 503816 | tf_op jit(solution)/shard_map/ppermute | solution.py:278
  14.5 0.4 %collective-permute-done.5.refs_6_ = bf16[656,128]{1,0:T(8,128)(2,1)S(1)} collective-permute-done((bf16[656,128]{1,0:T(8,128)(2,1)S(1)}, bf16[656,128]{1,0:T(8,128)(2,1)S(1)}, u32[]{:S(2)}, u32[]{:S(2)}) %collective-permute-start.5) | collective-permute-done | bytes 167968 | tf_op jit(solution)/shard_map/ppermute | solution.py:278
  14.9 2.0 %collective-permute-start.6 = (bf16[656,128]{1,0:T(8,128)(2,1)S(1)}, bf16[656,128]{1,0:T(8,128)(2,1)S(1)}, u32[]{:S(2)}, u32[]{:S(2)}) collective-permute-start(bf16[656,128]{1,0:T(8,128)(2,1)S(1)} %collective-permute-done.5.refs_6_), channel_id=1, source_target_pairs={{0,2},{1,5},{4,0},{5,9},{8,4},{9,13},{12,8},{13,15},{14,12},{15,11... | collective-permute-start | bytes 503816 | tf_op jit(solution)/shard_map/ppermute | solution.py:278
  16.9 0.4 %collective-permute-done.10.refs_5_ = bf16[640,128]{1,0:T(8,128)(2,1)S(1)} collective-permute-done((bf16[640,128]{1,0:T(8,128)(2,1)S(1)}, bf16[640,128]{1,0:T(8,128)(2,1)S(1)}, u32[]{:S(2)}, u32[]{:S(2)}) %collective-permute-start.10) | collective-permute-done | bytes 163872 | tf_op jit(solution)/shard_map/ppermute | solution.py:278
  17.3 0.7 %collective-permute-start.11 = (bf16[640,128]{1,0:T(8,128)(2,1)S(1)}, bf16[640,128]{1,0:T(8,128)(2,1)S(1)}, u32[]{:S(2)}, u32[]{:S(2)}) collective-permute-start(bf16[640,128]{1,0:T(8,128)(2,1)S(1)} %collective-permute-done.10.refs_5_), channel_id=1, source_target_pairs={{0,4},{1,3},{4,8},{5,1},{8,12},{9,5},{12,14},{13,9},{14,10},{15,13... | collective-permute-start | bytes 491528 | tf_op jit(solution)/shard_map/ppermute | solution.py:278
  18.0 0.4 %collective-permute-done.8.refs_7_ = bf16[640,128]{1,0:T(8,128)(2,1)S(1)} collective-permute-done((bf16[640,128]{1,0:T(8,128)(2,1)S(1)}, bf16[640,128]{1,0:T(8,128)(2,1)S(1)}, u32[]{:S(2)}, u32[]{:S(2)}) %collective-permute-start.8) | collective-permute-done | bytes 163872 | tf_op jit(solution)/shard_map/ppermute | solution.py:278
  18.5 2.0 %collective-permute-start.9 = (bf16[640,128]{1,0:T(8,128)(2,1)S(1)}, bf16[640,128]{1,0:T(8,128)(2,1)S(1)}, u32[]{:S(2)}, u32[]{:S(2)}) collective-permute-start(bf16[640,128]{1,0:T(8,128)(2,1)S(1)} %collective-permute-done.8.refs_7_), channel_id=1, source_target_pairs={{0,2},{1,5},{4,0},{5,9},{8,4},{9,13},{12,8},{13,15},{14,12},{15,11... | collective-permute-start | bytes 491528 | tf_op jit(solution)/shard_map/ppermute | solution.py:278
  20.4 1.1 %shard_map.39.before = f32[4,2,256,128]{3,2,1,0:T(8,128)S(1)} custom-call(bf16[8,2,256,128]{3,2,1,0:T(8,128)(2,1)S(1)} %shard_map.38.a_ref, bf16[656,128]{1,0:T(8,128)(2,1)S(1)} %get-tuple-element.17.refs_0_, bf16[640,128]{1,0:T(8,128)(2,1)S(1)} %get-tuple-element.21.refs_1_), custom_call_target="tpu_custom_call" | custom-call | flops 134217728 | tf_op jit(solution)/shard_map/pallas_call | solution.py:233
  21.6 0.0 collective-permute-done.3.refs_8_
  21.6 0.2 collective-permute-start.12
  21.7 0.4 %collective-permute-done.6.refs_0_ = bf16[656,128]{1,0:T(8,128)(2,1)S(1)} collective-permute-done((bf16[656,128]{1,0:T(8,128)(2,1)S(1)}, bf16[656,128]{1,0:T(8,128)(2,1)S(1)}, u32[]{:S(2)}, u32[]{:S(2)}) %collective-permute-start.6) | collective-permute-done | bytes 167968 | tf_op jit(solution)/shard_map/ppermute | solution.py:278
  22.2 1.9 %collective-permute-start.13 = (bf16[656,128]{1,0:T(8,128)(2,1)S(1)}, bf16[656,128]{1,0:T(8,128)(2,1)S(1)}, u32[]{:S(2)}, u32[]{:S(2)}) collective-permute-start(bf16[656,128]{1,0:T(8,128)(2,1)S(1)} %collective-permute-done.6.refs_0_), channel_id=1, source_target_pairs={{0,2},{1,5},{4,0},{5,9},{8,4},{9,13},{12,8},{13,15},{14,12},{15,11... | collective-permute-start | bytes 503816 | tf_op jit(solution)/shard_map/ppermute | solution.py:278
  24.0 0.5 %collective-permute-done.11.refs_9_ = bf16[640,128]{1,0:T(8,128)(2,1)S(1)} collective-permute-done((bf16[640,128]{1,0:T(8,128)(2,1)S(1)}, bf16[640,128]{1,0:T(8,128)(2,1)S(1)}, u32[]{:S(2)}, u32[]{:S(2)}) %collective-permute-start.11) | collective-permute-done | bytes 163872 | tf_op jit(solution)/shard_map/ppermute | solution.py:278
  24.5 0.7 %collective-permute-start.14 = (bf16[640,128]{1,0:T(8,128)(2,1)S(1)}, bf16[640,128]{1,0:T(8,128)(2,1)S(1)}, u32[]{:S(2)}, u32[]{:S(2)}) collective-permute-start(bf16[640,128]{1,0:T(8,128)(2,1)S(1)} %collective-permute-done.11.refs_9_), channel_id=1, source_target_pairs={{0,4},{1,3},{4,8},{5,1},{8,12},{9,5},{12,14},{13,9},{14,10},{15,13... | collective-permute-start | bytes 491528 | tf_op jit(solution)/shard_map/ppermute | solution.py:278
  25.3 0.4 %collective-permute-done.9.refs_1_ = bf16[640,128]{1,0:T(8,128)(2,1)S(1)} collective-permute-done((bf16[640,128]{1,0:T(8,128)(2,1)S(1)}, bf16[640,128]{1,0:T(8,128)(2,1)S(1)}, u32[]{:S(2)}, u32[]{:S(2)}) %collective-permute-start.9) | collective-permute-done | bytes 163872 | tf_op jit(solution)/shard_map/ppermute | solution.py:278
  25.7 1.9 %collective-permute-start.15 = (bf16[640,128]{1,0:T(8,128)(2,1)S(1)}, bf16[640,128]{1,0:T(8,128)(2,1)S(1)}, u32[]{:S(2)}, u32[]{:S(2)}) collective-permute-start(bf16[640,128]{1,0:T(8,128)(2,1)S(1)} %collective-permute-done.9.refs_1_), channel_id=1, source_target_pairs={{0,2},{1,5},{4,0},{5,9},{8,4},{9,13},{12,8},{13,15},{14,12},{15,11... | collective-permute-start | bytes 491528 | tf_op jit(solution)/shard_map/ppermute | solution.py:278
  27.6 2.8 %shard_map.40.before = f32[4,2,256,128]{3,2,1,0:T(8,128)S(1)} custom-call(bf16[8,2,256,128]{3,2,1,0:T(8,128)(2,1)S(1)} %shard_map.38.a_ref, f32[4,2,256,128]{3,2,1,0:T(8,128)S(1)} %shard_map.39.before, bf16[656,128]{1,0:T(8,128)(2,1)S(1)} %collective-permute-done.6.refs_0_, ...), custom_call_target="tpu_custom_call", output_to_operand_aliasing={{}: (1, {})} | custom-call | flops 671088640 | tf_op jit(solution)/shard_map/pallas_call | solution.py:233
  30.3 0.0 collective-permute-done.12.refs_0_
  30.3 0.0 collective-permute-done.13.refs_1_.refs_2_
  30.3 1.3 %shard_map.41.total = f32[4,2,256,128]{3,2,1,0:T(8,128)S(1)} custom-call(bf16[8,2,256,128]{3,2,1,0:T(8,128)(2,1)S(1)} %shard_map.38.a_ref, f32[4,2,256,128]{3,2,1,0:T(8,128)S(1)} %shard_map.40.before, bf16[656,128]{1,0:T(8,128)(2,1)S(1)} %collective-permute-done.12.refs_0_, ...), custom_call_target="tpu_custom_call", output_to_operand_aliasing={{}: (1, {})} | custom-call | flops 268435456 | tf_op jit(solution)/shard_map/pallas_call | solution.py:233
  31.6 0.3 collective-permute-done.14.refs_1_
  32.0 0.0 collective-permute-done.15.refs_3_
  32.0 2.3 %shard_map.42 = bf16[4,10,64,64]{3,2,1,0:T(8,128)(2,1)} custom-call(bf16[8,2,256,128]{3,2,1,0:T(8,128)(2,1)S(1)} %shard_map.38.a_ref, f32[4,2,256,128]{3,2,1,0:T(8,128)S(1)} %shard_map.41.total, s32[4,10]{1,0:T(4,128)S(1)} %copy-done.1, bf16[656,128]{1,0:T(8,128)(2,1)S(1)} %collective-permute-done.12.refs_0_, ...), custom_call_target="tpu_custom_call" | custom-call | flops 167772160 | tf_op jit(solution)/shard_map/pallas_call | solution.py:233
Async XLA Ops:
  0.0 4.3 %copy-start = (bf16[4,10,64,64]{3,2,1,0:T(8,128)(2,1)S(1)}, bf16[4,10,64,64]{3,2,1,0:T(8,128)(2,1)}, u32[]{:S(2)}) copy-start(bf16[4,10,64,64]{3,2,1,0:T(8,128)(2,1)} %own_ref.1) | copy-start | bytes 983044
  1.3 4.6 %copy-start.1 = (s32[4,10]{1,0:T(4,128)S(1)}, s32[4,10]{1,0:T(4,128)}, u32[]{:S(2)}) copy-start(s32[4,10]{1,0:T(4,128)} %cols_hbm.3) | copy-start | bytes 484
  1.3 6.4 %collective-permute-start.4 = (bf16[656,128]{1,0:T(8,128)(2,1)S(1)}, bf16[656,128]{1,0:T(8,128)(2,1)S(1)}, u32[]{:S(2)}, u32[]{:S(2)}) collective-permute-start(bf16[656,128]{1,0:T(8,128)(2,1)S(1)} %get-tuple-element.17.refs_0_), channel_id=1, source_target_pairs={{0,2},{1,5},{4,0},{5,9},{8,4},{9,13},{12,8},{13,15},{14,12},{15,11... | collective-permute-start | bytes 503816 | tf_op jit(solution)/shard_map/ppermute | solution.py:278
  4.3 7.4 %collective-permute-start.1 = (bf16[4,10,64,64]{3,2,1,0:T(8,128)(2,1)S(1)}, bf16[4,10,64,64]{3,2,1,0:T(8,128)(2,1)S(1)}, u32[]{:S(2)}, u32[]{:S(2)}) collective-permute-start(bf16[4,10,64,64]{3,2,1,0:T(8,128)(2,1)S(1)} %copy-done), channel_id=1, source_target_pairs={{0,1},{1,0},{2,3},{3,2},{4,5},{5,4},{6,7},{7,6},{8,9},{9,8},{10,11... | collective-permute-start | bytes 983048 | tf_op jit(solution)/shard_map/ppermute | solution.py:261
  4.3 5.4 %collective-permute-start.7 = (bf16[640,128]{1,0:T(8,128)(2,1)S(1)}, bf16[640,128]{1,0:T(8,128)(2,1)S(1)}, u32[]{:S(2)}, u32[]{:S(2)}) collective-permute-start(bf16[640,128]{1,0:T(8,128)(2,1)S(1)} %get-tuple-element.21.refs_1_), channel_id=1, source_target_pairs={{0,2},{1,5},{4,0},{5,9},{8,4},{9,13},{12,8},{13,15},{14,12},{15,11... | collective-permute-start | bytes 491528 | tf_op jit(solution)/shard_map/ppermute | solution.py:278
  5.9 1.2 %collective-permute-start = (s32[4,10]{1,0:T(4,128)S(1)}, s32[4,10]{1,0:T(4,128)S(1)}, u32[]{:S(2)}, u32[]{:S(2)}) collective-permute-start(s32[4,10]{1,0:T(4,128)S(1)} %copy-done.1), channel_id=1, source_target_pairs={{0,1},{1,0},{2,3},{3,2},{4,5},{5,4},{6,7},{7,6},{8,9},{9,8},{10,11... | collective-permute-start | bytes 488 | tf_op jit(solution)/shard_map/ppermute | solution.py:261
  7.1 6.7 %collective-permute-start.2 = (bf16[656,128]{1,0:T(8,128)(2,1)S(1)}, bf16[656,128]{1,0:T(8,128)(2,1)S(1)}, u32[]{:S(2)}, u32[]{:S(2)}) collective-permute-start(bf16[656,128]{1,0:T(8,128)(2,1)S(1)} %get-tuple-element.17.refs_0_), channel_id=1, source_target_pairs={{0,4},{1,3},{4,8},{5,1},{8,12},{9,5},{12,14},{13,9},{14,10},{15,13... | collective-permute-start | bytes 503816 | tf_op jit(solution)/shard_map/ppermute | solution.py:278
  7.7 7.2 %collective-permute-start.5 = (bf16[656,128]{1,0:T(8,128)(2,1)S(1)}, bf16[656,128]{1,0:T(8,128)(2,1)S(1)}, u32[]{:S(2)}, u32[]{:S(2)}) collective-permute-start(bf16[656,128]{1,0:T(8,128)(2,1)S(1)} %collective-permute-done.4.refs_2_), channel_id=1, source_target_pairs={{0,2},{1,5},{4,0},{5,9},{8,4},{9,13},{12,8},{13,15},{14,12},{15,11... | collective-permute-start | bytes 503816 | tf_op jit(solution)/shard_map/ppermute | solution.py:278
  9.7 7.6 %collective-permute-start.10 = (bf16[640,128]{1,0:T(8,128)(2,1)S(1)}, bf16[640,128]{1,0:T(8,128)(2,1)S(1)}, u32[]{:S(2)}, u32[]{:S(2)}) collective-permute-start(bf16[640,128]{1,0:T(8,128)(2,1)S(1)} %get-tuple-element.21.refs_1_), channel_id=1, source_target_pairs={{0,4},{1,3},{4,8},{5,1},{8,12},{9,5},{12,14},{13,9},{14,10},{15,13... | collective-permute-start | bytes 491528 | tf_op jit(solution)/shard_map/ppermute | solution.py:278
  9.8 8.7 %collective-permute-start.8 = (bf16[640,128]{1,0:T(8,128)(2,1)S(1)}, bf16[640,128]{1,0:T(8,128)(2,1)S(1)}, u32[]{:S(2)}, u32[]{:S(2)}) collective-permute-start(bf16[640,128]{1,0:T(8,128)(2,1)S(1)} %collective-permute-done.7.refs_3_), channel_id=1, source_target_pairs={{0,2},{1,5},{4,0},{5,9},{8,4},{9,13},{12,8},{13,15},{14,12},{15,11... | collective-permute-start | bytes 491528 | tf_op jit(solution)/shard_map/ppermute | solution.py:278
  13.8 7.8 %collective-permute-start.3 = (bf16[656,128]{1,0:T(8,128)(2,1)S(1)}, bf16[656,128]{1,0:T(8,128)(2,1)S(1)}, u32[]{:S(2)}, u32[]{:S(2)}) collective-permute-start(bf16[656,128]{1,0:T(8,128)(2,1)S(1)} %collective-permute-done.2.refs_4_), channel_id=1, source_target_pairs={{0,4},{1,3},{4,8},{5,1},{8,12},{9,5},{12,14},{13,9},{14,10},{15,13... | collective-permute-start | bytes 503816 | tf_op jit(solution)/shard_map/ppermute | solution.py:278
  14.9 7.2 %collective-permute-start.6 = (bf16[656,128]{1,0:T(8,128)(2,1)S(1)}, bf16[656,128]{1,0:T(8,128)(2,1)S(1)}, u32[]{:S(2)}, u32[]{:S(2)}) collective-permute-start(bf16[656,128]{1,0:T(8,128)(2,1)S(1)} %collective-permute-done.5.refs_6_), channel_id=1, source_target_pairs={{0,2},{1,5},{4,0},{5,9},{8,4},{9,13},{12,8},{13,15},{14,12},{15,11... | collective-permute-start | bytes 503816 | tf_op jit(solution)/shard_map/ppermute | solution.py:278
  17.3 7.2 %collective-permute-start.11 = (bf16[640,128]{1,0:T(8,128)(2,1)S(1)}, bf16[640,128]{1,0:T(8,128)(2,1)S(1)}, u32[]{:S(2)}, u32[]{:S(2)}) collective-permute-start(bf16[640,128]{1,0:T(8,128)(2,1)S(1)} %collective-permute-done.10.refs_5_), channel_id=1, source_target_pairs={{0,4},{1,3},{4,8},{5,1},{8,12},{9,5},{12,14},{13,9},{14,10},{15,13... | collective-permute-start | bytes 491528 | tf_op jit(solution)/shard_map/ppermute | solution.py:278
  18.5 7.2 %collective-permute-start.9 = (bf16[640,128]{1,0:T(8,128)(2,1)S(1)}, bf16[640,128]{1,0:T(8,128)(2,1)S(1)}, u32[]{:S(2)}, u32[]{:S(2)}) collective-permute-start(bf16[640,128]{1,0:T(8,128)(2,1)S(1)} %collective-permute-done.8.refs_7_), channel_id=1, source_target_pairs={{0,2},{1,5},{4,0},{5,9},{8,4},{9,13},{12,8},{13,15},{14,12},{15,11... | collective-permute-start | bytes 491528 | tf_op jit(solution)/shard_map/ppermute | solution.py:278
  21.6 8.8 %collective-permute-start.12 = (bf16[656,128]{1,0:T(8,128)(2,1)S(1)}, bf16[656,128]{1,0:T(8,128)(2,1)S(1)}, u32[]{:S(2)}, u32[]{:S(2)}) collective-permute-start(bf16[656,128]{1,0:T(8,128)(2,1)S(1)} %collective-permute-done.3.refs_8_), channel_id=1, source_target_pairs={{0,4},{1,3},{4,8},{5,1},{8,12},{9,5},{12,14},{13,9},{14,10},{15,13... | collective-permute-start | bytes 503816 | tf_op jit(solution)/shard_map/ppermute | solution.py:278
  22.2 8.2 %collective-permute-start.13 = (bf16[656,128]{1,0:T(8,128)(2,1)S(1)}, bf16[656,128]{1,0:T(8,128)(2,1)S(1)}, u32[]{:S(2)}, u32[]{:S(2)}) collective-permute-start(bf16[656,128]{1,0:T(8,128)(2,1)S(1)} %collective-permute-done.6.refs_0_), channel_id=1, source_target_pairs={{0,2},{1,5},{4,0},{5,9},{8,4},{9,13},{12,8},{13,15},{14,12},{15,11... | collective-permute-start | bytes 503816 | tf_op jit(solution)/shard_map/ppermute | solution.py:278
  24.5 7.4 %collective-permute-start.14 = (bf16[640,128]{1,0:T(8,128)(2,1)S(1)}, bf16[640,128]{1,0:T(8,128)(2,1)S(1)}, u32[]{:S(2)}, u32[]{:S(2)}) collective-permute-start(bf16[640,128]{1,0:T(8,128)(2,1)S(1)} %collective-permute-done.11.refs_9_), channel_id=1, source_target_pairs={{0,4},{1,3},{4,8},{5,1},{8,12},{9,5},{12,14},{13,9},{14,10},{15,13... | collective-permute-start | bytes 491528 | tf_op jit(solution)/shard_map/ppermute | solution.py:278
  25.7 6.3 %collective-permute-start.15 = (bf16[640,128]{1,0:T(8,128)(2,1)S(1)}, bf16[640,128]{1,0:T(8,128)(2,1)S(1)}, u32[]{:S(2)}, u32[]{:S(2)}) collective-permute-start(bf16[640,128]{1,0:T(8,128)(2,1)S(1)} %collective-permute-done.9.refs_1_), channel_id=1, source_target_pairs={{0,2},{1,5},{4,0},{5,9},{8,4},{9,13},{12,8},{13,15},{14,12},{15,11... | collective-permute-start | bytes 491528 | tf_op jit(solution)/shard_map/ppermute | solution.py:278

commit v18 on v17

--- a/solution.py
+++ b/solution.py
@@ -272,7 +272,7 @@
                 sent = [lax.optimization_barrier((part, others))[0] for part in sent]
             if (step, way) == (2, -1):
                 sent[0], _ = lax.optimization_barrier((sent[0], a))
-            if step > 2 and way == -1:
+            if step > 3 and way == -1:
                 total = product(order, rounds.pop(0), a, total, total_shape)
                 sent[0], total = lax.optimization_barrier((sent[0], total))
             held[way] = [lax.ppermute(part, ("row", "col"), ring(way)) for part in sent]

time: 34.4 us -> 34.6 us (level)
  Pallas kernels: 10.6 us -> 9.86 us
  starting transfers between devices: 19.2 us -> 19.9 us
    ppermute x14, starting transfers between devices: 19.1 us -> 19.9 us  [local(): held[way] = [lax.ppermute(part, ('row', 'col'), ring(way)) for part in sent]]
    pallas_call x4 -> x3, Pallas kernels: 7.48 us -> 6.75 us  [product(): pl.pallas_call(functools.partial(kernel, sources), out_shape=out, in_spec...]
  transfers between devices with their start and end apart: 16 -> 16, of which waited for: 10 -> 10; matrix products, arithmetic and copies ran while one was open for 0% -> 0% of each run, Pallas kernels for 20% -> 18%
where the time goes in v18:
time: 34.6 us; the launch traced here: 34.5 us
  starting transfers between devices  19.9 us (58%)
  Pallas kernels  9.86 us (28%)
  waiting for transfers between devices  4.6 us (13%)
    ppermute x14, starting transfers between devices, local(): held[way] = [lax.ppermute(part, ('row', 'col'), ring(way)) for part in sent]  19.9 us
    pallas_call x3, Pallas kernels, product(): pl.pallas_call(functools.partial(kernel, sources), out_shape=out, in_spec...  6.75 us
    ppermute x14, waiting for transfers between devices, local(): held[way] = [lax.ppermute(part, ('row', 'col'), ring(way)) for part in sent]  3.44 us
    pallas_call x1, Pallas kernels, dense_rows(): pl.pallas_call(dense_kernel, out_shape=jax.ShapeDtypeStruct((sources, row...  1.82 us
    pallas_call x1, Pallas kernels, pack(): pl.pallas_call(functools.partial(pack_kernel, half), out_shape=[jax.Shape...  1.29 us
    ppermute x2, waiting for transfers between devices, local(): a_other, others = (lax.ppermute(x, 'col', swap) for x in mine)  1.16 us
  transfers between devices with their start and end apart: 16, of which 10 were waited for; matrix products, arithmetic and copies ran while one was open for 0% of the time, Pallas kernels for 18%

profile of v18, /device:TPU:0, one launch (start us, length us, event | category | flops | bytes accessed | tf_op | source)
XLA Modules:
  0.0 34.5 jit_solution(16111543214164313087)
XLA Ops:
  0.0 0.0 copy-start
  0.0 1.3 %shard_map.37 = (bf16[656,128]{1,0:T(8,128)(2,1)S(1)}, bf16[640,128]{1,0:T(8,128)(2,1)S(1)}) custom-call(s32[4,10]{1,0:T(4,128)} %cols_hbm.3, bf16[4,10,64,64]{3,2,1,0:T(8,128)(2,1)} %b_hbm.1), custom_call_target="tpu_custom_call" | custom-call | bytes 655360 | tf_op jit(solution)/shard_map/pallas_call | solution.py:58
  1.3 0.0 copy-start.1
  1.3 3.0 %collective-permute-start.2 = (bf16[656,128]{1,0:T(8,128)(2,1)S(1)}, bf16[656,128]{1,0:T(8,128)(2,1)S(1)}, u32[]{:S(2)}, u32[]{:S(2)}) collective-permute-start(bf16[656,128]{1,0:T(8,128)(2,1)S(1)} %get-tuple-element.16.refs_2_), channel_id=1, source_target_pairs={{0,2},{1,5},{4,0},{5,9},{8,4},{9,13},{12,8},{13,15},{14,12},{15,11... | collective-permute-start | bytes 503816 | tf_op jit(solution)/shard_map/ppermute | solution.py:278
  4.3 0.0 copy-done
  4.3 0.0 collective-permute-start.1
  4.3 1.6 %collective-permute-start.5 = (bf16[640,128]{1,0:T(8,128)(2,1)S(1)}, bf16[640,128]{1,0:T(8,128)(2,1)S(1)}, u32[]{:S(2)}, u32[]{:S(2)}) collective-permute-start(bf16[640,128]{1,0:T(8,128)(2,1)S(1)} %get-tuple-element.17.refs_3_), channel_id=1, source_target_pairs={{0,2},{1,5},{4,0},{5,9},{8,4},{9,13},{12,8},{13,15},{14,12},{15,11... | collective-permute-start | bytes 491528 | tf_op jit(solution)/shard_map/ppermute | solution.py:278
  5.9 0.0 copy-done.1
  5.9 0.0 collective-permute-start
  5.9 1.2 %collective-permute-done.others_ref = s32[4,10]{1,0:T(4,128)S(1)} collective-permute-done((s32[4,10]{1,0:T(4,128)S(1)}, s32[4,10]{1,0:T(4,128)S(1)}, u32[]{:S(2)}, u32[]{:S(2)}) %collective-permute-start) | collective-permute-done | bytes 192 | tf_op jit(solution)/shard_map/ppermute | solution.py:261
  7.1 0.6 %collective-permute-start.8 = (bf16[656,128]{1,0:T(8,128)(2,1)S(1)}, bf16[656,128]{1,0:T(8,128)(2,1)S(1)}, u32[]{:S(2)}, u32[]{:S(2)}) collective-permute-start(bf16[656,128]{1,0:T(8,128)(2,1)S(1)} %get-tuple-element.16.refs_2_), channel_id=1, source_target_pairs={{0,4},{1,3},{4,8},{5,1},{8,12},{9,5},{12,14},{13,9},{14,10},{15,13... | collective-permute-start | bytes 503816 | tf_op jit(solution)/shard_map/ppermute | solution.py:278
  7.6 0.1 collective-permute-done.2.refs_4_
  7.7 2.0 %collective-permute-start.3 = (bf16[656,128]{1,0:T(8,128)(2,1)S(1)}, bf16[656,128]{1,0:T(8,128)(2,1)S(1)}, u32[]{:S(2)}, u32[]{:S(2)}) collective-permute-start(bf16[656,128]{1,0:T(8,128)(2,1)S(1)} %collective-permute-done.2.refs_4_), channel_id=1, source_target_pairs={{0,2},{1,5},{4,0},{5,9},{8,4},{9,13},{12,8},{13,15},{14,12},{15,11... | collective-permute-start | bytes 503816 | tf_op jit(solution)/shard_map/ppermute | solution.py:278
  9.7 0.1 collective-permute-start.9
  9.8 0.0 collective-permute-done.5.refs_5_
  9.8 2.0 %collective-permute-start.6 = (bf16[640,128]{1,0:T(8,128)(2,1)S(1)}, bf16[640,128]{1,0:T(8,128)(2,1)S(1)}, u32[]{:S(2)}, u32[]{:S(2)}) collective-permute-start(bf16[640,128]{1,0:T(8,128)(2,1)S(1)} %collective-permute-done.5.refs_5_), channel_id=1, source_target_pairs={{0,2},{1,5},{4,0},{5,9},{8,4},{9,13},{12,8},{13,15},{14,12},{15,11... | collective-permute-start | bytes 491528 | tf_op jit(solution)/shard_map/ppermute | solution.py:278
  11.7 0.0 collective-permute-done.1.other_ref
  11.7 1.8 %shard_map.38.a_ref = bf16[8,2,256,128]{3,2,1,0:T(8,128)(2,1)S(1)} custom-call(s32[4,10]{1,0:T(4,128)S(1)} %copy-done.1, s32[4,10]{1,0:T(4,128)S(1)} %collective-permute-done.others_ref, bf16[4,10,64,64]{3,2,1,0:T(8,128)(2,1)S(1)} %copy-done, bf16[4,10,64,64]{3,2,1,0:T(8,128)(2,1)S(1)} %collective-permute-done.1.other_ref), custom_call_target="tpu_custom_call" | custom-call | bytes 1310720 | tf_op jit(solution)/shard_map/pallas_call | solution.py:104
  13.6 0.2 collective-permute-done.8.refs_6_
  13.8 0.7 %collective-permute-start.10 = (bf16[656,128]{1,0:T(8,128)(2,1)S(1)}, bf16[656,128]{1,0:T(8,128)(2,1)S(1)}, u32[]{:S(2)}, u32[]{:S(2)}) collective-permute-start(bf16[656,128]{1,0:T(8,128)(2,1)S(1)} %collective-permute-done.8.refs_6_), channel_id=1, source_target_pairs={{0,4},{1,3},{4,8},{5,1},{8,12},{9,5},{12,14},{13,9},{14,10},{15,13... | collective-permute-start | bytes 503816 | tf_op jit(solution)/shard_map/ppermute | solution.py:278
  14.5 0.4 %collective-permute-done.3.refs_8_ = bf16[656,128]{1,0:T(8,128)(2,1)S(1)} collective-permute-done((bf16[656,128]{1,0:T(8,128)(2,1)S(1)}, bf16[656,128]{1,0:T(8,128)(2,1)S(1)}, u32[]{:S(2)}, u32[]{:S(2)}) %collective-permute-start.3) | collective-permute-done | bytes 167968 | tf_op jit(solution)/shard_map/ppermute | solution.py:278
  14.9 2.0 %collective-permute-start.4 = (bf16[656,128]{1,0:T(8,128)(2,1)S(1)}, bf16[656,128]{1,0:T(8,128)(2,1)S(1)}, u32[]{:S(2)}, u32[]{:S(2)}) collective-permute-start(bf16[656,128]{1,0:T(8,128)(2,1)S(1)} %collective-permute-done.3.refs_8_), channel_id=1, source_target_pairs={{0,2},{1,5},{4,0},{5,9},{8,4},{9,13},{12,8},{13,15},{14,12},{15,11... | collective-permute-start | bytes 503816 | tf_op jit(solution)/shard_map/ppermute | solution.py:278
  16.9 0.4 %collective-permute-done.9.refs_7_ = bf16[640,128]{1,0:T(8,128)(2,1)S(1)} collective-permute-done((bf16[640,128]{1,0:T(8,128)(2,1)S(1)}, bf16[640,128]{1,0:T(8,128)(2,1)S(1)}, u32[]{:S(2)}, u32[]{:S(2)}) %collective-permute-start.9) | collective-permute-done | bytes 163872 | tf_op jit(solution)/shard_map/ppermute | solution.py:278
  17.3 0.7 %collective-permute-start.11 = (bf16[640,128]{1,0:T(8,128)(2,1)S(1)}, bf16[640,128]{1,0:T(8,128)(2,1)S(1)}, u32[]{:S(2)}, u32[]{:S(2)}) collective-permute-start(bf16[640,128]{1,0:T(8,128)(2,1)S(1)} %collective-permute-done.9.refs_7_), channel_id=1, source_target_pairs={{0,4},{1,3},{4,8},{5,1},{8,12},{9,5},{12,14},{13,9},{14,10},{15,13... | collective-permute-start | bytes 491528 | tf_op jit(solution)/shard_map/ppermute | solution.py:278
  18.0 0.4 %collective-permute-done.6.refs_9_ = bf16[640,128]{1,0:T(8,128)(2,1)S(1)} collective-permute-done((bf16[640,128]{1,0:T(8,128)(2,1)S(1)}, bf16[640,128]{1,0:T(8,128)(2,1)S(1)}, u32[]{:S(2)}, u32[]{:S(2)}) %collective-permute-start.6) | collective-permute-done | bytes 163872 | tf_op jit(solution)/shard_map/ppermute | solution.py:278
  18.5 2.0 %collective-permute-start.7 = (bf16[640,128]{1,0:T(8,128)(2,1)S(1)}, bf16[640,128]{1,0:T(8,128)(2,1)S(1)}, u32[]{:S(2)}, u32[]{:S(2)}) collective-permute-start(bf16[640,128]{1,0:T(8,128)(2,1)S(1)} %collective-permute-done.6.refs_9_), channel_id=1, source_target_pairs={{0,2},{1,5},{4,0},{5,9},{8,4},{9,13},{12,8},{13,15},{14,12},{15,11... | collective-permute-start | bytes 491528 | tf_op jit(solution)/shard_map/ppermute | solution.py:278
  20.4 0.6 %collective-permute-done.10.refs_10_ = bf16[656,128]{1,0:T(8,128)(2,1)S(1)} collective-permute-done((bf16[656,128]{1,0:T(8,128)(2,1)S(1)}, bf16[656,128]{1,0:T(8,128)(2,1)S(1)}, u32[]{:S(2)}, u32[]{:S(2)}) %collective-permute-start.10) | collective-permute-done | bytes 167968 | tf_op jit(solution)/shard_map/ppermute | solution.py:278
  21.0 0.7 %collective-permute-start.12 = (bf16[656,128]{1,0:T(8,128)(2,1)S(1)}, bf16[656,128]{1,0:T(8,128)(2,1)S(1)}, u32[]{:S(2)}, u32[]{:S(2)}) collective-permute-start(bf16[656,128]{1,0:T(8,128)(2,1)S(1)} %collective-permute-done.10.refs_10_), channel_id=1, source_target_pairs={{0,4},{1,3},{4,8},{5,1},{8,12},{9,5},{12,14},{13,9},{14,10},{15,13... | collective-permute-start | bytes 503816 | tf_op jit(solution)/shard_map/ppermute | solution.py:278
  21.7 0.4 %collective-permute-done.4.refs_0_ = bf16[656,128]{1,0:T(8,128)(2,1)S(1)} collective-permute-done((bf16[656,128]{1,0:T(8,128)(2,1)S(1)}, bf16[656,128]{1,0:T(8,128)(2,1)S(1)}, u32[]{:S(2)}, u32[]{:S(2)}) %collective-permute-start.4) | collective-permute-done | bytes 167968 | tf_op jit(solution)/shard_map/ppermute | solution.py:278
  22.2 2.0 %collective-permute-start.13 = (bf16[656,128]{1,0:T(8,128)(2,1)S(1)}, bf16[656,128]{1,0:T(8,128)(2,1)S(1)}, u32[]{:S(2)}, u32[]{:S(2)}) collective-permute-start(bf16[656,128]{1,0:T(8,128)(2,1)S(1)} %collective-permute-done.4.refs_0_), channel_id=1, source_target_pairs={{0,2},{1,5},{4,0},{5,9},{8,4},{9,13},{12,8},{13,15},{14,12},{15,11... | collective-permute-start | bytes 503816 | tf_op jit(solution)/shard_map/ppermute | solution.py:278
  24.1 0.4 %collective-permute-done.11.refs_11_ = bf16[640,128]{1,0:T(8,128)(2,1)S(1)} collective-permute-done((bf16[640,128]{1,0:T(8,128)(2,1)S(1)}, bf16[640,128]{1,0:T(8,128)(2,1)S(1)}, u32[]{:S(2)}, u32[]{:S(2)}) %collective-permute-start.11) | collective-permute-done | bytes 163872 | tf_op jit(solution)/shard_map/ppermute | solution.py:278
  24.5 0.7 %collective-permute-start.14 = (bf16[640,128]{1,0:T(8,128)(2,1)S(1)}, bf16[640,128]{1,0:T(8,128)(2,1)S(1)}, u32[]{:S(2)}, u32[]{:S(2)}) collective-permute-start(bf16[640,128]{1,0:T(8,128)(2,1)S(1)} %collective-permute-done.11.refs_11_), channel_id=1, source_target_pairs={{0,4},{1,3},{4,8},{5,1},{8,12},{9,5},{12,14},{13,9},{14,10},{15,13... | collective-permute-start | bytes 491528 | tf_op jit(solution)/shard_map/ppermute | solution.py:278
  25.3 0.4 %collective-permute-done.7.refs_1_ = bf16[640,128]{1,0:T(8,128)(2,1)S(1)} collective-permute-done((bf16[640,128]{1,0:T(8,128)(2,1)S(1)}, bf16[640,128]{1,0:T(8,128)(2,1)S(1)}, u32[]{:S(2)}, u32[]{:S(2)}) %collective-permute-start.7) | collective-permute-done | bytes 163872 | tf_op jit(solution)/shard_map/ppermute | solution.py:278
  25.7 2.0 %collective-permute-start.15 = (bf16[640,128]{1,0:T(8,128)(2,1)S(1)}, bf16[640,128]{1,0:T(8,128)(2,1)S(1)}, u32[]{:S(2)}, u32[]{:S(2)}) collective-permute-start(bf16[640,128]{1,0:T(8,128)(2,1)S(1)} %collective-permute-done.7.refs_1_), channel_id=1, source_target_pairs={{0,2},{1,5},{4,0},{5,9},{8,4},{9,13},{12,8},{13,15},{14,12},{15,11... | collective-permute-start | bytes 491528 | tf_op jit(solution)/shard_map/ppermute | solution.py:278
  27.7 3.2 %shard_map.39.before = f32[4,2,256,128]{3,2,1,0:T(8,128)S(1)} custom-call(bf16[8,2,256,128]{3,2,1,0:T(8,128)(2,1)S(1)} %shard_map.38.a_ref, bf16[656,128]{1,0:T(8,128)(2,1)S(1)} %collective-permute-done.4.refs_0_, bf16[640,128]{1,0:T(8,128)(2,1)S(1)} %collective-permute-done.7.refs_1_, bf16[656,128]{1,0:T(8,128)(2,1)S(1)} %get-tuple-element.16.refs_2_, ...), custom_call_target="tpu_custom_call" | custom-call | flops 805306368 | tf_op jit(solution)/shard_map/pallas_call | solution.py:233
  30.8 0.0 collective-permute-done.12.refs_0_
  30.8 0.0 collective-permute-done.13.refs_1_.refs_2_
  30.9 1.3 %shard_map.40.total = f32[4,2,256,128]{3,2,1,0:T(8,128)S(1)} custom-call(bf16[8,2,256,128]{3,2,1,0:T(8,128)(2,1)S(1)} %shard_map.38.a_ref, f32[4,2,256,128]{3,2,1,0:T(8,128)S(1)} %shard_map.39.before, bf16[656,128]{1,0:T(8,128)(2,1)S(1)} %collective-permute-done.12.refs_0_, ...), custom_call_target="tpu_custom_call", output_to_operand_aliasing={{}: (1, {})} | custom-call | flops 268435456 | tf_op jit(solution)/shard_map/pallas_call | solution.py:233
  32.1 0.0 collective-permute-done.14.refs_1_
  32.1 0.0 collective-permute-done.15.refs_3_
  32.2 2.3 %shard_map.41 = bf16[4,10,64,64]{3,2,1,0:T(8,128)(2,1)} custom-call(bf16[8,2,256,128]{3,2,1,0:T(8,128)(2,1)S(1)} %shard_map.38.a_ref, f32[4,2,256,128]{3,2,1,0:T(8,128)S(1)} %shard_map.40.total, s32[4,10]{1,0:T(4,128)S(1)} %copy-done.1, bf16[656,128]{1,0:T(8,128)(2,1)S(1)} %collective-permute-done.12.refs_0_, ...), custom_call_target="tpu_custom_call" | custom-call | flops 167772160 | tf_op jit(solution)/shard_map/pallas_call | solution.py:233
Async XLA Ops:
  0.0 4.3 %copy-start = (bf16[4,10,64,64]{3,2,1,0:T(8,128)(2,1)S(1)}, bf16[4,10,64,64]{3,2,1,0:T(8,128)(2,1)}, u32[]{:S(2)}) copy-start(bf16[4,10,64,64]{3,2,1,0:T(8,128)(2,1)} %own_ref.1) | copy-start | bytes 983044
  1.3 4.6 %copy-start.1 = (s32[4,10]{1,0:T(4,128)S(1)}, s32[4,10]{1,0:T(4,128)}, u32[]{:S(2)}) copy-start(s32[4,10]{1,0:T(4,128)} %cols_hbm.3) | copy-start | bytes 484
  1.3 6.4 %collective-permute-start.2 = (bf16[656,128]{1,0:T(8,128)(2,1)S(1)}, bf16[656,128]{1,0:T(8,128)(2,1)S(1)}, u32[]{:S(2)}, u32[]{:S(2)}) collective-permute-start(bf16[656,128]{1,0:T(8,128)(2,1)S(1)} %get-tuple-element.16.refs_2_), channel_id=1, source_target_pairs={{0,2},{1,5},{4,0},{5,9},{8,4},{9,13},{12,8},{13,15},{14,12},{15,11... | collective-permute-start | bytes 503816 | tf_op jit(solution)/shard_map/ppermute | solution.py:278
  4.3 7.4 %collective-permute-start.1 = (bf16[4,10,64,64]{3,2,1,0:T(8,128)(2,1)S(1)}, bf16[4,10,64,64]{3,2,1,0:T(8,128)(2,1)S(1)}, u32[]{:S(2)}, u32[]{:S(2)}) collective-permute-start(bf16[4,10,64,64]{3,2,1,0:T(8,128)(2,1)S(1)} %copy-done), channel_id=1, source_target_pairs={{0,1},{1,0},{2,3},{3,2},{4,5},{5,4},{6,7},{7,6},{8,9},{9,8},{10,11... | collective-permute-start | bytes 983048 | tf_op jit(solution)/shard_map/ppermute | solution.py:261
  4.3 5.4 %collective-permute-start.5 = (bf16[640,128]{1,0:T(8,128)(2,1)S(1)}, bf16[640,128]{1,0:T(8,128)(2,1)S(1)}, u32[]{:S(2)}, u32[]{:S(2)}) collective-permute-start(bf16[640,128]{1,0:T(8,128)(2,1)S(1)} %get-tuple-element.17.refs_3_), channel_id=1, source_target_pairs={{0,2},{1,5},{4,0},{5,9},{8,4},{9,13},{12,8},{13,15},{14,12},{15,11... | collective-permute-start | bytes 491528 | tf_op jit(solution)/shard_map/ppermute | solution.py:278
  5.9 1.2 %collective-permute-start = (s32[4,10]{1,0:T(4,128)S(1)}, s32[4,10]{1,0:T(4,128)S(1)}, u32[]{:S(2)}, u32[]{:S(2)}) collective-permute-start(s32[4,10]{1,0:T(4,128)S(1)} %copy-done.1), channel_id=1, source_target_pairs={{0,1},{1,0},{2,3},{3,2},{4,5},{5,4},{6,7},{7,6},{8,9},{9,8},{10,11... | collective-permute-start | bytes 488 | tf_op jit(solution)/shard_map/ppermute | solution.py:261
  7.1 6.7 %collective-permute-start.8 = (bf16[656,128]{1,0:T(8,128)(2,1)S(1)}, bf16[656,128]{1,0:T(8,128)(2,1)S(1)}, u32[]{:S(2)}, u32[]{:S(2)}) collective-permute-start(bf16[656,128]{1,0:T(8,128)(2,1)S(1)} %get-tuple-element.16.refs_2_), channel_id=1, source_target_pairs={{0,4},{1,3},{4,8},{5,1},{8,12},{9,5},{12,14},{13,9},{14,10},{15,13... | collective-permute-start | bytes 503816 | tf_op jit(solution)/shard_map/ppermute | solution.py:278
  7.7 7.2 %collective-permute-start.3 = (bf16[656,128]{1,0:T(8,128)(2,1)S(1)}, bf16[656,128]{1,0:T(8,128)(2,1)S(1)}, u32[]{:S(2)}, u32[]{:S(2)}) collective-permute-start(bf16[656,128]{1,0:T(8,128)(2,1)S(1)} %collective-permute-done.2.refs_4_), channel_id=1, source_target_pairs={{0,2},{1,5},{4,0},{5,9},{8,4},{9,13},{12,8},{13,15},{14,12},{15,11... | collective-permute-start | bytes 503816 | tf_op jit(solution)/shard_map/ppermute | solution.py:278
  9.7 7.6 %collective-permute-start.9 = (bf16[640,128]{1,0:T(8,128)(2,1)S(1)}, bf16[640,128]{1,0:T(8,128)(2,1)S(1)}, u32[]{:S(2)}, u32[]{:S(2)}) collective-permute-start(bf16[640,128]{1,0:T(8,128)(2,1)S(1)} %get-tuple-element.17.refs_3_), channel_id=1, source_target_pairs={{0,4},{1,3},{4,8},{5,1},{8,12},{9,5},{12,14},{13,9},{14,10},{15,13... | collective-permute-start | bytes 491528 | tf_op jit(solution)/shard_map/ppermute | solution.py:278
  9.8 8.7 %collective-permute-start.6 = (bf16[640,128]{1,0:T(8,128)(2,1)S(1)}, bf16[640,128]{1,0:T(8,128)(2,1)S(1)}, u32[]{:S(2)}, u32[]{:S(2)}) collective-permute-start(bf16[640,128]{1,0:T(8,128)(2,1)S(1)} %collective-permute-done.5.refs_5_), channel_id=1, source_target_pairs={{0,2},{1,5},{4,0},{5,9},{8,4},{9,13},{12,8},{13,15},{14,12},{15,11... | collective-permute-start | bytes 491528 | tf_op jit(solution)/shard_map/ppermute | solution.py:278
  13.8 7.2 %collective-permute-start.10 = (bf16[656,128]{1,0:T(8,128)(2,1)S(1)}, bf16[656,128]{1,0:T(8,128)(2,1)S(1)}, u32[]{:S(2)}, u32[]{:S(2)}) collective-permute-start(bf16[656,128]{1,0:T(8,128)(2,1)S(1)} %collective-permute-done.8.refs_6_), channel_id=1, source_target_pairs={{0,4},{1,3},{4,8},{5,1},{8,12},{9,5},{12,14},{13,9},{14,10},{15,13... | collective-permute-start | bytes 503816 | tf_op jit(solution)/shard_map/ppermute | solution.py:278
  14.9 7.2 %collective-permute-start.4 = (bf16[656,128]{1,0:T(8,128)(2,1)S(1)}, bf16[656,128]{1,0:T(8,128)(2,1)S(1)}, u32[]{:S(2)}, u32[]{:S(2)}) collective-permute-start(bf16[656,128]{1,0:T(8,128)(2,1)S(1)} %collective-permute-done.3.refs_8_), channel_id=1, source_target_pairs={{0,2},{1,5},{4,0},{5,9},{8,4},{9,13},{12,8},{13,15},{14,12},{15,11... | collective-permute-start | bytes 503816 | tf_op jit(solution)/shard_map/ppermute | solution.py:278
  17.3 7.2 %collective-permute-start.11 = (bf16[640,128]{1,0:T(8,128)(2,1)S(1)}, bf16[640,128]{1,0:T(8,128)(2,1)S(1)}, u32[]{:S(2)}, u32[]{:S(2)}) collective-permute-start(bf16[640,128]{1,0:T(8,128)(2,1)S(1)} %collective-permute-done.9.refs_7_), channel_id=1, source_target_pairs={{0,4},{1,3},{4,8},{5,1},{8,12},{9,5},{12,14},{13,9},{14,10},{15,13... | collective-permute-start | bytes 491528 | tf_op jit(solution)/shard_map/ppermute | solution.py:278
  18.5 7.2 %collective-permute-start.7 = (bf16[640,128]{1,0:T(8,128)(2,1)S(1)}, bf16[640,128]{1,0:T(8,128)(2,1)S(1)}, u32[]{:S(2)}, u32[]{:S(2)}) collective-permute-start(bf16[640,128]{1,0:T(8,128)(2,1)S(1)} %collective-permute-done.6.refs_9_), channel_id=1, source_target_pairs={{0,2},{1,5},{4,0},{5,9},{8,4},{9,13},{12,8},{13,15},{14,12},{15,11... | collective-permute-start | bytes 491528 | tf_op jit(solution)/shard_map/ppermute | solution.py:278
  21.0 9.8 %collective-permute-start.12 = (bf16[656,128]{1,0:T(8,128)(2,1)S(1)}, bf16[656,128]{1,0:T(8,128)(2,1)S(1)}, u32[]{:S(2)}, u32[]{:S(2)}) collective-permute-start(bf16[656,128]{1,0:T(8,128)(2,1)S(1)} %collective-permute-done.10.refs_10_), channel_id=1, source_target_pairs={{0,4},{1,3},{4,8},{5,1},{8,12},{9,5},{12,14},{13,9},{14,10},{15,13... | collective-permute-start | bytes 503816 | tf_op jit(solution)/shard_map/ppermute | solution.py:278
  22.2 8.7 %collective-permute-start.13 = (bf16[656,128]{1,0:T(8,128)(2,1)S(1)}, bf16[656,128]{1,0:T(8,128)(2,1)S(1)}, u32[]{:S(2)}, u32[]{:S(2)}) collective-permute-start(bf16[656,128]{1,0:T(8,128)(2,1)S(1)} %collective-permute-done.4.refs_0_), channel_id=1, source_target_pairs={{0,2},{1,5},{4,0},{5,9},{8,4},{9,13},{12,8},{13,15},{14,12},{15,11... | collective-permute-start | bytes 503816 | tf_op jit(solution)/shard_map/ppermute | solution.py:278
  24.5 7.6 %collective-permute-start.14 = (bf16[640,128]{1,0:T(8,128)(2,1)S(1)}, bf16[640,128]{1,0:T(8,128)(2,1)S(1)}, u32[]{:S(2)}, u32[]{:S(2)}) collective-permute-start(bf16[640,128]{1,0:T(8,128)(2,1)S(1)} %collective-permute-done.11.refs_11_), channel_id=1, source_target_pairs={{0,4},{1,3},{4,8},{5,1},{8,12},{9,5},{12,14},{13,9},{14,10},{15,13... | collective-permute-start | bytes 491528 | tf_op jit(solution)/shard_map/ppermute | solution.py:278
  25.7 6.5 %collective-permute-start.15 = (bf16[640,128]{1,0:T(8,128)(2,1)S(1)}, bf16[640,128]{1,0:T(8,128)(2,1)S(1)}, u32[]{:S(2)}, u32[]{:S(2)}) collective-permute-start(bf16[640,128]{1,0:T(8,128)(2,1)S(1)} %collective-permute-done.7.refs_1_), channel_id=1, source_target_pairs={{0,2},{1,5},{4,0},{5,9},{8,4},{9,13},{12,8},{13,15},{14,12},{15,11... | collective-permute-start | bytes 491528 | tf_op jit(solution)/shard_map/ppermute | solution.py:278

commit v19 on v18

--- a/solution.py
+++ b/solution.py
@@ -279,10 +279,8 @@
         rounds.append([(way, step, held[way], 0) for way in ways])
     *_, late, last = rounds
     total = product(order, sum(rounds[:-2], late[:1]), a, total, total_shape)
-    late = late[1:] + last
-    total = product(order, [(*what, refs[:1], 0) for *what, refs, _ in late], a, total, total_shape)
     out = jax.ShapeDtypeStruct(a_vals.shape, a_vals.dtype)
-    return product(order, [(*what, refs, 1) for *what, refs, _ in late], a, total, out, cols)
+    return product(order, late[1:] + last, a, total, out, cols)
 
 
 def ring_order(mesh):

time: 34.6 us -> 34.5 us (level)
  Pallas kernels: 9.86 us -> 8.85 us
  waiting for transfers between devices: 4.6 us -> 5.52 us
    pallas_call x3 -> x2, Pallas kernels: 6.75 us -> 5.74 us  [product(): pl.pallas_call(functools.partial(kernel, sources), out_shape=out, in_spec...]
    ppermute x14, waiting for transfers between devices: 3.44 us -> 4.37 us  [local(): held[way] = [lax.ppermute(part, ('row', 'col'), ring(way)) for part in sent]]
  transfers between devices with their start and end apart: 16 -> 16, of which waited for: 10 -> 11; matrix products, arithmetic and copies ran while one was open for 0% -> 0% of each run, Pallas kernels for 18% -> 15%
where the time goes in v19:
time: 34.5 us; the launch traced here: 34.3 us
  starting transfers between devices  19.9 us (58%)
  Pallas kernels  8.85 us (26%)
  waiting for transfers between devices  5.52 us (16%)
    ppermute x14, starting transfers between devices, local(): held[way] = [lax.ppermute(part, ('row', 'col'), ring(way)) for part in sent]  19.9 us
    pallas_call x2, Pallas kernels, product(): pl.pallas_call(functools.partial(kernel, sources), out_shape=out, in_spec...  5.74 us
    ppermute x14, waiting for transfers between devices, local(): held[way] = [lax.ppermute(part, ('row', 'col'), ring(way)) for part in sent]  4.37 us
    pallas_call x1, Pallas kernels, dense_rows(): pl.pallas_call(dense_kernel, out_shape=jax.ShapeDtypeStruct((sources, row...  1.82 us
    pallas_call x1, Pallas kernels, pack(): pl.pallas_call(functools.partial(pack_kernel, half), out_shape=[jax.Shape...  1.29 us
    ppermute x2, waiting for transfers between devices, local(): a_other, others = (lax.ppermute(x, 'col', swap) for x in mine)  1.16 us
  transfers between devices with their start and end apart: 16, of which 11 were waited for; matrix products, arithmetic and copies ran while one was open for 0% of the time, Pallas kernels for 15%

profile of v19, /device:TPU:0, one launch (start us, length us, event | category | flops | bytes accessed | tf_op | source)
XLA Modules:
  0.0 34.3 jit_solution(3894685196191827474)
XLA Ops:
  0.0 0.0 copy-start
  0.0 1.3 %shard_map.37 = (bf16[656,128]{1,0:T(8,128)(2,1)S(1)}, bf16[640,128]{1,0:T(8,128)(2,1)S(1)}) custom-call(s32[4,10]{1,0:T(4,128)} %cols_hbm.3, bf16[4,10,64,64]{3,2,1,0:T(8,128)(2,1)} %b_hbm.1), custom_call_target="tpu_custom_call" | custom-call | bytes 655360 | tf_op jit(solution)/shard_map/pallas_call | solution.py:58
  1.3 0.0 copy-start.1
  1.3 3.0 %collective-permute-start.2 = (bf16[656,128]{1,0:T(8,128)(2,1)S(1)}, bf16[656,128]{1,0:T(8,128)(2,1)S(1)}, u32[]{:S(2)}, u32[]{:S(2)}) collective-permute-start(bf16[656,128]{1,0:T(8,128)(2,1)S(1)} %get-tuple-element.16.refs_2_), channel_id=1, source_target_pairs={{0,2},{1,5},{4,0},{5,9},{8,4},{9,13},{12,8},{13,15},{14,12},{15,11... | collective-permute-start | bytes 503816 | tf_op jit(solution)/shard_map/ppermute | solution.py:278
  4.3 0.0 copy-done
  4.3 0.0 collective-permute-start.1
  4.3 1.6 %collective-permute-start.5 = (bf16[640,128]{1,0:T(8,128)(2,1)S(1)}, bf16[640,128]{1,0:T(8,128)(2,1)S(1)}, u32[]{:S(2)}, u32[]{:S(2)}) collective-permute-start(bf16[640,128]{1,0:T(8,128)(2,1)S(1)} %get-tuple-element.17.refs_3_), channel_id=1, source_target_pairs={{0,2},{1,5},{4,0},{5,9},{8,4},{9,13},{12,8},{13,15},{14,12},{15,11... | collective-permute-start | bytes 491528 | tf_op jit(solution)/shard_map/ppermute | solution.py:278
  5.9 0.0 copy-done.1
  5.9 0.0 collective-permute-start
  5.9 1.2 %collective-permute-done.others_ref = s32[4,10]{1,0:T(4,128)S(1)} collective-permute-done((s32[4,10]{1,0:T(4,128)S(1)}, s32[4,10]{1,0:T(4,128)S(1)}, u32[]{:S(2)}, u32[]{:S(2)}) %collective-permute-start) | collective-permute-done | bytes 192 | tf_op jit(solution)/shard_map/ppermute | solution.py:261
  7.1 0.6 %collective-permute-start.8 = (bf16[656,128]{1,0:T(8,128)(2,1)S(1)}, bf16[656,128]{1,0:T(8,128)(2,1)S(1)}, u32[]{:S(2)}, u32[]{:S(2)}) collective-permute-start(bf16[656,128]{1,0:T(8,128)(2,1)S(1)} %get-tuple-element.16.refs_2_), channel_id=1, source_target_pairs={{0,4},{1,3},{4,8},{5,1},{8,12},{9,5},{12,14},{13,9},{14,10},{15,13... | collective-permute-start | bytes 503816 | tf_op jit(solution)/shard_map/ppermute | solution.py:278
  7.6 0.1 collective-permute-done.2.refs_4_
  7.7 2.0 %collective-permute-start.3 = (bf16[656,128]{1,0:T(8,128)(2,1)S(1)}, bf16[656,128]{1,0:T(8,128)(2,1)S(1)}, u32[]{:S(2)}, u32[]{:S(2)}) collective-permute-start(bf16[656,128]{1,0:T(8,128)(2,1)S(1)} %collective-permute-done.2.refs_4_), channel_id=1, source_target_pairs={{0,2},{1,5},{4,0},{5,9},{8,4},{9,13},{12,8},{13,15},{14,12},{15,11... | collective-permute-start | bytes 503816 | tf_op jit(solution)/shard_map/ppermute | solution.py:278
  9.7 0.1 collective-permute-start.9
  9.8 0.0 collective-permute-done.5.refs_5_
  9.8 2.0 %collective-permute-start.6 = (bf16[640,128]{1,0:T(8,128)(2,1)S(1)}, bf16[640,128]{1,0:T(8,128)(2,1)S(1)}, u32[]{:S(2)}, u32[]{:S(2)}) collective-permute-start(bf16[640,128]{1,0:T(8,128)(2,1)S(1)} %collective-permute-done.5.refs_5_), channel_id=1, source_target_pairs={{0,2},{1,5},{4,0},{5,9},{8,4},{9,13},{12,8},{13,15},{14,12},{15,11... | collective-permute-start | bytes 491528 | tf_op jit(solution)/shard_map/ppermute | solution.py:278
  11.7 0.0 collective-permute-done.1.other_ref
  11.7 1.8 %shard_map.38.a_ref = bf16[8,2,256,128]{3,2,1,0:T(8,128)(2,1)S(1)} custom-call(s32[4,10]{1,0:T(4,128)S(1)} %copy-done.1, s32[4,10]{1,0:T(4,128)S(1)} %collective-permute-done.others_ref, bf16[4,10,64,64]{3,2,1,0:T(8,128)(2,1)S(1)} %copy-done, bf16[4,10,64,64]{3,2,1,0:T(8,128)(2,1)S(1)} %collective-permute-done.1.other_ref), custom_call_target="tpu_custom_call" | custom-call | bytes 1310720 | tf_op jit(solution)/shard_map/pallas_call | solution.py:104
  13.6 0.2 collective-permute-done.8.refs_6_
  13.8 0.7 %collective-permute-start.10 = (bf16[656,128]{1,0:T(8,128)(2,1)S(1)}, bf16[656,128]{1,0:T(8,128)(2,1)S(1)}, u32[]{:S(2)}, u32[]{:S(2)}) collective-permute-start(bf16[656,128]{1,0:T(8,128)(2,1)S(1)} %collective-permute-done.8.refs_6_), channel_id=1, source_target_pairs={{0,4},{1,3},{4,8},{5,1},{8,12},{9,5},{12,14},{13,9},{14,10},{15,13... | collective-permute-start | bytes 503816 | tf_op jit(solution)/shard_map/ppermute | solution.py:278
  14.5 0.4 %collective-permute-done.3.refs_8_ = bf16[656,128]{1,0:T(8,128)(2,1)S(1)} collective-permute-done((bf16[656,128]{1,0:T(8,128)(2,1)S(1)}, bf16[656,128]{1,0:T(8,128)(2,1)S(1)}, u32[]{:S(2)}, u32[]{:S(2)}) %collective-permute-start.3) | collective-permute-done | bytes 167968 | tf_op jit(solution)/shard_map/ppermute | solution.py:278
  14.9 2.0 %collective-permute-start.4 = (bf16[656,128]{1,0:T(8,128)(2,1)S(1)}, bf16[656,128]{1,0:T(8,128)(2,1)S(1)}, u32[]{:S(2)}, u32[]{:S(2)}) collective-permute-start(bf16[656,128]{1,0:T(8,128)(2,1)S(1)} %collective-permute-done.3.refs_8_), channel_id=1, source_target_pairs={{0,2},{1,5},{4,0},{5,9},{8,4},{9,13},{12,8},{13,15},{14,12},{15,11... | collective-permute-start | bytes 503816 | tf_op jit(solution)/shard_map/ppermute | solution.py:278
  16.9 0.4 %collective-permute-done.9.refs_7_ = bf16[640,128]{1,0:T(8,128)(2,1)S(1)} collective-permute-done((bf16[640,128]{1,0:T(8,128)(2,1)S(1)}, bf16[640,128]{1,0:T(8,128)(2,1)S(1)}, u32[]{:S(2)}, u32[]{:S(2)}) %collective-permute-start.9) | collective-permute-done | bytes 163872 | tf_op jit(solution)/shard_map/ppermute | solution.py:278
  17.3 0.7 %collective-permute-start.11 = (bf16[640,128]{1,0:T(8,128)(2,1)S(1)}, bf16[640,128]{1,0:T(8,128)(2,1)S(1)}, u32[]{:S(2)}, u32[]{:S(2)}) collective-permute-start(bf16[640,128]{1,0:T(8,128)(2,1)S(1)} %collective-permute-done.9.refs_7_), channel_id=1, source_target_pairs={{0,4},{1,3},{4,8},{5,1},{8,12},{9,5},{12,14},{13,9},{14,10},{15,13... | collective-permute-start | bytes 491528 | tf_op jit(solution)/shard_map/ppermute | solution.py:278
  18.0 0.4 %collective-permute-done.6.refs_9_ = bf16[640,128]{1,0:T(8,128)(2,1)S(1)} collective-permute-done((bf16[640,128]{1,0:T(8,128)(2,1)S(1)}, bf16[640,128]{1,0:T(8,128)(2,1)S(1)}, u32[]{:S(2)}, u32[]{:S(2)}) %collective-permute-start.6) | collective-permute-done | bytes 163872 | tf_op jit(solution)/shard_map/ppermute | solution.py:278
  18.5 2.0 %collective-permute-start.7 = (bf16[640,128]{1,0:T(8,128)(2,1)S(1)}, bf16[640,128]{1,0:T(8,128)(2,1)S(1)}, u32[]{:S(2)}, u32[]{:S(2)}) collective-permute-start(bf16[640,128]{1,0:T(8,128)(2,1)S(1)} %collective-permute-done.6.refs_9_), channel_id=1, source_target_pairs={{0,2},{1,5},{4,0},{5,9},{8,4},{9,13},{12,8},{13,15},{14,12},{15,11... | collective-permute-start | bytes 491528 | tf_op jit(solution)/shard_map/ppermute | solution.py:278
  20.4 0.6 %collective-permute-done.10.refs_10_ = bf16[656,128]{1,0:T(8,128)(2,1)S(1)} collective-permute-done((bf16[656,128]{1,0:T(8,128)(2,1)S(1)}, bf16[656,128]{1,0:T(8,128)(2,1)S(1)}, u32[]{:S(2)}, u32[]{:S(2)}) %collective-permute-start.10) | collective-permute-done | bytes 167968 | tf_op jit(solution)/shard_map/ppermute | solution.py:278
  21.0 0.7 %collective-permute-start.12 = (bf16[656,128]{1,0:T(8,128)(2,1)S(1)}, bf16[656,128]{1,0:T(8,128)(2,1)S(1)}, u32[]{:S(2)}, u32[]{:S(2)}) collective-permute-start(bf16[656,128]{1,0:T(8,128)(2,1)S(1)} %collective-permute-done.10.refs_10_), channel_id=1, source_target_pairs={{0,4},{1,3},{4,8},{5,1},{8,12},{9,5},{12,14},{13,9},{14,10},{15,13... | collective-permute-start | bytes 503816 | tf_op jit(solution)/shard_map/ppermute | solution.py:278
  21.7 0.4 %collective-permute-done.4.refs_0_ = bf16[656,128]{1,0:T(8,128)(2,1)S(1)} collective-permute-done((bf16[656,128]{1,0:T(8,128)(2,1)S(1)}, bf16[656,128]{1,0:T(8,128)(2,1)S(1)}, u32[]{:S(2)}, u32[]{:S(2)}) %collective-permute-start.4) | collective-permute-done | bytes 167968 | tf_op jit(solution)/shard_map/ppermute | solution.py:278
  22.2 2.0 %collective-permute-start.14 = (bf16[656,128]{1,0:T(8,128)(2,1)S(1)}, bf16[656,128]{1,0:T(8,128)(2,1)S(1)}, u32[]{:S(2)}, u32[]{:S(2)}) collective-permute-start(bf16[656,128]{1,0:T(8,128)(2,1)S(1)} %collective-permute-done.4.refs_0_), channel_id=1, source_target_pairs={{0,2},{1,5},{4,0},{5,9},{8,4},{9,13},{12,8},{13,15},{14,12},{15,11... | collective-permute-start | bytes 503816 | tf_op jit(solution)/shard_map/ppermute | solution.py:278
  24.1 0.4 %collective-permute-done.11.refs_11_ = bf16[640,128]{1,0:T(8,128)(2,1)S(1)} collective-permute-done((bf16[640,128]{1,0:T(8,128)(2,1)S(1)}, bf16[640,128]{1,0:T(8,128)(2,1)S(1)}, u32[]{:S(2)}, u32[]{:S(2)}) %collective-permute-start.11) | collective-permute-done | bytes 163872 | tf_op jit(solution)/shard_map/ppermute | solution.py:278
  24.5 0.7 %collective-permute-start.13 = (bf16[640,128]{1,0:T(8,128)(2,1)S(1)}, bf16[640,128]{1,0:T(8,128)(2,1)S(1)}, u32[]{:S(2)}, u32[]{:S(2)}) collective-permute-start(bf16[640,128]{1,0:T(8,128)(2,1)S(1)} %collective-permute-done.11.refs_11_), channel_id=1, source_target_pairs={{0,4},{1,3},{4,8},{5,1},{8,12},{9,5},{12,14},{13,9},{14,10},{15,13... | collective-permute-start | bytes 491528 | tf_op jit(solution)/shard_map/ppermute | solution.py:278
  25.3 0.4 %collective-permute-done.7.refs_1_ = bf16[640,128]{1,0:T(8,128)(2,1)S(1)} collective-permute-done((bf16[640,128]{1,0:T(8,128)(2,1)S(1)}, bf16[640,128]{1,0:T(8,128)(2,1)S(1)}, u32[]{:S(2)}, u32[]{:S(2)}) %collective-permute-start.7) | collective-permute-done | bytes 163872 | tf_op jit(solution)/shard_map/ppermute | solution.py:278
  25.7 2.0 %collective-permute-start.15 = (bf16[640,128]{1,0:T(8,128)(2,1)S(1)}, bf16[640,128]{1,0:T(8,128)(2,1)S(1)}, u32[]{:S(2)}, u32[]{:S(2)}) collective-permute-start(bf16[640,128]{1,0:T(8,128)(2,1)S(1)} %collective-permute-done.7.refs_1_), channel_id=1, source_target_pairs={{0,2},{1,5},{4,0},{5,9},{8,4},{9,13},{12,8},{13,15},{14,12},{15,11... | collective-permute-start | bytes 491528 | tf_op jit(solution)/shard_map/ppermute | solution.py:278
  27.7 3.2 %shard_map.39.total = f32[4,2,256,128]{3,2,1,0:T(8,128)S(1)} custom-call(bf16[8,2,256,128]{3,2,1,0:T(8,128)(2,1)S(1)} %shard_map.38.a_ref, bf16[656,128]{1,0:T(8,128)(2,1)S(1)} %collective-permute-done.4.refs_0_, bf16[640,128]{1,0:T(8,128)(2,1)S(1)} %collective-permute-done.7.refs_1_, bf16[656,128]{1,0:T(8,128)(2,1)S(1)} %get-tuple-element.16.refs_2_, ...), custom_call_target="tpu_custom_call" | custom-call | flops 805306368 | tf_op jit(solution)/shard_map/pallas_call | solution.py:233
  30.8 0.9 %collective-permute-done.13.refs_1_ = bf16[640,128]{1,0:T(8,128)(2,1)S(1)} collective-permute-done((bf16[640,128]{1,0:T(8,128)(2,1)S(1)}, bf16[640,128]{1,0:T(8,128)(2,1)S(1)}, u32[]{:S(2)}, u32[]{:S(2)}) %collective-permute-start.13) | collective-permute-done | bytes 163872 | tf_op jit(solution)/shard_map/ppermute | solution.py:278
  31.8 0.0 collective-permute-done.15.refs_3_
  31.8 0.0 collective-permute-done.12.refs_0_
  31.8 0.0 collective-permute-done.14.refs_2_
  31.8 2.6 %shard_map.40 = bf16[4,10,64,64]{3,2,1,0:T(8,128)(2,1)} custom-call(bf16[8,2,256,128]{3,2,1,0:T(8,128)(2,1)S(1)} %shard_map.38.a_ref, f32[4,2,256,128]{3,2,1,0:T(8,128)S(1)} %shard_map.39.total, s32[4,10]{1,0:T(4,128)S(1)} %copy-done.1, bf16[656,128]{1,0:T(8,128)(2,1)S(1)} %collective-permute-done.12.refs_0_, ...), custom_call_target="tpu_custom_call" | custom-call | flops 167772160 | tf_op jit(solution)/shard_map/pallas_call | solution.py:233
Async XLA Ops:
  0.0 4.3 %copy-start = (bf16[4,10,64,64]{3,2,1,0:T(8,128)(2,1)S(1)}, bf16[4,10,64,64]{3,2,1,0:T(8,128)(2,1)}, u32[]{:S(2)}) copy-start(bf16[4,10,64,64]{3,2,1,0:T(8,128)(2,1)} %own_ref.1) | copy-start | bytes 983044
  1.3 4.6 %copy-start.1 = (s32[4,10]{1,0:T(4,128)S(1)}, s32[4,10]{1,0:T(4,128)}, u32[]{:S(2)}) copy-start(s32[4,10]{1,0:T(4,128)} %cols_hbm.3) | copy-start | bytes 484
  1.3 6.4 %collective-permute-start.2 = (bf16[656,128]{1,0:T(8,128)(2,1)S(1)}, bf16[656,128]{1,0:T(8,128)(2,1)S(1)}, u32[]{:S(2)}, u32[]{:S(2)}) collective-permute-start(bf16[656,128]{1,0:T(8,128)(2,1)S(1)} %get-tuple-element.16.refs_2_), channel_id=1, source_target_pairs={{0,2},{1,5},{4,0},{5,9},{8,4},{9,13},{12,8},{13,15},{14,12},{15,11... | collective-permute-start | bytes 503816 | tf_op jit(solution)/shard_map/ppermute | solution.py:278
  4.3 7.4 %collective-permute-start.1 = (bf16[4,10,64,64]{3,2,1,0:T(8,128)(2,1)S(1)}, bf16[4,10,64,64]{3,2,1,0:T(8,128)(2,1)S(1)}, u32[]{:S(2)}, u32[]{:S(2)}) collective-permute-start(bf16[4,10,64,64]{3,2,1,0:T(8,128)(2,1)S(1)} %copy-done), channel_id=1, source_target_pairs={{0,1},{1,0},{2,3},{3,2},{4,5},{5,4},{6,7},{7,6},{8,9},{9,8},{10,11... | collective-permute-start | bytes 983048 | tf_op jit(solution)/shard_map/ppermute | solution.py:261
  4.3 5.4 %collective-permute-start.5 = (bf16[640,128]{1,0:T(8,128)(2,1)S(1)}, bf16[640,128]{1,0:T(8,128)(2,1)S(1)}, u32[]{:S(2)}, u32[]{:S(2)}) collective-permute-start(bf16[640,128]{1,0:T(8,128)(2,1)S(1)} %get-tuple-element.17.refs_3_), channel_id=1, source_target_pairs={{0,2},{1,5},{4,0},{5,9},{8,4},{9,13},{12,8},{13,15},{14,12},{15,11... | collective-permute-start | bytes 491528 | tf_op jit(solution)/shard_map/ppermute | solution.py:278
  5.9 1.2 %collective-permute-start = (s32[4,10]{1,0:T(4,128)S(1)}, s32[4,10]{1,0:T(4,128)S(1)}, u32[]{:S(2)}, u32[]{:S(2)}) collective-permute-start(s32[4,10]{1,0:T(4,128)S(1)} %copy-done.1), channel_id=1, source_target_pairs={{0,1},{1,0},{2,3},{3,2},{4,5},{5,4},{6,7},{7,6},{8,9},{9,8},{10,11... | collective-permute-start | bytes 488 | tf_op jit(solution)/shard_map/ppermute | solution.py:261
  7.1 6.7 %collective-permute-start.8 = (bf16[656,128]{1,0:T(8,128)(2,1)S(1)}, bf16[656,128]{1,0:T(8,128)(2,1)S(1)}, u32[]{:S(2)}, u32[]{:S(2)}) collective-permute-start(bf16[656,128]{1,0:T(8,128)(2,1)S(1)} %get-tuple-element.16.refs_2_), channel_id=1, source_target_pairs={{0,4},{1,3},{4,8},{5,1},{8,12},{9,5},{12,14},{13,9},{14,10},{15,13... | collective-permute-start | bytes 503816 | tf_op jit(solution)/shard_map/ppermute | solution.py:278
  7.7 7.2 %collective-permute-start.3 = (bf16[656,128]{1,0:T(8,128)(2,1)S(1)}, bf16[656,128]{1,0:T(8,128)(2,1)S(1)}, u32[]{:S(2)}, u32[]{:S(2)}) collective-permute-start(bf16[656,128]{1,0:T(8,128)(2,1)S(1)} %collective-permute-done.2.refs_4_), channel_id=1, source_target_pairs={{0,2},{1,5},{4,0},{5,9},{8,4},{9,13},{12,8},{13,15},{14,12},{15,11... | collective-permute-start | bytes 503816 | tf_op jit(solution)/shard_map/ppermute | solution.py:278
  9.7 7.6 %collective-permute-start.9 = (bf16[640,128]{1,0:T(8,128)(2,1)S(1)}, bf16[640,128]{1,0:T(8,128)(2,1)S(1)}, u32[]{:S(2)}, u32[]{:S(2)}) collective-permute-start(bf16[640,128]{1,0:T(8,128)(2,1)S(1)} %get-tuple-element.17.refs_3_), channel_id=1, source_target_pairs={{0,4},{1,3},{4,8},{5,1},{8,12},{9,5},{12,14},{13,9},{14,10},{15,13... | collective-permute-start | bytes 491528 | tf_op jit(solution)/shard_map/ppermute | solution.py:278
  9.8 8.7 %collective-permute-start.6 = (bf16[640,128]{1,0:T(8,128)(2,1)S(1)}, bf16[640,128]{1,0:T(8,128)(2,1)S(1)}, u32[]{:S(2)}, u32[]{:S(2)}) collective-permute-start(bf16[640,128]{1,0:T(8,128)(2,1)S(1)} %collective-permute-done.5.refs_5_), channel_id=1, source_target_pairs={{0,2},{1,5},{4,0},{5,9},{8,4},{9,13},{12,8},{13,15},{14,12},{15,11... | collective-permute-start | bytes 491528 | tf_op jit(solution)/shard_map/ppermute | solution.py:278
  13.8 7.2 %collective-permute-start.10 = (bf16[656,128]{1,0:T(8,128)(2,1)S(1)}, bf16[656,128]{1,0:T(8,128)(2,1)S(1)}, u32[]{:S(2)}, u32[]{:S(2)}) collective-permute-start(bf16[656,128]{1,0:T(8,128)(2,1)S(1)} %collective-permute-done.8.refs_6_), channel_id=1, source_target_pairs={{0,4},{1,3},{4,8},{5,1},{8,12},{9,5},{12,14},{13,9},{14,10},{15,13... | collective-permute-start | bytes 503816 | tf_op jit(solution)/shard_map/ppermute | solution.py:278
  14.9 7.2 %collective-permute-start.4 = (bf16[656,128]{1,0:T(8,128)(2,1)S(1)}, bf16[656,128]{1,0:T(8,128)(2,1)S(1)}, u32[]{:S(2)}, u32[]{:S(2)}) collective-permute-start(bf16[656,128]{1,0:T(8,128)(2,1)S(1)} %collective-permute-done.3.refs_8_), channel_id=1, source_target_pairs={{0,2},{1,5},{4,0},{5,9},{8,4},{9,13},{12,8},{13,15},{14,12},{15,11... | collective-permute-start | bytes 503816 | tf_op jit(solution)/shard_map/ppermute | solution.py:278
  17.3 7.2 %collective-permute-start.11 = (bf16[640,128]{1,0:T(8,128)(2,1)S(1)}, bf16[640,128]{1,0:T(8,128)(2,1)S(1)}, u32[]{:S(2)}, u32[]{:S(2)}) collective-permute-start(bf16[640,128]{1,0:T(8,128)(2,1)S(1)} %collective-permute-done.9.refs_7_), channel_id=1, source_target_pairs={{0,4},{1,3},{4,8},{5,1},{8,12},{9,5},{12,14},{13,9},{14,10},{15,13... | collective-permute-start | bytes 491528 | tf_op jit(solution)/shard_map/ppermute | solution.py:278
  18.5 7.2 %collective-permute-start.7 = (bf16[640,128]{1,0:T(8,128)(2,1)S(1)}, bf16[640,128]{1,0:T(8,128)(2,1)S(1)}, u32[]{:S(2)}, u32[]{:S(2)}) collective-permute-start(bf16[640,128]{1,0:T(8,128)(2,1)S(1)} %collective-permute-done.6.refs_9_), channel_id=1, source_target_pairs={{0,2},{1,5},{4,0},{5,9},{8,4},{9,13},{12,8},{13,15},{14,12},{15,11... | collective-permute-start | bytes 491528 | tf_op jit(solution)/shard_map/ppermute | solution.py:278
  21.0 10.7 %collective-permute-start.12 = (bf16[656,128]{1,0:T(8,128)(2,1)S(1)}, bf16[656,128]{1,0:T(8,128)(2,1)S(1)}, u32[]{:S(2)}, u32[]{:S(2)}) collective-permute-start(bf16[656,128]{1,0:T(8,128)(2,1)S(1)} %collective-permute-done.10.refs_10_), channel_id=1, source_target_pairs={{0,4},{1,3},{4,8},{5,1},{8,12},{9,5},{12,14},{13,9},{14,10},{15,13... | collective-permute-start | bytes 503816 | tf_op jit(solution)/shard_map/ppermute | solution.py:278
  22.2 9.6 %collective-permute-start.14 = (bf16[656,128]{1,0:T(8,128)(2,1)S(1)}, bf16[656,128]{1,0:T(8,128)(2,1)S(1)}, u32[]{:S(2)}, u32[]{:S(2)}) collective-permute-start(bf16[656,128]{1,0:T(8,128)(2,1)S(1)} %collective-permute-done.4.refs_0_), channel_id=1, source_target_pairs={{0,2},{1,5},{4,0},{5,9},{8,4},{9,13},{12,8},{13,15},{14,12},{15,11... | collective-permute-start | bytes 503816 | tf_op jit(solution)/shard_map/ppermute | solution.py:278
  24.5 7.2 %collective-permute-start.13 = (bf16[640,128]{1,0:T(8,128)(2,1)S(1)}, bf16[640,128]{1,0:T(8,128)(2,1)S(1)}, u32[]{:S(2)}, u32[]{:S(2)}) collective-permute-start(bf16[640,128]{1,0:T(8,128)(2,1)S(1)} %collective-permute-done.11.refs_11_), channel_id=1, source_target_pairs={{0,4},{1,3},{4,8},{5,1},{8,12},{9,5},{12,14},{13,9},{14,10},{15,13... | collective-permute-start | bytes 491528 | tf_op jit(solution)/shard_map/ppermute | solution.py:278
  25.7 6.1 %collective-permute-start.15 = (bf16[640,128]{1,0:T(8,128)(2,1)S(1)}, bf16[640,128]{1,0:T(8,128)(2,1)S(1)}, u32[]{:S(2)}, u32[]{:S(2)}) collective-permute-start(bf16[640,128]{1,0:T(8,128)(2,1)S(1)} %collective-permute-done.7.refs_1_), channel_id=1, source_target_pairs={{0,2},{1,5},{4,0},{5,9},{8,4},{9,13},{12,8},{13,15},{14,12},{15,11... | collective-permute-start | bytes 491528 | tf_op jit(solution)/shard_map/ppermute | solution.py:278

commit v20 on v19

--- a/solution.py
+++ b/solution.py
@@ -278,9 +278,12 @@
             held[way] = [lax.ppermute(part, ("row", "col"), ring(way)) for part in sent]
         rounds.append([(way, step, held[way], 0) for way in ways])
     *_, late, last = rounds
-    total = product(order, sum(rounds[:-2], late[:1]), a, total, total_shape)
+    total = product(order, rounds[0] + rounds[1], a, total, total_shape)
+    early, late = sum(rounds[2:-2], late[:1]), late[1:] + last
+    early += [(*what, refs[:1], 0) for *what, refs, _ in late]
+    total = product(order, early, a, total, total_shape)
     out = jax.ShapeDtypeStruct(a_vals.shape, a_vals.dtype)
-    return product(order, late[1:] + last, a, total, out, cols)
+    return product(order, [(*what, refs, 1) for *what, refs, _ in late], a, total, out, cols)
 
 
 def ring_order(mesh):

time: 34.5 us -> 34.6 us (level)
  Pallas kernels: 8.85 us -> 9.84 us
  waiting for transfers between devices: 5.52 us -> 4.6 us
    pallas_call x2 -> x3, Pallas kernels: 5.74 us -> 6.73 us  [product(): pl.pallas_call(functools.partial(kernel, sources), out_shape=out, in_spec...]
    ppermute x14, waiting for transfers between devices: 4.37 us -> 3.44 us  [local(): held[way] = [lax.ppermute(part, ('row', 'col'), ring(way)) for part in sent]]
  transfers between devices with their start and end apart: 16 -> 16, of which waited for: 11 -> 10; matrix products, arithmetic and copies ran while one was open for 0% -> 0% of each run, Pallas kernels for 15% -> 18%
where the time goes in v20:
time: 34.6 us; the launch traced here: 34.4 us
  starting transfers between devices  19.9 us (58%)
  Pallas kernels  9.84 us (28%)
  waiting for transfers between devices  4.6 us (13%)
    ppermute x14, starting transfers between devices, local(): held[way] = [lax.ppermute(part, ('row', 'col'), ring(way)) for part in sent]  19.9 us
    pallas_call x3, Pallas kernels, product(): pl.pallas_call(functools.partial(kernel, sources), out_shape=out, in_spec...  6.73 us
    ppermute x14, waiting for transfers between devices, local(): held[way] = [lax.ppermute(part, ('row', 'col'), ring(way)) for part in sent]  3.44 us
    pallas_call x1, Pallas kernels, dense_rows(): pl.pallas_call(dense_kernel, out_shape=jax.ShapeDtypeStruct((sources, row...  1.82 us
    pallas_call x1, Pallas kernels, pack(): pl.pallas_call(functools.partial(pack_kernel, half), out_shape=[jax.Shape...  1.29 us
    ppermute x2, waiting for transfers between devices, local(): a_other, others = (lax.ppermute(x, 'col', swap) for x in mine)  1.16 us
  transfers between devices with their start and end apart: 16, of which 10 were waited for; matrix products, arithmetic and copies ran while one was open for 0% of the time, Pallas kernels for 18%

profile of v20, /device:TPU:0, one launch (start us, length us, event | category | flops | bytes accessed | tf_op | source)
XLA Modules:
  0.0 34.4 jit_solution(12460988585487736788)
XLA Ops:
  0.0 0.0 copy-start
  0.0 1.3 %shard_map.37 = (bf16[656,128]{1,0:T(8,128)(2,1)S(1)}, bf16[640,128]{1,0:T(8,128)(2,1)S(1)}) custom-call(s32[4,10]{1,0:T(4,128)} %cols_hbm.3, bf16[4,10,64,64]{3,2,1,0:T(8,128)(2,1)} %b_hbm.1), custom_call_target="tpu_custom_call" | custom-call | bytes 655360 | tf_op jit(solution)/shard_map/pallas_call | solution.py:58
  1.3 0.0 copy-start.1
  1.3 3.0 %collective-permute-start.2 = (bf16[656,128]{1,0:T(8,128)(2,1)S(1)}, bf16[656,128]{1,0:T(8,128)(2,1)S(1)}, u32[]{:S(2)}, u32[]{:S(2)}) collective-permute-start(bf16[656,128]{1,0:T(8,128)(2,1)S(1)} %get-tuple-element.16.refs_0_), channel_id=1, source_target_pairs={{0,2},{1,5},{4,0},{5,9},{8,4},{9,13},{12,8},{13,15},{14,12},{15,11... | collective-permute-start | bytes 503816 | tf_op jit(solution)/shard_map/ppermute | solution.py:278
  4.3 0.0 copy-done
  4.3 0.0 collective-permute-start.1
  4.3 1.6 %collective-permute-start.3 = (bf16[640,128]{1,0:T(8,128)(2,1)S(1)}, bf16[640,128]{1,0:T(8,128)(2,1)S(1)}, u32[]{:S(2)}, u32[]{:S(2)}) collective-permute-start(bf16[640,128]{1,0:T(8,128)(2,1)S(1)} %get-tuple-element.17.refs_1_), channel_id=1, source_target_pairs={{0,2},{1,5},{4,0},{5,9},{8,4},{9,13},{12,8},{13,15},{14,12},{15,11... | collective-permute-start | bytes 491528 | tf_op jit(solution)/shard_map/ppermute | solution.py:278
  5.9 0.0 copy-done.1
  5.9 0.0 collective-permute-start
  5.9 1.2 %collective-permute-done.others_ref = s32[4,10]{1,0:T(4,128)S(1)} collective-permute-done((s32[4,10]{1,0:T(4,128)S(1)}, s32[4,10]{1,0:T(4,128)S(1)}, u32[]{:S(2)}, u32[]{:S(2)}) %collective-permute-start) | collective-permute-done | bytes 192 | tf_op jit(solution)/shard_map/ppermute | solution.py:261
  7.1 0.6 %collective-permute-start.4 = (bf16[656,128]{1,0:T(8,128)(2,1)S(1)}, bf16[656,128]{1,0:T(8,128)(2,1)S(1)}, u32[]{:S(2)}, u32[]{:S(2)}) collective-permute-start(bf16[656,128]{1,0:T(8,128)(2,1)S(1)} %get-tuple-element.16.refs_0_), channel_id=1, source_target_pairs={{0,4},{1,3},{4,8},{5,1},{8,12},{9,5},{12,14},{13,9},{14,10},{15,13... | collective-permute-start | bytes 503816 | tf_op jit(solution)/shard_map/ppermute | solution.py:278
  7.6 0.1 collective-permute-done.2.refs_2_
  7.7 2.0 %collective-permute-start.6 = (bf16[656,128]{1,0:T(8,128)(2,1)S(1)}, bf16[656,128]{1,0:T(8,128)(2,1)S(1)}, u32[]{:S(2)}, u32[]{:S(2)}) collective-permute-start(bf16[656,128]{1,0:T(8,128)(2,1)S(1)} %collective-permute-done.2.refs_2_), channel_id=1, source_target_pairs={{0,2},{1,5},{4,0},{5,9},{8,4},{9,13},{12,8},{13,15},{14,12},{15,11... | collective-permute-start | bytes 503816 | tf_op jit(solution)/shard_map/ppermute | solution.py:278
  9.7 0.1 collective-permute-start.5
  9.8 0.0 collective-permute-done.3.refs_3_
  9.8 2.0 %collective-permute-start.8 = (bf16[640,128]{1,0:T(8,128)(2,1)S(1)}, bf16[640,128]{1,0:T(8,128)(2,1)S(1)}, u32[]{:S(2)}, u32[]{:S(2)}) collective-permute-start(bf16[640,128]{1,0:T(8,128)(2,1)S(1)} %collective-permute-done.3.refs_3_), channel_id=1, source_target_pairs={{0,2},{1,5},{4,0},{5,9},{8,4},{9,13},{12,8},{13,15},{14,12},{15,11... | collective-permute-start | bytes 491528 | tf_op jit(solution)/shard_map/ppermute | solution.py:278
  11.7 0.0 collective-permute-done.1.other_ref
  11.7 1.8 %shard_map.38.a_ref = bf16[8,2,256,128]{3,2,1,0:T(8,128)(2,1)S(1)} custom-call(s32[4,10]{1,0:T(4,128)S(1)} %copy-done.1, s32[4,10]{1,0:T(4,128)S(1)} %collective-permute-done.others_ref, bf16[4,10,64,64]{3,2,1,0:T(8,128)(2,1)S(1)} %copy-done, bf16[4,10,64,64]{3,2,1,0:T(8,128)(2,1)S(1)} %collective-permute-done.1.other_ref), custom_call_target="tpu_custom_call" | custom-call | bytes 1310720 | tf_op jit(solution)/shard_map/pallas_call | solution.py:104
  13.6 0.2 collective-permute-done.4.refs_4_
  13.8 0.7 %collective-permute-start.10 = (bf16[656,128]{1,0:T(8,128)(2,1)S(1)}, bf16[656,128]{1,0:T(8,128)(2,1)S(1)}, u32[]{:S(2)}, u32[]{:S(2)}) collective-permute-start(bf16[656,128]{1,0:T(8,128)(2,1)S(1)} %collective-permute-done.4.refs_4_), channel_id=1, source_target_pairs={{0,4},{1,3},{4,8},{5,1},{8,12},{9,5},{12,14},{13,9},{14,10},{15,13... | collective-permute-start | bytes 503816 | tf_op jit(solution)/shard_map/ppermute | solution.py:278
  14.5 0.4 %collective-permute-done.6.refs_2_ = bf16[656,128]{1,0:T(8,128)(2,1)S(1)} collective-permute-done((bf16[656,128]{1,0:T(8,128)(2,1)S(1)}, bf16[656,128]{1,0:T(8,128)(2,1)S(1)}, u32[]{:S(2)}, u32[]{:S(2)}) %collective-permute-start.6) | collective-permute-done | bytes 167968 | tf_op jit(solution)/shard_map/ppermute | solution.py:278
  14.9 2.0 %collective-permute-start.7 = (bf16[656,128]{1,0:T(8,128)(2,1)S(1)}, bf16[656,128]{1,0:T(8,128)(2,1)S(1)}, u32[]{:S(2)}, u32[]{:S(2)}) collective-permute-start(bf16[656,128]{1,0:T(8,128)(2,1)S(1)} %collective-permute-done.6.refs_2_), channel_id=1, source_target_pairs={{0,2},{1,5},{4,0},{5,9},{8,4},{9,13},{12,8},{13,15},{14,12},{15,11... | collective-permute-start | bytes 503816 | tf_op jit(solution)/shard_map/ppermute | solution.py:278
  16.9 0.4 %collective-permute-done.5.refs_5_ = bf16[640,128]{1,0:T(8,128)(2,1)S(1)} collective-permute-done((bf16[640,128]{1,0:T(8,128)(2,1)S(1)}, bf16[640,128]{1,0:T(8,128)(2,1)S(1)}, u32[]{:S(2)}, u32[]{:S(2)}) %collective-permute-start.5) | collective-permute-done | bytes 163872 | tf_op jit(solution)/shard_map/ppermute | solution.py:278
  17.3 0.7 %collective-permute-start.11 = (bf16[640,128]{1,0:T(8,128)(2,1)S(1)}, bf16[640,128]{1,0:T(8,128)(2,1)S(1)}, u32[]{:S(2)}, u32[]{:S(2)}) collective-permute-start(bf16[640,128]{1,0:T(8,128)(2,1)S(1)} %collective-permute-done.5.refs_5_), channel_id=1, source_target_pairs={{0,4},{1,3},{4,8},{5,1},{8,12},{9,5},{12,14},{13,9},{14,10},{15,13... | collective-permute-start | bytes 491528 | tf_op jit(solution)/shard_map/ppermute | solution.py:278
  18.0 0.4 %collective-permute-done.8.refs_3_ = bf16[640,128]{1,0:T(8,128)(2,1)S(1)} collective-permute-done((bf16[640,128]{1,0:T(8,128)(2,1)S(1)}, bf16[640,128]{1,0:T(8,128)(2,1)S(1)}, u32[]{:S(2)}, u32[]{:S(2)}) %collective-permute-start.8) | collective-permute-done | bytes 163872 | tf_op jit(solution)/shard_map/ppermute | solution.py:278
  18.5 2.0 %collective-permute-start.9 = (bf16[640,128]{1,0:T(8,128)(2,1)S(1)}, bf16[640,128]{1,0:T(8,128)(2,1)S(1)}, u32[]{:S(2)}, u32[]{:S(2)}) collective-permute-start(bf16[640,128]{1,0:T(8,128)(2,1)S(1)} %collective-permute-done.8.refs_3_), channel_id=1, source_target_pairs={{0,2},{1,5},{4,0},{5,9},{8,4},{9,13},{12,8},{13,15},{14,12},{15,11... | collective-permute-start | bytes 491528 | tf_op jit(solution)/shard_map/ppermute | solution.py:278
  20.4 0.6 %collective-permute-done.10.refs_4_ = bf16[656,128]{1,0:T(8,128)(2,1)S(1)} collective-permute-done((bf16[656,128]{1,0:T(8,128)(2,1)S(1)}, bf16[656,128]{1,0:T(8,128)(2,1)S(1)}, u32[]{:S(2)}, u32[]{:S(2)}) %collective-permute-start.10) | collective-permute-done | bytes 167968 | tf_op jit(solution)/shard_map/ppermute | solution.py:278
  21.0 0.7 %collective-permute-start.12 = (bf16[656,128]{1,0:T(8,128)(2,1)S(1)}, bf16[656,128]{1,0:T(8,128)(2,1)S(1)}, u32[]{:S(2)}, u32[]{:S(2)}) collective-permute-start(bf16[656,128]{1,0:T(8,128)(2,1)S(1)} %collective-permute-done.10.refs_4_), channel_id=1, source_target_pairs={{0,4},{1,3},{4,8},{5,1},{8,12},{9,5},{12,14},{13,9},{14,10},{15,13... | collective-permute-start | bytes 503816 | tf_op jit(solution)/shard_map/ppermute | solution.py:278
  21.7 0.4 %collective-permute-done.7.refs_0_ = bf16[656,128]{1,0:T(8,128)(2,1)S(1)} collective-permute-done((bf16[656,128]{1,0:T(8,128)(2,1)S(1)}, bf16[656,128]{1,0:T(8,128)(2,1)S(1)}, u32[]{:S(2)}, u32[]{:S(2)}) %collective-permute-start.7) | collective-permute-done | bytes 167968 | tf_op jit(solution)/shard_map/ppermute | solution.py:278
  22.2 2.0 %collective-permute-start.13 = (bf16[656,128]{1,0:T(8,128)(2,1)S(1)}, bf16[656,128]{1,0:T(8,128)(2,1)S(1)}, u32[]{:S(2)}, u32[]{:S(2)}) collective-permute-start(bf16[656,128]{1,0:T(8,128)(2,1)S(1)} %collective-permute-done.7.refs_0_), channel_id=1, source_target_pairs={{0,2},{1,5},{4,0},{5,9},{8,4},{9,13},{12,8},{13,15},{14,12},{15,11... | collective-permute-start | bytes 503816 | tf_op jit(solution)/shard_map/ppermute | solution.py:278
  24.1 0.4 %collective-permute-done.11.refs_5_ = bf16[640,128]{1,0:T(8,128)(2,1)S(1)} collective-permute-done((bf16[640,128]{1,0:T(8,128)(2,1)S(1)}, bf16[640,128]{1,0:T(8,128)(2,1)S(1)}, u32[]{:S(2)}, u32[]{:S(2)}) %collective-permute-start.11) | collective-permute-done | bytes 163872 | tf_op jit(solution)/shard_map/ppermute | solution.py:278
  24.5 0.7 %collective-permute-start.14 = (bf16[640,128]{1,0:T(8,128)(2,1)S(1)}, bf16[640,128]{1,0:T(8,128)(2,1)S(1)}, u32[]{:S(2)}, u32[]{:S(2)}) collective-permute-start(bf16[640,128]{1,0:T(8,128)(2,1)S(1)} %collective-permute-done.11.refs_5_), channel_id=1, source_target_pairs={{0,4},{1,3},{4,8},{5,1},{8,12},{9,5},{12,14},{13,9},{14,10},{15,13... | collective-permute-start | bytes 491528 | tf_op jit(solution)/shard_map/ppermute | solution.py:278
  25.3 0.4 %collective-permute-done.9.refs_1_ = bf16[640,128]{1,0:T(8,128)(2,1)S(1)} collective-permute-done((bf16[640,128]{1,0:T(8,128)(2,1)S(1)}, bf16[640,128]{1,0:T(8,128)(2,1)S(1)}, u32[]{:S(2)}, u32[]{:S(2)}) %collective-permute-start.9) | collective-permute-done | bytes 163872 | tf_op jit(solution)/shard_map/ppermute | solution.py:278
  25.7 2.0 %collective-permute-start.15 = (bf16[640,128]{1,0:T(8,128)(2,1)S(1)}, bf16[640,128]{1,0:T(8,128)(2,1)S(1)}, u32[]{:S(2)}, u32[]{:S(2)}) collective-permute-start(bf16[640,128]{1,0:T(8,128)(2,1)S(1)} %collective-permute-done.9.refs_1_), channel_id=1, source_target_pairs={{0,2},{1,5},{4,0},{5,9},{8,4},{9,13},{12,8},{13,15},{14,12},{15,11... | collective-permute-start | bytes 491528 | tf_op jit(solution)/shard_map/ppermute | solution.py:278
  27.7 1.9 %shard_map.39.before = f32[4,2,256,128]{3,2,1,0:T(8,128)S(1)} custom-call(bf16[8,2,256,128]{3,2,1,0:T(8,128)(2,1)S(1)} %shard_map.38.a_ref, bf16[656,128]{1,0:T(8,128)(2,1)S(1)} %get-tuple-element.16.refs_0_, bf16[640,128]{1,0:T(8,128)(2,1)S(1)} %get-tuple-element.17.refs_1_, bf16[656,128]{1,0:T(8,128)(2,1)S(1)} %collective-permute-done.2.refs_2_, ...), custom_call_target="tpu_custom_call" | custom-call | flops 402653184 | tf_op jit(solution)/shard_map/pallas_call | solution.py:233
  29.6 0.0 collective-permute-done.12.refs_6_.refs_0_
  29.6 0.0 collective-permute-done.13.refs_7_.refs_2_
  29.6 2.5 %shard_map.40.total = f32[4,2,256,128]{3,2,1,0:T(8,128)S(1)} custom-call(bf16[8,2,256,128]{3,2,1,0:T(8,128)(2,1)S(1)} %shard_map.38.a_ref, f32[4,2,256,128]{3,2,1,0:T(8,128)S(1)} %shard_map.39.before, bf16[656,128]{1,0:T(8,128)(2,1)S(1)} %collective-permute-done.7.refs_0_, ...), custom_call_target="tpu_custom_call", output_to_operand_aliasing={{}: (1, {})} | custom-call | flops 671088640 | tf_op jit(solution)/shard_map/pallas_call | solution.py:233
  32.1 0.0 collective-permute-done.14.refs_1_
  32.1 0.0 collective-permute-done.15.refs_3_
  32.1 2.3 %shard_map.41 = bf16[4,10,64,64]{3,2,1,0:T(8,128)(2,1)} custom-call(bf16[8,2,256,128]{3,2,1,0:T(8,128)(2,1)S(1)} %shard_map.38.a_ref, f32[4,2,256,128]{3,2,1,0:T(8,128)S(1)} %shard_map.40.total, s32[4,10]{1,0:T(4,128)S(1)} %copy-done.1, bf16[656,128]{1,0:T(8,128)(2,1)S(1)} %collective-permute-done.12.refs_6_.refs_0_, ...), custom_call_target="tpu_custom_call" | custom-call | flops 167772160 | tf_op jit(solution)/shard_map/pallas_call | solution.py:233
Async XLA Ops:
  0.0 4.3 %copy-start = (bf16[4,10,64,64]{3,2,1,0:T(8,128)(2,1)S(1)}, bf16[4,10,64,64]{3,2,1,0:T(8,128)(2,1)}, u32[]{:S(2)}) copy-start(bf16[4,10,64,64]{3,2,1,0:T(8,128)(2,1)} %own_ref.1) | copy-start | bytes 983044
  1.3 4.6 %copy-start.1 = (s32[4,10]{1,0:T(4,128)S(1)}, s32[4,10]{1,0:T(4,128)}, u32[]{:S(2)}) copy-start(s32[4,10]{1,0:T(4,128)} %cols_hbm.3) | copy-start | bytes 484
  1.3 6.4 %collective-permute-start.2 = (bf16[656,128]{1,0:T(8,128)(2,1)S(1)}, bf16[656,128]{1,0:T(8,128)(2,1)S(1)}, u32[]{:S(2)}, u32[]{:S(2)}) collective-permute-start(bf16[656,128]{1,0:T(8,128)(2,1)S(1)} %get-tuple-element.16.refs_0_), channel_id=1, source_target_pairs={{0,2},{1,5},{4,0},{5,9},{8,4},{9,13},{12,8},{13,15},{14,12},{15,11... | collective-permute-start | bytes 503816 | tf_op jit(solution)/shard_map/ppermute | solution.py:278
  4.3 7.4 %collective-permute-start.1 = (bf16[4,10,64,64]{3,2,1,0:T(8,128)(2,1)S(1)}, bf16[4,10,64,64]{3,2,1,0:T(8,128)(2,1)S(1)}, u32[]{:S(2)}, u32[]{:S(2)}) collective-permute-start(bf16[4,10,64,64]{3,2,1,0:T(8,128)(2,1)S(1)} %copy-done), channel_id=1, source_target_pairs={{0,1},{1,0},{2,3},{3,2},{4,5},{5,4},{6,7},{7,6},{8,9},{9,8},{10,11... | collective-permute-start | bytes 983048 | tf_op jit(solution)/shard_map/ppermute | solution.py:261
  4.3 5.4 %collective-permute-start.3 = (bf16[640,128]{1,0:T(8,128)(2,1)S(1)}, bf16[640,128]{1,0:T(8,128)(2,1)S(1)}, u32[]{:S(2)}, u32[]{:S(2)}) collective-permute-start(bf16[640,128]{1,0:T(8,128)(2,1)S(1)} %get-tuple-element.17.refs_1_), channel_id=1, source_target_pairs={{0,2},{1,5},{4,0},{5,9},{8,4},{9,13},{12,8},{13,15},{14,12},{15,11... | collective-permute-start | bytes 491528 | tf_op jit(solution)/shard_map/ppermute | solution.py:278
  5.9 1.2 %collective-permute-start = (s32[4,10]{1,0:T(4,128)S(1)}, s32[4,10]{1,0:T(4,128)S(1)}, u32[]{:S(2)}, u32[]{:S(2)}) collective-permute-start(s32[4,10]{1,0:T(4,128)S(1)} %copy-done.1), channel_id=1, source_target_pairs={{0,1},{1,0},{2,3},{3,2},{4,5},{5,4},{6,7},{7,6},{8,9},{9,8},{10,11... | collective-permute-start | bytes 488 | tf_op jit(solution)/shard_map/ppermute | solution.py:261
  7.1 6.7 %collective-permute-start.4 = (bf16[656,128]{1,0:T(8,128)(2,1)S(1)}, bf16[656,128]{1,0:T(8,128)(2,1)S(1)}, u32[]{:S(2)}, u32[]{:S(2)}) collective-permute-start(bf16[656,128]{1,0:T(8,128)(2,1)S(1)} %get-tuple-element.16.refs_0_), channel_id=1, source_target_pairs={{0,4},{1,3},{4,8},{5,1},{8,12},{9,5},{12,14},{13,9},{14,10},{15,13... | collective-permute-start | bytes 503816 | tf_op jit(solution)/shard_map/ppermute | solution.py:278
  7.7 7.2 %collective-permute-start.6 = (bf16[656,128]{1,0:T(8,128)(2,1)S(1)}, bf16[656,128]{1,0:T(8,128)(2,1)S(1)}, u32[]{:S(2)}, u32[]{:S(2)}) collective-permute-start(bf16[656,128]{1,0:T(8,128)(2,1)S(1)} %collective-permute-done.2.refs_2_), channel_id=1, source_target_pairs={{0,2},{1,5},{4,0},{5,9},{8,4},{9,13},{12,8},{13,15},{14,12},{15,11... | collective-permute-start | bytes 503816 | tf_op jit(solution)/shard_map/ppermute | solution.py:278
  9.7 7.6 %collective-permute-start.5 = (bf16[640,128]{1,0:T(8,128)(2,1)S(1)}, bf16[640,128]{1,0:T(8,128)(2,1)S(1)}, u32[]{:S(2)}, u32[]{:S(2)}) collective-permute-start(bf16[640,128]{1,0:T(8,128)(2,1)S(1)} %get-tuple-element.17.refs_1_), channel_id=1, source_target_pairs={{0,4},{1,3},{4,8},{5,1},{8,12},{9,5},{12,14},{13,9},{14,10},{15,13... | collective-permute-start | bytes 491528 | tf_op jit(solution)/shard_map/ppermute | solution.py:278
  9.8 8.7 %collective-permute-start.8 = (bf16[640,128]{1,0:T(8,128)(2,1)S(1)}, bf16[640,128]{1,0:T(8,128)(2,1)S(1)}, u32[]{:S(2)}, u32[]{:S(2)}) collective-permute-start(bf16[640,128]{1,0:T(8,128)(2,1)S(1)} %collective-permute-done.3.refs_3_), channel_id=1, source_target_pairs={{0,2},{1,5},{4,0},{5,9},{8,4},{9,13},{12,8},{13,15},{14,12},{15,11... | collective-permute-start | bytes 491528 | tf_op jit(solution)/shard_map/ppermute | solution.py:278
  13.8 7.2 %collective-permute-start.10 = (bf16[656,128]{1,0:T(8,128)(2,1)S(1)}, bf16[656,128]{1,0:T(8,128)(2,1)S(1)}, u32[]{:S(2)}, u32[]{:S(2)}) collective-permute-start(bf16[656,128]{1,0:T(8,128)(2,1)S(1)} %collective-permute-done.4.refs_4_), channel_id=1, source_target_pairs={{0,4},{1,3},{4,8},{5,1},{8,12},{9,5},{12,14},{13,9},{14,10},{15,13... | collective-permute-start | bytes 503816 | tf_op jit(solution)/shard_map/ppermute | solution.py:278
  14.9 7.2 %collective-permute-start.7 = (bf16[656,128]{1,0:T(8,128)(2,1)S(1)}, bf16[656,128]{1,0:T(8,128)(2,1)S(1)}, u32[]{:S(2)}, u32[]{:S(2)}) collective-permute-start(bf16[656,128]{1,0:T(8,128)(2,1)S(1)} %collective-permute-done.6.refs_2_), channel_id=1, source_target_pairs={{0,2},{1,5},{4,0},{5,9},{8,4},{9,13},{12,8},{13,15},{14,12},{15,11... | collective-permute-start | bytes 503816 | tf_op jit(solution)/shard_map/ppermute | solution.py:278
  17.3 7.2 %collective-permute-start.11 = (bf16[640,128]{1,0:T(8,128)(2,1)S(1)}, bf16[640,128]{1,0:T(8,128)(2,1)S(1)}, u32[]{:S(2)}, u32[]{:S(2)}) collective-permute-start(bf16[640,128]{1,0:T(8,128)(2,1)S(1)} %collective-permute-done.5.refs_5_), channel_id=1, source_target_pairs={{0,4},{1,3},{4,8},{5,1},{8,12},{9,5},{12,14},{13,9},{14,10},{15,13... | collective-permute-start | bytes 491528 | tf_op jit(solution)/shard_map/ppermute | solution.py:278
  18.5 7.2 %collective-permute-start.9 = (bf16[640,128]{1,0:T(8,128)(2,1)S(1)}, bf16[640,128]{1,0:T(8,128)(2,1)S(1)}, u32[]{:S(2)}, u32[]{:S(2)}) collective-permute-start(bf16[640,128]{1,0:T(8,128)(2,1)S(1)} %collective-permute-done.8.refs_3_), channel_id=1, source_target_pairs={{0,2},{1,5},{4,0},{5,9},{8,4},{9,13},{12,8},{13,15},{14,12},{15,11... | collective-permute-start | bytes 491528 | tf_op jit(solution)/shard_map/ppermute | solution.py:278
  21.0 8.5 %collective-permute-start.12 = (bf16[656,128]{1,0:T(8,128)(2,1)S(1)}, bf16[656,128]{1,0:T(8,128)(2,1)S(1)}, u32[]{:S(2)}, u32[]{:S(2)}) collective-permute-start(bf16[656,128]{1,0:T(8,128)(2,1)S(1)} %collective-permute-done.10.refs_4_), channel_id=1, source_target_pairs={{0,4},{1,3},{4,8},{5,1},{8,12},{9,5},{12,14},{13,9},{14,10},{15,13... | collective-permute-start | bytes 503816 | tf_op jit(solution)/shard_map/ppermute | solution.py:278
  22.2 7.4 %collective-permute-start.13 = (bf16[656,128]{1,0:T(8,128)(2,1)S(1)}, bf16[656,128]{1,0:T(8,128)(2,1)S(1)}, u32[]{:S(2)}, u32[]{:S(2)}) collective-permute-start(bf16[656,128]{1,0:T(8,128)(2,1)S(1)} %collective-permute-done.7.refs_0_), channel_id=1, source_target_pairs={{0,2},{1,5},{4,0},{5,9},{8,4},{9,13},{12,8},{13,15},{14,12},{15,11... | collective-permute-start | bytes 503816 | tf_op jit(solution)/shard_map/ppermute | solution.py:278
  24.5 7.6 %collective-permute-start.14 = (bf16[640,128]{1,0:T(8,128)(2,1)S(1)}, bf16[640,128]{1,0:T(8,128)(2,1)S(1)}, u32[]{:S(2)}, u32[]{:S(2)}) collective-permute-start(bf16[640,128]{1,0:T(8,128)(2,1)S(1)} %collective-permute-done.11.refs_5_), channel_id=1, source_target_pairs={{0,4},{1,3},{4,8},{5,1},{8,12},{9,5},{12,14},{13,9},{14,10},{15,13... | collective-permute-start | bytes 491528 | tf_op jit(solution)/shard_map/ppermute | solution.py:278
  25.7 6.4 %collective-permute-start.15 = (bf16[640,128]{1,0:T(8,128)(2,1)S(1)}, bf16[640,128]{1,0:T(8,128)(2,1)S(1)}, u32[]{:S(2)}, u32[]{:S(2)}) collective-permute-start(bf16[640,128]{1,0:T(8,128)(2,1)S(1)} %collective-permute-done.9.refs_1_), channel_id=1, source_target_pairs={{0,2},{1,5},{4,0},{5,9},{8,4},{9,13},{12,8},{13,15},{14,12},{15,11... | collective-permute-start | bytes 491528 | tf_op jit(solution)/shard_map/ppermute | solution.py:278

commit v21 on v17

--- a/solution.py
+++ b/solution.py
@@ -11,7 +11,7 @@
 VMEM = pltpu.VMEM
 SMEM = pltpu.SMEM
 LIMIT = 48 * 1024 * 1024
-STRIDE = 5
+STRIDE = 10
 FOOT = 16
 
 

time: 34.4 us -> 34.4 us (level)
  no operation moved by 1% of the time
where the time goes in v21:
time: 34.4 us; the launch traced here: 34.3 us
  starting transfers between devices  19.2 us (56%)
  Pallas kernels  10.6 us (31%)
  waiting for transfers between devices  4.44 us (13%)
    ppermute x14, starting transfers between devices, local(): held[way] = [lax.ppermute(part, ('row', 'col'), ring(way)) for part in sent]  19.1 us
    pallas_call x4, Pallas kernels, product(): pl.pallas_call(functools.partial(kernel, sources), out_shape=out, in_spec...  7.47 us
    ppermute x14, waiting for transfers between devices, local(): held[way] = [lax.ppermute(part, ('row', 'col'), ring(way)) for part in sent]  3.28 us
    pallas_call x1, Pallas kernels, dense_rows(): pl.pallas_call(dense_kernel, out_shape=jax.ShapeDtypeStruct((sources, row...  1.82 us
    pallas_call x1, Pallas kernels, pack(): pl.pallas_call(functools.partial(pack_kernel, half), out_shape=[jax.Shape...  1.29 us
    ppermute x2, waiting for transfers between devices, local(): a_other, others = (lax.ppermute(x, 'col', swap) for x in mine)  1.16 us
  transfers between devices with their start and end apart: 16, of which 10 were waited for; matrix products, arithmetic and copies ran while one was open for 0% of the time, Pallas kernels for 20%

profile of v21, /device:TPU:0, one launch (start us, length us, event | category | flops | bytes accessed | tf_op | source)
XLA Modules:
  0.0 34.3 jit_solution(7901381024510259537)
XLA Ops:
  0.0 0.0 copy-start
  0.0 1.3 %shard_map.37 = (bf16[656,128]{1,0:T(8,128)(2,1)S(1)}, bf16[640,128]{1,0:T(8,128)(2,1)S(1)}) custom-call(s32[4,10]{1,0:T(4,128)} %cols_hbm.3, bf16[4,10,64,64]{3,2,1,0:T(8,128)(2,1)} %b_hbm.1), custom_call_target="tpu_custom_call" | custom-call | bytes 655360 | tf_op jit(solution)/shard_map/pallas_call | solution.py:58
  1.3 0.0 copy-start.1
  1.3 3.0 %collective-permute-start.4 = (bf16[656,128]{1,0:T(8,128)(2,1)S(1)}, bf16[656,128]{1,0:T(8,128)(2,1)S(1)}, u32[]{:S(2)}, u32[]{:S(2)}) collective-permute-start(bf16[656,128]{1,0:T(8,128)(2,1)S(1)} %get-tuple-element.17.refs_0_), channel_id=1, source_target_pairs={{0,2},{1,5},{4,0},{5,9},{8,4},{9,13},{12,8},{13,15},{14,12},{15,11... | collective-permute-start | bytes 503816 | tf_op jit(solution)/shard_map/ppermute | solution.py:278
  4.3 0.0 copy-done
  4.3 0.0 collective-permute-start.1
  4.3 1.6 %collective-permute-start.7 = (bf16[640,128]{1,0:T(8,128)(2,1)S(1)}, bf16[640,128]{1,0:T(8,128)(2,1)S(1)}, u32[]{:S(2)}, u32[]{:S(2)}) collective-permute-start(bf16[640,128]{1,0:T(8,128)(2,1)S(1)} %get-tuple-element.21.refs_1_), channel_id=1, source_target_pairs={{0,2},{1,5},{4,0},{5,9},{8,4},{9,13},{12,8},{13,15},{14,12},{15,11... | collective-permute-start | bytes 491528 | tf_op jit(solution)/shard_map/ppermute | solution.py:278
  5.9 0.0 copy-done.1
  5.9 0.0 collective-permute-start
  5.9 1.2 %collective-permute-done.others_ref = s32[4,10]{1,0:T(4,128)S(1)} collective-permute-done((s32[4,10]{1,0:T(4,128)S(1)}, s32[4,10]{1,0:T(4,128)S(1)}, u32[]{:S(2)}, u32[]{:S(2)}) %collective-permute-start) | collective-permute-done | bytes 192 | tf_op jit(solution)/shard_map/ppermute | solution.py:261
  7.1 0.6 %collective-permute-start.2 = (bf16[656,128]{1,0:T(8,128)(2,1)S(1)}, bf16[656,128]{1,0:T(8,128)(2,1)S(1)}, u32[]{:S(2)}, u32[]{:S(2)}) collective-permute-start(bf16[656,128]{1,0:T(8,128)(2,1)S(1)} %get-tuple-element.17.refs_0_), channel_id=1, source_target_pairs={{0,4},{1,3},{4,8},{5,1},{8,12},{9,5},{12,14},{13,9},{14,10},{15,13... | collective-permute-start | bytes 503816 | tf_op jit(solution)/shard_map/ppermute | solution.py:278
  7.6 0.1 collective-permute-done.4.refs_2_
  7.7 2.0 %collective-permute-start.5 = (bf16[656,128]{1,0:T(8,128)(2,1)S(1)}, bf16[656,128]{1,0:T(8,128)(2,1)S(1)}, u32[]{:S(2)}, u32[]{:S(2)}) collective-permute-start(bf16[656,128]{1,0:T(8,128)(2,1)S(1)} %collective-permute-done.4.refs_2_), channel_id=1, source_target_pairs={{0,2},{1,5},{4,0},{5,9},{8,4},{9,13},{12,8},{13,15},{14,12},{15,11... | collective-permute-start | bytes 503816 | tf_op jit(solution)/shard_map/ppermute | solution.py:278
  9.7 0.1 collective-permute-start.10
  9.8 0.0 collective-permute-done.7.refs_3_
  9.8 2.0 %collective-permute-start.8 = (bf16[640,128]{1,0:T(8,128)(2,1)S(1)}, bf16[640,128]{1,0:T(8,128)(2,1)S(1)}, u32[]{:S(2)}, u32[]{:S(2)}) collective-permute-start(bf16[640,128]{1,0:T(8,128)(2,1)S(1)} %collective-permute-done.7.refs_3_), channel_id=1, source_target_pairs={{0,2},{1,5},{4,0},{5,9},{8,4},{9,13},{12,8},{13,15},{14,12},{15,11... | collective-permute-start | bytes 491528 | tf_op jit(solution)/shard_map/ppermute | solution.py:278
  11.7 0.0 collective-permute-done.1.other_ref
  11.7 1.8 %shard_map.38.a_ref = bf16[8,2,256,128]{3,2,1,0:T(8,128)(2,1)S(1)} custom-call(s32[4,10]{1,0:T(4,128)S(1)} %copy-done.1, s32[4,10]{1,0:T(4,128)S(1)} %collective-permute-done.others_ref, bf16[4,10,64,64]{3,2,1,0:T(8,128)(2,1)S(1)} %copy-done, bf16[4,10,64,64]{3,2,1,0:T(8,128)(2,1)S(1)} %collective-permute-done.1.other_ref), custom_call_target="tpu_custom_call" | custom-call | bytes 1310720 | tf_op jit(solution)/shard_map/pallas_call | solution.py:104
  13.6 0.2 collective-permute-done.2.refs_4_
  13.8 0.7 %collective-permute-start.3 = (bf16[656,128]{1,0:T(8,128)(2,1)S(1)}, bf16[656,128]{1,0:T(8,128)(2,1)S(1)}, u32[]{:S(2)}, u32[]{:S(2)}) collective-permute-start(bf16[656,128]{1,0:T(8,128)(2,1)S(1)} %collective-permute-done.2.refs_4_), channel_id=1, source_target_pairs={{0,4},{1,3},{4,8},{5,1},{8,12},{9,5},{12,14},{13,9},{14,10},{15,13... | collective-permute-start | bytes 503816 | tf_op jit(solution)/shard_map/ppermute | solution.py:278
  14.5 0.4 %collective-permute-done.5.refs_6_ = bf16[656,128]{1,0:T(8,128)(2,1)S(1)} collective-permute-done((bf16[656,128]{1,0:T(8,128)(2,1)S(1)}, bf16[656,128]{1,0:T(8,128)(2,1)S(1)}, u32[]{:S(2)}, u32[]{:S(2)}) %collective-permute-start.5) | collective-permute-done | bytes 167968 | tf_op jit(solution)/shard_map/ppermute | solution.py:278
  14.9 2.0 %collective-permute-start.6 = (bf16[656,128]{1,0:T(8,128)(2,1)S(1)}, bf16[656,128]{1,0:T(8,128)(2,1)S(1)}, u32[]{:S(2)}, u32[]{:S(2)}) collective-permute-start(bf16[656,128]{1,0:T(8,128)(2,1)S(1)} %collective-permute-done.5.refs_6_), channel_id=1, source_target_pairs={{0,2},{1,5},{4,0},{5,9},{8,4},{9,13},{12,8},{13,15},{14,12},{15,11... | collective-permute-start | bytes 503816 | tf_op jit(solution)/shard_map/ppermute | solution.py:278
  16.9 0.4 %collective-permute-done.10.refs_5_ = bf16[640,128]{1,0:T(8,128)(2,1)S(1)} collective-permute-done((bf16[640,128]{1,0:T(8,128)(2,1)S(1)}, bf16[640,128]{1,0:T(8,128)(2,1)S(1)}, u32[]{:S(2)}, u32[]{:S(2)}) %collective-permute-start.10) | collective-permute-done | bytes 163872 | tf_op jit(solution)/shard_map/ppermute | solution.py:278
  17.3 0.7 %collective-permute-start.11 = (bf16[640,128]{1,0:T(8,128)(2,1)S(1)}, bf16[640,128]{1,0:T(8,128)(2,1)S(1)}, u32[]{:S(2)}, u32[]{:S(2)}) collective-permute-start(bf16[640,128]{1,0:T(8,128)(2,1)S(1)} %collective-permute-done.10.refs_5_), channel_id=1, source_target_pairs={{0,4},{1,3},{4,8},{5,1},{8,12},{9,5},{12,14},{13,9},{14,10},{15,13... | collective-permute-start | bytes 491528 | tf_op jit(solution)/shard_map/ppermute | solution.py:278
  18.0 0.4 %collective-permute-done.8.refs_7_ = bf16[640,128]{1,0:T(8,128)(2,1)S(1)} collective-permute-done((bf16[640,128]{1,0:T(8,128)(2,1)S(1)}, bf16[640,128]{1,0:T(8,128)(2,1)S(1)}, u32[]{:S(2)}, u32[]{:S(2)}) %collective-permute-start.8) | collective-permute-done | bytes 163872 | tf_op jit(solution)/shard_map/ppermute | solution.py:278
  18.5 2.0 %collective-permute-start.9 = (bf16[640,128]{1,0:T(8,128)(2,1)S(1)}, bf16[640,128]{1,0:T(8,128)(2,1)S(1)}, u32[]{:S(2)}, u32[]{:S(2)}) collective-permute-start(bf16[640,128]{1,0:T(8,128)(2,1)S(1)} %collective-permute-done.8.refs_7_), channel_id=1, source_target_pairs={{0,2},{1,5},{4,0},{5,9},{8,4},{9,13},{12,8},{13,15},{14,12},{15,11... | collective-permute-start | bytes 491528 | tf_op jit(solution)/shard_map/ppermute | solution.py:278
  20.4 1.1 %shard_map.39.before = f32[4,2,256,128]{3,2,1,0:T(8,128)S(1)} custom-call(bf16[8,2,256,128]{3,2,1,0:T(8,128)(2,1)S(1)} %shard_map.38.a_ref, bf16[656,128]{1,0:T(8,128)(2,1)S(1)} %get-tuple-element.17.refs_0_, bf16[640,128]{1,0:T(8,128)(2,1)S(1)} %get-tuple-element.21.refs_1_), custom_call_target="tpu_custom_call" | custom-call | flops 134217728 | tf_op jit(solution)/shard_map/pallas_call | solution.py:233
  21.6 0.0 collective-permute-done.3.refs_8_
  21.6 0.2 collective-permute-start.12
  21.7 0.4 %collective-permute-done.6.refs_0_ = bf16[656,128]{1,0:T(8,128)(2,1)S(1)} collective-permute-done((bf16[656,128]{1,0:T(8,128)(2,1)S(1)}, bf16[656,128]{1,0:T(8,128)(2,1)S(1)}, u32[]{:S(2)}, u32[]{:S(2)}) %collective-permute-start.6) | collective-permute-done | bytes 167968 | tf_op jit(solution)/shard_map/ppermute | solution.py:278
  22.2 1.9 %collective-permute-start.13 = (bf16[656,128]{1,0:T(8,128)(2,1)S(1)}, bf16[656,128]{1,0:T(8,128)(2,1)S(1)}, u32[]{:S(2)}, u32[]{:S(2)}) collective-permute-start(bf16[656,128]{1,0:T(8,128)(2,1)S(1)} %collective-permute-done.6.refs_0_), channel_id=1, source_target_pairs={{0,2},{1,5},{4,0},{5,9},{8,4},{9,13},{12,8},{13,15},{14,12},{15,11... | collective-permute-start | bytes 503816 | tf_op jit(solution)/shard_map/ppermute | solution.py:278
  24.0 0.5 %collective-permute-done.11.refs_9_ = bf16[640,128]{1,0:T(8,128)(2,1)S(1)} collective-permute-done((bf16[640,128]{1,0:T(8,128)(2,1)S(1)}, bf16[640,128]{1,0:T(8,128)(2,1)S(1)}, u32[]{:S(2)}, u32[]{:S(2)}) %collective-permute-start.11) | collective-permute-done | bytes 163872 | tf_op jit(solution)/shard_map/ppermute | solution.py:278
  24.5 0.7 %collective-permute-start.14 = (bf16[640,128]{1,0:T(8,128)(2,1)S(1)}, bf16[640,128]{1,0:T(8,128)(2,1)S(1)}, u32[]{:S(2)}, u32[]{:S(2)}) collective-permute-start(bf16[640,128]{1,0:T(8,128)(2,1)S(1)} %collective-permute-done.11.refs_9_), channel_id=1, source_target_pairs={{0,4},{1,3},{4,8},{5,1},{8,12},{9,5},{12,14},{13,9},{14,10},{15,13... | collective-permute-start | bytes 491528 | tf_op jit(solution)/shard_map/ppermute | solution.py:278
  25.3 0.4 %collective-permute-done.9.refs_1_ = bf16[640,128]{1,0:T(8,128)(2,1)S(1)} collective-permute-done((bf16[640,128]{1,0:T(8,128)(2,1)S(1)}, bf16[640,128]{1,0:T(8,128)(2,1)S(1)}, u32[]{:S(2)}, u32[]{:S(2)}) %collective-permute-start.9) | collective-permute-done | bytes 163872 | tf_op jit(solution)/shard_map/ppermute | solution.py:278
  25.7 1.9 %collective-permute-start.15 = (bf16[640,128]{1,0:T(8,128)(2,1)S(1)}, bf16[640,128]{1,0:T(8,128)(2,1)S(1)}, u32[]{:S(2)}, u32[]{:S(2)}) collective-permute-start(bf16[640,128]{1,0:T(8,128)(2,1)S(1)} %collective-permute-done.9.refs_1_), channel_id=1, source_target_pairs={{0,2},{1,5},{4,0},{5,9},{8,4},{9,13},{12,8},{13,15},{14,12},{15,11... | collective-permute-start | bytes 491528 | tf_op jit(solution)/shard_map/ppermute | solution.py:278
  27.6 2.8 %shard_map.40.before = f32[4,2,256,128]{3,2,1,0:T(8,128)S(1)} custom-call(bf16[8,2,256,128]{3,2,1,0:T(8,128)(2,1)S(1)} %shard_map.38.a_ref, f32[4,2,256,128]{3,2,1,0:T(8,128)S(1)} %shard_map.39.before, bf16[656,128]{1,0:T(8,128)(2,1)S(1)} %collective-permute-done.6.refs_0_, ...), custom_call_target="tpu_custom_call", output_to_operand_aliasing={{}: (1, {})} | custom-call | flops 671088640 | tf_op jit(solution)/shard_map/pallas_call | solution.py:233
  30.3 0.0 collective-permute-done.12.refs_0_
  30.3 0.0 collective-permute-done.13.refs_1_.refs_2_
  30.3 1.3 %shard_map.41.total = f32[4,2,256,128]{3,2,1,0:T(8,128)S(1)} custom-call(bf16[8,2,256,128]{3,2,1,0:T(8,128)(2,1)S(1)} %shard_map.38.a_ref, f32[4,2,256,128]{3,2,1,0:T(8,128)S(1)} %shard_map.40.before, bf16[656,128]{1,0:T(8,128)(2,1)S(1)} %collective-permute-done.12.refs_0_, ...), custom_call_target="tpu_custom_call", output_to_operand_aliasing={{}: (1, {})} | custom-call | flops 268435456 | tf_op jit(solution)/shard_map/pallas_call | solution.py:233
  31.6 0.3 collective-permute-done.14.refs_1_
  32.0 0.0 collective-permute-done.15.refs_3_
  32.0 2.3 %shard_map.42 = bf16[4,10,64,64]{3,2,1,0:T(8,128)(2,1)} custom-call(bf16[8,2,256,128]{3,2,1,0:T(8,128)(2,1)S(1)} %shard_map.38.a_ref, f32[4,2,256,128]{3,2,1,0:T(8,128)S(1)} %shard_map.41.total, s32[4,10]{1,0:T(4,128)S(1)} %copy-done.1, bf16[656,128]{1,0:T(8,128)(2,1)S(1)} %collective-permute-done.12.refs_0_, ...), custom_call_target="tpu_custom_call" | custom-call | flops 167772160 | tf_op jit(solution)/shard_map/pallas_call | solution.py:233
Async XLA Ops:
  0.0 4.3 %copy-start = (bf16[4,10,64,64]{3,2,1,0:T(8,128)(2,1)S(1)}, bf16[4,10,64,64]{3,2,1,0:T(8,128)(2,1)}, u32[]{:S(2)}) copy-start(bf16[4,10,64,64]{3,2,1,0:T(8,128)(2,1)} %own_ref.1) | copy-start | bytes 983044
  1.3 4.6 %copy-start.1 = (s32[4,10]{1,0:T(4,128)S(1)}, s32[4,10]{1,0:T(4,128)}, u32[]{:S(2)}) copy-start(s32[4,10]{1,0:T(4,128)} %cols_hbm.3) | copy-start | bytes 484
  1.3 6.4 %collective-permute-start.4 = (bf16[656,128]{1,0:T(8,128)(2,1)S(1)}, bf16[656,128]{1,0:T(8,128)(2,1)S(1)}, u32[]{:S(2)}, u32[]{:S(2)}) collective-permute-start(bf16[656,128]{1,0:T(8,128)(2,1)S(1)} %get-tuple-element.17.refs_0_), channel_id=1, source_target_pairs={{0,2},{1,5},{4,0},{5,9},{8,4},{9,13},{12,8},{13,15},{14,12},{15,11... | collective-permute-start | bytes 503816 | tf_op jit(solution)/shard_map/ppermute | solution.py:278
  4.3 7.4 %collective-permute-start.1 = (bf16[4,10,64,64]{3,2,1,0:T(8,128)(2,1)S(1)}, bf16[4,10,64,64]{3,2,1,0:T(8,128)(2,1)S(1)}, u32[]{:S(2)}, u32[]{:S(2)}) collective-permute-start(bf16[4,10,64,64]{3,2,1,0:T(8,128)(2,1)S(1)} %copy-done), channel_id=1, source_target_pairs={{0,1},{1,0},{2,3},{3,2},{4,5},{5,4},{6,7},{7,6},{8,9},{9,8},{10,11... | collective-permute-start | bytes 983048 | tf_op jit(solution)/shard_map/ppermute | solution.py:261
  4.3 5.4 %collective-permute-start.7 = (bf16[640,128]{1,0:T(8,128)(2,1)S(1)}, bf16[640,128]{1,0:T(8,128)(2,1)S(1)}, u32[]{:S(2)}, u32[]{:S(2)}) collective-permute-start(bf16[640,128]{1,0:T(8,128)(2,1)S(1)} %get-tuple-element.21.refs_1_), channel_id=1, source_target_pairs={{0,2},{1,5},{4,0},{5,9},{8,4},{9,13},{12,8},{13,15},{14,12},{15,11... | collective-permute-start | bytes 491528 | tf_op jit(solution)/shard_map/ppermute | solution.py:278
  5.9 1.2 %collective-permute-start = (s32[4,10]{1,0:T(4,128)S(1)}, s32[4,10]{1,0:T(4,128)S(1)}, u32[]{:S(2)}, u32[]{:S(2)}) collective-permute-start(s32[4,10]{1,0:T(4,128)S(1)} %copy-done.1), channel_id=1, source_target_pairs={{0,1},{1,0},{2,3},{3,2},{4,5},{5,4},{6,7},{7,6},{8,9},{9,8},{10,11... | collective-permute-start | bytes 488 | tf_op jit(solution)/shard_map/ppermute | solution.py:261
  7.1 6.7 %collective-permute-start.2 = (bf16[656,128]{1,0:T(8,128)(2,1)S(1)}, bf16[656,128]{1,0:T(8,128)(2,1)S(1)}, u32[]{:S(2)}, u32[]{:S(2)}) collective-permute-start(bf16[656,128]{1,0:T(8,128)(2,1)S(1)} %get-tuple-element.17.refs_0_), channel_id=1, source_target_pairs={{0,4},{1,3},{4,8},{5,1},{8,12},{9,5},{12,14},{13,9},{14,10},{15,13... | collective-permute-start | bytes 503816 | tf_op jit(solution)/shard_map/ppermute | solution.py:278
  7.7 7.2 %collective-permute-start.5 = (bf16[656,128]{1,0:T(8,128)(2,1)S(1)}, bf16[656,128]{1,0:T(8,128)(2,1)S(1)}, u32[]{:S(2)}, u32[]{:S(2)}) collective-permute-start(bf16[656,128]{1,0:T(8,128)(2,1)S(1)} %collective-permute-done.4.refs_2_), channel_id=1, source_target_pairs={{0,2},{1,5},{4,0},{5,9},{8,4},{9,13},{12,8},{13,15},{14,12},{15,11... | collective-permute-start | bytes 503816 | tf_op jit(solution)/shard_map/ppermute | solution.py:278
  9.7 7.6 %collective-permute-start.10 = (bf16[640,128]{1,0:T(8,128)(2,1)S(1)}, bf16[640,128]{1,0:T(8,128)(2,1)S(1)}, u32[]{:S(2)}, u32[]{:S(2)}) collective-permute-start(bf16[640,128]{1,0:T(8,128)(2,1)S(1)} %get-tuple-element.21.refs_1_), channel_id=1, source_target_pairs={{0,4},{1,3},{4,8},{5,1},{8,12},{9,5},{12,14},{13,9},{14,10},{15,13... | collective-permute-start | bytes 491528 | tf_op jit(solution)/shard_map/ppermute | solution.py:278
  9.8 8.7 %collective-permute-start.8 = (bf16[640,128]{1,0:T(8,128)(2,1)S(1)}, bf16[640,128]{1,0:T(8,128)(2,1)S(1)}, u32[]{:S(2)}, u32[]{:S(2)}) collective-permute-start(bf16[640,128]{1,0:T(8,128)(2,1)S(1)} %collective-permute-done.7.refs_3_), channel_id=1, source_target_pairs={{0,2},{1,5},{4,0},{5,9},{8,4},{9,13},{12,8},{13,15},{14,12},{15,11... | collective-permute-start | bytes 491528 | tf_op jit(solution)/shard_map/ppermute | solution.py:278
  13.8 7.8 %collective-permute-start.3 = (bf16[656,128]{1,0:T(8,128)(2,1)S(1)}, bf16[656,128]{1,0:T(8,128)(2,1)S(1)}, u32[]{:S(2)}, u32[]{:S(2)}) collective-permute-start(bf16[656,128]{1,0:T(8,128)(2,1)S(1)} %collective-permute-done.2.refs_4_), channel_id=1, source_target_pairs={{0,4},{1,3},{4,8},{5,1},{8,12},{9,5},{12,14},{13,9},{14,10},{15,13... | collective-permute-start | bytes 503816 | tf_op jit(solution)/shard_map/ppermute | solution.py:278
  14.9 7.2 %collective-permute-start.6 = (bf16[656,128]{1,0:T(8,128)(2,1)S(1)}, bf16[656,128]{1,0:T(8,128)(2,1)S(1)}, u32[]{:S(2)}, u32[]{:S(2)}) collective-permute-start(bf16[656,128]{1,0:T(8,128)(2,1)S(1)} %collective-permute-done.5.refs_6_), channel_id=1, source_target_pairs={{0,2},{1,5},{4,0},{5,9},{8,4},{9,13},{12,8},{13,15},{14,12},{15,11... | collective-permute-start | bytes 503816 | tf_op jit(solution)/shard_map/ppermute | solution.py:278
  17.3 7.2 %collective-permute-start.11 = (bf16[640,128]{1,0:T(8,128)(2,1)S(1)}, bf16[640,128]{1,0:T(8,128)(2,1)S(1)}, u32[]{:S(2)}, u32[]{:S(2)}) collective-permute-start(bf16[640,128]{1,0:T(8,128)(2,1)S(1)} %collective-permute-done.10.refs_5_), channel_id=1, source_target_pairs={{0,4},{1,3},{4,8},{5,1},{8,12},{9,5},{12,14},{13,9},{14,10},{15,13... | collective-permute-start | bytes 491528 | tf_op jit(solution)/shard_map/ppermute | solution.py:278
  18.5 7.2 %collective-permute-start.9 = (bf16[640,128]{1,0:T(8,128)(2,1)S(1)}, bf16[640,128]{1,0:T(8,128)(2,1)S(1)}, u32[]{:S(2)}, u32[]{:S(2)}) collective-permute-start(bf16[640,128]{1,0:T(8,128)(2,1)S(1)} %collective-permute-done.8.refs_7_), channel_id=1, source_target_pairs={{0,2},{1,5},{4,0},{5,9},{8,4},{9,13},{12,8},{13,15},{14,12},{15,11... | collective-permute-start | bytes 491528 | tf_op jit(solution)/shard_map/ppermute | solution.py:278
  21.6 8.8 %collective-permute-start.12 = (bf16[656,128]{1,0:T(8,128)(2,1)S(1)}, bf16[656,128]{1,0:T(8,128)(2,1)S(1)}, u32[]{:S(2)}, u32[]{:S(2)}) collective-permute-start(bf16[656,128]{1,0:T(8,128)(2,1)S(1)} %collective-permute-done.3.refs_8_), channel_id=1, source_target_pairs={{0,4},{1,3},{4,8},{5,1},{8,12},{9,5},{12,14},{13,9},{14,10},{15,13... | collective-permute-start | bytes 503816 | tf_op jit(solution)/shard_map/ppermute | solution.py:278
  22.2 8.2 %collective-permute-start.13 = (bf16[656,128]{1,0:T(8,128)(2,1)S(1)}, bf16[656,128]{1,0:T(8,128)(2,1)S(1)}, u32[]{:S(2)}, u32[]{:S(2)}) collective-permute-start(bf16[656,128]{1,0:T(8,128)(2,1)S(1)} %collective-permute-done.6.refs_0_), channel_id=1, source_target_pairs={{0,2},{1,5},{4,0},{5,9},{8,4},{9,13},{12,8},{13,15},{14,12},{15,11... | collective-permute-start | bytes 503816 | tf_op jit(solution)/shard_map/ppermute | solution.py:278
  24.5 7.4 %collective-permute-start.14 = (bf16[640,128]{1,0:T(8,128)(2,1)S(1)}, bf16[640,128]{1,0:T(8,128)(2,1)S(1)}, u32[]{:S(2)}, u32[]{:S(2)}) collective-permute-start(bf16[640,128]{1,0:T(8,128)(2,1)S(1)} %collective-permute-done.11.refs_9_), channel_id=1, source_target_pairs={{0,4},{1,3},{4,8},{5,1},{8,12},{9,5},{12,14},{13,9},{14,10},{15,13... | collective-permute-start | bytes 491528 | tf_op jit(solution)/shard_map/ppermute | solution.py:278
  25.7 6.3 %collective-permute-start.15 = (bf16[640,128]{1,0:T(8,128)(2,1)S(1)}, bf16[640,128]{1,0:T(8,128)(2,1)S(1)}, u32[]{:S(2)}, u32[]{:S(2)}) collective-permute-start(bf16[640,128]{1,0:T(8,128)(2,1)S(1)} %collective-permute-done.9.refs_1_), channel_id=1, source_target_pairs={{0,2},{1,5},{4,0},{5,9},{8,4},{9,13},{12,8},{13,15},{14,12},{15,11... | collective-permute-start | bytes 491528 | tf_op jit(solution)/shard_map/ppermute | solution.py:278
